TPU v7x, 32 devices: a whole 2x2x4 slice. The times are simulated.
32 devices in a mesh: groups: 2 (over x), expert: 16 (over z, y, core).
Axes of the slice: x: 2, y: 2, z: 4, core: 2. Of those that a mesh axis runs over, the one named last changes fastest.
Arguments:
- hidden: bfloat16 [2, 256, 4096], P(None, ('groups', 'expert')), parts along dimension 1, may hold values from -6 to 6
- queries: bfloat16 [2, 256, 8192], P(None, ('groups', 'expert')), parts along dimension 1
- kv_cache: bfloat16 [2, 256, 128, 2, 512], P(None, ('groups', 'expert')), parts along dimension 1, may hold values from -6 to 6
- lengths: int32 [2, 256], P(None, ('groups', 'expert')), parts along dimension 1, may hold values from 1 to 128, as said below
- routes: int32 [2, 256, 8], P(None, ('groups', 'expert')), parts along dimension 1, may hold values from 0 to 15, all different within a row; in each aligned block of 8 rows (0 to 7, 8 to 15, ..., all dimensions but the last counted through in order) at most 8 rows name the same one
- out_weight: bfloat16 [8192, 4096], P(None, 'expert'), may hold values from -0.0625 to 0.0625
- norm_gain: float32 [4096], replicated, may hold values from 0.5 to 1.5
- router_weight: bfloat16 [4096, 16], replicated, may hold values from -0.09375 to 0.09375
- gate_codes: bfloat16 [16, 4096, 192], P('expert'), may hold values from 0 to 255, as said below
- up_codes: bfloat16 [16, 4096, 192], P('expert'), may hold values from 0 to 255, as said below
- down_codes: bfloat16 [16, 768, 1024], P('expert'), may hold values from 0 to 255, as said below
- codebooks: bfloat16 [16, 3, 256, 4], P('expert'), may hold values from -4 to 4
- gate_up_scale: float32 [16, 2, 768], P('expert'), may hold values from 0.0078125 to 0.03125
- down_scale: float32 [16, 4096], P('expert'), may hold values from 0.018042196 to 0.07216878
Outputs:
- layer_out: bfloat16 [2, 256, 4096], P(None, ('groups', 'expert')), parts along dimension 1
There are 2 independent parts, one for each index of `groups`. A program takes and returns all parts, laid end to end along the dimension named above; an argument that names none is the same for every part. Nothing has to cross between parts.
Inputs may be any that keep to these rules, and one draw needn't show every extreme that they name: `lengths`: at least one sequence of every draw has exactly 128 filled positions. `routes`: A token names 8 different experts; among the sequences of one device in one micro-batch no expert is named more than 8 times, a bound that some block reaches. `gate_codes`: whole numbers. `up_codes`: whole numbers. `down_codes`: whole numbers.
All inputs are finite; a program needn't handle non-finite values.
Results may differ from a plain program's by a relative error of at most 0.0091.
Values may be sent and summed in bfloat16 or wider, within the bound.
No kernel may reach another device: no remote copies, remote signals or barrier semaphores. Data moves between devices by JAX's collectives and lax.ppermute only.
A program may use at most 128 MiB of HBM per device.

v0:
```python
import jax
import jax.numpy as jnp
from jax import lax
from jax.sharding import PartitionSpec as P

HEADS = 64
KV_HEADS = 4
HEAD_DIM = 128


def attend(query_rows, cache_rows, length):
    row_count, positions = (cache_rows.shape[0], cache_rows.shape[1])
    query_heads = query_rows.reshape(row_count, KV_HEADS, HEADS // KV_HEADS, HEAD_DIM)
    key_rows = cache_rows[:, :, 0].reshape(row_count, positions, KV_HEADS, HEAD_DIM)
    value_rows = cache_rows[:, :, 1].reshape(row_count, positions, KV_HEADS, HEAD_DIM)
    scores = jnp.einsum(
        "rgqd,rlgd->rgql", query_heads, key_rows, preferred_element_type=jnp.float32
    ) * HEAD_DIM ** (-0.5)
    visible = jnp.arange(positions, dtype=jnp.int32)[None, :] < length[:, None]
    scores = jnp.where(visible[:, None, None, :], scores, -1e30)
    row_max = jnp.max(scores, axis=-1, keepdims=True)
    weights = jnp.exp(scores - row_max)
    weights = (weights / jnp.sum(weights, axis=-1, keepdims=True)).astype(jnp.bfloat16)
    mixture = jnp.einsum("rgql,rlgd->rgqd", weights, value_rows, preferred_element_type=jnp.float32)
    return mixture.reshape(row_count, HEADS * HEAD_DIM).astype(jnp.bfloat16)


def rms_norm(stream, gain):
    values = stream.astype(jnp.float32)
    return (
        values * lax.rsqrt(jnp.mean(values * values, axis=-1, keepdims=True) + 1e-06) * gain
    ).astype(jnp.bfloat16)


def slot_numbers(choices, experts):
    flattened = choices.reshape(-1)
    matches = (flattened[:, None] == jnp.arange(experts, dtype=jnp.int32)[None, :]).astype(
        jnp.int32
    )
    earlier = jnp.cumsum(matches, axis=0) - matches
    return jnp.sum(earlier * matches, axis=1).reshape(choices.shape)


def expand(code_block, codebook, scales):
    row_total, columns = code_block.shape
    block_rows = row_total // 16
    levels = jnp.arange(codebook.shape[0], dtype=jnp.float32).astype(jnp.bfloat16)
    stacked = code_block.reshape(16, block_rows, columns)
    scale_grid = scales.reshape(1, 4, columns)

    def one_block(segment):
        one_hot = (segment[:, :, None] == levels).astype(jnp.bfloat16)
        partial_value = jnp.einsum(
            "rjk,kc->rcj", one_hot, codebook, preferred_element_type=jnp.float32
        )
        return (partial_value * scale_grid).astype(jnp.bfloat16)

    return lax.map(one_block, stacked).reshape(row_total, 4 * columns)


def experts_apply(rows_in, w_gate, w_up, w_down):
    gate_vals = jnp.dot(rows_in, w_gate, preferred_element_type=jnp.float32)
    up_vals = jnp.dot(rows_in, w_up, preferred_element_type=jnp.float32)
    inner = (jax.nn.silu(gate_vals) * up_vals).astype(jnp.bfloat16)
    return jnp.dot(inner, w_down, preferred_element_type=jnp.float32).astype(jnp.bfloat16)


def body(
    hidden,
    queries,
    kv_cache,
    lengths,
    routes,
    out_weight,
    norm_gain,
    router_weight,
    gate_codes,
    up_codes,
    down_codes,
    codebooks,
    gate_up_scale,
    down_scale,
):
    micro_count, row_count, model_width = hidden.shape
    experts = lax.axis_size("expert")
    top_count = routes.shape[2]
    capacity = max(2, 2 * row_count * top_count // experts)
    w_gate = expand(gate_codes[0], codebooks[0, 0], gate_up_scale[0, 0])
    w_up = expand(up_codes[0], codebooks[0, 1], gate_up_scale[0, 1])
    w_down = expand(down_codes[0], codebooks[0, 2], down_scale[0])
    streams = []
    normed = []
    for micro_idx in range(micro_count):
        attended = attend(queries[micro_idx], kv_cache[micro_idx], lengths[micro_idx])
        column_part = jnp.dot(
            lax.all_gather(attended, "expert", axis=0, tiled=True),
            out_weight,
            preferred_element_type=jnp.float32,
        ).astype(jnp.bfloat16)
        projected = lax.all_to_all(column_part, "expert", split_axis=0, concat_axis=1, tiled=True)
        stream = (hidden[micro_idx].astype(jnp.float32) + projected.astype(jnp.float32)).astype(
            jnp.bfloat16
        )
        streams.append(stream)
        normed.append(rms_norm(stream, norm_gain))
    spans_list = [(index, index + 1) for index in range(micro_count)]
    outputs = []
    for first_idx, last_idx in spans_list:
        tokens = jnp.stack(normed[first_idx:last_idx])
        choices = routes[first_idx:last_idx]
        group_count = tokens.shape[0]
        logits = jnp.einsum(
            "mrd,de->mre", tokens, router_weight, preferred_element_type=jnp.float32
        )
        expert_hot = choices[..., None] == jnp.arange(experts, dtype=jnp.int32)
        chosen = jnp.sum(jnp.where(expert_hot, logits[:, :, None, :], 0.0), axis=-1)
        gate_weights = jax.nn.softmax(chosen, axis=-1).astype(jnp.bfloat16)
        slots = jax.vmap(lambda blocks: slot_numbers(blocks, experts))(choices)
        slot_hot = slots[..., None] == jnp.arange(capacity, dtype=jnp.int32)
        select_own = jnp.einsum(
            "mrke,mrkc->mecr",
            expert_hot.astype(jnp.bfloat16),
            slot_hot.astype(jnp.bfloat16),
            preferred_element_type=jnp.float32,
        ).astype(jnp.bfloat16)
        outgoing = jnp.einsum(
            "mecr,mrd->emcd", select_own, tokens, preferred_element_type=jnp.float32
        ).astype(jnp.bfloat16)
        outgoing = outgoing.reshape(experts, group_count * capacity, model_width)
        arrived = lax.all_to_all(outgoing, "expert", split_axis=0, concat_axis=0, tiled=True)
        results = experts_apply(arrived.reshape(-1, model_width), w_gate, w_up, w_down).reshape(
            arrived.shape
        )
        returned = lax.all_to_all(results, "expert", split_axis=0, concat_axis=0, tiled=True)
        returned = returned.reshape(experts, group_count, capacity, model_width)
        landing_own = expert_hot[..., None] & slot_hot[:, :, :, None, :]
        combine = jnp.sum(
            jnp.where(landing_own, gate_weights.astype(jnp.float32)[..., None, None], 0.0), axis=2
        ).astype(jnp.bfloat16)
        mixture = jnp.einsum(
            "mrec,emcd->mrd", combine, returned, preferred_element_type=jnp.float32
        )
        outputs.append((streams[first_idx].astype(jnp.float32) + mixture[0]).astype(jnp.bfloat16))
    return jnp.stack(outputs)


def solution(mesh):
    in_specs = (
        P(None, ("groups", "expert"), None),
        P(None, ("groups", "expert"), None),
        P(None, ("groups", "expert"), None, None, None),
        P(None, ("groups", "expert")),
        P(None, ("groups", "expert"), None),
        P(None, "expert"),
        P(),
        P(),
        P("expert", None, None),
        P("expert", None, None),
        P("expert", None, None),
        P("expert", None, None, None),
        P("expert", None, None),
        P("expert", None),
    )
    out_specs = P(None, ("groups", "expert"), None)
    return jax.shard_map(body, mesh=mesh, in_specs=in_specs, out_specs=out_specs, check_vma=False)
```

profile of v0, /device:TPU:0, one launch (start us, length us, event | category | flops | bytes accessed | tf_op | source)
XLA Modules:
  0.0 854.3 jit_solution(7250577097165830851)
XLA Ops:
  8.3 6.0 fusion.144
  37.7 217.7 %while.34 = (s32[]{:T(128)}, bf16[16,256,4,192]{1,2,3,0:T(4,128)(2,1)}, bf16[16,256,192]{1,2,0:T(8,128)(2,1)S(1)}, bf16[256,4]{0,1:T(4,128)(2,1)S(1)}, f32[1,4,192]{1,2,0:T(8,128)S(1)}, /*index=5*/s32[]{:T(128)}) while((s32[]{:T(128)}, bf16[16,256,4,192]{1,2,3,0:T(4,128)(2,1)}, bf16[16,256,192]{1,2,0:T(8,128)(2,1)S(1)}, ...), condition=%wide.region_12.13_spmd.clone, body=%wide.region_11.12_spmd.clone.sunk | while | flops 113639680 | bytes 694357 | solution.py:58
  37.7 13.6 %fusion.190 = bf16[16,256,4,192]{1,2,3,0:T(4,128)(2,1)} fusion(bf16[16,256,4,192]{1,2,3,0:T(4,128)(2,1)} %get-tuple-element.345, s32[]{:T(128)S(6)} %copy.123, bf16[256]{0:T(256)(128)(2,1)S(1)} %iota_convert_fusion.7, bf16[256,192]{0,1:T(8,128)(2,1)S(1)} %dynamic-slice_bitcast_fusion.7, f32[4,192]{0,1:T(8,128)S(1)} %bitcast.311, ...), kind=kOutput, calls=%fused_computation.23.clone.1 | convolution fusion | flops 113639424 | bytes 497156 | tf_op jit(solution)/shard_map/while/body/eval_jaxpr/rjk,kc->rcj/dot_general | solution.py:53
  51.3 13.6 %fusion.190 = bf16[16,256,4,192]{1,2,3,0:T(4,128)(2,1)} fusion(bf16[16,256,4,192]{1,2,3,0:T(4,128)(2,1)} %get-tuple-element.345, s32[]{:T(128)S(6)} %copy.123, bf16[256]{0:T(256)(128)(2,1)S(1)} %iota_convert_fusion.7, bf16[256,192]{0,1:T(8,128)(2,1)S(1)} %dynamic-slice_bitcast_fusion.7, f32[4,192]{0,1:T(8,128)S(1)} %bitcast.311, ...), kind=kOutput, calls=%fused_computation.23.clone.1 | convolution fusion | flops 113639424 | bytes 497156 | tf_op jit(solution)/shard_map/while/body/eval_jaxpr/rjk,kc->rcj/dot_general | solution.py:53
  64.9 13.6 %fusion.190 = bf16[16,256,4,192]{1,2,3,0:T(4,128)(2,1)} fusion(bf16[16,256,4,192]{1,2,3,0:T(4,128)(2,1)} %get-tuple-element.345, s32[]{:T(128)S(6)} %copy.123, bf16[256]{0:T(256)(128)(2,1)S(1)} %iota_convert_fusion.7, bf16[256,192]{0,1:T(8,128)(2,1)S(1)} %dynamic-slice_bitcast_fusion.7, f32[4,192]{0,1:T(8,128)S(1)} %bitcast.311, ...), kind=kOutput, calls=%fused_computation.23.clone.1 | convolution fusion | flops 113639424 | bytes 497156 | tf_op jit(solution)/shard_map/while/body/eval_jaxpr/rjk,kc->rcj/dot_general | solution.py:53
  78.5 13.6 %fusion.190 = bf16[16,256,4,192]{1,2,3,0:T(4,128)(2,1)} fusion(bf16[16,256,4,192]{1,2,3,0:T(4,128)(2,1)} %get-tuple-element.345, s32[]{:T(128)S(6)} %copy.123, bf16[256]{0:T(256)(128)(2,1)S(1)} %iota_convert_fusion.7, bf16[256,192]{0,1:T(8,128)(2,1)S(1)} %dynamic-slice_bitcast_fusion.7, f32[4,192]{0,1:T(8,128)S(1)} %bitcast.311, ...), kind=kOutput, calls=%fused_computation.23.clone.1 | convolution fusion | flops 113639424 | bytes 497156 | tf_op jit(solution)/shard_map/while/body/eval_jaxpr/rjk,kc->rcj/dot_general | solution.py:53
  92.1 13.6 %fusion.190 = bf16[16,256,4,192]{1,2,3,0:T(4,128)(2,1)} fusion(bf16[16,256,4,192]{1,2,3,0:T(4,128)(2,1)} %get-tuple-element.345, s32[]{:T(128)S(6)} %copy.123, bf16[256]{0:T(256)(128)(2,1)S(1)} %iota_convert_fusion.7, bf16[256,192]{0,1:T(8,128)(2,1)S(1)} %dynamic-slice_bitcast_fusion.7, f32[4,192]{0,1:T(8,128)S(1)} %bitcast.311, ...), kind=kOutput, calls=%fused_computation.23.clone.1 | convolution fusion | flops 113639424 | bytes 497156 | tf_op jit(solution)/shard_map/while/body/eval_jaxpr/rjk,kc->rcj/dot_general | solution.py:53
  105.7 13.6 %fusion.190 = bf16[16,256,4,192]{1,2,3,0:T(4,128)(2,1)} fusion(bf16[16,256,4,192]{1,2,3,0:T(4,128)(2,1)} %get-tuple-element.345, s32[]{:T(128)S(6)} %copy.123, bf16[256]{0:T(256)(128)(2,1)S(1)} %iota_convert_fusion.7, bf16[256,192]{0,1:T(8,128)(2,1)S(1)} %dynamic-slice_bitcast_fusion.7, f32[4,192]{0,1:T(8,128)S(1)} %bitcast.311, ...), kind=kOutput, calls=%fused_computation.23.clone.1 | convolution fusion | flops 113639424 | bytes 497156 | tf_op jit(solution)/shard_map/while/body/eval_jaxpr/rjk,kc->rcj/dot_general | solution.py:53
  119.3 13.6 %fusion.190 = bf16[16,256,4,192]{1,2,3,0:T(4,128)(2,1)} fusion(bf16[16,256,4,192]{1,2,3,0:T(4,128)(2,1)} %get-tuple-element.345, s32[]{:T(128)S(6)} %copy.123, bf16[256]{0:T(256)(128)(2,1)S(1)} %iota_convert_fusion.7, bf16[256,192]{0,1:T(8,128)(2,1)S(1)} %dynamic-slice_bitcast_fusion.7, f32[4,192]{0,1:T(8,128)S(1)} %bitcast.311, ...), kind=kOutput, calls=%fused_computation.23.clone.1 | convolution fusion | flops 113639424 | bytes 497156 | tf_op jit(solution)/shard_map/while/body/eval_jaxpr/rjk,kc->rcj/dot_general | solution.py:53
  132.9 13.6 %fusion.190 = bf16[16,256,4,192]{1,2,3,0:T(4,128)(2,1)} fusion(bf16[16,256,4,192]{1,2,3,0:T(4,128)(2,1)} %get-tuple-element.345, s32[]{:T(128)S(6)} %copy.123, bf16[256]{0:T(256)(128)(2,1)S(1)} %iota_convert_fusion.7, bf16[256,192]{0,1:T(8,128)(2,1)S(1)} %dynamic-slice_bitcast_fusion.7, f32[4,192]{0,1:T(8,128)S(1)} %bitcast.311, ...), kind=kOutput, calls=%fused_computation.23.clone.1 | convolution fusion | flops 113639424 | bytes 497156 | tf_op jit(solution)/shard_map/while/body/eval_jaxpr/rjk,kc->rcj/dot_general | solution.py:53
  146.5 13.6 %fusion.190 = bf16[16,256,4,192]{1,2,3,0:T(4,128)(2,1)} fusion(bf16[16,256,4,192]{1,2,3,0:T(4,128)(2,1)} %get-tuple-element.345, s32[]{:T(128)S(6)} %copy.123, bf16[256]{0:T(256)(128)(2,1)S(1)} %iota_convert_fusion.7, bf16[256,192]{0,1:T(8,128)(2,1)S(1)} %dynamic-slice_bitcast_fusion.7, f32[4,192]{0,1:T(8,128)S(1)} %bitcast.311, ...), kind=kOutput, calls=%fused_computation.23.clone.1 | convolution fusion | flops 113639424 | bytes 497156 | tf_op jit(solution)/shard_map/while/body/eval_jaxpr/rjk,kc->rcj/dot_general | solution.py:53
  160.1 13.6 %fusion.190 = bf16[16,256,4,192]{1,2,3,0:T(4,128)(2,1)} fusion(bf16[16,256,4,192]{1,2,3,0:T(4,128)(2,1)} %get-tuple-element.345, s32[]{:T(128)S(6)} %copy.123, bf16[256]{0:T(256)(128)(2,1)S(1)} %iota_convert_fusion.7, bf16[256,192]{0,1:T(8,128)(2,1)S(1)} %dynamic-slice_bitcast_fusion.7, f32[4,192]{0,1:T(8,128)S(1)} %bitcast.311, ...), kind=kOutput, calls=%fused_computation.23.clone.1 | convolution fusion | flops 113639424 | bytes 497156 | tf_op jit(solution)/shard_map/while/body/eval_jaxpr/rjk,kc->rcj/dot_general | solution.py:53
  173.7 13.6 %fusion.190 = bf16[16,256,4,192]{1,2,3,0:T(4,128)(2,1)} fusion(bf16[16,256,4,192]{1,2,3,0:T(4,128)(2,1)} %get-tuple-element.345, s32[]{:T(128)S(6)} %copy.123, bf16[256]{0:T(256)(128)(2,1)S(1)} %iota_convert_fusion.7, bf16[256,192]{0,1:T(8,128)(2,1)S(1)} %dynamic-slice_bitcast_fusion.7, f32[4,192]{0,1:T(8,128)S(1)} %bitcast.311, ...), kind=kOutput, calls=%fused_computation.23.clone.1 | convolution fusion | flops 113639424 | bytes 497156 | tf_op jit(solution)/shard_map/while/body/eval_jaxpr/rjk,kc->rcj/dot_general | solution.py:53
  187.3 13.6 %fusion.190 = bf16[16,256,4,192]{1,2,3,0:T(4,128)(2,1)} fusion(bf16[16,256,4,192]{1,2,3,0:T(4,128)(2,1)} %get-tuple-element.345, s32[]{:T(128)S(6)} %copy.123, bf16[256]{0:T(256)(128)(2,1)S(1)} %iota_convert_fusion.7, bf16[256,192]{0,1:T(8,128)(2,1)S(1)} %dynamic-slice_bitcast_fusion.7, f32[4,192]{0,1:T(8,128)S(1)} %bitcast.311, ...), kind=kOutput, calls=%fused_computation.23.clone.1 | convolution fusion | flops 113639424 | bytes 497156 | tf_op jit(solution)/shard_map/while/body/eval_jaxpr/rjk,kc->rcj/dot_general | solution.py:53
  200.9 13.6 %fusion.190 = bf16[16,256,4,192]{1,2,3,0:T(4,128)(2,1)} fusion(bf16[16,256,4,192]{1,2,3,0:T(4,128)(2,1)} %get-tuple-element.345, s32[]{:T(128)S(6)} %copy.123, bf16[256]{0:T(256)(128)(2,1)S(1)} %iota_convert_fusion.7, bf16[256,192]{0,1:T(8,128)(2,1)S(1)} %dynamic-slice_bitcast_fusion.7, f32[4,192]{0,1:T(8,128)S(1)} %bitcast.311, ...), kind=kOutput, calls=%fused_computation.23.clone.1 | convolution fusion | flops 113639424 | bytes 497156 | tf_op jit(solution)/shard_map/while/body/eval_jaxpr/rjk,kc->rcj/dot_general | solution.py:53
  214.5 13.6 %fusion.190 = bf16[16,256,4,192]{1,2,3,0:T(4,128)(2,1)} fusion(bf16[16,256,4,192]{1,2,3,0:T(4,128)(2,1)} %get-tuple-element.345, s32[]{:T(128)S(6)} %copy.123, bf16[256]{0:T(256)(128)(2,1)S(1)} %iota_convert_fusion.7, bf16[256,192]{0,1:T(8,128)(2,1)S(1)} %dynamic-slice_bitcast_fusion.7, f32[4,192]{0,1:T(8,128)S(1)} %bitcast.311, ...), kind=kOutput, calls=%fused_computation.23.clone.1 | convolution fusion | flops 113639424 | bytes 497156 | tf_op jit(solution)/shard_map/while/body/eval_jaxpr/rjk,kc->rcj/dot_general | solution.py:53
  228.1 13.6 %fusion.190 = bf16[16,256,4,192]{1,2,3,0:T(4,128)(2,1)} fusion(bf16[16,256,4,192]{1,2,3,0:T(4,128)(2,1)} %get-tuple-element.345, s32[]{:T(128)S(6)} %copy.123, bf16[256]{0:T(256)(128)(2,1)S(1)} %iota_convert_fusion.7, bf16[256,192]{0,1:T(8,128)(2,1)S(1)} %dynamic-slice_bitcast_fusion.7, f32[4,192]{0,1:T(8,128)S(1)} %bitcast.311, ...), kind=kOutput, calls=%fused_computation.23.clone.1 | convolution fusion | flops 113639424 | bytes 497156 | tf_op jit(solution)/shard_map/while/body/eval_jaxpr/rjk,kc->rcj/dot_general | solution.py:53
  241.7 13.6 %fusion.190 = bf16[16,256,4,192]{1,2,3,0:T(4,128)(2,1)} fusion(bf16[16,256,4,192]{1,2,3,0:T(4,128)(2,1)} %get-tuple-element.345, s32[]{:T(128)S(6)} %copy.123, bf16[256]{0:T(256)(128)(2,1)S(1)} %iota_convert_fusion.7, bf16[256,192]{0,1:T(8,128)(2,1)S(1)} %dynamic-slice_bitcast_fusion.7, f32[4,192]{0,1:T(8,128)S(1)} %bitcast.311, ...), kind=kOutput, calls=%fused_computation.23.clone.1 | convolution fusion | flops 113639424 | bytes 497156 | tf_op jit(solution)/shard_map/while/body/eval_jaxpr/rjk,kc->rcj/dot_general | solution.py:53
  261.3 7.4 all-to-all-start
  279.4 6.6 all-to-all-done.3
  297.4 217.7 %while.33 = (s32[]{:T(128)}, bf16[16,256,4,192]{1,2,3,0:T(4,128)(2,1)}, bf16[16,256,192]{1,2,0:T(8,128)(2,1)S(1)}, bf16[256,4]{0,1:T(4,128)(2,1)S(1)}, f32[1,4,192]{1,2,0:T(8,128)S(1)}, /*index=5*/s32[]{:T(128)}) while((s32[]{:T(128)}, bf16[16,256,4,192]{1,2,3,0:T(4,128)(2,1)}, bf16[16,256,192]{1,2,0:T(8,128)(2,1)S(1)}, ...), condition=%wide.region_10.11_spmd.clone, body=%wide.region_9.10_spmd.clone.sunk | while | flops 113639680 | bytes 694357 | solution.py:58
  297.4 13.6 %fusion.187 = bf16[16,256,4,192]{1,2,3,0:T(4,128)(2,1)} fusion(bf16[16,256,4,192]{1,2,3,0:T(4,128)(2,1)} %get-tuple-element.363, s32[]{:T(128)S(6)} %copy.129, bf16[256]{0:T(256)(128)(2,1)S(1)} %iota_convert_fusion.6, bf16[256,192]{0,1:T(8,128)(2,1)S(1)} %dynamic-slice_bitcast_fusion.6, f32[4,192]{0,1:T(8,128)S(1)} %bitcast.310, ...), kind=kOutput, calls=%fused_computation.11.clone.1 | convolution fusion | flops 113639424 | bytes 497156 | tf_op jit(solution)/shard_map/while/body/eval_jaxpr/rjk,kc->rcj/dot_general | solution.py:53
  311.0 13.6 %fusion.187 = bf16[16,256,4,192]{1,2,3,0:T(4,128)(2,1)} fusion(bf16[16,256,4,192]{1,2,3,0:T(4,128)(2,1)} %get-tuple-element.363, s32[]{:T(128)S(6)} %copy.129, bf16[256]{0:T(256)(128)(2,1)S(1)} %iota_convert_fusion.6, bf16[256,192]{0,1:T(8,128)(2,1)S(1)} %dynamic-slice_bitcast_fusion.6, f32[4,192]{0,1:T(8,128)S(1)} %bitcast.310, ...), kind=kOutput, calls=%fused_computation.11.clone.1 | convolution fusion | flops 113639424 | bytes 497156 | tf_op jit(solution)/shard_map/while/body/eval_jaxpr/rjk,kc->rcj/dot_general | solution.py:53
  324.6 13.6 %fusion.187 = bf16[16,256,4,192]{1,2,3,0:T(4,128)(2,1)} fusion(bf16[16,256,4,192]{1,2,3,0:T(4,128)(2,1)} %get-tuple-element.363, s32[]{:T(128)S(6)} %copy.129, bf16[256]{0:T(256)(128)(2,1)S(1)} %iota_convert_fusion.6, bf16[256,192]{0,1:T(8,128)(2,1)S(1)} %dynamic-slice_bitcast_fusion.6, f32[4,192]{0,1:T(8,128)S(1)} %bitcast.310, ...), kind=kOutput, calls=%fused_computation.11.clone.1 | convolution fusion | flops 113639424 | bytes 497156 | tf_op jit(solution)/shard_map/while/body/eval_jaxpr/rjk,kc->rcj/dot_general | solution.py:53
  338.2 13.6 %fusion.187 = bf16[16,256,4,192]{1,2,3,0:T(4,128)(2,1)} fusion(bf16[16,256,4,192]{1,2,3,0:T(4,128)(2,1)} %get-tuple-element.363, s32[]{:T(128)S(6)} %copy.129, bf16[256]{0:T(256)(128)(2,1)S(1)} %iota_convert_fusion.6, bf16[256,192]{0,1:T(8,128)(2,1)S(1)} %dynamic-slice_bitcast_fusion.6, f32[4,192]{0,1:T(8,128)S(1)} %bitcast.310, ...), kind=kOutput, calls=%fused_computation.11.clone.1 | convolution fusion | flops 113639424 | bytes 497156 | tf_op jit(solution)/shard_map/while/body/eval_jaxpr/rjk,kc->rcj/dot_general | solution.py:53
  351.9 13.6 %fusion.187 = bf16[16,256,4,192]{1,2,3,0:T(4,128)(2,1)} fusion(bf16[16,256,4,192]{1,2,3,0:T(4,128)(2,1)} %get-tuple-element.363, s32[]{:T(128)S(6)} %copy.129, bf16[256]{0:T(256)(128)(2,1)S(1)} %iota_convert_fusion.6, bf16[256,192]{0,1:T(8,128)(2,1)S(1)} %dynamic-slice_bitcast_fusion.6, f32[4,192]{0,1:T(8,128)S(1)} %bitcast.310, ...), kind=kOutput, calls=%fused_computation.11.clone.1 | convolution fusion | flops 113639424 | bytes 497156 | tf_op jit(solution)/shard_map/while/body/eval_jaxpr/rjk,kc->rcj/dot_general | solution.py:53
  365.5 13.6 %fusion.187 = bf16[16,256,4,192]{1,2,3,0:T(4,128)(2,1)} fusion(bf16[16,256,4,192]{1,2,3,0:T(4,128)(2,1)} %get-tuple-element.363, s32[]{:T(128)S(6)} %copy.129, bf16[256]{0:T(256)(128)(2,1)S(1)} %iota_convert_fusion.6, bf16[256,192]{0,1:T(8,128)(2,1)S(1)} %dynamic-slice_bitcast_fusion.6, f32[4,192]{0,1:T(8,128)S(1)} %bitcast.310, ...), kind=kOutput, calls=%fused_computation.11.clone.1 | convolution fusion | flops 113639424 | bytes 497156 | tf_op jit(solution)/shard_map/while/body/eval_jaxpr/rjk,kc->rcj/dot_general | solution.py:53
  379.1 13.6 %fusion.187 = bf16[16,256,4,192]{1,2,3,0:T(4,128)(2,1)} fusion(bf16[16,256,4,192]{1,2,3,0:T(4,128)(2,1)} %get-tuple-element.363, s32[]{:T(128)S(6)} %copy.129, bf16[256]{0:T(256)(128)(2,1)S(1)} %iota_convert_fusion.6, bf16[256,192]{0,1:T(8,128)(2,1)S(1)} %dynamic-slice_bitcast_fusion.6, f32[4,192]{0,1:T(8,128)S(1)} %bitcast.310, ...), kind=kOutput, calls=%fused_computation.11.clone.1 | convolution fusion | flops 113639424 | bytes 497156 | tf_op jit(solution)/shard_map/while/body/eval_jaxpr/rjk,kc->rcj/dot_general | solution.py:53
  392.7 13.6 %fusion.187 = bf16[16,256,4,192]{1,2,3,0:T(4,128)(2,1)} fusion(bf16[16,256,4,192]{1,2,3,0:T(4,128)(2,1)} %get-tuple-element.363, s32[]{:T(128)S(6)} %copy.129, bf16[256]{0:T(256)(128)(2,1)S(1)} %iota_convert_fusion.6, bf16[256,192]{0,1:T(8,128)(2,1)S(1)} %dynamic-slice_bitcast_fusion.6, f32[4,192]{0,1:T(8,128)S(1)} %bitcast.310, ...), kind=kOutput, calls=%fused_computation.11.clone.1 | convolution fusion | flops 113639424 | bytes 497156 | tf_op jit(solution)/shard_map/while/body/eval_jaxpr/rjk,kc->rcj/dot_general | solution.py:53
  406.3 13.6 %fusion.187 = bf16[16,256,4,192]{1,2,3,0:T(4,128)(2,1)} fusion(bf16[16,256,4,192]{1,2,3,0:T(4,128)(2,1)} %get-tuple-element.363, s32[]{:T(128)S(6)} %copy.129, bf16[256]{0:T(256)(128)(2,1)S(1)} %iota_convert_fusion.6, bf16[256,192]{0,1:T(8,128)(2,1)S(1)} %dynamic-slice_bitcast_fusion.6, f32[4,192]{0,1:T(8,128)S(1)} %bitcast.310, ...), kind=kOutput, calls=%fused_computation.11.clone.1 | convolution fusion | flops 113639424 | bytes 497156 | tf_op jit(solution)/shard_map/while/body/eval_jaxpr/rjk,kc->rcj/dot_general | solution.py:53
  419.9 13.6 %fusion.187 = bf16[16,256,4,192]{1,2,3,0:T(4,128)(2,1)} fusion(bf16[16,256,4,192]{1,2,3,0:T(4,128)(2,1)} %get-tuple-element.363, s32[]{:T(128)S(6)} %copy.129, bf16[256]{0:T(256)(128)(2,1)S(1)} %iota_convert_fusion.6, bf16[256,192]{0,1:T(8,128)(2,1)S(1)} %dynamic-slice_bitcast_fusion.6, f32[4,192]{0,1:T(8,128)S(1)} %bitcast.310, ...), kind=kOutput, calls=%fused_computation.11.clone.1 | convolution fusion | flops 113639424 | bytes 497156 | tf_op jit(solution)/shard_map/while/body/eval_jaxpr/rjk,kc->rcj/dot_general | solution.py:53
  433.5 13.6 %fusion.187 = bf16[16,256,4,192]{1,2,3,0:T(4,128)(2,1)} fusion(bf16[16,256,4,192]{1,2,3,0:T(4,128)(2,1)} %get-tuple-element.363, s32[]{:T(128)S(6)} %copy.129, bf16[256]{0:T(256)(128)(2,1)S(1)} %iota_convert_fusion.6, bf16[256,192]{0,1:T(8,128)(2,1)S(1)} %dynamic-slice_bitcast_fusion.6, f32[4,192]{0,1:T(8,128)S(1)} %bitcast.310, ...), kind=kOutput, calls=%fused_computation.11.clone.1 | convolution fusion | flops 113639424 | bytes 497156 | tf_op jit(solution)/shard_map/while/body/eval_jaxpr/rjk,kc->rcj/dot_general | solution.py:53
  447.1 13.6 %fusion.187 = bf16[16,256,4,192]{1,2,3,0:T(4,128)(2,1)} fusion(bf16[16,256,4,192]{1,2,3,0:T(4,128)(2,1)} %get-tuple-element.363, s32[]{:T(128)S(6)} %copy.129, bf16[256]{0:T(256)(128)(2,1)S(1)} %iota_convert_fusion.6, bf16[256,192]{0,1:T(8,128)(2,1)S(1)} %dynamic-slice_bitcast_fusion.6, f32[4,192]{0,1:T(8,128)S(1)} %bitcast.310, ...), kind=kOutput, calls=%fused_computation.11.clone.1 | convolution fusion | flops 113639424 | bytes 497156 | tf_op jit(solution)/shard_map/while/body/eval_jaxpr/rjk,kc->rcj/dot_general | solution.py:53
  460.7 13.6 %fusion.187 = bf16[16,256,4,192]{1,2,3,0:T(4,128)(2,1)} fusion(bf16[16,256,4,192]{1,2,3,0:T(4,128)(2,1)} %get-tuple-element.363, s32[]{:T(128)S(6)} %copy.129, bf16[256]{0:T(256)(128)(2,1)S(1)} %iota_convert_fusion.6, bf16[256,192]{0,1:T(8,128)(2,1)S(1)} %dynamic-slice_bitcast_fusion.6, f32[4,192]{0,1:T(8,128)S(1)} %bitcast.310, ...), kind=kOutput, calls=%fused_computation.11.clone.1 | convolution fusion | flops 113639424 | bytes 497156 | tf_op jit(solution)/shard_map/while/body/eval_jaxpr/rjk,kc->rcj/dot_general | solution.py:53
  474.3 13.6 %fusion.187 = bf16[16,256,4,192]{1,2,3,0:T(4,128)(2,1)} fusion(bf16[16,256,4,192]{1,2,3,0:T(4,128)(2,1)} %get-tuple-element.363, s32[]{:T(128)S(6)} %copy.129, bf16[256]{0:T(256)(128)(2,1)S(1)} %iota_convert_fusion.6, bf16[256,192]{0,1:T(8,128)(2,1)S(1)} %dynamic-slice_bitcast_fusion.6, f32[4,192]{0,1:T(8,128)S(1)} %bitcast.310, ...), kind=kOutput, calls=%fused_computation.11.clone.1 | convolution fusion | flops 113639424 | bytes 497156 | tf_op jit(solution)/shard_map/while/body/eval_jaxpr/rjk,kc->rcj/dot_general | solution.py:53
  487.9 13.6 %fusion.187 = bf16[16,256,4,192]{1,2,3,0:T(4,128)(2,1)} fusion(bf16[16,256,4,192]{1,2,3,0:T(4,128)(2,1)} %get-tuple-element.363, s32[]{:T(128)S(6)} %copy.129, bf16[256]{0:T(256)(128)(2,1)S(1)} %iota_convert_fusion.6, bf16[256,192]{0,1:T(8,128)(2,1)S(1)} %dynamic-slice_bitcast_fusion.6, f32[4,192]{0,1:T(8,128)S(1)} %bitcast.310, ...), kind=kOutput, calls=%fused_computation.11.clone.1 | convolution fusion | flops 113639424 | bytes 497156 | tf_op jit(solution)/shard_map/while/body/eval_jaxpr/rjk,kc->rcj/dot_general | solution.py:53
  501.5 13.6 %fusion.187 = bf16[16,256,4,192]{1,2,3,0:T(4,128)(2,1)} fusion(bf16[16,256,4,192]{1,2,3,0:T(4,128)(2,1)} %get-tuple-element.363, s32[]{:T(128)S(6)} %copy.129, bf16[256]{0:T(256)(128)(2,1)S(1)} %iota_convert_fusion.6, bf16[256,192]{0,1:T(8,128)(2,1)S(1)} %dynamic-slice_bitcast_fusion.6, f32[4,192]{0,1:T(8,128)S(1)} %bitcast.310, ...), kind=kOutput, calls=%fused_computation.11.clone.1 | convolution fusion | flops 113639424 | bytes 497156 | tf_op jit(solution)/shard_map/while/body/eval_jaxpr/rjk,kc->rcj/dot_general | solution.py:53
  519.2 6.1 all-to-all-start.4
  525.3 207.8 %while.35 = (s32[]{:T(128)}, bf16[16,48,4,1024]{3,2,1,0:T(4,128)(2,1)}, bf16[16,48,1024]{2,1,0:T(8,128)(2,1)}, bf16[256,4]{0,1:T(4,128)(2,1)S(1)}, f32[1,4,1024]{2,1,0:T(4,128)S(1)}, /*index=5*/s32[]{:T(128)}) while((s32[]{:T(128)}, bf16[16,48,4,1024]{3,2,1,0:T(4,128)(2,1)}, bf16[16,48,1024]{2,1,0:T(8,128)(2,1)}, ...), condition=%wide.region_14.15_spmd.clone, body=%wide.region_13.14_spmd.clone.sunk | while | flops 113639680 | bytes 707669 | solution.py:58
  526.2 12.1 %fusion.193 = bf16[16,48,4,1024]{3,2,1,0:T(4,128)(2,1)} fusion(bf16[16,48,4,1024]{3,2,1,0:T(4,128)(2,1)} %get-tuple-element.327, s32[]{:T(128)S(6)} %copy.117, bf16[256]{0:T(256)(128)(2,1)S(1)} %iota_convert_fusion.8, bf16[48,1024]{1,0:T(8,128)(2,1)S(1)} %dynamic-slice_bitcast_fusion.8, f32[4,1024]{1,0:T(4,128)S(1)} %bitcast.312, ...), kind=kOutput, calls=%fused_computation.35.clone.1 | convolution fusion | flops 113639424 | bytes 510468 | tf_op jit(solution)/shard_map/while/body/eval_jaxpr/rjk,kc->rcj/dot_general | solution.py:53
  539.2 12.1 %fusion.193 = bf16[16,48,4,1024]{3,2,1,0:T(4,128)(2,1)} fusion(bf16[16,48,4,1024]{3,2,1,0:T(4,128)(2,1)} %get-tuple-element.327, s32[]{:T(128)S(6)} %copy.117, bf16[256]{0:T(256)(128)(2,1)S(1)} %iota_convert_fusion.8, bf16[48,1024]{1,0:T(8,128)(2,1)S(1)} %dynamic-slice_bitcast_fusion.8, f32[4,1024]{1,0:T(4,128)S(1)} %bitcast.312, ...), kind=kOutput, calls=%fused_computation.35.clone.1 | convolution fusion | flops 113639424 | bytes 510468 | tf_op jit(solution)/shard_map/while/body/eval_jaxpr/rjk,kc->rcj/dot_general | solution.py:53
  552.2 12.1 %fusion.193 = bf16[16,48,4,1024]{3,2,1,0:T(4,128)(2,1)} fusion(bf16[16,48,4,1024]{3,2,1,0:T(4,128)(2,1)} %get-tuple-element.327, s32[]{:T(128)S(6)} %copy.117, bf16[256]{0:T(256)(128)(2,1)S(1)} %iota_convert_fusion.8, bf16[48,1024]{1,0:T(8,128)(2,1)S(1)} %dynamic-slice_bitcast_fusion.8, f32[4,1024]{1,0:T(4,128)S(1)} %bitcast.312, ...), kind=kOutput, calls=%fused_computation.35.clone.1 | convolution fusion | flops 113639424 | bytes 510468 | tf_op jit(solution)/shard_map/while/body/eval_jaxpr/rjk,kc->rcj/dot_general | solution.py:53
  565.2 12.1 %fusion.193 = bf16[16,48,4,1024]{3,2,1,0:T(4,128)(2,1)} fusion(bf16[16,48,4,1024]{3,2,1,0:T(4,128)(2,1)} %get-tuple-element.327, s32[]{:T(128)S(6)} %copy.117, bf16[256]{0:T(256)(128)(2,1)S(1)} %iota_convert_fusion.8, bf16[48,1024]{1,0:T(8,128)(2,1)S(1)} %dynamic-slice_bitcast_fusion.8, f32[4,1024]{1,0:T(4,128)S(1)} %bitcast.312, ...), kind=kOutput, calls=%fused_computation.35.clone.1 | convolution fusion | flops 113639424 | bytes 510468 | tf_op jit(solution)/shard_map/while/body/eval_jaxpr/rjk,kc->rcj/dot_general | solution.py:53
  578.1 12.1 %fusion.193 = bf16[16,48,4,1024]{3,2,1,0:T(4,128)(2,1)} fusion(bf16[16,48,4,1024]{3,2,1,0:T(4,128)(2,1)} %get-tuple-element.327, s32[]{:T(128)S(6)} %copy.117, bf16[256]{0:T(256)(128)(2,1)S(1)} %iota_convert_fusion.8, bf16[48,1024]{1,0:T(8,128)(2,1)S(1)} %dynamic-slice_bitcast_fusion.8, f32[4,1024]{1,0:T(4,128)S(1)} %bitcast.312, ...), kind=kOutput, calls=%fused_computation.35.clone.1 | convolution fusion | flops 113639424 | bytes 510468 | tf_op jit(solution)/shard_map/while/body/eval_jaxpr/rjk,kc->rcj/dot_general | solution.py:53
  591.1 12.1 %fusion.193 = bf16[16,48,4,1024]{3,2,1,0:T(4,128)(2,1)} fusion(bf16[16,48,4,1024]{3,2,1,0:T(4,128)(2,1)} %get-tuple-element.327, s32[]{:T(128)S(6)} %copy.117, bf16[256]{0:T(256)(128)(2,1)S(1)} %iota_convert_fusion.8, bf16[48,1024]{1,0:T(8,128)(2,1)S(1)} %dynamic-slice_bitcast_fusion.8, f32[4,1024]{1,0:T(4,128)S(1)} %bitcast.312, ...), kind=kOutput, calls=%fused_computation.35.clone.1 | convolution fusion | flops 113639424 | bytes 510468 | tf_op jit(solution)/shard_map/while/body/eval_jaxpr/rjk,kc->rcj/dot_general | solution.py:53
  604.1 12.1 %fusion.193 = bf16[16,48,4,1024]{3,2,1,0:T(4,128)(2,1)} fusion(bf16[16,48,4,1024]{3,2,1,0:T(4,128)(2,1)} %get-tuple-element.327, s32[]{:T(128)S(6)} %copy.117, bf16[256]{0:T(256)(128)(2,1)S(1)} %iota_convert_fusion.8, bf16[48,1024]{1,0:T(8,128)(2,1)S(1)} %dynamic-slice_bitcast_fusion.8, f32[4,1024]{1,0:T(4,128)S(1)} %bitcast.312, ...), kind=kOutput, calls=%fused_computation.35.clone.1 | convolution fusion | flops 113639424 | bytes 510468 | tf_op jit(solution)/shard_map/while/body/eval_jaxpr/rjk,kc->rcj/dot_general | solution.py:53
  617.1 12.1 %fusion.193 = bf16[16,48,4,1024]{3,2,1,0:T(4,128)(2,1)} fusion(bf16[16,48,4,1024]{3,2,1,0:T(4,128)(2,1)} %get-tuple-element.327, s32[]{:T(128)S(6)} %copy.117, bf16[256]{0:T(256)(128)(2,1)S(1)} %iota_convert_fusion.8, bf16[48,1024]{1,0:T(8,128)(2,1)S(1)} %dynamic-slice_bitcast_fusion.8, f32[4,1024]{1,0:T(4,128)S(1)} %bitcast.312, ...), kind=kOutput, calls=%fused_computation.35.clone.1 | convolution fusion | flops 113639424 | bytes 510468 | tf_op jit(solution)/shard_map/while/body/eval_jaxpr/rjk,kc->rcj/dot_general | solution.py:53
  630.1 12.1 %fusion.193 = bf16[16,48,4,1024]{3,2,1,0:T(4,128)(2,1)} fusion(bf16[16,48,4,1024]{3,2,1,0:T(4,128)(2,1)} %get-tuple-element.327, s32[]{:T(128)S(6)} %copy.117, bf16[256]{0:T(256)(128)(2,1)S(1)} %iota_convert_fusion.8, bf16[48,1024]{1,0:T(8,128)(2,1)S(1)} %dynamic-slice_bitcast_fusion.8, f32[4,1024]{1,0:T(4,128)S(1)} %bitcast.312, ...), kind=kOutput, calls=%fused_computation.35.clone.1 | convolution fusion | flops 113639424 | bytes 510468 | tf_op jit(solution)/shard_map/while/body/eval_jaxpr/rjk,kc->rcj/dot_general | solution.py:53
  643.1 12.1 %fusion.193 = bf16[16,48,4,1024]{3,2,1,0:T(4,128)(2,1)} fusion(bf16[16,48,4,1024]{3,2,1,0:T(4,128)(2,1)} %get-tuple-element.327, s32[]{:T(128)S(6)} %copy.117, bf16[256]{0:T(256)(128)(2,1)S(1)} %iota_convert_fusion.8, bf16[48,1024]{1,0:T(8,128)(2,1)S(1)} %dynamic-slice_bitcast_fusion.8, f32[4,1024]{1,0:T(4,128)S(1)} %bitcast.312, ...), kind=kOutput, calls=%fused_computation.35.clone.1 | convolution fusion | flops 113639424 | bytes 510468 | tf_op jit(solution)/shard_map/while/body/eval_jaxpr/rjk,kc->rcj/dot_general | solution.py:53
  656.0 12.1 %fusion.193 = bf16[16,48,4,1024]{3,2,1,0:T(4,128)(2,1)} fusion(bf16[16,48,4,1024]{3,2,1,0:T(4,128)(2,1)} %get-tuple-element.327, s32[]{:T(128)S(6)} %copy.117, bf16[256]{0:T(256)(128)(2,1)S(1)} %iota_convert_fusion.8, bf16[48,1024]{1,0:T(8,128)(2,1)S(1)} %dynamic-slice_bitcast_fusion.8, f32[4,1024]{1,0:T(4,128)S(1)} %bitcast.312, ...), kind=kOutput, calls=%fused_computation.35.clone.1 | convolution fusion | flops 113639424 | bytes 510468 | tf_op jit(solution)/shard_map/while/body/eval_jaxpr/rjk,kc->rcj/dot_general | solution.py:53
  669.0 12.1 %fusion.193 = bf16[16,48,4,1024]{3,2,1,0:T(4,128)(2,1)} fusion(bf16[16,48,4,1024]{3,2,1,0:T(4,128)(2,1)} %get-tuple-element.327, s32[]{:T(128)S(6)} %copy.117, bf16[256]{0:T(256)(128)(2,1)S(1)} %iota_convert_fusion.8, bf16[48,1024]{1,0:T(8,128)(2,1)S(1)} %dynamic-slice_bitcast_fusion.8, f32[4,1024]{1,0:T(4,128)S(1)} %bitcast.312, ...), kind=kOutput, calls=%fused_computation.35.clone.1 | convolution fusion | flops 113639424 | bytes 510468 | tf_op jit(solution)/shard_map/while/body/eval_jaxpr/rjk,kc->rcj/dot_general | solution.py:53
  682.0 12.1 %fusion.193 = bf16[16,48,4,1024]{3,2,1,0:T(4,128)(2,1)} fusion(bf16[16,48,4,1024]{3,2,1,0:T(4,128)(2,1)} %get-tuple-element.327, s32[]{:T(128)S(6)} %copy.117, bf16[256]{0:T(256)(128)(2,1)S(1)} %iota_convert_fusion.8, bf16[48,1024]{1,0:T(8,128)(2,1)S(1)} %dynamic-slice_bitcast_fusion.8, f32[4,1024]{1,0:T(4,128)S(1)} %bitcast.312, ...), kind=kOutput, calls=%fused_computation.35.clone.1 | convolution fusion | flops 113639424 | bytes 510468 | tf_op jit(solution)/shard_map/while/body/eval_jaxpr/rjk,kc->rcj/dot_general | solution.py:53
  695.0 12.1 %fusion.193 = bf16[16,48,4,1024]{3,2,1,0:T(4,128)(2,1)} fusion(bf16[16,48,4,1024]{3,2,1,0:T(4,128)(2,1)} %get-tuple-element.327, s32[]{:T(128)S(6)} %copy.117, bf16[256]{0:T(256)(128)(2,1)S(1)} %iota_convert_fusion.8, bf16[48,1024]{1,0:T(8,128)(2,1)S(1)} %dynamic-slice_bitcast_fusion.8, f32[4,1024]{1,0:T(4,128)S(1)} %bitcast.312, ...), kind=kOutput, calls=%fused_computation.35.clone.1 | convolution fusion | flops 113639424 | bytes 510468 | tf_op jit(solution)/shard_map/while/body/eval_jaxpr/rjk,kc->rcj/dot_general | solution.py:53
  708.0 12.1 %fusion.193 = bf16[16,48,4,1024]{3,2,1,0:T(4,128)(2,1)} fusion(bf16[16,48,4,1024]{3,2,1,0:T(4,128)(2,1)} %get-tuple-element.327, s32[]{:T(128)S(6)} %copy.117, bf16[256]{0:T(256)(128)(2,1)S(1)} %iota_convert_fusion.8, bf16[48,1024]{1,0:T(8,128)(2,1)S(1)} %dynamic-slice_bitcast_fusion.8, f32[4,1024]{1,0:T(4,128)S(1)} %bitcast.312, ...), kind=kOutput, calls=%fused_computation.35.clone.1 | convolution fusion | flops 113639424 | bytes 510468 | tf_op jit(solution)/shard_map/while/body/eval_jaxpr/rjk,kc->rcj/dot_general | solution.py:53
  721.0 12.1 %fusion.193 = bf16[16,48,4,1024]{3,2,1,0:T(4,128)(2,1)} fusion(bf16[16,48,4,1024]{3,2,1,0:T(4,128)(2,1)} %get-tuple-element.327, s32[]{:T(128)S(6)} %copy.117, bf16[256]{0:T(256)(128)(2,1)S(1)} %iota_convert_fusion.8, bf16[48,1024]{1,0:T(8,128)(2,1)S(1)} %dynamic-slice_bitcast_fusion.8, f32[4,1024]{1,0:T(4,128)S(1)} %bitcast.312, ...), kind=kOutput, calls=%fused_computation.35.clone.1 | convolution fusion | flops 113639424 | bytes 510468 | tf_op jit(solution)/shard_map/while/body/eval_jaxpr/rjk,kc->rcj/dot_general | solution.py:53
  733.0 6.5 copy.72
  739.6 6.9 copy.100
  750.1 13.0 %copy.98 = bf16[96,8,16,256]{3,1,2,0:T(8,128)(2,1)S(1)} copy(bf16[96,8,16,256]{3,2,1,0:T(8,128)(2,1)S(1)} %bitcast.287) | data formatting | bytes 12582912
  763.1 11.8 %copy.101 = bf16[96,8,4,1024]{3,1,2,0:T(8,128)(2,1)} copy(bf16[96,8,4,1024]{3,2,1,0:T(4,128)(2,1)} %bitcast.290) | data formatting | bytes 12582912
  777.2 9.9 %fusion.70 = bf16[16,8,4096]{2,1,0:T(8,128)(2,1)} fusion(bf16[768,4096]{1,0:T(8,128)(2,1)} %bitcast.280, bf16[4096,768]{0,1:T(8,128)(2,1)} %bitcast.278, bf16[16,8,4096]{2,1,0:T(8,128)(2,1)S(1)} %all-to-all-done.1, f32[128,768]{1,0:T(8,128)S(1)} %fusion.92), kind=kOutput, calls=%fused_computation.47 | convolution fusion | flops 1611726848 | bytes 15073280 | tf_op jit(solution)/shard_map/dot_general | solution.py:65
  798.2 9.6 %fusion.71 = bf16[16,8,4096]{2,1,0:T(8,128)(2,1)} fusion(bf16[768,4096]{1,0:T(8,128)(2,1)} %bitcast.281, bf16[4096,768]{0,1:T(8,128)(2,1)} %bitcast.279, bf16[16,8,4096]{2,1,0:T(8,128)(2,1)S(1)} %all-to-all-done.4, f32[128,768]{1,0:T(8,128)S(1)} %fusion.89), kind=kOutput, calls=%fused_computation.48 | convolution fusion | flops 1611726848 | bytes 15073280 | tf_op jit(solution)/shard_map/dot_general | solution.py:65
  807.9 8.2 all-to-all-done.2
  816.1 6.9 all-to-all-start.5
  826.0 19.9 %all-to-all-done.5 = bf16[16,8,4096]{2,1,0:T(8,128)(2,1)S(1)} async-done(((bf16[16,8,4096]{2,1,0:T(8,128)(2,1)}), bf16[16,8,4096]{2,1,0:T(8,128)(2,1)S(1)}, u32[]{:S(2)}, u32[]{:S(2)}) %all-to-all-start.5) | async-done | bytes 1048608 | tf_op jit(solution)/shard_map/all_to_all | solution.py:134
  (216 shorter events, 93.1 us)
Async XLA Ops:
  6.5 816.6 %copy-start = (bf16[4096,16]{0,1:T(8,128)(2,1)S(1)}, bf16[4096,16]{0,1:T(8,128)(2,1)}, u32[]{:S(2)}) copy-start(bf16[4096,16]{0,1:T(8,128)(2,1)} %param.27) | copy-start | bytes 393220
  6.5 250.6 %all-gather.3.cloned.1.call-start = ((), (), s32[]{:S(2)}) async-start(), calls=%async_computation.6 | async-start | bytes 2228224 | tf_op jit(solution)/shard_map/all_gather | solution.py:96
  22.4 7.5 copy-start.8
  22.4 7.5 copy-start.7
  22.4 246.4 %all-gather.5.cloned.1.call-start = ((), (), s32[]{:S(2)}) async-start(), calls=%async_computation.7 | async-start | bytes 2228224 | tf_op jit(solution)/shard_map/all_gather | solution.py:96
  22.5 5.1 copy-start.9
  37.7 217.8 %copy-start.6 = (s32[2,8,8]{2,1,0:T(8,128)S(1)}, s32[2,8,8]{2,1,0:T(8,128)}, u32[]{:S(2)}) copy-start(s32[2,8,8]{2,1,0:T(8,128)} %param.24) | copy-start | bytes 1540
  37.7 218.4 %copy-start.2 = (bf16[1,4096,192]{1,2,0:T(8,128)(2,1)S(1)}, bf16[1,4096,192]{1,2,0:T(8,128)(2,1)}, u32[]{:S(2)}) copy-start(bf16[1,4096,192]{1,2,0:T(8,128)(2,1)} %param.28) | copy-start | bytes 4718596
  257.1 29.0 %copy-start.3 = (bf16[2,8,4096]{2,1,0:T(8,128)(2,1)S(1)}, bf16[2,8,4096]{2,1,0:T(8,128)(2,1)}, u32[]{:S(2)}) copy-start(bf16[2,8,4096]{2,1,0:T(8,128)(2,1)} %param.20) | copy-start | bytes 393220
  257.1 29.2 %copy-start.4 = (f32[4096]{0:T(1024)S(1)}, f32[4096]{0:T(1024)}, u32[]{:S(2)}) copy-start(f32[4096]{0:T(1024)} %param.26) | copy-start | bytes 49156
  261.3 14.3 %all-to-all-start = ((bf16[16,8,256]{2,1,0:T(8,128)(2,1)}), bf16[16,8,256]{2,1,0:T(8,128)(2,1)S(1)}, u32[]{:S(2)}, u32[]{:S(2)}) async-start(bf16[16,8,256]{2,1,0:T(8,128)(2,1)} %fusion.84), calls=%async_computation | async-start | bytes 131072 | tf_op jit(solution)/shard_map/all_to_all | solution.py:100
  275.7 10.4 %all-to-all-start.3 = ((bf16[16,8,256]{2,1,0:T(8,128)(2,1)}), bf16[16,8,256]{2,1,0:T(8,128)(2,1)S(1)}, u32[]{:S(2)}, u32[]{:S(2)}) async-start(bf16[16,8,256]{2,1,0:T(8,128)(2,1)} %fusion.85), calls=%async_computation.3 | async-start | bytes 131072 | tf_op jit(solution)/shard_map/all_to_all | solution.py:100
  288.3 230.8 %all-to-all-start.1 = ((bf16[16,8,4096]{2,1,0:T(8,128)(2,1)}), bf16[16,8,4096]{2,1,0:T(8,128)(2,1)S(1)}, u32[]{:S(2)}, u32[]{:S(2)}) async-start(bf16[16,8,4096]{2,1,0:T(8,128)(2,1)} %copy.66), calls=%async_computation.1 | async-start | bytes 2097152 | tf_op jit(solution)/shard_map/all_to_all | solution.py:130
  297.4 218.2 %copy-start.5 = (f32[1,4096]{1,0:T(1,128)S(1)}, f32[1,4096]{1,0:T(1,128)}, u32[]{:S(2)}) copy-start(f32[1,4096]{1,0:T(1,128)} %param.33) | copy-start | bytes 49156
  519.2 267.9 %all-to-all-start.4 = ((bf16[16,8,4096]{2,1,0:T(8,128)(2,1)}), bf16[16,8,4096]{2,1,0:T(8,128)(2,1)S(1)}, u32[]{:S(2)}, u32[]{:S(2)}) async-start(bf16[16,8,4096]{2,1,0:T(8,128)(2,1)} %copy.80), calls=%async_computation.4 | async-start | bytes 2097152 | tf_op jit(solution)/shard_map/all_to_all | solution.py:130
  733.0 13.4 %slice-start = ((s8[6291456]{0:T(1024)(128)(4,1)}), s8[4194304]{0:T(1024)(128)(4,1)S(1)}, s32[]{:S(2)}) async-start(s8[6291456]{0:T(1024)(128)(4,1)} %bitcast.284), calls=%async_computation.8 | async-start | bytes 8388608
  739.5 6.9 slice-start.1
  763.1 11.8 %copy-start.1 = (bf16[96,8,16,256]{3,1,2,0:T(8,128)(2,1)}, bf16[96,8,16,256]{3,1,2,0:T(8,128)(2,1)S(1)}, u32[]{:S(2)}) copy-start(bf16[96,8,16,256]{3,1,2,0:T(8,128)(2,1)S(1)} %copy.98) | copy-start | bytes 18874372
  787.1 28.9 %all-to-all-start.2 = ((bf16[16,8,4096]{2,1,0:T(8,128)(2,1)}), bf16[16,8,4096]{2,1,0:T(8,128)(2,1)S(1)}, u32[]{:S(2)}, u32[]{:S(2)}) async-start(bf16[16,8,4096]{2,1,0:T(8,128)(2,1)} %fusion.70), calls=%async_computation.2 | async-start | bytes 2097152 | tf_op jit(solution)/shard_map/all_to_all | solution.py:134
  816.1 29.8 %all-to-all-start.5 = ((bf16[16,8,4096]{2,1,0:T(8,128)(2,1)}), bf16[16,8,4096]{2,1,0:T(8,128)(2,1)S(1)}, u32[]{:S(2)}, u32[]{:S(2)}) async-start(bf16[16,8,4096]{2,1,0:T(8,128)(2,1)} %fusion.71), calls=%async_computation.5 | async-start | bytes 2097152 | tf_op jit(solution)/shard_map/all_to_all | solution.py:134
Sparse Core Ops, SparseCore 0:
  22.5 44.2 all-gather.2
  69.0 40.4 all-gather.4
where the time goes:
time: 861 us; the launch traced here: 854 us
  matrix products  669 us (78%)
  local copies, waits for them, and re-layouts  94.4 us (11%)
  waiting for transfers between devices  37.5 us (4%)
  starting transfers between devices  33.9 us (4%)
  between operations  14.1 us (2%)
    dot_general x48, matrix products, one_block(): jnp.einsum('rjk,kc->rcj', one_hot, codebook, preferred_element_type=jnp.f...  628 us
    unnamed x41, local copies, waits for them, and re-layouts  48.2 us
    all_to_all x2, waiting for transfers between devices, body(): lax.all_to_all(results, 'expert', split_axis=0, concat_axis=0, tiled=True)  28.1 us
    dot_general x2, matrix products, experts_apply(): jnp.dot(inner, w_down, preferred_element_type=jnp.float32)  19.6 us
  transfers between devices with their start and end apart: 8, of which 4 were waited for; matrix products, arithmetic and copies ran while one was open for 88% of the time, Pallas kernels for 0%

commit v1 on v0

v1 whole, which is shorter than its diff:
```python
import functools

import jax
import jax.numpy as jnp
from jax import lax
from jax.experimental import pallas as pl
from jax.experimental.pallas import tpu as pltpu
from jax.sharding import PartitionSpec as P

LANES = 128
KV_HEADS = 4
HEAD_DIM = 128
VMEM = 60 << 20


def attend_kernel(micro, span, kv_heads, len_ref, q_ref, kv_ref, out_ref, q_scr, o_scr):
    step = pl.program_id(0)
    rows, width = q_ref.shape
    heads = width // HEAD_DIM
    per_group = heads // kv_heads
    positions = kv_ref.shape[1]

    @pl.when(step == 0)
    def _():
        for h in range(heads):
            q_scr[h] = q_ref[:, h * HEAD_DIM : (h + 1) * HEAD_DIM].astype(jnp.float32)

    column = lax.broadcasted_iota(jnp.int32, (heads, 2 * positions), 1)
    is_key = column % 2 == 0
    blocks, weights = [], []
    for i in range(span):
        row = step * span + i
        parts = [
            kv_ref[i, :, :, g * HEAD_DIM : (g + 1) * HEAD_DIM].reshape(2 * positions, HEAD_DIM)
            for g in range(kv_heads)
        ]
        blocks.append(parts)
        scores = jnp.concatenate(
            [
                lax.dot_general(
                    q_scr[g * per_group : (g + 1) * per_group, row, :].astype(jnp.bfloat16),
                    parts[g],
                    (((1,), (1,)), ((), ())),
                    preferred_element_type=jnp.float32,
                )
                for g in range(kv_heads)
            ],
            axis=0,
        ) * HEAD_DIM ** (-0.5)
        visible = is_key & (column < 2 * len_ref[micro, row])
        scores = jnp.where(visible, scores, -1e30)
        raised = jnp.exp(scores - jnp.max(scores, axis=-1, keepdims=True))
        raised = raised / jnp.sum(raised, axis=-1, keepdims=True)
        weights.append(pltpu.roll(raised, 1, 1).astype(jnp.bfloat16))
    for i in range(span):
        row = step * span + i
        for g in range(kv_heads):
            o_scr[g * per_group : (g + 1) * per_group, row, :] = jnp.dot(
                weights[i][g * per_group : (g + 1) * per_group],
                blocks[i][g],
                preferred_element_type=jnp.float32,
            )

    @pl.when(step == pl.num_programs(0) - 1)
    def _():
        for h in range(heads):
            out_ref[:, h * HEAD_DIM : (h + 1) * HEAD_DIM] = o_scr[h].astype(jnp.bfloat16)


def attend(queries, kv_cache, lengths, micro):
    _, rows, width = queries.shape
    heads = width // HEAD_DIM
    span = 4 if rows % 4 == 0 else 1
    kv_shape = kv_cache.shape[2:]
    return pl.pallas_call(
        functools.partial(attend_kernel, micro, span, KV_HEADS),
        grid_spec=pltpu.PrefetchScalarGridSpec(
            num_scalar_prefetch=1,
            grid=(rows // span,),
            in_specs=[
                pl.BlockSpec((None, rows, width), lambda r, n: (micro, 0, 0)),
                pl.BlockSpec((None, span) + kv_shape, lambda r, n: (micro, r, 0, 0, 0)),
            ],
            out_specs=pl.BlockSpec((rows, width), lambda r, n: (0, 0)),
            scratch_shapes=[pltpu.VMEM((heads, rows, HEAD_DIM), jnp.float32)] * 2,
        ),
        out_shape=jax.ShapeDtypeStruct((rows, width), jnp.bfloat16),
        name="attend",
        compiler_params=pltpu.CompilerParams(vmem_limit_bytes=VMEM),
        cost_estimate=pl.CostEstimate(
            flops=rows * width * 4 * 256, bytes_accessed=rows << 18, transcendentals=0
        ),
    )(lengths, queries, kv_cache)


def expand_kernel(stacked, table_ref, code_ref, out_ref):
    rows, columns = code_ref.shape
    tile = 16
    tables = [jnp.broadcast_to(table_ref[i : i + 1], (tile, LANES)) for i in range(8)]

    def one(i, lane):
        at = pl.ds(pl.multiple_of(i * tile, tile), tile)
        codes = code_ref[at, lane * LANES : (lane + 1) * LANES]
        codes = codes.astype(jnp.float32).astype(jnp.int32)
        upper = codes >= LANES
        low = jnp.bitwise_and(codes, LANES - 1)

        def take(table):
            return jnp.take_along_axis(table, low, axis=1, mode="promise_in_bounds")

        for q in range(4):
            value = jnp.where(upper, take(tables[2 * q + 1]), take(tables[2 * q]))
            value = value.astype(jnp.bfloat16)
            if stacked:
                out_ref[q, at, lane * LANES : (lane + 1) * LANES] = value
            else:
                first = q * columns + lane * LANES
                out_ref[at, first : first + LANES] = value

    for lane in range(columns // LANES):

        def body(i, _, lane=lane):
            one(i, lane)
            return 0

        lax.fori_loop(0, rows // tile, body, 0, unroll=rows // tile if rows // tile <= 12 else 8)


def expand(table, codes, stacked):
    rows, columns = codes.shape
    if stacked:
        block = 512
        grid = (columns // block,)
        code_spec = pl.BlockSpec((rows, block), lambda b: (0, b))
        out_spec = pl.BlockSpec((4, rows, block), lambda b: (0, 0, b))
        out_shape = (4, rows, columns)
    else:
        block = 128
        grid = (rows // block,)
        code_spec = pl.BlockSpec((block, columns), lambda b: (b, 0))
        out_spec = pl.BlockSpec((block, 4 * columns), lambda b: (b, 0))
        out_shape = (rows, 4 * columns)
    out = pl.pallas_call(
        functools.partial(expand_kernel, stacked),
        grid=grid,
        in_specs=[pl.BlockSpec((8, LANES), lambda b: (0, 0)), code_spec],
        out_specs=out_spec,
        out_shape=jax.ShapeDtypeStruct(out_shape, jnp.bfloat16),
        name="expand",
        compiler_params=pltpu.CompilerParams(vmem_limit_bytes=VMEM),
        cost_estimate=pl.CostEstimate(
            flops=rows * columns * 8000, bytes_accessed=10 * rows * columns, transcendentals=0
        ),
    )(table, codes)
    return out.reshape(4 * rows, columns) if stacked else out


def project_kernel(blocks, me_ref, att_ref, weight_ref, hidden_ref, out_ref, acc_ref):
    step = pl.program_id(0)
    shards, rows, depth = att_ref.shape

    @pl.when(step == 0)
    def _():
        acc_ref[...] = jnp.zeros_like(acc_ref)

    product = jnp.dot(
        att_ref[...].reshape(shards * rows, depth),
        weight_ref[...],
        preferred_element_type=jnp.float32,
    )
    acc_ref[...] += product.reshape(acc_ref.shape)

    @pl.when(step == pl.num_programs(0) - 1)
    def _():
        me = me_ref[0]
        for p in range(shards):
            source = me ^ blocks[p]
            projected = acc_ref[p].astype(jnp.bfloat16).astype(jnp.float32)
            out_ref[source] = (hidden_ref[source].astype(jnp.float32) + projected).astype(
                jnp.bfloat16
            )


def project(me, attended, out_weight, hidden_columns, blocks):
    shards, rows, depth = attended.shape
    columns = out_weight.shape[1]
    block = 2048
    return pl.pallas_call(
        functools.partial(project_kernel, blocks),
        grid_spec=pltpu.PrefetchScalarGridSpec(
            num_scalar_prefetch=1,
            grid=(depth // block,),
            in_specs=[
                pl.BlockSpec((shards, rows, block), lambda k, n: (0, 0, k)),
                pl.BlockSpec((block, columns), lambda k, n: (k, 0)),
                pl.BlockSpec((shards, rows, columns), lambda k, n: (0, 0, 0)),
            ],
            out_specs=pl.BlockSpec((shards, rows, columns), lambda k, n: (0, 0, 0)),
            scratch_shapes=[pltpu.VMEM((shards, rows, columns), jnp.float32)],
        ),
        out_shape=jax.ShapeDtypeStruct((shards, rows, columns), jnp.bfloat16),
        name="project",
        compiler_params=pltpu.CompilerParams(vmem_limit_bytes=VMEM),
        cost_estimate=pl.CostEstimate(
            flops=2 * shards * rows * depth * columns,
            bytes_accessed=2 * depth * columns,
            transcendentals=0,
        ),
    )(me, attended, out_weight, hidden_columns)


def experts_kernel(
    blocks,
    me_ref,
    stream_ref,
    gain_ref,
    router_ref,
    hot_ref,
    gate_ref,
    up_ref,
    down_ref,
    gu_scale_ref,
    down_scale_ref,
    out_ref,
    own_ref,
    token_scr,
    weight_scr,
    acc_ref,
):
    step = pl.program_id(0)
    pieces, shards, rows, columns = stream_ref.shape
    total, width = token_scr.shape
    me = me_ref[0]

    @pl.when(step == 0)
    def _():
        squares = jnp.zeros((total, columns), jnp.float32)
        for p in range(pieces):
            value = stream_ref[p].reshape(total, columns).astype(jnp.float32)
            squares += value * value
        mean = jnp.sum(squares, axis=-1, keepdims=True) / width
        inverse = lax.rsqrt(mean + 1e-06)
        for p in range(pieces):
            at = pl.ds(0, columns)
            if pieces > 1:
                at = pl.ds(pl.multiple_of((me ^ blocks[p]) * columns, columns), columns)
            value = stream_ref[p].reshape(total, columns)
            own_ref[:, at] = stream_ref[p, me]
            token_scr[:, at] = (value.astype(jnp.float32) * inverse * gain_ref[:, at]).astype(
                jnp.bfloat16
            )
        logits = lax.dot_general(
            token_scr[...],
            router_ref[...],
            (((1,), (1,)), ((), ())),
            preferred_element_type=jnp.float32,
        )
        hot = hot_ref[...].astype(jnp.float32) > 0.5
        logits = jnp.where(hot, logits, -1e30)
        raised = jnp.where(hot, jnp.exp(logits - jnp.max(logits, axis=-1, keepdims=True)), 0.0)
        raised = raised / jnp.sum(raised, axis=-1, keepdims=True)
        mine = lax.broadcasted_iota(jnp.int32, raised.shape, 1) == me
        weight = jnp.sum(jnp.where(mine, raised, 0.0), axis=-1, keepdims=True)
        weight = weight.astype(jnp.bfloat16).astype(jnp.float32)
        weight_scr[...] = jnp.broadcast_to(weight, (total, LANES)).reshape(weight_scr.shape)
        acc_ref[...] = jnp.zeros_like(acc_ref)

    nt = (((1,), (1,)), ((), ()))
    tokens = token_scr[...]
    gate = lax.dot_general(tokens, gate_ref[...], nt, preferred_element_type=jnp.float32)
    up = lax.dot_general(tokens, up_ref[...], nt, preferred_element_type=jnp.float32)
    gate = gate * gu_scale_ref[0:1, :]
    up = up * gu_scale_ref[1:2, :]
    inner = (gate / (1.0 + jnp.exp(-gate)) * up).astype(jnp.bfloat16)
    piece = 1024
    for c in range(width // piece):
        at = slice(c * piece, (c + 1) * piece)
        part = jnp.dot(inner, down_ref[:, at], preferred_element_type=jnp.float32)
        acc_ref[:, :, at] += part.reshape(shards, rows, piece)

    @pl.when(step == pl.num_programs(0) - 1)
    def _():
        for p in range(shards):
            source = me ^ blocks[p]
            value = (acc_ref[source] * down_scale_ref[...]).astype(jnp.bfloat16)
            value = value.astype(jnp.float32) * weight_scr[source][:, 0:1]
            out_ref[p] = value.astype(jnp.bfloat16)


def run_experts(me, streams, gain, router, hot, gate, up, down, gu_scale, down_scale, blocks):
    pieces, shards, rows, columns = streams.shape
    hidden_units, width = gate.shape
    total = shards * rows
    block = 256
    full = lambda f, n: (0, 0)
    return pl.pallas_call(
        functools.partial(experts_kernel, blocks),
        grid_spec=pltpu.PrefetchScalarGridSpec(
            num_scalar_prefetch=1,
            grid=(hidden_units // block,),
            in_specs=[
                pl.BlockSpec(streams.shape, lambda f, n: (0, 0, 0, 0)),
                pl.BlockSpec((1, width), full),
                pl.BlockSpec(router.shape, full),
                pl.BlockSpec(hot.shape, full),
                pl.BlockSpec((block, width), lambda f, n: (f, 0)),
                pl.BlockSpec((block, width), lambda f, n: (f, 0)),
                pl.BlockSpec((block, width), lambda f, n: (f, 0)),
                pl.BlockSpec((2, block), lambda f, n: (0, f)),
                pl.BlockSpec((1, width), full),
            ],
            out_specs=[
                pl.BlockSpec((shards, rows, width), lambda f, n: (0, 0, 0)),
                pl.BlockSpec((rows, width), full),
            ],
            scratch_shapes=[
                pltpu.VMEM((total, width), jnp.bfloat16),
                pltpu.VMEM((shards, rows, LANES), jnp.float32),
                pltpu.VMEM((shards, rows, width), jnp.float32),
            ],
        ),
        out_shape=[
            jax.ShapeDtypeStruct((shards, rows, width), jnp.bfloat16),
            jax.ShapeDtypeStruct((rows, width), jnp.bfloat16),
        ],
        name="experts",
        compiler_params=pltpu.CompilerParams(vmem_limit_bytes=VMEM),
        cost_estimate=pl.CostEstimate(
            flops=6 * total * width * hidden_units,
            bytes_accessed=6 * width * hidden_units,
            transcendentals=0,
        ),
    )(me, streams, gain, router, hot, gate, up, down, gu_scale, down_scale)


def swap(value, bit, count):
    return lax.ppermute(value, "expert", [(i, i ^ bit) for i in range(count)])


def gather_all(value, count):
    bits = [1 << b for b in reversed(range(count.bit_length() - 1))]
    if len(bits) >= 2:
        far = swap(value, bits[0], count)
        near = swap(value, bits[1], count)
        both = swap(far, bits[1], count)
        held, bits = jnp.stack([value, far, near, both]), bits[2:]
    else:
        held = value[None]
    for bit in bits:
        held = jnp.concatenate([held, swap(held, bit, count)])
    return held


def reduce_own(parts, count):
    for bit in [1 << b for b in range(count.bit_length() - 1)]:
        half = parts.shape[0] // 2
        other = swap(parts[half:], bit, count)
        total = parts[:half].astype(jnp.float32) + other.astype(jnp.float32)
        parts = total if half == 1 else total.astype(jnp.bfloat16)
    return parts[0]


def body(
    hidden,
    queries,
    kv_cache,
    lengths,
    routes,
    out_weight,
    norm_gain,
    router_weight,
    gate_codes,
    up_codes,
    down_codes,
    codebooks,
    gate_up_scale,
    down_scale,
):
    micro_count, rows, width = hidden.shape
    count = lax.axis_size("expert")
    me = lax.axis_index("expert").astype(jnp.int32)
    me_list = me.reshape(1)
    columns = out_weight.shape[1]
    width_bits = count.bit_length() - 1
    blocks = tuple(
        sum(((p >> b) & 1) << (width_bits - 1 - b) for b in range(width_bits)) for p in range(count)
    )

    hot = (routes[..., None] == jnp.arange(count, dtype=jnp.int32)).any(axis=2)
    lead = hidden.reshape(micro_count, rows, count, columns).transpose(2, 0, 1, 3)
    tail = jnp.broadcast_to(hot.astype(jnp.bfloat16)[None], (count,) + hot.shape)
    packed = lax.all_to_all(
        jnp.concatenate([lead, tail], axis=-1), "expert", split_axis=0, concat_axis=0, tiled=True
    )
    hidden_columns = packed[..., :columns]
    hot_all = packed[..., columns:]

    tables = codebooks[0].astype(jnp.float32).transpose(0, 2, 1).reshape(3, 8, LANES)
    gathered = [
        gather_all(attend(queries, kv_cache, lengths, m), count) for m in range(micro_count)
    ]
    gate = expand(tables[0], gate_codes[0].T, True)
    up = expand(tables[1], up_codes[0].T, True)
    down = expand(tables[2], down_codes[0], False)

    outputs = []
    for m in range(micro_count):
        stream = project(me_list, gathered[m], out_weight, hidden_columns[:, m], blocks)
        streams = gather_all(stream, count)
        if columns % LANES:
            order = jnp.arange(count, dtype=jnp.int32)
            place = jnp.asarray(blocks, jnp.int32)
            inverse = jnp.argsort(place)
            streams = streams[inverse[order ^ me]]
            streams = streams.transpose(1, 2, 0, 3).reshape(1, count, rows, width)
        parts, own = run_experts(
            me_list,
            streams,
            norm_gain.reshape(1, width),
            router_weight.T,
            hot_all[:, m].reshape(count * rows, count),
            gate,
            up,
            down,
            gate_up_scale[0],
            down_scale,
            blocks,
        )
        mixture = reduce_own(parts, count)
        outputs.append((own.astype(jnp.float32) + mixture).astype(jnp.bfloat16))
    return jnp.stack(outputs)


def solution(mesh):
    in_specs = (
        P(None, ("groups", "expert"), None),
        P(None, ("groups", "expert"), None),
        P(None, ("groups", "expert"), None, None, None),
        P(None, ("groups", "expert")),
        P(None, ("groups", "expert"), None),
        P(None, "expert"),
        P(),
        P(),
        P("expert", None, None),
        P("expert", None, None),
        P("expert", None, None),
        P("expert", None, None, None),
        P("expert", None, None),
        P("expert", None),
    )
    out_specs = P(None, ("groups", "expert"), None)
    return jax.shard_map(body, mesh=mesh, in_specs=in_specs, out_specs=out_specs, check_vma=False)
```

time: 861 us -> 190 us (0.22)
  matrix products: 669 us -> 0 us
  Pallas kernels: 0 us -> 75.2 us
  local copies, waits for them, and re-layouts: 94.4 us -> 28.4 us
  between operations: 14.1 us -> 0.28 us
  waiting for transfers between devices: 37.5 us -> 46.7 us
    dot_general x66 -> x0, matrix products: 669 us -> none  [the longest x48 628 us: one_block(): jnp.einsum('rjk,kc->rcj', one_hot, codebook, preferred_element_type=jnp.f...]
    pallas_call x0 -> x9, Pallas kernels: none -> 75.2 us  [the longest x3 29.8 us: expand(): pl.pallas_call(functools.partial(expand_kernel, stacked), grid=grid, in_s...]
    ppermute x0 -> x28, waiting for transfers between devices: none -> 46.7 us  [swap(): return lax.ppermute(value, 'expert', [(i, i ^ bit) for i in range(count)])]
    all_to_all x6 -> x1, waiting for transfers between devices: 37.5 us -> 0.01 us  [body(): lax.all_to_all(jnp.concatenate([lead, tail], axis=-1), 'expert', split_ax...]
    unnamed x41 -> x45, local copies, waits for them, and re-layouts: 48.2 us -> 16.6 us
    ppermute x0 -> x28, starting transfers between devices: none -> 29.3 us  [swap(): return lax.ppermute(value, 'expert', [(i, i ^ bit) for i in range(count)])]
    all_to_all x6 -> x1, starting transfers between devices: 33.8 us -> 6.28 us  [body(): lax.all_to_all(jnp.concatenate([lead, tail], axis=-1), 'expert', split_ax...]
    eq x54 -> x0, local copies, waits for them, and re-layouts: 15.1 us -> none  [the longest x48 14.6 us: one_block(): one_hot = (segment[:, :, None] == levels).astype(jnp.bfloat16)]
  transfers between devices with their start and end apart: 8 -> 29, of which waited for: 4 -> 12; matrix products, arithmetic and copies ran while one was open for 88% -> 14% of each run, Pallas kernels for 0% -> 37%
where the time goes in v1:
time: 190 us; the launch traced here: 188 us
  Pallas kernels  75.2 us (40%)
  waiting for transfers between devices  46.7 us (25%)
  starting transfers between devices  35.6 us (19%)
  local copies, waits for them, and re-layouts  28.4 us (15%)
  other arithmetic  2.34 us (1%)
    ppermute x28, waiting for transfers between devices, swap(): return lax.ppermute(value, 'expert', [(i, i ^ bit) for i in range(count)])  46.7 us
    pallas_call x3, Pallas kernels, expand(): pl.pallas_call(functools.partial(expand_kernel, stacked), grid=grid, in_s...  29.8 us
    ppermute x28, starting transfers between devices, swap(): return lax.ppermute(value, 'expert', [(i, i ^ bit) for i in range(count)])  29.3 us
    pallas_call x2, Pallas kernels, run_experts(): pl.pallas_call(functools.partial(experts_kernel, blocks), grid_spec=pltpu...  26.2 us
    unnamed x45, local copies, waits for them, and re-layouts  16.6 us
    pallas_call x2, Pallas kernels, attend(): pl.pallas_call(functools.partial(attend_kernel, micro, span, KV_HEADS), g...  9.74 us
    pallas_call x2, Pallas kernels, project(): pl.pallas_call(functools.partial(project_kernel, blocks), grid_spec=pltpu...  9.49 us
    all_to_all x1, starting transfers between devices, body(): lax.all_to_all(jnp.concatenate([lead, tail], axis=-1), 'expert', split_ax...  6.28 us
  transfers between devices with their start and end apart: 29, of which 12 were waited for; matrix products, arithmetic and copies ran while one was open for 14% of the time, Pallas kernels for 37%

profile of v1, /device:TPU:0, one launch (start us, length us, event | category | flops | bytes accessed | tf_op | source)
XLA Modules:
  0.0 188.5 jit_solution(12317178399578093403)
XLA Ops:
  0.0 4.9 %attend.2 = bf16[8,8192]{1,0:T(8,128)(2,1)} custom-call(s32[2,8]{1,0:T(2,128)} %len_ref.3, bf16[2,8,8192]{2,1,0:T(8,128)(2,1)} %q_ref.3, bf16[2,8,128,2,512]{4,3,2,1,0:T(2,128)(2,1)} %kv_ref.3), custom_call_target="tpu_custom_call" | custom-call | flops 67108864 | bytes 2097152 | tf_op jit(solution)/shard_map/attend/pallas_call | solution.py:75
  4.9 3.1 %collective-permute-start.1 = (bf16[8,8192]{1,0:T(8,128)(2,1)}, bf16[8,8192]{1,0:T(8,128)(2,1)S(1)}, u32[]{:S(2)}, u32[]{:S(2)}) collective-permute-start(bf16[8,8192]{1,0:T(8,128)(2,1)} %attend.2), channel_id=1, source_target_pairs={{0,4},{1,5},{2,6},{3,7},{4,0},{5,1},{6,2},{7,3},{8,12},{9,13},{10,... | collective-permute-start | bytes 393224 | tf_op jit(solution)/shard_map/ppermute | solution.py:337
  8.0 2.6 %collective-permute-start = (bf16[8,8192]{1,0:T(8,128)(2,1)}, bf16[8,8192]{1,0:T(8,128)(2,1)S(1)}, u32[]{:S(2)}, u32[]{:S(2)}) collective-permute-start(bf16[8,8192]{1,0:T(8,128)(2,1)} %attend.2), channel_id=1, source_target_pairs={{0,8},{1,9},{2,10},{3,11},{4,12},{5,13},{6,14},{7,15},{8,0},{9,1},... | collective-permute-start | bytes 393224 | tf_op jit(solution)/shard_map/ppermute | solution.py:337
  10.6 4.9 %attend.3 = bf16[8,8192]{1,0:T(8,128)(2,1)} custom-call(s32[2,8]{1,0:T(2,128)} %len_ref.3, bf16[2,8,8192]{2,1,0:T(8,128)(2,1)} %q_ref.3, bf16[2,8,128,2,512]{4,3,2,1,0:T(2,128)(2,1)} %kv_ref.3), custom_call_target="tpu_custom_call" | custom-call | flops 67108864 | bytes 2097152 | tf_op jit(solution)/shard_map/attend/pallas_call | solution.py:75
  16.1 0.7 copy.20
  16.8 6.3 %all-to-all-start = ((bf16[16,2,8,272]{3,2,1,0:T(8,128)(2,1)}), bf16[16,2,8,272]{3,2,1,0:T(8,128)(2,1)S(1)}, u32[]{:S(2)}, u32[]{:S(2)}) async-start(bf16[16,2,8,272]{3,2,1,0:T(8,128)(2,1)} %copy.20), calls=%async_computation | async-start | bytes 393216 | tf_op jit(solution)/shard_map/all_to_all | solution.py:392
  23.1 0.7 constant_dynamic-update-slice_fusion.4
  23.8 1.6 constant_dynamic-update-slice_fusion.26
  27.2 9.5 %expand.5.down_ref = bf16[768,4096]{1,0:T(8,128)(2,1)} custom-call(f32[8,128]{1,0:T(8,128)} %squeeze.40.table_ref, bf16[768,1024]{1,0:T(8,128)(2,1)} %bitcast.131), custom_call_target="tpu_custom_call" | custom-call | flops 6291456000 | bytes 7864320 | tf_op jit(solution)/shard_map/expand/pallas_call | solution.py:143
  36.7 10.1 %expand.3 = bf16[4,192,4096]{2,1,0:T(8,128)(2,1)} custom-call(f32[8,128]{1,0:T(8,128)} %squeeze.36.table_ref, bf16[192,4096]{1,0:T(8,128)(2,1)} %bitcast.132), custom_call_target="tpu_custom_call" | custom-call | flops 6291456000 | bytes 7864320 | tf_op jit(solution)/shard_map/expand/pallas_call | solution.py:143
  46.8 10.2 %expand.4 = bf16[4,192,4096]{2,1,0:T(8,128)(2,1)} custom-call(f32[8,128]{1,0:T(8,128)} %squeeze.38.table_ref, bf16[192,4096]{1,0:T(8,128)(2,1)} %bitcast.133), custom_call_target="tpu_custom_call" | custom-call | flops 6291456000 | bytes 7864320 | tf_op jit(solution)/shard_map/expand/pallas_call | solution.py:143
  57.0 1.9 %collective-permute-start.2 = (bf16[8,8192]{1,0:T(8,128)(2,1)S(1)}, bf16[8,8192]{1,0:T(8,128)(2,1)S(1)}, u32[]{:S(2)}, u32[]{:S(2)}) collective-permute-start(bf16[8,8192]{1,0:T(8,128)(2,1)S(1)} %collective-permute-done), channel_id=1, source_target_pairs={{0,4},{1,5},{2,6},{3,7},{4,0},{5,1},{6,2},{7,3},{8,12},{9,13},{10,... | collective-permute-start | bytes 393224 | tf_op jit(solution)/shard_map/ppermute | solution.py:337
  59.0 0.7 constant_dynamic-update-slice_fusion.3
  59.7 0.7 constant_dynamic-update-slice_fusion.25
  60.4 0.7 constant_dynamic-update-slice_fusion.2
  61.1 0.7 constant_dynamic-update-slice_fusion.24
  61.8 0.7 slice_bitcast_fusion.1
  63.4 2.0 %collective-permute-start.3 = (bf16[4,8,8192]{2,1,0:T(8,128)(2,1)S(1)}, bf16[4,8,8192]{2,1,0:T(8,128)(2,1)S(1)}, u32[]{:S(2)}, u32[]{:S(2)}) collective-permute-start(bf16[4,8,8192]{2,1,0:T(8,128)(2,1)S(1)} %pad_maximum_fusion), channel_id=1, source_target_pairs={{0,2},{1,3},{2,0},{3,1},{4,6},{5,7},{6,4},{7,5},{8,10},{9,11},{10,... | collective-permute-start | bytes 1572872 | tf_op jit(solution)/shard_map/ppermute | solution.py:337
  65.7 1.7 collective-permute-start.17
  67.4 0.7 constant_dynamic-update-slice_fusion.1
  68.1 10.2 %collective-permute-done.3 = bf16[4,8,8192]{2,1,0:T(8,128)(2,1)S(1)} collective-permute-done((bf16[4,8,8192]{2,1,0:T(8,128)(2,1)S(1)}, bf16[4,8,8192]{2,1,0:T(8,128)(2,1)S(1)}, u32[]{:S(2)}, u32[]{:S(2)}) %collective-permute-start.3) | collective-permute-done | bytes 524320 | tf_op jit(solution)/shard_map/ppermute | solution.py:337
  78.3 0.9 constant_dynamic-update-slice_fusion
  79.1 0.7 constant_dynamic-update-slice_fusion.23
  79.8 8.4 %collective-permute-done.17 = bf16[4,8,8192]{2,1,0:T(8,128)(2,1)S(1)} collective-permute-done((bf16[4,8,8192]{2,1,0:T(8,128)(2,1)S(1)}, bf16[4,8,8192]{2,1,0:T(8,128)(2,1)S(1)}, u32[]{:S(2)}, u32[]{:S(2)}) %collective-permute-start.17) | collective-permute-done | bytes 524320 | tf_op jit(solution)/shard_map/ppermute | solution.py:337
  88.2 0.9 constant_dynamic-update-slice_fusion.22
  89.1 1.1 constant_dynamic-update-slice_fusion.5.att_ref
  90.1 4.7 %project.2 = bf16[16,8,256]{2,1,0:T(8,128)(2,1)} custom-call(s32[1]{0:T(128)} %bitcast.me_ref, bf16[16,8,8192]{2,1,0:T(8,128)(2,1)} %constant_dynamic-update-slice_fusion.5.att_ref, bf16[8192,256]{1,0:T(8,128)(2,1)} %weight_ref.3, bf16[16,8,256]{2,1,0:T(8,128)(2,1)} %get-tuple-element.23.hidden_ref), custom_call_target="tpu_custom_call" | custom-call | flops 536870912 | bytes 4194304 | tf_op jit(solution)/shard_map/project/pallas_call | solution.py:188
  94.9 1.6 collective-permute-start.6
  96.5 2.4 %collective-permute-start.5 = (bf16[16,8,256]{2,1,0:T(8,128)(2,1)}, bf16[16,8,256]{2,1,0:T(8,128)(2,1)S(1)}, u32[]{:S(2)}, u32[]{:S(2)}) collective-permute-start(bf16[16,8,256]{2,1,0:T(8,128)(2,1)} %project.2), channel_id=1, source_target_pairs={{0,8},{1,9},{2,10},{3,11},{4,12},{5,13},{6,14},{7,15},{8,0},{9,1},... | collective-permute-start | bytes 196616 | tf_op jit(solution)/shard_map/ppermute | solution.py:337
  98.9 1.5 constant_dynamic-update-slice_fusion.15
  100.4 1.3 constant_dynamic-update-slice_fusion.27.att_ref
  101.7 1.3 copy-done
  103.0 4.8 %project.3 = bf16[16,8,256]{2,1,0:T(8,128)(2,1)} custom-call(s32[1]{0:T(128)} %bitcast.me_ref, bf16[16,8,8192]{2,1,0:T(8,128)(2,1)} %copy-done, bf16[8192,256]{1,0:T(8,128)(2,1)} %weight_ref.3, bf16[16,8,256]{2,1,0:T(8,128)(2,1)} %get-tuple-element.24.hidden_ref), custom_call_target="tpu_custom_call" | custom-call | flops 536870912 | bytes 4194304 | tf_op jit(solution)/shard_map/project/pallas_call | solution.py:188
  108.7 1.5 constant_dynamic-update-slice_fusion.37
  110.2 1.6 collective-permute-start.7
  111.9 2.3 %collective-permute-done.19 = bf16[16,8,256]{2,1,0:T(8,128)(2,1)S(1)} collective-permute-done((bf16[16,8,256]{2,1,0:T(8,128)(2,1)}, bf16[16,8,256]{2,1,0:T(8,128)(2,1)S(1)}, u32[]{:S(2)}, u32[]{:S(2)}) %collective-permute-start.19) | collective-permute-done | bytes 65568 | tf_op jit(solution)/shard_map/ppermute | solution.py:337
  114.1 1.5 collective-permute-start.21
  115.6 0.6 constant_dynamic-update-slice_fusion.14
  116.2 0.6 constant_dynamic-update-slice_fusion.36
  117.5 1.5 collective-permute-start.8
  119.1 0.9 pad_maximum_fusion.3
  120.0 0.8 collective-permute-start.22
  120.8 0.6 constant_dynamic-update-slice_fusion.12
  121.4 5.0 %collective-permute-done.8 = bf16[4,16,8,256]{3,2,1,0:T(8,128)(2,1)S(1)} collective-permute-done((bf16[4,16,8,256]{3,2,1,0:T(8,128)(2,1)S(1)}, bf16[4,16,8,256]{3,2,1,0:T(8,128)(2,1)S(1)}, u32[]{:S(2)}, u32[]{:S(2)}) %collective-permute-start.8) | collective-permute-done | bytes 262176 | tf_op jit(solution)/shard_map/ppermute | solution.py:337
  126.5 0.7 constant_dynamic-update-slice_fusion.11
  127.2 0.6 constant_dynamic-update-slice_fusion.35
  128.5 0.8 collective-permute-done.22
  129.3 0.8 constant_dynamic-update-slice_fusion.33
  130.1 1.0 copy-done.1
  131.1 13.0 %experts.2 = (bf16[16,8,4096]{2,1,0:T(8,128)(2,1)}, bf16[8,4096]{1,0:T(8,128)(2,1)}) custom-call(s32[1]{0:T(128)} %bitcast.me_ref, bf16[16,16,8,256]{3,2,1,0:T(8,128)(2,1)} %copy-done.1, f32[1,4096]{1,0:T(1,128)} %bitcast.127, bf16[16,4096]{1,0:T(8,128)(2,1)} %bitcast.111, bf16[128,16]{1,0:T(8,128)(2,1)} %get-tuple-element.21.hot_ref, ...), custom_call_target="tpu_custom_call" | custom-call | flops 2415919104 | bytes 18874368 | tf_op jit(solution)/shard_map/experts/pallas_call | solution.py:296
  144.1 1.1 slice.84
  145.8 1.0 copy-done.2
  146.8 13.1 %experts.3 = (bf16[16,8,4096]{2,1,0:T(8,128)(2,1)}, bf16[8,4096]{1,0:T(8,128)(2,1)}) custom-call(s32[1]{0:T(128)} %bitcast.me_ref, bf16[16,16,8,256]{3,2,1,0:T(8,128)(2,1)} %copy-done.2, f32[1,4096]{1,0:T(1,128)} %bitcast.128, bf16[16,4096]{1,0:T(8,128)(2,1)} %bitcast.112, bf16[128,16]{1,0:T(8,128)(2,1)} %get-tuple-element.22.hot_ref, ...), custom_call_target="tpu_custom_call" | custom-call | flops 2415919104 | bytes 18874368 | tf_op jit(solution)/shard_map/experts/pallas_call | solution.py:296
  160.0 1.2 slice.94
  161.4 1.5 collective-permute-start.11
  163.3 1.5 collective-permute-start.25
  164.8 5.7 %collective-permute-done.11 = bf16[4,8,4096]{2,1,0:T(8,128)(2,1)S(1)} collective-permute-done((bf16[4,8,4096]{2,1,0:T(8,128)(2,1)S(1)}, bf16[4,8,4096]{2,1,0:T(8,128)(2,1)S(1)}, u32[]{:S(2)}, u32[]{:S(2)}) %collective-permute-start.11) | collective-permute-done | bytes 262176 | tf_op jit(solution)/shard_map/ppermute | solution.py:337
  170.6 0.7 collective-permute-start.12
  171.4 4.4 %collective-permute-done.25 = bf16[4,8,4096]{2,1,0:T(8,128)(2,1)S(1)} collective-permute-done((bf16[4,8,4096]{2,1,0:T(8,128)(2,1)S(1)}, bf16[4,8,4096]{2,1,0:T(8,128)(2,1)S(1)}, u32[]{:S(2)}, u32[]{:S(2)}) %collective-permute-start.25) | collective-permute-done | bytes 262176 | tf_op jit(solution)/shard_map/ppermute | solution.py:337
  175.8 0.7 collective-permute-start.26
  176.6 1.3 collective-permute-start.13
  177.9 4.5 %collective-permute-done.26 = bf16[2,8,4096]{2,1,0:T(8,128)(2,1)S(1)} collective-permute-done((bf16[2,8,4096]{2,1,0:T(8,128)(2,1)S(1)}, bf16[2,8,4096]{2,1,0:T(8,128)(2,1)S(1)}, u32[]{:S(2)}, u32[]{:S(2)}) %collective-permute-start.26) | collective-permute-done | bytes 131104 | tf_op jit(solution)/shard_map/ppermute | solution.py:337
  183.0 4.8 %collective-permute-done.27 = bf16[1,8,4096]{2,1,0:T(8,128)(2,1)S(1)} collective-permute-done((bf16[1,8,4096]{2,1,0:T(8,128)(2,1)S(1)}, bf16[1,8,4096]{2,1,0:T(8,128)(2,1)S(1)}, u32[]{:S(2)}, u32[]{:S(2)}) %collective-permute-start.27) | collective-permute-done | bytes 65568 | tf_op jit(solution)/shard_map/ppermute | solution.py:337
  187.8 0.7 pad_maximum_fusion.5
  (89 shorter events, 8.0 us)
Async XLA Ops:
  4.9 11.0 %copy-start.12 = (s32[2,8,8]{2,1,0:T(8,128)S(1)}, s32[2,8,8]{2,1,0:T(8,128)}, u32[]{:S(2)}) copy-start(s32[2,8,8]{2,1,0:T(8,128)} %param.18) | copy-start | bytes 1540
  4.9 11.1 %copy-start.8 = (bf16[2,8,4096]{2,1,0:T(8,128)(2,1)S(1)}, bf16[2,8,4096]{2,1,0:T(8,128)(2,1)}, u32[]{:S(2)}) copy-start(bf16[2,8,4096]{2,1,0:T(8,128)(2,1)} %param.14) | copy-start | bytes 393220
  4.9 18.2 %copy-start.4 = (bf16[8,8192]{1,0:T(8,128)(2,1)S(1)}, bf16[8,8192]{1,0:T(8,128)(2,1)}, u32[]{:S(2)}) copy-start(bf16[8,8192]{1,0:T(8,128)(2,1)} %attend.2) | copy-start | bytes 393220
  4.9 55.5 %collective-permute-start.1 = (bf16[8,8192]{1,0:T(8,128)(2,1)}, bf16[8,8192]{1,0:T(8,128)(2,1)S(1)}, u32[]{:S(2)}, u32[]{:S(2)}) collective-permute-start(bf16[8,8192]{1,0:T(8,128)(2,1)} %attend.2), channel_id=1, source_target_pairs={{0,4},{1,5},{2,6},{3,7},{4,0},{5,1},{6,2},{7,3},{8,12},{9,13},{10,... | collective-permute-start | bytes 393224 | tf_op jit(solution)/shard_map/ppermute | solution.py:337
  8.0 49.0 %collective-permute-start = (bf16[8,8192]{1,0:T(8,128)(2,1)}, bf16[8,8192]{1,0:T(8,128)(2,1)S(1)}, u32[]{:S(2)}, u32[]{:S(2)}) collective-permute-start(bf16[8,8192]{1,0:T(8,128)(2,1)} %attend.2), channel_id=1, source_target_pairs={{0,8},{1,9},{2,10},{3,11},{4,12},{5,13},{6,14},{7,15},{8,0},{9,1},... | collective-permute-start | bytes 393224 | tf_op jit(solution)/shard_map/ppermute | solution.py:337
  15.4 10.0 %copy-start.13 = (bf16[1,3,256,4]{2,3,1,0:T(4,128)(2,1)S(1)}, bf16[1,3,256,4]{2,3,1,0:T(4,128)(2,1)}, u32[]{:S(2)}) copy-start(bf16[1,3,256,4]{2,3,1,0:T(4,128)(2,1)} %param.25) | copy-start | bytes 18436
  15.4 45.7 %collective-permute-start.15 = (bf16[8,8192]{1,0:T(8,128)(2,1)}, bf16[8,8192]{1,0:T(8,128)(2,1)S(1)}, u32[]{:S(2)}, u32[]{:S(2)}) collective-permute-start(bf16[8,8192]{1,0:T(8,128)(2,1)} %attend.3), channel_id=1, source_target_pairs={{0,4},{1,5},{2,6},{3,7},{4,0},{5,1},{6,2},{7,3},{8,12},{9,13},{10,... | collective-permute-start | bytes 393224 | tf_op jit(solution)/shard_map/ppermute | solution.py:337
  15.9 43.0 %collective-permute-start.14 = (bf16[8,8192]{1,0:T(8,128)(2,1)}, bf16[8,8192]{1,0:T(8,128)(2,1)S(1)}, u32[]{:S(2)}, u32[]{:S(2)}) collective-permute-start(bf16[8,8192]{1,0:T(8,128)(2,1)} %attend.3), channel_id=1, source_target_pairs={{0,8},{1,9},{2,10},{3,11},{4,12},{5,13},{6,14},{7,15},{8,0},{9,1},... | collective-permute-start | bytes 393224 | tf_op jit(solution)/shard_map/ppermute | solution.py:337
  16.8 45.0 %all-to-all-start = ((bf16[16,2,8,272]{3,2,1,0:T(8,128)(2,1)}), bf16[16,2,8,272]{3,2,1,0:T(8,128)(2,1)S(1)}, u32[]{:S(2)}, u32[]{:S(2)}) async-start(bf16[16,2,8,272]{3,2,1,0:T(8,128)(2,1)} %copy.20), calls=%async_computation | async-start | bytes 393216 | tf_op jit(solution)/shard_map/all_to_all | solution.py:392
  57.0 8.6 %copy-start.3 = (bf16[8,8192]{1,0:T(8,128)(2,1)S(1)}, bf16[8,8192]{1,0:T(8,128)(2,1)}, u32[]{:S(2)}) copy-start(bf16[8,8192]{1,0:T(8,128)(2,1)} %attend.3) | copy-start | bytes 393220
  57.0 6.3 %collective-permute-start.2 = (bf16[8,8192]{1,0:T(8,128)(2,1)S(1)}, bf16[8,8192]{1,0:T(8,128)(2,1)S(1)}, u32[]{:S(2)}, u32[]{:S(2)}) collective-permute-start(bf16[8,8192]{1,0:T(8,128)(2,1)S(1)} %collective-permute-done), channel_id=1, source_target_pairs={{0,4},{1,5},{2,6},{3,7},{4,0},{5,1},{6,2},{7,3},{8,12},{9,13},{10,... | collective-permute-start | bytes 393224 | tf_op jit(solution)/shard_map/ppermute | solution.py:337
  58.9 6.7 %collective-permute-start.16 = (bf16[8,8192]{1,0:T(8,128)(2,1)S(1)}, bf16[8,8192]{1,0:T(8,128)(2,1)S(1)}, u32[]{:S(2)}, u32[]{:S(2)}) collective-permute-start(bf16[8,8192]{1,0:T(8,128)(2,1)S(1)} %collective-permute-done.14), channel_id=1, source_target_pairs={{0,4},{1,5},{2,6},{3,7},{4,0},{5,1},{6,2},{7,3},{8,12},{9,13},{10,... | collective-permute-start | bytes 393224 | tf_op jit(solution)/shard_map/ppermute | solution.py:337
  61.8 5.6 %copy-start.11 = (bf16[8,8,8192]{2,1,0:T(8,128)(2,1)S(1)}, bf16[8,8,8192]{2,1,0:T(8,128)(2,1)}, u32[]{:S(2)}) copy-start(bf16[8,8,8192]{2,1,0:T(8,128)(2,1)} %get-tuple-element.27) | copy-start | bytes 3145732
  63.4 14.9 %collective-permute-start.3 = (bf16[4,8,8192]{2,1,0:T(8,128)(2,1)S(1)}, bf16[4,8,8192]{2,1,0:T(8,128)(2,1)S(1)}, u32[]{:S(2)}, u32[]{:S(2)}) collective-permute-start(bf16[4,8,8192]{2,1,0:T(8,128)(2,1)S(1)} %pad_maximum_fusion), channel_id=1, source_target_pairs={{0,2},{1,3},{2,0},{3,1},{4,6},{5,7},{6,4},{7,5},{8,10},{9,11},{10,... | collective-permute-start | bytes 1572872 | tf_op jit(solution)/shard_map/ppermute | solution.py:337
  65.7 22.5 %collective-permute-start.17 = (bf16[4,8,8192]{2,1,0:T(8,128)(2,1)S(1)}, bf16[4,8,8192]{2,1,0:T(8,128)(2,1)S(1)}, u32[]{:S(2)}, u32[]{:S(2)}) collective-permute-start(bf16[4,8,8192]{2,1,0:T(8,128)(2,1)S(1)} %pad_maximum_fusion.1), channel_id=1, source_target_pairs={{0,2},{1,3},{2,0},{3,1},{4,6},{5,7},{6,4},{7,5},{8,10},{9,11},{10,... | collective-permute-start | bytes 1572872 | tf_op jit(solution)/shard_map/ppermute | solution.py:337
  79.1 9.9 %collective-permute-start.4 = (bf16[8,8,8192]{2,1,0:T(8,128)(2,1)S(1)}, bf16[8,8,8192]{2,1,0:T(8,128)(2,1)S(1)}, u32[]{:S(2)}, u32[]{:S(2)}) collective-permute-start(bf16[8,8,8192]{2,1,0:T(8,128)(2,1)S(1)} %get-tuple-element.13), channel_id=1, source_target_pairs={{0,1},{1,0},{2,3},{3,2},{4,5},{5,4},{6,7},{7,6},{8,9},{9,8},{10,11... | collective-permute-start | bytes 3145736 | tf_op jit(solution)/shard_map/ppermute | solution.py:337
  89.1 11.3 %collective-permute-start.18 = (bf16[8,8,8192]{2,1,0:T(8,128)(2,1)}, bf16[8,8,8192]{2,1,0:T(8,128)(2,1)}, u32[]{:S(2)}, u32[]{:S(2)}) collective-permute-start(bf16[8,8,8192]{2,1,0:T(8,128)(2,1)} %get-tuple-element.15), channel_id=1, source_target_pairs={{0,1},{1,0},{2,3},{3,2},{4,5},{5,4},{6,7},{7,6},{8,9},{9,8},{10,11... | collective-permute-start | bytes 3145736 | tf_op jit(solution)/shard_map/ppermute | solution.py:337
  94.9 22.0 %collective-permute-start.6 = (bf16[16,8,256]{2,1,0:T(8,128)(2,1)}, bf16[16,8,256]{2,1,0:T(8,128)(2,1)S(1)}, u32[]{:S(2)}, u32[]{:S(2)}) collective-permute-start(bf16[16,8,256]{2,1,0:T(8,128)(2,1)} %project.2), channel_id=1, source_target_pairs={{0,4},{1,5},{2,6},{3,7},{4,0},{5,1},{6,2},{7,3},{8,12},{9,13},{10,... | collective-permute-start | bytes 196616 | tf_op jit(solution)/shard_map/ppermute | solution.py:337
  96.5 13.7 %collective-permute-start.5 = (bf16[16,8,256]{2,1,0:T(8,128)(2,1)}, bf16[16,8,256]{2,1,0:T(8,128)(2,1)S(1)}, u32[]{:S(2)}, u32[]{:S(2)}) collective-permute-start(bf16[16,8,256]{2,1,0:T(8,128)(2,1)} %project.2), channel_id=1, source_target_pairs={{0,8},{1,9},{2,10},{3,11},{4,12},{5,13},{6,14},{7,15},{8,0},{9,1},... | collective-permute-start | bytes 196616 | tf_op jit(solution)/shard_map/ppermute | solution.py:337
  101.7 1.4 copy-start
  103.0 14.5 %copy-start.7 = (bf16[16,8,256]{2,1,0:T(8,128)(2,1)S(1)}, bf16[16,8,256]{2,1,0:T(8,128)(2,1)}, u32[]{:S(2)}) copy-start(bf16[16,8,256]{2,1,0:T(8,128)(2,1)} %project.2) | copy-start | bytes 196612
  107.8 11.3 %collective-permute-start.20 = (bf16[16,8,256]{2,1,0:T(8,128)(2,1)}, bf16[16,8,256]{2,1,0:T(8,128)(2,1)S(1)}, u32[]{:S(2)}, u32[]{:S(2)}) collective-permute-start(bf16[16,8,256]{2,1,0:T(8,128)(2,1)} %project.3), channel_id=1, source_target_pairs={{0,4},{1,5},{2,6},{3,7},{4,0},{5,1},{6,2},{7,3},{8,12},{9,13},{10,... | collective-permute-start | bytes 196616 | tf_op jit(solution)/shard_map/ppermute | solution.py:337
  108.4 5.8 %collective-permute-start.19 = (bf16[16,8,256]{2,1,0:T(8,128)(2,1)}, bf16[16,8,256]{2,1,0:T(8,128)(2,1)S(1)}, u32[]{:S(2)}, u32[]{:S(2)}) collective-permute-start(bf16[16,8,256]{2,1,0:T(8,128)(2,1)} %project.3), channel_id=1, source_target_pairs={{0,8},{1,9},{2,10},{3,11},{4,12},{5,13},{6,14},{7,15},{8,0},{9,1},... | collective-permute-start | bytes 196616 | tf_op jit(solution)/shard_map/ppermute | solution.py:337
  110.2 7.3 %collective-permute-start.7 = (bf16[16,8,256]{2,1,0:T(8,128)(2,1)S(1)}, bf16[16,8,256]{2,1,0:T(8,128)(2,1)S(1)}, u32[]{:S(2)}, u32[]{:S(2)}) collective-permute-start(bf16[16,8,256]{2,1,0:T(8,128)(2,1)S(1)} %collective-permute-done.5), channel_id=1, source_target_pairs={{0,4},{1,5},{2,6},{3,7},{4,0},{5,1},{6,2},{7,3},{8,12},{9,13},{10,... | collective-permute-start | bytes 196616 | tf_op jit(solution)/shard_map/ppermute | solution.py:337
  114.1 5.0 %collective-permute-start.21 = (bf16[16,8,256]{2,1,0:T(8,128)(2,1)S(1)}, bf16[16,8,256]{2,1,0:T(8,128)(2,1)S(1)}, u32[]{:S(2)}, u32[]{:S(2)}) collective-permute-start(bf16[16,8,256]{2,1,0:T(8,128)(2,1)S(1)} %collective-permute-done.19), channel_id=1, source_target_pairs={{0,4},{1,5},{2,6},{3,7},{4,0},{5,1},{6,2},{7,3},{8,12},{9,13},{10,... | collective-permute-start | bytes 196616 | tf_op jit(solution)/shard_map/ppermute | solution.py:337
  117.5 8.9 %collective-permute-start.8 = (bf16[4,16,8,256]{3,2,1,0:T(8,128)(2,1)S(1)}, bf16[4,16,8,256]{3,2,1,0:T(8,128)(2,1)S(1)}, u32[]{:S(2)}, u32[]{:S(2)}) collective-permute-start(bf16[4,16,8,256]{3,2,1,0:T(8,128)(2,1)S(1)} %pad_maximum_fusion.2), channel_id=1, source_target_pairs={{0,2},{1,3},{2,0},{3,1},{4,6},{5,7},{6,4},{7,5},{8,10},{9,11},{10,... | collective-permute-start | bytes 786440 | tf_op jit(solution)/shard_map/ppermute | solution.py:337
  120.0 9.3 %collective-permute-start.22 = (bf16[4,16,8,256]{3,2,1,0:T(8,128)(2,1)S(1)}, bf16[4,16,8,256]{3,2,1,0:T(8,128)(2,1)S(1)}, u32[]{:S(2)}, u32[]{:S(2)}) collective-permute-start(bf16[4,16,8,256]{3,2,1,0:T(8,128)(2,1)S(1)} %pad_maximum_fusion.3), channel_id=1, source_target_pairs={{0,2},{1,3},{2,0},{3,1},{4,6},{5,7},{6,4},{7,5},{8,10},{9,11},{10,... | collective-permute-start | bytes 786440 | tf_op jit(solution)/shard_map/ppermute | solution.py:337
  127.2 2.9 %collective-permute-start.9 = (bf16[8,16,8,256]{3,2,1,0:T(8,128)(2,1)}, bf16[8,16,8,256]{3,2,1,0:T(8,128)(2,1)S(1)}, u32[]{:S(2)}, u32[]{:S(2)}) collective-permute-start(bf16[8,16,8,256]{3,2,1,0:T(8,128)(2,1)} %get-tuple-element.17), channel_id=1, source_target_pairs={{0,1},{1,0},{2,3},{3,2},{4,5},{5,4},{6,7},{7,6},{8,9},{9,8},{10,11... | collective-permute-start | bytes 1572872 | tf_op jit(solution)/shard_map/ppermute | solution.py:337
  130.1 15.7 %collective-permute-start.23 = (bf16[8,16,8,256]{3,2,1,0:T(8,128)(2,1)}, bf16[8,16,8,256]{3,2,1,0:T(8,128)(2,1)S(1)}, u32[]{:S(2)}, u32[]{:S(2)}) collective-permute-start(bf16[8,16,8,256]{3,2,1,0:T(8,128)(2,1)} %get-tuple-element.19), channel_id=1, source_target_pairs={{0,1},{1,0},{2,3},{3,2},{4,5},{5,4},{6,7},{7,6},{8,9},{9,8},{10,11... | collective-permute-start | bytes 1572872 | tf_op jit(solution)/shard_map/ppermute | solution.py:337
  130.1 1.0 copy-start.1
  145.2 16.0 %collective-permute-start.10 = (bf16[8,8,4096]{2,1,0:T(8,128)(2,1)S(1)}, bf16[8,8,4096]{2,1,0:T(8,128)(2,1)S(1)}, u32[]{:S(2)}, u32[]{:S(2)}) collective-permute-start(bf16[8,8,4096]{2,1,0:T(8,128)(2,1)S(1)} %slice.84), channel_id=1, source_target_pairs={{0,1},{1,0},{2,3},{3,2},{4,5},{5,4},{6,7},{7,6},{8,9},{9,8},{10,11... | collective-permute-start | bytes 1572872 | tf_op jit(solution)/shard_map/ppermute | solution.py:337
  145.8 1.0 copy-start.2
  146.8 14.4 %copy-start.5 = (bf16[16,8,4096]{2,1,0:T(8,128)(2,1)S(1)}, bf16[16,8,4096]{2,1,0:T(8,128)(2,1)}, u32[]{:S(2)}) copy-start(bf16[16,8,4096]{2,1,0:T(8,128)(2,1)} %get-tuple-element.10) | copy-start | bytes 3145732
  159.9 3.2 %copy-start.6 = (bf16[16,8,4096]{2,1,0:T(8,128)(2,1)S(1)}, bf16[16,8,4096]{2,1,0:T(8,128)(2,1)}, u32[]{:S(2)}) copy-start(bf16[16,8,4096]{2,1,0:T(8,128)(2,1)} %get-tuple-element.12) | copy-start | bytes 3145732
  161.1 2.0 %collective-permute-start.24 = (bf16[8,8,4096]{2,1,0:T(8,128)(2,1)S(1)}, bf16[8,8,4096]{2,1,0:T(8,128)(2,1)S(1)}, u32[]{:S(2)}, u32[]{:S(2)}) collective-permute-start(bf16[8,8,4096]{2,1,0:T(8,128)(2,1)S(1)} %slice.94), channel_id=1, source_target_pairs={{0,1},{1,0},{2,3},{3,2},{4,5},{5,4},{6,7},{7,6},{8,9},{9,8},{10,11... | collective-permute-start | bytes 1572872 | tf_op jit(solution)/shard_map/ppermute | solution.py:337
  161.4 9.2 %collective-permute-start.11 = (bf16[4,8,4096]{2,1,0:T(8,128)(2,1)S(1)}, bf16[4,8,4096]{2,1,0:T(8,128)(2,1)S(1)}, u32[]{:S(2)}, u32[]{:S(2)}) collective-permute-start(bf16[4,8,4096]{2,1,0:T(8,128)(2,1)S(1)} %slice.107), channel_id=1, source_target_pairs={{0,2},{1,3},{2,0},{3,1},{4,6},{5,7},{6,4},{7,5},{8,10},{9,11},{10,... | collective-permute-start | bytes 786440 | tf_op jit(solution)/shard_map/ppermute | solution.py:337
  163.2 19.7 %copy-start.9 = (bf16[8,4096]{1,0:T(8,128)(2,1)S(1)}, bf16[8,4096]{1,0:T(8,128)(2,1)}, u32[]{:S(2)}) copy-start(bf16[8,4096]{1,0:T(8,128)(2,1)} %get-tuple-element.9) | copy-start | bytes 196612
  163.2 24.5 %copy-start.10 = (bf16[8,4096]{1,0:T(8,128)(2,1)S(1)}, bf16[8,4096]{1,0:T(8,128)(2,1)}, u32[]{:S(2)}) copy-start(bf16[8,4096]{1,0:T(8,128)(2,1)} %get-tuple-element.11) | copy-start | bytes 196612
  163.3 12.5 %collective-permute-start.25 = (bf16[4,8,4096]{2,1,0:T(8,128)(2,1)S(1)}, bf16[4,8,4096]{2,1,0:T(8,128)(2,1)S(1)}, u32[]{:S(2)}, u32[]{:S(2)}) collective-permute-start(bf16[4,8,4096]{2,1,0:T(8,128)(2,1)S(1)} %slice.115), channel_id=1, source_target_pairs={{0,2},{1,3},{2,0},{3,1},{4,6},{5,7},{6,4},{7,5},{8,10},{9,11},{10,... | collective-permute-start | bytes 786440 | tf_op jit(solution)/shard_map/ppermute | solution.py:337
  170.6 5.9 %collective-permute-start.12 = (bf16[2,8,4096]{2,1,0:T(8,128)(2,1)S(1)}, bf16[2,8,4096]{2,1,0:T(8,128)(2,1)S(1)}, u32[]{:S(2)}, u32[]{:S(2)}) collective-permute-start(bf16[2,8,4096]{2,1,0:T(8,128)(2,1)S(1)} %slice.109), channel_id=1, source_target_pairs={{0,4},{1,5},{2,6},{3,7},{4,0},{5,1},{6,2},{7,3},{8,12},{9,13},{10,... | collective-permute-start | bytes 393224 | tf_op jit(solution)/shard_map/ppermute | solution.py:337
  175.8 6.6 %collective-permute-start.26 = (bf16[2,8,4096]{2,1,0:T(8,128)(2,1)S(1)}, bf16[2,8,4096]{2,1,0:T(8,128)(2,1)S(1)}, u32[]{:S(2)}, u32[]{:S(2)}) collective-permute-start(bf16[2,8,4096]{2,1,0:T(8,128)(2,1)S(1)} %slice.117), channel_id=1, source_target_pairs={{0,4},{1,5},{2,6},{3,7},{4,0},{5,1},{6,2},{7,3},{8,12},{9,13},{10,... | collective-permute-start | bytes 393224 | tf_op jit(solution)/shard_map/ppermute | solution.py:337
  176.6 6.3 %collective-permute-start.13 = (bf16[1,8,4096]{2,1,0:T(8,128)(2,1)S(1)}, bf16[1,8,4096]{2,1,0:T(8,128)(2,1)S(1)}, u32[]{:S(2)}, u32[]{:S(2)}) collective-permute-start(bf16[1,8,4096]{2,1,0:T(8,128)(2,1)S(1)} %slice.111), channel_id=1, source_target_pairs={{0,8},{1,9},{2,10},{3,11},{4,12},{5,13},{6,14},{7,15},{8,0},{9,1},... | collective-permute-start | bytes 196616 | tf_op jit(solution)/shard_map/ppermute | solution.py:337
  182.5 5.3 %collective-permute-start.27 = (bf16[1,8,4096]{2,1,0:T(8,128)(2,1)S(1)}, bf16[1,8,4096]{2,1,0:T(8,128)(2,1)S(1)}, u32[]{:S(2)}, u32[]{:S(2)}) collective-permute-start(bf16[1,8,4096]{2,1,0:T(8,128)(2,1)S(1)} %slice.119), channel_id=1, source_target_pairs={{0,8},{1,9},{2,10},{3,11},{4,12},{5,13},{6,14},{7,15},{8,0},{9,1},... | collective-permute-start | bytes 196616 | tf_op jit(solution)/shard_map/ppermute | solution.py:337

commit v2 on v1

v2 whole, which is shorter than its diff:
```python
import functools

import jax
import jax.numpy as jnp
from jax import lax
from jax.experimental import pallas as pl
from jax.experimental.pallas import tpu as pltpu
from jax.sharding import PartitionSpec as P

LANES = 128
KV_HEADS = 4
HEAD_DIM = 128
MIB = 1 << 20


def attend_kernel(micro, span, kv_heads, len_ref, q_ref, kv_ref, out_ref, q_scr, o_scr):
    step = pl.program_id(0)
    rows, width = q_ref.shape
    heads = width // HEAD_DIM
    per_group = heads // kv_heads
    positions = kv_ref.shape[1]

    @pl.when(step == 0)
    def _():
        for h in range(heads):
            q_scr[h] = q_ref[:, h * HEAD_DIM : (h + 1) * HEAD_DIM].astype(jnp.float32)

    column = lax.broadcasted_iota(jnp.int32, (heads, 2 * positions), 1)
    is_key = column % 2 == 0
    blocks, weights = [], []
    for i in range(span):
        row = step * span + i
        parts = [
            kv_ref[i, :, :, g * HEAD_DIM : (g + 1) * HEAD_DIM].reshape(2 * positions, HEAD_DIM)
            for g in range(kv_heads)
        ]
        blocks.append(parts)
        scores = jnp.concatenate(
            [
                lax.dot_general(
                    q_scr[g * per_group : (g + 1) * per_group, row, :].astype(jnp.bfloat16),
                    parts[g],
                    (((1,), (1,)), ((), ())),
                    preferred_element_type=jnp.float32,
                )
                for g in range(kv_heads)
            ],
            axis=0,
        ) * HEAD_DIM ** (-0.5)
        visible = is_key & (column < 2 * len_ref[micro, row])
        scores = jnp.where(visible, scores, -1e30)
        raised = jnp.exp(scores - jnp.max(scores, axis=-1, keepdims=True))
        raised = raised / jnp.sum(raised, axis=-1, keepdims=True)
        weights.append(pltpu.roll(raised, 1, 1).astype(jnp.bfloat16))
    for i in range(span):
        row = step * span + i
        for g in range(kv_heads):
            o_scr[g * per_group : (g + 1) * per_group, row, :] = jnp.dot(
                weights[i][g * per_group : (g + 1) * per_group],
                blocks[i][g],
                preferred_element_type=jnp.float32,
            )

    @pl.when(step == pl.num_programs(0) - 1)
    def _():
        for h in range(heads):
            out_ref[:, h * HEAD_DIM : (h + 1) * HEAD_DIM] = o_scr[h].astype(jnp.bfloat16)


def attend(queries, kv_cache, lengths, micro):
    _, rows, width = queries.shape
    heads = width // HEAD_DIM
    span = 4 if rows % 4 == 0 else 1
    kv_shape = kv_cache.shape[2:]
    return pl.pallas_call(
        functools.partial(attend_kernel, micro, span, KV_HEADS),
        grid_spec=pltpu.PrefetchScalarGridSpec(
            num_scalar_prefetch=1,
            grid=(rows // span,),
            in_specs=[
                pl.BlockSpec((None, rows, width), lambda r, n: (micro, 0, 0)),
                pl.BlockSpec((None, span) + kv_shape, lambda r, n: (micro, r, 0, 0, 0)),
            ],
            out_specs=pl.BlockSpec((rows, width), lambda r, n: (0, 0)),
            scratch_shapes=[pltpu.VMEM((heads, rows, HEAD_DIM), jnp.float32)] * 2,
        ),
        out_shape=jax.ShapeDtypeStruct((rows, width), jnp.bfloat16),
        name="attend",
        compiler_params=pltpu.CompilerParams(vmem_limit_bytes=16 * MIB),
        cost_estimate=pl.CostEstimate(
            flops=rows * width * 4 * 256, bytes_accessed=rows << 18, transcendentals=0
        ),
    )(lengths, queries, kv_cache)


def expand_kernel(stacked, table_ref, code_ref, *rest):
    out_ref = rest[-1]
    rows, columns = code_ref.shape
    tile = 16
    tables = [jnp.broadcast_to(table_ref[i : i + 1], (tile, LANES)) for i in range(8)]

    def one(i, lane):
        at = pl.ds(pl.multiple_of(i * tile, tile), tile)
        codes = code_ref[at, lane * LANES : (lane + 1) * LANES]
        codes = codes.astype(jnp.float32).astype(jnp.int32)
        upper = codes >= LANES
        low = jnp.bitwise_and(codes, LANES - 1)

        def take(table):
            return jnp.take_along_axis(table, low, axis=1, mode="promise_in_bounds")

        for q in range(4):
            value = jnp.where(upper, take(tables[2 * q + 1]), take(tables[2 * q]))
            value = value.astype(jnp.bfloat16)
            if stacked:
                out_ref[q, at, lane * LANES : (lane + 1) * LANES] = value
            else:
                first = q * columns + lane * LANES
                out_ref[at, first : first + LANES] = value

    for lane in range(columns // LANES):

        def body(i, _, lane=lane):
            one(i, lane)
            return 0

        lax.fori_loop(0, rows // tile, body, 0, unroll=rows // tile if rows // tile <= 12 else 8)


def expand(table, codes, stacked, after=()):
    rows, columns = codes.shape
    if stacked:
        block = 512
        grid = (columns // block,)
        code_spec = pl.BlockSpec((rows, block), lambda b: (0, b))
        out_spec = pl.BlockSpec((4, rows, block), lambda b: (0, 0, b))
        out_shape = (4, rows, columns)
    else:
        block = 128
        grid = (rows // block,)
        code_spec = pl.BlockSpec((block, columns), lambda b: (b, 0))
        out_spec = pl.BlockSpec((block, 4 * columns), lambda b: (b, 0))
        out_shape = (rows, 4 * columns)
    out = pl.pallas_call(
        functools.partial(expand_kernel, stacked),
        grid=grid,
        in_specs=[pl.BlockSpec((8, LANES), lambda b: (0, 0)), code_spec]
        + [pl.BlockSpec(memory_space=pl.ANY) for _ in after],
        out_specs=out_spec,
        out_shape=jax.ShapeDtypeStruct(out_shape, jnp.bfloat16),
        name="expand",
        compiler_params=pltpu.CompilerParams(vmem_limit_bytes=10 * MIB),
        cost_estimate=pl.CostEstimate(
            flops=rows * columns * 8000, bytes_accessed=10 * rows * columns, transcendentals=0
        ),
    )(table, codes, *after)
    return out.reshape(4 * rows, columns) if stacked else out


def project_kernel(masks, counts, me_ref, *refs):
    pieces, refs = refs[: len(masks)], refs[len(masks) :]
    weight_ref, hidden_ref = refs[:2]
    out_refs, acc_ref = refs[2:-1], refs[-1]
    step = pl.program_id(0)
    depth = weight_ref.shape[0]

    @pl.when(step == 0)
    def _():
        acc_ref[...] = jnp.zeros_like(acc_ref)

    rows_in = jnp.concatenate([ref[...].reshape(-1, depth) for ref in pieces], axis=0)
    product = jnp.dot(rows_in, weight_ref[...], preferred_element_type=jnp.float32)
    acc_ref[...] += product.reshape(acc_ref.shape)

    @pl.when(step == pl.num_programs(0) - 1)
    def _():
        me = me_ref[0]
        at = 0
        for mask_list, m in zip(masks, counts):
            for mask in mask_list:
                source = me ^ mask
                projected = acc_ref[at].astype(jnp.bfloat16).astype(jnp.float32)
                out_refs[m][source] = (
                    hidden_ref[source, m].astype(jnp.float32) + projected
                ).astype(jnp.bfloat16)
                at += 1


def project(me, gathered, out_weight, hidden_columns):
    pieces = [array for chain in gathered for array, _ in chain]
    masks = tuple(mask for chain in gathered for _, mask in chain)
    counts = tuple(m for m, chain in enumerate(gathered) for _ in chain)
    shards, micro_count, rows, columns = hidden_columns.shape
    depth = out_weight.shape[0]
    block = 2048
    return pl.pallas_call(
        functools.partial(project_kernel, masks, counts),
        grid_spec=pltpu.PrefetchScalarGridSpec(
            num_scalar_prefetch=1,
            grid=(depth // block,),
            in_specs=[
                pl.BlockSpec((piece.shape[0], rows, block), lambda k, n: (0, 0, k))
                for piece in pieces
            ]
            + [
                pl.BlockSpec((block, columns), lambda k, n: (k, 0)),
                pl.BlockSpec(hidden_columns.shape, lambda k, n: (0, 0, 0, 0)),
            ],
            out_specs=[
                pl.BlockSpec((shards, rows, columns), lambda k, n: (0, 0, 0))
                for _ in range(micro_count)
            ],
            scratch_shapes=[pltpu.VMEM((shards * micro_count, rows, columns), jnp.float32)],
        ),
        out_shape=[jax.ShapeDtypeStruct((shards, rows, columns), jnp.bfloat16)] * micro_count,
        name="project",
        compiler_params=pltpu.CompilerParams(vmem_limit_bytes=24 * MIB),
        cost_estimate=pl.CostEstimate(
            flops=2 * shards * micro_count * rows * depth * columns,
            bytes_accessed=2 * depth * columns,
            transcendentals=0,
        ),
    )(me, *pieces, out_weight, hidden_columns)


def experts_kernel(masks, counts, orders, me_ref, *refs):
    pieces, refs = refs[: len(masks)], refs[len(masks) :]
    gain_ref, router_ref, hot_ref, gate_ref, up_ref, down_ref, gu_scale_ref, down_scale_ref = refs[
        :8
    ]
    groups = len(orders)
    send_refs, keep_refs, own_refs = (
        refs[8 + i * groups : 8 + (i + 1) * groups] for i in range(3)
    )
    token_scr, weight_scr, acc_ref = refs[-3:]
    step = pl.program_id(0)
    _, shards, rows, columns = pieces[0].shape
    total, width = token_scr.shape
    part = shards * rows
    me = me_ref[0]

    @pl.when(step == 0)
    def _():
        for m in range(groups):
            mine = [
                (ref, i, mask)
                for ref, mask_list, n in zip(pieces, masks, counts)
                if n == m
                for i, mask in enumerate(mask_list)
            ]
            squares = jnp.zeros((part, columns), jnp.float32)
            for ref, i, _ in mine:
                value = ref[i].reshape(part, columns).astype(jnp.float32)
                squares += value * value
            mean = jnp.sum(squares, axis=-1, keepdims=True) / width
            inverse = lax.rsqrt(mean + 1e-06)
            for ref, i, mask in mine:
                at = pl.ds(0, columns)
                if len(mine) > 1:
                    at = pl.ds(pl.multiple_of((me ^ mask) * columns, columns), columns)
                value = ref[i].reshape(part, columns).astype(jnp.float32)
                own_refs[m][:, at] = ref[i, me]
                token_scr[m * part : (m + 1) * part, at] = (
                    value * inverse * gain_ref[:, at]
                ).astype(jnp.bfloat16)
        logits = lax.dot_general(
            token_scr[...],
            router_ref[...],
            (((1,), (1,)), ((), ())),
            preferred_element_type=jnp.float32,
        )
        hot = hot_ref[...].astype(jnp.float32) > 0.5
        logits = jnp.where(hot, logits, -1e30)
        raised = jnp.where(hot, jnp.exp(logits - jnp.max(logits, axis=-1, keepdims=True)), 0.0)
        raised = raised / jnp.sum(raised, axis=-1, keepdims=True)
        mine = lax.broadcasted_iota(jnp.int32, raised.shape, 1) == me
        weight = jnp.sum(jnp.where(mine, raised, 0.0), axis=-1, keepdims=True)
        weight = weight.astype(jnp.bfloat16).astype(jnp.float32)
        weight_scr[...] = jnp.broadcast_to(weight, (total, LANES)).reshape(weight_scr.shape)
        acc_ref[...] = jnp.zeros_like(acc_ref)

    nt = (((1,), (1,)), ((), ()))
    tokens = token_scr[...]
    gate = lax.dot_general(tokens, gate_ref[...], nt, preferred_element_type=jnp.float32)
    up = lax.dot_general(tokens, up_ref[...], nt, preferred_element_type=jnp.float32)
    gate = gate * gu_scale_ref[0:1, :]
    up = up * gu_scale_ref[1:2, :]
    inner = (gate / (1.0 + jnp.exp(-gate)) * up).astype(jnp.bfloat16)
    piece = 1024
    for c in range(width // piece):
        at = slice(c * piece, (c + 1) * piece)
        product = jnp.dot(inner, down_ref[:, at], preferred_element_type=jnp.float32)
        acc_ref[:, :, at] += product.reshape(groups * shards, rows, piece)

    @pl.when(step == pl.num_programs(0) - 1)
    def _():
        half = shards // 2
        for m, order in enumerate(orders):
            for p, mask in enumerate(order):
                source = m * shards + (me ^ mask)
                value = (acc_ref[source] * down_scale_ref[...]).astype(jnp.bfloat16)
                value = (value.astype(jnp.float32) * weight_scr[source][:, 0:1]).astype(
                    jnp.bfloat16
                )
                if p < half:
                    keep_refs[m][p] = value
                else:
                    send_refs[m][p - half] = value


def run_experts(me, streams, gain, router, hot, gate, up, down, gu_scale, down_scale, orders):
    pieces = [array for chain in streams for array, _ in chain]
    masks = tuple(mask for chain in streams for _, mask in chain)
    counts = tuple(m for m, chain in enumerate(streams) for _ in chain)
    groups = len(streams)
    _, shards, rows, _ = pieces[0].shape
    hidden_units, width = gate.shape
    total = groups * shards * rows
    block = 256
    full = lambda f, n: (0, 0)
    half_spec = pl.BlockSpec((shards // 2, rows, width), lambda f, n: (0, 0, 0))
    half_shape = jax.ShapeDtypeStruct((shards // 2, rows, width), jnp.bfloat16)
    outs = pl.pallas_call(
        functools.partial(experts_kernel, masks, counts, orders),
        grid_spec=pltpu.PrefetchScalarGridSpec(
            num_scalar_prefetch=1,
            grid=(hidden_units // block,),
            in_specs=[pl.BlockSpec(piece.shape, lambda f, n: (0, 0, 0, 0)) for piece in pieces]
            + [
                pl.BlockSpec((1, width), full),
                pl.BlockSpec(router.shape, full),
                pl.BlockSpec(hot.shape, full),
                pl.BlockSpec((block, width), lambda f, n: (f, 0)),
                pl.BlockSpec((block, width), lambda f, n: (f, 0)),
                pl.BlockSpec((block, width), lambda f, n: (f, 0)),
                pl.BlockSpec((2, block), lambda f, n: (0, f)),
                pl.BlockSpec((1, width), full),
            ],
            out_specs=[half_spec] * (2 * groups) + [pl.BlockSpec((rows, width), full)] * groups,
            scratch_shapes=[
                pltpu.VMEM((total, width), jnp.bfloat16),
                pltpu.VMEM((groups * shards, rows, LANES), jnp.float32),
                pltpu.VMEM((groups * shards, rows, width), jnp.float32),
            ],
        ),
        out_shape=[half_shape] * (2 * groups)
        + [jax.ShapeDtypeStruct((rows, width), jnp.bfloat16)] * groups,
        name="experts",
        compiler_params=pltpu.CompilerParams(
            vmem_limit_bytes=(36 if total <= 256 else 60) * MIB
        ),
        cost_estimate=pl.CostEstimate(
            flops=6 * total * width * hidden_units,
            bytes_accessed=6 * width * hidden_units,
            transcendentals=0,
        ),
    )(me, *pieces, gain, router, hot, gate, up, down, gu_scale, down_scale)
    return [tuple(outs[i * groups + m] for i in range(3)) for m in range(groups)]


def swap(value, bit, count):
    return lax.ppermute(value, "expert", [(i, i ^ bit) for i in range(count)])


def gather_all(value, count, near_first):
    if count != 16:
        held, masks = value[None], (0,)
        for bit in [1 << b for b in reversed(range(count.bit_length() - 1))]:
            held = jnp.concatenate([held, swap(held, bit, count)])
            masks = masks + tuple(mask ^ bit for mask in masks)
        return [(held, masks)], []
    if near_first:
        first = jnp.stack([value, swap(value, 2, count)])
        far, near = swap(first, 8, count), swap(first, 4, count)
        both = swap(far, 4, count)
        chain = [(first, (0, 2)), (far, (8, 10)), (near, (4, 6)), (both, (12, 14))]
        marks = [first, far]
    else:
        far, near = swap(value, 8, count), swap(value, 4, count)
        both = swap(far, 4, count)
        first = jnp.stack([value, far, near, both])
        chain = [(first, (0, 8, 4, 12)), (swap(first, 2, count), (2, 10, 6, 14))]
        marks = [far, first]
    chain += [(swap(held, 1, count), tuple(m ^ 1 for m in masks)) for held, masks in chain]
    return chain, marks


def reduce_order(count, flipped):
    bits = [1 << b for b in range(count.bit_length() - 1)]
    if flipped:
        bits = [bits[0]] + bits[2:] + [bits[1]]
    order = tuple(
        sum(bit for i, bit in enumerate(bits) if (p >> (len(bits) - 1 - i)) & 1)
        for p in range(count)
    )
    return bits, order


def reduce_own(send, keep, own, bits, count):
    for i, bit in enumerate(bits):
        other = swap(send, bit, count)
        half = keep.shape[0] // 2
        if half == 0:
            break
        add = lambda a, b: (a.astype(jnp.float32) + b.astype(jnp.float32)).astype(jnp.bfloat16)
        send, keep = add(keep[half:], other[half:]), add(keep[:half], other[:half])
    mixture = keep[0].astype(jnp.float32) + other[0].astype(jnp.float32)
    return (own.astype(jnp.float32) + mixture).astype(jnp.bfloat16)


def body(
    hidden,
    queries,
    kv_cache,
    lengths,
    routes,
    out_weight,
    norm_gain,
    router_weight,
    gate_codes,
    up_codes,
    down_codes,
    codebooks,
    gate_up_scale,
    down_scale,
):
    micro_count, rows, width = hidden.shape
    count = lax.axis_size("expert")
    me = lax.axis_index("expert").astype(jnp.int32)
    me_list = me.reshape(1)
    columns = out_weight.shape[1]
    hot = (routes[..., None] == jnp.arange(count, dtype=jnp.int32)).any(axis=2)
    lead = hidden.reshape(micro_count, rows, count, columns).transpose(2, 0, 1, 3)
    tail = jnp.broadcast_to(hot.astype(jnp.bfloat16)[None], (count,) + hot.shape)
    packed = lax.all_to_all(
        jnp.concatenate([lead, tail], axis=-1), "expert", split_axis=0, concat_axis=0, tiled=True
    )
    hidden_columns = packed[..., :columns]
    hot_all = packed[..., columns:].transpose(1, 0, 2, 3).reshape(micro_count, count * rows, count)

    tables = codebooks[0].astype(jnp.float32).transpose(0, 2, 1).reshape(3, 8, LANES)
    gathered, marks = [], []
    for m in range(micro_count):
        chain, seen = gather_all(attend(queries, kv_cache, lengths, m), count, m % 2 == 1)
        gathered.append(chain)
        marks.append(seen)
    after = [tuple(seen[i] for seen in marks if seen) for i in range(2)]
    gate = expand(tables[0], gate_codes[0].T, True)
    up = expand(tables[1], up_codes[0].T, True, after[0] if marks[0] else ())
    down = expand(tables[2], down_codes[0], False, after[1] if marks[0] else ())

    columns_of = project(me_list, gathered, out_weight, hidden_columns)
    streams = []
    for m in range(micro_count):
        chain, _ = gather_all(columns_of[m], count, m % 2 == 1)
        if columns % LANES:
            held, masks = chain[0]
            place = [masks.index(i) for i in range(count)]
            order = jnp.asarray(place, jnp.int32)[jnp.arange(count, dtype=jnp.int32) ^ me]
            held = held[order].transpose(1, 2, 0, 3).reshape(1, count, rows, width)
            chain = [(held, (0,))]
        streams.append(chain)

    plans = [reduce_order(count, m % 2 == 1) for m in range(micro_count)]
    batches = [list(range(micro_count))] if count * rows <= 128 else [[m] for m in range(micro_count)]
    outputs = []
    for batch in batches:
        results = run_experts(
            me_list,
            [streams[m] for m in batch],
            norm_gain.reshape(1, width),
            router_weight.T,
            jnp.concatenate([hot_all[m] for m in batch]),
            gate,
            up,
            down,
            gate_up_scale[0],
            down_scale,
            tuple(plans[m][1] for m in batch),
        )
        for m, (send, keep, own) in zip(batch, results):
            outputs.append(reduce_own(send, keep, own, plans[m][0], count))
    return jnp.stack(outputs)


def solution(mesh):
    in_specs = (
        P(None, ("groups", "expert"), None),
        P(None, ("groups", "expert"), None),
        P(None, ("groups", "expert"), None, None, None),
        P(None, ("groups", "expert")),
        P(None, ("groups", "expert"), None),
        P(None, "expert"),
        P(),
        P(),
        P("expert", None, None),
        P("expert", None, None),
        P("expert", None, None),
        P("expert", None, None, None),
        P("expert", None, None),
        P("expert", None),
    )
    out_specs = P(None, ("groups", "expert"), None)
    return jax.shard_map(body, mesh=mesh, in_specs=in_specs, out_specs=out_specs, check_vma=False)
```

time: 190 us -> 150 us (0.79)
  Pallas kernels: 75.2 us -> 43.6 us
  local copies, waits for them, and re-layouts: 28.4 us -> 14.6 us
  waiting for transfers between devices: 46.7 us -> 53.9 us
    pallas_call x4 -> x2, Pallas kernels: 35.6 us -> 14.3 us  [the longest x1 10.6 us: run_experts(): pl.pallas_call(functools.partial(experts_kernel, masks, counts, orders),...]
    ppermute x28 -> x36, waiting for transfers between devices: 46.7 us -> 53.9 us  [swap(): return lax.ppermute(value, 'expert', [(i, i ^ bit) for i in range(count)])]
    concatenate x9 -> x0, local copies, waits for them, and re-layouts: 6.38 us -> none  [the longest x8 5.66 us: gather_all(): held = jnp.concatenate([held, swap(held, bit, count)])]
    pallas_call x3, Pallas kernels: 29.8 us -> 23.5 us  [expand(): pl.pallas_call(functools.partial(expand_kernel, stacked), grid=grid, in_s...]
    pallas_call x2, Pallas kernels: 9.74 us -> 5.74 us  [attend(): pl.pallas_call(functools.partial(attend_kernel, micro, span, KV_HEADS), g...]
    unnamed x45 -> x36, local copies, waits for them, and re-layouts: 16.6 us -> 12.8 us
    ppermute x28 -> x36, starting transfers between devices: 29.3 us -> 29.9 us  [swap(): return lax.ppermute(value, 'expert', [(i, i ^ bit) for i in range(count)])]
  transfers between devices with their start and end apart: 29 -> 37, of which waited for: 12 -> 17; matrix products, arithmetic and copies ran while one was open for 14% -> 2% of each run, Pallas kernels for 37% -> 18%
where the time goes in v2:
time: 150 us; the launch traced here: 149 us
  waiting for transfers between devices  53.9 us (36%)
  Pallas kernels  43.6 us (29%)
  starting transfers between devices  34.5 us (23%)
  local copies, waits for them, and re-layouts  14.6 us (10%)
  other arithmetic  2.18 us (1%)
    ppermute x36, waiting for transfers between devices, swap(): return lax.ppermute(value, 'expert', [(i, i ^ bit) for i in range(count)])  53.9 us
    ppermute x36, starting transfers between devices, swap(): return lax.ppermute(value, 'expert', [(i, i ^ bit) for i in range(count)])  29.9 us
    pallas_call x3, Pallas kernels, expand(): pl.pallas_call(functools.partial(expand_kernel, stacked), grid=grid, in_s...  23.5 us
    unnamed x36, local copies, waits for them, and re-layouts  12.8 us
    pallas_call x1, Pallas kernels, run_experts(): pl.pallas_call(functools.partial(experts_kernel, masks, counts, orders),...  10.6 us
    pallas_call x2, Pallas kernels, attend(): pl.pallas_call(functools.partial(attend_kernel, micro, span, KV_HEADS), g...  5.74 us
    all_to_all x1, starting transfers between devices, body(): lax.all_to_all(jnp.concatenate([lead, tail], axis=-1), 'expert', split_ax...  4.56 us
    pallas_call x1, Pallas kernels, project(): pl.pallas_call(functools.partial(project_kernel, masks, counts), grid_spe...  3.71 us
  transfers between devices with their start and end apart: 37, of which 17 were waited for; matrix products, arithmetic and copies ran while one was open for 2% of the time, Pallas kernels for 18%

profile of v2, /device:TPU:0, one launch (start us, length us, event | category | flops | bytes accessed | tf_op | source)
XLA Modules:
  0.0 149.1 jit_solution(3484997957990404435)
XLA Ops:
  0.0 2.2 %copy-done = bf16[2,8,128,2,512]{4,3,2,1,0:T(2,128)(2,1)S(1)} copy-done((bf16[2,8,128,2,512]{4,3,2,1,0:T(2,128)(2,1)S(1)}, bf16[2,8,128,2,512]{4,3,2,1,0:T(2,128)(2,1)}, u32[]{:S(2)}) %copy-start) | copy-done | bytes 4194328
  2.2 0.9 copy-done.4
  3.1 0.7 copy-done.9
  3.8 2.9 %attend.2 = bf16[8,8192]{1,0:T(8,128)(2,1)S(1)} custom-call(s32[2,8]{1,0:T(2,128)S(1)} %copy-done.9, bf16[2,8,8192]{2,1,0:T(8,128)(2,1)S(1)} %copy-done.4, bf16[2,8,128,2,512]{4,3,2,1,0:T(2,128)(2,1)S(1)} %copy-done), custom_call_target="tpu_custom_call" | custom-call | flops 67108864 | bytes 2097152 | tf_op jit(solution)/shard_map/attend/pallas_call | solution.py:75
  6.7 4.1 %collective-permute-start = (bf16[8,8192]{1,0:T(8,128)(2,1)S(1)}, bf16[8,8192]{1,0:T(8,128)(2,1)S(1)}, u32[]{:S(2)}, u32[]{:S(2)}) collective-permute-start(bf16[8,8192]{1,0:T(8,128)(2,1)S(1)} %attend.2), channel_id=1, source_target_pairs={{0,8},{1,9},{2,10},{3,11},{4,12},{5,13},{6,14},{7,15},{8,0},{9,1},... | collective-permute-start | bytes 393224 | tf_op jit(solution)/shard_map/ppermute | solution.py:362
  10.8 2.9 %attend.3 = bf16[8,8192]{1,0:T(8,128)(2,1)S(1)} custom-call(s32[2,8]{1,0:T(2,128)S(1)} %copy-done.9, bf16[2,8,8192]{2,1,0:T(8,128)(2,1)S(1)} %copy-done.4, bf16[2,8,128,2,512]{4,3,2,1,0:T(2,128)(2,1)S(1)} %copy-done), custom_call_target="tpu_custom_call" | custom-call | flops 67108864 | bytes 2097152 | tf_op jit(solution)/shard_map/attend/pallas_call | solution.py:75
  13.7 1.6 %collective-permute-start.6 = (bf16[8,8192]{1,0:T(8,128)(2,1)S(1)}, bf16[8,8192]{1,0:T(8,128)(2,1)S(1)}, u32[]{:S(2)}, u32[]{:S(2)}) collective-permute-start(bf16[8,8192]{1,0:T(8,128)(2,1)S(1)} %attend.3), channel_id=1, source_target_pairs={{0,2},{1,3},{2,0},{3,1},{4,6},{5,7},{6,4},{7,5},{8,10},{9,11},{10,... | collective-permute-start | bytes 393224 | tf_op jit(solution)/shard_map/ppermute | solution.py:362
  15.3 1.6 %collective-permute-start.1 = (bf16[8,8192]{1,0:T(8,128)(2,1)S(1)}, bf16[8,8192]{1,0:T(8,128)(2,1)S(1)}, u32[]{:S(2)}, u32[]{:S(2)}) collective-permute-start(bf16[8,8192]{1,0:T(8,128)(2,1)S(1)} %attend.2), channel_id=1, source_target_pairs={{0,4},{1,5},{2,6},{3,7},{4,0},{5,1},{6,2},{7,3},{8,12},{9,13},{10,... | collective-permute-start | bytes 393224 | tf_op jit(solution)/shard_map/ppermute | solution.py:362
  16.9 0.1 fusion.4
  17.0 0.1 collective-permute-done.rest_0_
  17.1 0.8 collective-permute-start.2
  17.9 0.8 collective-permute-done.6
  18.8 2.7 %collective-permute-start.7 = (bf16[2,8,8192]{2,1,0:T(8,128)(2,1)S(1)}, bf16[2,8,8192]{2,1,0:T(8,128)(2,1)S(1)}, u32[]{:S(2)}, u32[]{:S(2)}) collective-permute-start(bf16[2,8,8192]{2,1,0:T(8,128)(2,1)S(1)} %pad_maximum_fusion.1.refs_4_.rest_1_), channel_id=1, source_target_pairs={{0,8},{1,9},{2,10},{3,11},{4,12},{5,13},{6,14},{7,15},{8,0},{9,1},... | collective-permute-start | bytes 786440 | tf_op jit(solution)/shard_map/ppermute | solution.py:362
  21.5 4.0 %collective-permute-done.2 = bf16[8,8192]{1,0:T(8,128)(2,1)S(1)} collective-permute-done((bf16[8,8192]{1,0:T(8,128)(2,1)S(1)}, bf16[8,8192]{1,0:T(8,128)(2,1)S(1)}, u32[]{:S(2)}, u32[]{:S(2)}) %collective-permute-start.2) | collective-permute-done | bytes 131104 | tf_op jit(solution)/shard_map/ppermute | solution.py:362
  25.6 1.3 collective-permute-start.3
  26.9 0.7 pad_maximum_fusion.3
  27.7 4.6 %all-to-all-start = ((bf16[16,2,8,272]{3,2,1,0:T(8,128)(2,1)}), bf16[16,2,8,272]{3,2,1,0:T(8,128)(2,1)}, u32[]{:S(2)}, u32[]{:S(2)}) async-start(bf16[16,2,8,272]{3,2,1,0:T(8,128)(2,1)} %pad_maximum_fusion.3), calls=%async_computation | async-start | bytes 393216 | tf_op jit(solution)/shard_map/all_to_all | solution.py:435
  32.2 0.4 collective-permute-start.10
  32.6 1.7 %collective-permute-start.8 = (bf16[2,8,8192]{2,1,0:T(8,128)(2,1)S(1)}, bf16[2,8,8192]{2,1,0:T(8,128)(2,1)S(1)}, u32[]{:S(2)}, u32[]{:S(2)}) collective-permute-start(bf16[2,8,8192]{2,1,0:T(8,128)(2,1)S(1)} %pad_maximum_fusion.1.refs_4_.rest_1_), channel_id=1, source_target_pairs={{0,4},{1,5},{2,6},{3,7},{4,0},{5,1},{6,2},{7,3},{8,12},{9,13},{10,... | collective-permute-start | bytes 786440 | tf_op jit(solution)/shard_map/ppermute | solution.py:362
  34.3 0.3 collective-permute-start.9
  34.8 0.5 collective-permute-start.11
  35.3 9.3 %collective-permute-done.8.refs_6_ = bf16[2,8,8192]{2,1,0:T(8,128)(2,1)S(1)} collective-permute-done((bf16[2,8,8192]{2,1,0:T(8,128)(2,1)S(1)}, bf16[2,8,8192]{2,1,0:T(8,128)(2,1)S(1)}, u32[]{:S(2)}, u32[]{:S(2)}) %collective-permute-start.8) | collective-permute-done | bytes 262176 | tf_op jit(solution)/shard_map/ppermute | solution.py:362
  44.6 5.1 %collective-permute-done.9.refs_7_ = bf16[2,8,8192]{2,1,0:T(8,128)(2,1)S(1)} collective-permute-done((bf16[2,8,8192]{2,1,0:T(8,128)(2,1)S(1)}, bf16[2,8,8192]{2,1,0:T(8,128)(2,1)S(1)}, u32[]{:S(2)}, u32[]{:S(2)}) %collective-permute-start.9) | collective-permute-done | bytes 262176 | tf_op jit(solution)/shard_map/ppermute | solution.py:362
  49.7 0.5 collective-permute-start.5
  50.2 1.4 copy-done.10
  51.6 8.0 %expand.3 = bf16[4,192,4096]{2,1,0:T(8,128)(2,1)S(1)} custom-call(f32[8,128]{1,0:T(8,128)S(1)} %squeeze.34.table_ref, bf16[192,4096]{1,0:T(8,128)(2,1)S(1)} %bitcast.71), custom_call_target="tpu_custom_call" | custom-call | flops 6291456000 | bytes 7864320 | tf_op jit(solution)/shard_map/expand/pallas_call | solution.py:144
  59.7 2.6 %copy-done.1 = bf16[4,192,4096]{2,1,0:T(8,128)(2,1)} copy-done((bf16[4,192,4096]{2,1,0:T(8,128)(2,1)}, bf16[4,192,4096]{2,1,0:T(8,128)(2,1)S(1)}, u32[]{:S(2)}) %copy-start.1) | copy-done | bytes 6291480
  62.3 0.9 slice.129.refs_13_
  63.3 2.2 %copy-done.3 = bf16[8192,256]{1,0:T(8,128)(2,1)S(1)} copy-done((bf16[8192,256]{1,0:T(8,128)(2,1)S(1)}, bf16[8192,256]{1,0:T(8,128)(2,1)}, u32[]{:S(2)}) %copy-start.3) | copy-done | bytes 4194328
  65.5 3.7 %project.1 = (bf16[16,8,256]{2,1,0:T(8,128)(2,1)S(1)}, bf16[16,8,256]{2,1,0:T(8,128)(2,1)S(1)}) custom-call(s32[1]{0:T(128)} %bitcast.me_ref, bf16[4,8,8192]{2,1,0:T(8,128)(2,1)S(1)} %pad_maximum_fusion.refs_0_.rest_0_, bf16[4,8,8192]{2,1,0:T(8,128)(2,1)S(1)} %collective-permute-done.3.refs_1_, bf16[4,8,8192]{2,1,0:T(8,128)(2,1)S(1)} %collective-permute-done.4.refs_2_, ...), custom_call_target="tpu_custom_call" | custom-call | flops 1073741824 | bytes 4194304 | tf_op jit(solution)/shard_map/project/pallas_call | solution.py:196
  69.2 1.5 %collective-permute-start.20 = (bf16[16,8,256]{2,1,0:T(8,128)(2,1)S(1)}, bf16[16,8,256]{2,1,0:T(8,128)(2,1)S(1)}, u32[]{:S(2)}, u32[]{:S(2)}) collective-permute-start(bf16[16,8,256]{2,1,0:T(8,128)(2,1)S(1)} %get-tuple-element.14), channel_id=1, source_target_pairs={{0,2},{1,3},{2,0},{3,1},{4,6},{5,7},{6,4},{7,5},{8,10},{9,11},{10,... | collective-permute-start | bytes 196616 | tf_op jit(solution)/shard_map/ppermute | solution.py:362
  70.7 8.0 %expand.4 = bf16[4,192,4096]{2,1,0:T(8,128)(2,1)S(1)} custom-call(f32[8,128]{1,0:T(8,128)S(1)} %squeeze.36.table_ref, bf16[192,4096]{1,0:T(8,128)(2,1)S(1)} %bitcast.72, bf16[8,8192]{1,0:T(8,128)(2,1)S(1)} %collective-permute-done.rest_0_, bf16[2,8,8192]{2,1,0:T(8,128)(2,1)S(1)} %pad_maximum_fusion.1.refs_4_.rest_1_), custom_call_target="tpu_custom_call" | custom-call | flops 6291456000 | bytes 7864320 | tf_op jit(solution)/shard_map/expand/pallas_call | solution.py:144
  78.8 0.6 collective-permute-start.15
  79.4 2.4 %collective-permute-start.14 = (bf16[16,8,256]{2,1,0:T(8,128)(2,1)S(1)}, bf16[16,8,256]{2,1,0:T(8,128)(2,1)S(1)}, u32[]{:S(2)}, u32[]{:S(2)}) collective-permute-start(bf16[16,8,256]{2,1,0:T(8,128)(2,1)S(1)} %get-tuple-element.13), channel_id=1, source_target_pairs={{0,8},{1,9},{2,10},{3,11},{4,12},{5,13},{6,14},{7,15},{8,0},{9,1},... | collective-permute-start | bytes 196616 | tf_op jit(solution)/shard_map/ppermute | solution.py:362
  81.8 0.6 collective-permute-start.21
  82.4 6.7 %collective-permute-done.14 = bf16[16,8,256]{2,1,0:T(8,128)(2,1)S(1)} collective-permute-done((bf16[16,8,256]{2,1,0:T(8,128)(2,1)S(1)}, bf16[16,8,256]{2,1,0:T(8,128)(2,1)S(1)}, u32[]{:S(2)}, u32[]{:S(2)}) %collective-permute-start.14) | collective-permute-done | bytes 65568 | tf_op jit(solution)/shard_map/ppermute | solution.py:362
  89.1 0.8 slice_bitcast_fusion
  90.0 2.0 %collective-permute-start.22 = (bf16[2,16,8,256]{3,2,1,0:T(8,128)(2,1)S(1)}, bf16[2,16,8,256]{3,2,1,0:T(8,128)(2,1)S(1)}, u32[]{:S(2)}, u32[]{:S(2)}) collective-permute-start(bf16[2,16,8,256]{3,2,1,0:T(8,128)(2,1)S(1)} %pad_maximum_fusion.4.refs_4_), channel_id=1, source_target_pairs={{0,4},{1,5},{2,6},{3,7},{4,0},{5,1},{6,2},{7,3},{8,12},{9,13},{10,... | collective-permute-start | bytes 393224 | tf_op jit(solution)/shard_map/ppermute | solution.py:362
  92.0 1.5 collective-permute-done.16
  93.5 0.6 collective-permute-start.17
  94.3 0.5 collective-permute-start.25
  94.8 1.6 %collective-permute-done.22.refs_6_ = bf16[2,16,8,256]{3,2,1,0:T(8,128)(2,1)S(1)} collective-permute-done((bf16[2,16,8,256]{3,2,1,0:T(8,128)(2,1)S(1)}, bf16[2,16,8,256]{3,2,1,0:T(8,128)(2,1)S(1)}, u32[]{:S(2)}, u32[]{:S(2)}) %collective-permute-start.22) | collective-permute-done | bytes 131104 | tf_op jit(solution)/shard_map/ppermute | solution.py:362
  96.4 2.8 %collective-permute-done.23.refs_7_ = bf16[2,16,8,256]{3,2,1,0:T(8,128)(2,1)S(1)} collective-permute-done((bf16[2,16,8,256]{3,2,1,0:T(8,128)(2,1)S(1)}, bf16[2,16,8,256]{3,2,1,0:T(8,128)(2,1)S(1)}, u32[]{:S(2)}, u32[]{:S(2)}) %collective-permute-start.23) | collective-permute-done | bytes 131104 | tf_op jit(solution)/shard_map/ppermute | solution.py:362
  99.1 1.4 collective-permute-done.17.refs_1_
  100.6 7.5 %expand.5.refs_17_ = bf16[768,4096]{1,0:T(8,128)(2,1)S(1)} custom-call(f32[8,128]{1,0:T(8,128)S(1)} %squeeze.38.table_ref, bf16[768,1024]{1,0:T(8,128)(2,1)S(1)} %bitcast.73, bf16[4,8,8192]{2,1,0:T(8,128)(2,1)S(1)} %pad_maximum_fusion.refs_0_.rest_0_, bf16[2,8,8192]{2,1,0:T(8,128)(2,1)S(1)} %collective-permute-done.7.refs_5_.rest_1_), custom_call_target="tpu_custom_call" | custom-call | flops 6291456000 | bytes 7864320 | tf_op jit(solution)/shard_map/expand/pallas_call | solution.py:144
  108.1 2.7 %copy-done.2 = bf16[768,4096]{1,0:T(8,128)(2,1)} copy-done((bf16[768,4096]{1,0:T(8,128)(2,1)}, bf16[768,4096]{1,0:T(8,128)(2,1)S(1)}, u32[]{:S(2)}) %copy-start.2) | copy-done | bytes 6291480
  110.9 10.6 %experts.1 = (bf16[8,8,4096]{2,1,0:T(8,128)(2,1)S(1)}, bf16[8,8,4096]{2,1,0:T(8,128)(2,1)S(1)}, bf16[8,8,4096]{2,1,0:T(8,128)(2,1)S(1)}, bf16[8,8,4096]{2,1,0:T(...) custom-call(s32[1]{0:T(128)} %bitcast.me_ref, ...), custom_call_target="tpu_custom_call" | custom-call | flops 4831838208 | bytes 18874368 | tf_op jit(solution)/shard_map/experts/pallas_call | solution.py:323
  121.6 0.6 collective-permute-start.28
  122.1 0.1 collective-permute-start.32
  122.2 1.5 collective-permute-done.28
  123.7 0.1 add_convert_fusion.3
  123.8 0.6 collective-permute-start.29
  124.4 0.1 add_convert_fusion.1
  124.6 0.6 collective-permute-start.33
  125.2 7.3 %collective-permute-done.29 = bf16[4,8,4096]{2,1,0:T(8,128)(2,1)S(1)} collective-permute-done((bf16[4,8,4096]{2,1,0:T(8,128)(2,1)S(1)}, bf16[4,8,4096]{2,1,0:T(8,128)(2,1)S(1)}, u32[]{:S(2)}, u32[]{:S(2)}) %collective-permute-start.29) | collective-permute-done | bytes 262176 | tf_op jit(solution)/shard_map/ppermute | solution.py:362
  132.5 0.4 collective-permute-start.30
  132.9 0.3 collective-permute-done.33
  133.3 2.3 %collective-permute-start.34 = (bf16[2,8,4096]{2,1,0:T(8,128)(2,1)S(1)}, bf16[2,8,4096]{2,1,0:T(8,128)(2,1)S(1)}, u32[]{:S(2)}, u32[]{:S(2)}) collective-permute-start(bf16[2,8,4096]{2,1,0:T(8,128)(2,1)S(1)} %get-tuple-element.28), channel_id=1, source_target_pairs={{0,8},{1,9},{2,10},{3,11},{4,12},{5,13},{6,14},{7,15},{8,0},{9,1},... | collective-permute-start | bytes 393224 | tf_op jit(solution)/shard_map/ppermute | solution.py:362
  135.6 3.8 %collective-permute-done.30 = bf16[2,8,4096]{2,1,0:T(8,128)(2,1)S(1)} collective-permute-done((bf16[2,8,4096]{2,1,0:T(8,128)(2,1)S(1)}, bf16[2,8,4096]{2,1,0:T(8,128)(2,1)S(1)}, u32[]{:S(2)}, u32[]{:S(2)}) %collective-permute-start.30) | collective-permute-done | bytes 131104 | tf_op jit(solution)/shard_map/ppermute | solution.py:362
  139.4 0.5 collective-permute-start.31
  139.9 4.2 %collective-permute-done.34 = bf16[2,8,4096]{2,1,0:T(8,128)(2,1)S(1)} collective-permute-done((bf16[2,8,4096]{2,1,0:T(8,128)(2,1)S(1)}, bf16[2,8,4096]{2,1,0:T(8,128)(2,1)S(1)}, u32[]{:S(2)}, u32[]{:S(2)}) %collective-permute-start.34) | collective-permute-done | bytes 131104 | tf_op jit(solution)/shard_map/ppermute | solution.py:362
  144.1 1.0 collective-permute-start.35
  145.1 3.3 %collective-permute-done.35 = bf16[1,8,4096]{2,1,0:T(8,128)(2,1)S(1)} collective-permute-done((bf16[1,8,4096]{2,1,0:T(8,128)(2,1)S(1)}, bf16[1,8,4096]{2,1,0:T(8,128)(2,1)S(1)}, u32[]{:S(2)}, u32[]{:S(2)}) %collective-permute-start.35) | collective-permute-done | bytes 65568 | tf_op jit(solution)/shard_map/ppermute | solution.py:362
  148.5 0.7 pad_maximum_fusion.5
  (81 shorter events, 0.8 us)
Async XLA Ops:
  0.0 2.2 %copy-start = (bf16[2,8,128,2,512]{4,3,2,1,0:T(2,128)(2,1)S(1)}, bf16[2,8,128,2,512]{4,3,2,1,0:T(2,128)(2,1)}, u32[]{:S(2)}) copy-start(bf16[2,8,128,2,512]{4,3,2,1,0:T(2,128)(2,1)} %kv_ref.3) | copy-start | bytes 12582916
  2.2 0.9 copy-start.4
  3.1 0.7 copy-start.9
  3.8 13.0 %copy-start.14 = (s32[2,8,8]{2,1,0:T(8,128)S(1)}, s32[2,8,8]{2,1,0:T(8,128)}, u32[]{:S(2)}) copy-start(s32[2,8,8]{2,1,0:T(8,128)} %param.18) | copy-start | bytes 1540
  3.8 13.2 %copy-start.13 = (bf16[2,8,4096]{2,1,0:T(8,128)(2,1)S(1)}, bf16[2,8,4096]{2,1,0:T(8,128)(2,1)}, u32[]{:S(2)}) copy-start(bf16[2,8,4096]{2,1,0:T(8,128)(2,1)} %param.14) | copy-start | bytes 393220
  6.7 28.0 %copy-start.15 = (bf16[1,3,256,4]{2,3,1,0:T(4,128)(2,1)S(1)}, bf16[1,3,256,4]{2,3,1,0:T(4,128)(2,1)}, u32[]{:S(2)}) copy-start(bf16[1,3,256,4]{2,3,1,0:T(4,128)(2,1)} %param.25) | copy-start | bytes 18436
  6.7 10.4 %collective-permute-start = (bf16[8,8192]{1,0:T(8,128)(2,1)S(1)}, bf16[8,8192]{1,0:T(8,128)(2,1)S(1)}, u32[]{:S(2)}, u32[]{:S(2)}) collective-permute-start(bf16[8,8192]{1,0:T(8,128)(2,1)S(1)} %attend.2), channel_id=1, source_target_pairs={{0,8},{1,9},{2,10},{3,11},{4,12},{5,13},{6,14},{7,15},{8,0},{9,1},... | collective-permute-start | bytes 393224 | tf_op jit(solution)/shard_map/ppermute | solution.py:362
  13.7 5.0 %collective-permute-start.6 = (bf16[8,8192]{1,0:T(8,128)(2,1)S(1)}, bf16[8,8192]{1,0:T(8,128)(2,1)S(1)}, u32[]{:S(2)}, u32[]{:S(2)}) collective-permute-start(bf16[8,8192]{1,0:T(8,128)(2,1)S(1)} %attend.3), channel_id=1, source_target_pairs={{0,2},{1,3},{2,0},{3,1},{4,6},{5,7},{6,4},{7,5},{8,10},{9,11},{10,... | collective-permute-start | bytes 393224 | tf_op jit(solution)/shard_map/ppermute | solution.py:362
  15.3 6.2 %collective-permute-start.1 = (bf16[8,8192]{1,0:T(8,128)(2,1)S(1)}, bf16[8,8192]{1,0:T(8,128)(2,1)S(1)}, u32[]{:S(2)}, u32[]{:S(2)}) collective-permute-start(bf16[8,8192]{1,0:T(8,128)(2,1)S(1)} %attend.2), channel_id=1, source_target_pairs={{0,4},{1,5},{2,6},{3,7},{4,0},{5,1},{6,2},{7,3},{8,12},{9,13},{10,... | collective-permute-start | bytes 393224 | tf_op jit(solution)/shard_map/ppermute | solution.py:362
  17.1 8.4 %collective-permute-start.2 = (bf16[8,8192]{1,0:T(8,128)(2,1)S(1)}, bf16[8,8192]{1,0:T(8,128)(2,1)S(1)}, u32[]{:S(2)}, u32[]{:S(2)}) collective-permute-start(bf16[8,8192]{1,0:T(8,128)(2,1)S(1)} %collective-permute-done.rest_0_), channel_id=1, source_target_pairs={{0,4},{1,5},{2,6},{3,7},{4,0},{5,1},{6,2},{7,3},{8,12},{9,13},{10,... | collective-permute-start | bytes 393224 | tf_op jit(solution)/shard_map/ppermute | solution.py:362
  18.8 15.6 %collective-permute-start.7 = (bf16[2,8,8192]{2,1,0:T(8,128)(2,1)S(1)}, bf16[2,8,8192]{2,1,0:T(8,128)(2,1)S(1)}, u32[]{:S(2)}, u32[]{:S(2)}) collective-permute-start(bf16[2,8,8192]{2,1,0:T(8,128)(2,1)S(1)} %pad_maximum_fusion.1.refs_4_.rest_1_), channel_id=1, source_target_pairs={{0,8},{1,9},{2,10},{3,11},{4,12},{5,13},{6,14},{7,15},{8,0},{9,1},... | collective-permute-start | bytes 786440 | tf_op jit(solution)/shard_map/ppermute | solution.py:362
  25.6 24.1 %collective-permute-start.3 = (bf16[4,8,8192]{2,1,0:T(8,128)(2,1)S(1)}, bf16[4,8,8192]{2,1,0:T(8,128)(2,1)S(1)}, u32[]{:S(2)}, u32[]{:S(2)}) collective-permute-start(bf16[4,8,8192]{2,1,0:T(8,128)(2,1)S(1)} %pad_maximum_fusion.refs_0_.rest_0_), channel_id=1, source_target_pairs={{0,2},{1,3},{2,0},{3,1},{4,6},{5,7},{6,4},{7,5},{8,10},{9,11},{10,... | collective-permute-start | bytes 1572872 | tf_op jit(solution)/shard_map/ppermute | solution.py:362
  27.7 34.7 %all-to-all-start = ((bf16[16,2,8,272]{3,2,1,0:T(8,128)(2,1)}), bf16[16,2,8,272]{3,2,1,0:T(8,128)(2,1)}, u32[]{:S(2)}, u32[]{:S(2)}) async-start(bf16[16,2,8,272]{3,2,1,0:T(8,128)(2,1)} %pad_maximum_fusion.3), calls=%async_computation | async-start | bytes 393216 | tf_op jit(solution)/shard_map/all_to_all | solution.py:435
  32.2 2.5 %collective-permute-start.10 = (bf16[2,8,8192]{2,1,0:T(8,128)(2,1)S(1)}, bf16[2,8,8192]{2,1,0:T(8,128)(2,1)S(1)}, u32[]{:S(2)}, u32[]{:S(2)}) collective-permute-start(bf16[2,8,8192]{2,1,0:T(8,128)(2,1)S(1)} %pad_maximum_fusion.1.refs_4_.rest_1_), channel_id=1, source_target_pairs={{0,1},{1,0},{2,3},{3,2},{4,5},{5,4},{6,7},{7,6},{8,9},{9,8},{10,11... | collective-permute-start | bytes 786440 | tf_op jit(solution)/shard_map/ppermute | solution.py:362
  32.6 11.9 %collective-permute-start.8 = (bf16[2,8,8192]{2,1,0:T(8,128)(2,1)S(1)}, bf16[2,8,8192]{2,1,0:T(8,128)(2,1)S(1)}, u32[]{:S(2)}, u32[]{:S(2)}) collective-permute-start(bf16[2,8,8192]{2,1,0:T(8,128)(2,1)S(1)} %pad_maximum_fusion.1.refs_4_.rest_1_), channel_id=1, source_target_pairs={{0,4},{1,5},{2,6},{3,7},{4,0},{5,1},{6,2},{7,3},{8,12},{9,13},{10,... | collective-permute-start | bytes 786440 | tf_op jit(solution)/shard_map/ppermute | solution.py:362
  34.3 15.4 %collective-permute-start.9 = (bf16[2,8,8192]{2,1,0:T(8,128)(2,1)S(1)}, bf16[2,8,8192]{2,1,0:T(8,128)(2,1)S(1)}, u32[]{:S(2)}, u32[]{:S(2)}) collective-permute-start(bf16[2,8,8192]{2,1,0:T(8,128)(2,1)S(1)} %collective-permute-done.7.refs_5_.rest_1_), channel_id=1, source_target_pairs={{0,4},{1,5},{2,6},{3,7},{4,0},{5,1},{6,2},{7,3},{8,12},{9,13},{10,... | collective-permute-start | bytes 786440 | tf_op jit(solution)/shard_map/ppermute | solution.py:362
  34.7 28.6 %collective-permute-start.4 = (bf16[4,8,8192]{2,1,0:T(8,128)(2,1)S(1)}, bf16[4,8,8192]{2,1,0:T(8,128)(2,1)S(1)}, u32[]{:S(2)}, u32[]{:S(2)}) collective-permute-start(bf16[4,8,8192]{2,1,0:T(8,128)(2,1)S(1)} %pad_maximum_fusion.refs_0_.rest_0_), channel_id=1, source_target_pairs={{0,1},{1,0},{2,3},{3,2},{4,5},{5,4},{6,7},{7,6},{8,9},{9,8},{10,11... | collective-permute-start | bytes 1572872 | tf_op jit(solution)/shard_map/ppermute | solution.py:362
  34.8 28.5 %collective-permute-start.11 = (bf16[2,8,8192]{2,1,0:T(8,128)(2,1)S(1)}, bf16[2,8,8192]{2,1,0:T(8,128)(2,1)}, u32[]{:S(2)}, u32[]{:S(2)}) collective-permute-start(bf16[2,8,8192]{2,1,0:T(8,128)(2,1)S(1)} %collective-permute-done.7.refs_5_.rest_1_), channel_id=1, source_target_pairs={{0,1},{1,0},{2,3},{3,2},{4,5},{5,4},{6,7},{7,6},{8,9},{9,8},{10,11... | collective-permute-start | bytes 786440 | tf_op jit(solution)/shard_map/ppermute | solution.py:362
  44.6 18.7 %collective-permute-start.12 = (bf16[2,8,8192]{2,1,0:T(8,128)(2,1)S(1)}, bf16[2,8,8192]{2,1,0:T(8,128)(2,1)}, u32[]{:S(2)}, u32[]{:S(2)}) collective-permute-start(bf16[2,8,8192]{2,1,0:T(8,128)(2,1)S(1)} %collective-permute-done.8.refs_6_), channel_id=1, source_target_pairs={{0,1},{1,0},{2,3},{3,2},{4,5},{5,4},{6,7},{7,6},{8,9},{9,8},{10,11... | collective-permute-start | bytes 786440 | tf_op jit(solution)/shard_map/ppermute | solution.py:362
  49.7 13.6 %collective-permute-start.13 = (bf16[2,8,8192]{2,1,0:T(8,128)(2,1)S(1)}, bf16[2,8,8192]{2,1,0:T(8,128)(2,1)}, u32[]{:S(2)}, u32[]{:S(2)}) collective-permute-start(bf16[2,8,8192]{2,1,0:T(8,128)(2,1)S(1)} %collective-permute-done.9.refs_7_), channel_id=1, source_target_pairs={{0,1},{1,0},{2,3},{3,2},{4,5},{5,4},{6,7},{7,6},{8,9},{9,8},{10,11... | collective-permute-start | bytes 786440 | tf_op jit(solution)/shard_map/ppermute | solution.py:362
  49.7 13.6 %collective-permute-start.5 = (bf16[4,8,8192]{2,1,0:T(8,128)(2,1)S(1)}, bf16[4,8,8192]{2,1,0:T(8,128)(2,1)S(1)}, u32[]{:S(2)}, u32[]{:S(2)}) collective-permute-start(bf16[4,8,8192]{2,1,0:T(8,128)(2,1)S(1)} %collective-permute-done.3.refs_1_), channel_id=1, source_target_pairs={{0,1},{1,0},{2,3},{3,2},{4,5},{5,4},{6,7},{7,6},{8,9},{9,8},{10,11... | collective-permute-start | bytes 1572872 | tf_op jit(solution)/shard_map/ppermute | solution.py:362
  50.2 1.4 copy-start.10
  59.7 2.7 %copy-start.1 = (bf16[4,192,4096]{2,1,0:T(8,128)(2,1)}, bf16[4,192,4096]{2,1,0:T(8,128)(2,1)S(1)}, u32[]{:S(2)}) copy-start(bf16[4,192,4096]{2,1,0:T(8,128)(2,1)S(1)} %expand.3) | copy-start | bytes 18874372
  63.3 2.2 %copy-start.3 = (bf16[8192,256]{1,0:T(8,128)(2,1)S(1)}, bf16[8192,256]{1,0:T(8,128)(2,1)}, u32[]{:S(2)}) copy-start(bf16[8192,256]{1,0:T(8,128)(2,1)} %refs_12_.1) | copy-start | bytes 12582916
  65.5 5.3 %copy-start.11 = (bf16[1,4096,192]{1,2,0:T(8,128)(2,1)S(1)}, bf16[1,4096,192]{1,2,0:T(8,128)(2,1)}, u32[]{:S(2)}) copy-start(bf16[1,4096,192]{1,2,0:T(8,128)(2,1)} %param.23) | copy-start | bytes 4718596
  69.2 12.6 %collective-permute-start.20 = (bf16[16,8,256]{2,1,0:T(8,128)(2,1)S(1)}, bf16[16,8,256]{2,1,0:T(8,128)(2,1)S(1)}, u32[]{:S(2)}, u32[]{:S(2)}) collective-permute-start(bf16[16,8,256]{2,1,0:T(8,128)(2,1)S(1)} %get-tuple-element.14), channel_id=1, source_target_pairs={{0,2},{1,3},{2,0},{3,1},{4,6},{5,7},{6,4},{7,5},{8,10},{9,11},{10,... | collective-permute-start | bytes 196616 | tf_op jit(solution)/shard_map/ppermute | solution.py:362
  70.7 29.8 %copy-start.12 = (bf16[1,768,1024]{2,1,0:T(8,128)(2,1)S(1)}, bf16[1,768,1024]{2,1,0:T(8,128)(2,1)}, u32[]{:S(2)}) copy-start(bf16[1,768,1024]{2,1,0:T(8,128)(2,1)} %param.24) | copy-start | bytes 4718596
  78.8 13.2 %collective-permute-start.15 = (bf16[16,8,256]{2,1,0:T(8,128)(2,1)S(1)}, bf16[16,8,256]{2,1,0:T(8,128)(2,1)S(1)}, u32[]{:S(2)}, u32[]{:S(2)}) collective-permute-start(bf16[16,8,256]{2,1,0:T(8,128)(2,1)S(1)} %get-tuple-element.13), channel_id=1, source_target_pairs={{0,4},{1,5},{2,6},{3,7},{4,0},{5,1},{6,2},{7,3},{8,12},{9,13},{10,... | collective-permute-start | bytes 196616 | tf_op jit(solution)/shard_map/ppermute | solution.py:362
  79.4 9.7 %collective-permute-start.14 = (bf16[16,8,256]{2,1,0:T(8,128)(2,1)S(1)}, bf16[16,8,256]{2,1,0:T(8,128)(2,1)S(1)}, u32[]{:S(2)}, u32[]{:S(2)}) collective-permute-start(bf16[16,8,256]{2,1,0:T(8,128)(2,1)S(1)} %get-tuple-element.13), channel_id=1, source_target_pairs={{0,8},{1,9},{2,10},{3,11},{4,12},{5,13},{6,14},{7,15},{8,0},{9,1},... | collective-permute-start | bytes 196616 | tf_op jit(solution)/shard_map/ppermute | solution.py:362
  81.8 12.4 %collective-permute-start.21 = (bf16[2,16,8,256]{3,2,1,0:T(8,128)(2,1)S(1)}, bf16[2,16,8,256]{3,2,1,0:T(8,128)(2,1)S(1)}, u32[]{:S(2)}, u32[]{:S(2)}) collective-permute-start(bf16[2,16,8,256]{3,2,1,0:T(8,128)(2,1)S(1)} %pad_maximum_fusion.4.refs_4_), channel_id=1, source_target_pairs={{0,8},{1,9},{2,10},{3,11},{4,12},{5,13},{6,14},{7,15},{8,0},{9,1},... | collective-permute-start | bytes 393224 | tf_op jit(solution)/shard_map/ppermute | solution.py:362
  89.1 4.3 %collective-permute-start.16 = (bf16[16,8,256]{2,1,0:T(8,128)(2,1)S(1)}, bf16[16,8,256]{2,1,0:T(8,128)(2,1)S(1)}, u32[]{:S(2)}, u32[]{:S(2)}) collective-permute-start(bf16[16,8,256]{2,1,0:T(8,128)(2,1)S(1)} %collective-permute-done.14), channel_id=1, source_target_pairs={{0,4},{1,5},{2,6},{3,7},{4,0},{5,1},{6,2},{7,3},{8,12},{9,13},{10,... | collective-permute-start | bytes 196616 | tf_op jit(solution)/shard_map/ppermute | solution.py:362
  90.0 4.3 %collective-permute-start.24 = (bf16[2,16,8,256]{3,2,1,0:T(8,128)(2,1)S(1)}, bf16[2,16,8,256]{3,2,1,0:T(8,128)(2,1)S(1)}, u32[]{:S(2)}, u32[]{:S(2)}) collective-permute-start(bf16[2,16,8,256]{3,2,1,0:T(8,128)(2,1)S(1)} %pad_maximum_fusion.4.refs_4_), channel_id=1, source_target_pairs={{0,1},{1,0},{2,3},{3,2},{4,5},{5,4},{6,7},{7,6},{8,9},{9,8},{10,11... | collective-permute-start | bytes 393224 | tf_op jit(solution)/shard_map/ppermute | solution.py:362
  90.0 6.4 %collective-permute-start.22 = (bf16[2,16,8,256]{3,2,1,0:T(8,128)(2,1)S(1)}, bf16[2,16,8,256]{3,2,1,0:T(8,128)(2,1)S(1)}, u32[]{:S(2)}, u32[]{:S(2)}) collective-permute-start(bf16[2,16,8,256]{3,2,1,0:T(8,128)(2,1)S(1)} %pad_maximum_fusion.4.refs_4_), channel_id=1, source_target_pairs={{0,4},{1,5},{2,6},{3,7},{4,0},{5,1},{6,2},{7,3},{8,12},{9,13},{10,... | collective-permute-start | bytes 393224 | tf_op jit(solution)/shard_map/ppermute | solution.py:362
  93.5 17.4 %slice-start = ((s8[6291456]{0:T(1024)(128)(4,1)}), s8[4194304]{0:T(1024)(128)(4,1)S(1)}, s32[]{:S(2)}) async-start(s8[6291456]{0:T(1024)(128)(4,1)} %bitcast.59), calls=%async_computation.1 | async-start | bytes 8388608
  93.5 7.0 %collective-permute-start.17 = (bf16[4,16,8,256]{3,2,1,0:T(8,128)(2,1)S(1)}, bf16[4,16,8,256]{3,2,1,0:T(8,128)(2,1)S(1)}, u32[]{:S(2)}, u32[]{:S(2)}) collective-permute-start(bf16[4,16,8,256]{3,2,1,0:T(8,128)(2,1)S(1)} %pad_maximum_fusion.2.refs_0_), channel_id=1, source_target_pairs={{0,2},{1,3},{2,0},{3,1},{4,6},{5,7},{6,4},{7,5},{8,10},{9,11},{10,... | collective-permute-start | bytes 786440 | tf_op jit(solution)/shard_map/ppermute | solution.py:362
  94.2 5.0 %collective-permute-start.23 = (bf16[2,16,8,256]{3,2,1,0:T(8,128)(2,1)S(1)}, bf16[2,16,8,256]{3,2,1,0:T(8,128)(2,1)S(1)}, u32[]{:S(2)}, u32[]{:S(2)}) collective-permute-start(bf16[2,16,8,256]{3,2,1,0:T(8,128)(2,1)S(1)} %collective-permute-done.21.refs_5_), channel_id=1, source_target_pairs={{0,4},{1,5},{2,6},{3,7},{4,0},{5,1},{6,2},{7,3},{8,12},{9,13},{10,... | collective-permute-start | bytes 393224 | tf_op jit(solution)/shard_map/ppermute | solution.py:362
  94.2 16.6 %collective-permute-start.18 = (bf16[4,16,8,256]{3,2,1,0:T(8,128)(2,1)S(1)}, bf16[4,16,8,256]{3,2,1,0:T(8,128)(2,1)S(1)}, u32[]{:S(2)}, u32[]{:S(2)}) collective-permute-start(bf16[4,16,8,256]{3,2,1,0:T(8,128)(2,1)S(1)} %pad_maximum_fusion.2.refs_0_), channel_id=1, source_target_pairs={{0,1},{1,0},{2,3},{3,2},{4,5},{5,4},{6,7},{7,6},{8,9},{9,8},{10,11... | collective-permute-start | bytes 786440 | tf_op jit(solution)/shard_map/ppermute | solution.py:362
  94.3 16.6 %collective-permute-start.25 = (bf16[2,16,8,256]{3,2,1,0:T(8,128)(2,1)S(1)}, bf16[2,16,8,256]{3,2,1,0:T(8,128)(2,1)S(1)}, u32[]{:S(2)}, u32[]{:S(2)}) collective-permute-start(bf16[2,16,8,256]{3,2,1,0:T(8,128)(2,1)S(1)} %collective-permute-done.21.refs_5_), channel_id=1, source_target_pairs={{0,1},{1,0},{2,3},{3,2},{4,5},{5,4},{6,7},{7,6},{8,9},{9,8},{10,11... | collective-permute-start | bytes 393224 | tf_op jit(solution)/shard_map/ppermute | solution.py:362
  96.4 14.5 %collective-permute-start.26 = (bf16[2,16,8,256]{3,2,1,0:T(8,128)(2,1)S(1)}, bf16[2,16,8,256]{3,2,1,0:T(8,128)(2,1)S(1)}, u32[]{:S(2)}, u32[]{:S(2)}) collective-permute-start(bf16[2,16,8,256]{3,2,1,0:T(8,128)(2,1)S(1)} %collective-permute-done.22.refs_6_), channel_id=1, source_target_pairs={{0,1},{1,0},{2,3},{3,2},{4,5},{5,4},{6,7},{7,6},{8,9},{9,8},{10,11... | collective-permute-start | bytes 393224 | tf_op jit(solution)/shard_map/ppermute | solution.py:362
  99.1 11.7 %collective-permute-start.27 = (bf16[2,16,8,256]{3,2,1,0:T(8,128)(2,1)S(1)}, bf16[2,16,8,256]{3,2,1,0:T(8,128)(2,1)S(1)}, u32[]{:S(2)}, u32[]{:S(2)}) collective-permute-start(bf16[2,16,8,256]{3,2,1,0:T(8,128)(2,1)S(1)} %collective-permute-done.23.refs_7_), channel_id=1, source_target_pairs={{0,1},{1,0},{2,3},{3,2},{4,5},{5,4},{6,7},{7,6},{8,9},{9,8},{10,11... | collective-permute-start | bytes 393224 | tf_op jit(solution)/shard_map/ppermute | solution.py:362
  100.6 10.3 %collective-permute-start.19 = (bf16[4,16,8,256]{3,2,1,0:T(8,128)(2,1)S(1)}, bf16[4,16,8,256]{3,2,1,0:T(8,128)(2,1)S(1)}, u32[]{:S(2)}, u32[]{:S(2)}) collective-permute-start(bf16[4,16,8,256]{3,2,1,0:T(8,128)(2,1)S(1)} %collective-permute-done.17.refs_1_), channel_id=1, source_target_pairs={{0,1},{1,0},{2,3},{3,2},{4,5},{5,4},{6,7},{7,6},{8,9},{9,8},{10,11... | collective-permute-start | bytes 786440 | tf_op jit(solution)/shard_map/ppermute | solution.py:362
  100.6 10.3 %slice-start.1 = ((s8[6291456]{0:T(1024)(128)(4,1)}), s8[2097152]{0:T(1024)(128)(4,1)S(1)}, s32[]{:S(2)}) async-start(s8[6291456]{0:T(1024)(128)(4,1)} %bitcast.59), calls=%async_computation.2 | async-start | bytes 4194304
  100.6 10.3 %copy-start.5 = (bf16[4096,16]{0,1:T(8,128)(2,1)S(1)}, bf16[4096,16]{0,1:T(8,128)(2,1)}, u32[]{:S(2)}) copy-start(bf16[4096,16]{0,1:T(8,128)(2,1)} %param.21) | copy-start | bytes 393220
  100.6 10.3 %copy-start.6 = (f32[4096]{0:T(1024)S(1)}, f32[4096]{0:T(1024)}, u32[]{:S(2)}) copy-start(f32[4096]{0:T(1024)} %param.20) | copy-start | bytes 49156
  100.6 10.3 %copy-start.7 = (f32[1,4096]{1,0:T(1,128)S(1)}, f32[1,4096]{1,0:T(1,128)}, u32[]{:S(2)}) copy-start(f32[1,4096]{1,0:T(1,128)} %refs_19_.1) | copy-start | bytes 49156
  100.6 10.3 %copy-start.8 = (f32[1,2,768]{2,1,0:T(2,128)S(1)}, f32[1,2,768]{2,1,0:T(2,128)}, u32[]{:S(2)}) copy-start(f32[1,2,768]{2,1,0:T(2,128)} %param.26) | copy-start | bytes 18436
  108.1 2.7 %copy-start.2 = (bf16[768,4096]{1,0:T(8,128)(2,1)}, bf16[768,4096]{1,0:T(8,128)(2,1)S(1)}, u32[]{:S(2)}) copy-start(bf16[768,4096]{1,0:T(8,128)(2,1)S(1)} %expand.5.refs_17_) | copy-start | bytes 18874372
  121.6 2.1 %collective-permute-start.28 = (bf16[8,8,4096]{2,1,0:T(8,128)(2,1)S(1)}, bf16[8,8,4096]{2,1,0:T(8,128)(2,1)S(1)}, u32[]{:S(2)}, u32[]{:S(2)}) collective-permute-start(bf16[8,8,4096]{2,1,0:T(8,128)(2,1)S(1)} %get-tuple-element.17), channel_id=1, source_target_pairs={{0,1},{1,0},{2,3},{3,2},{4,5},{5,4},{6,7},{7,6},{8,9},{9,8},{10,11... | collective-permute-start | bytes 1572872 | tf_op jit(solution)/shard_map/ppermute | solution.py:362
  122.1 2.3 %collective-permute-start.32 = (bf16[8,8,4096]{2,1,0:T(8,128)(2,1)S(1)}, bf16[8,8,4096]{2,1,0:T(8,128)(2,1)S(1)}, u32[]{:S(2)}, u32[]{:S(2)}) collective-permute-start(bf16[8,8,4096]{2,1,0:T(8,128)(2,1)S(1)} %get-tuple-element.20), channel_id=1, source_target_pairs={{0,1},{1,0},{2,3},{3,2},{4,5},{5,4},{6,7},{7,6},{8,9},{9,8},{10,11... | collective-permute-start | bytes 1572872 | tf_op jit(solution)/shard_map/ppermute | solution.py:362
  123.8 8.7 %collective-permute-start.29 = (bf16[4,8,4096]{2,1,0:T(8,128)(2,1)S(1)}, bf16[4,8,4096]{2,1,0:T(8,128)(2,1)S(1)}, u32[]{:S(2)}, u32[]{:S(2)}) collective-permute-start(bf16[4,8,4096]{2,1,0:T(8,128)(2,1)S(1)} %get-tuple-element.22), channel_id=1, source_target_pairs={{0,2},{1,3},{2,0},{3,1},{4,6},{5,7},{6,4},{7,5},{8,10},{9,11},{10,... | collective-permute-start | bytes 786440 | tf_op jit(solution)/shard_map/ppermute | solution.py:362
  124.6 8.6 %collective-permute-start.33 = (bf16[4,8,4096]{2,1,0:T(8,128)(2,1)S(1)}, bf16[4,8,4096]{2,1,0:T(8,128)(2,1)S(1)}, u32[]{:S(2)}, u32[]{:S(2)}) collective-permute-start(bf16[4,8,4096]{2,1,0:T(8,128)(2,1)S(1)} %get-tuple-element.24), channel_id=1, source_target_pairs={{0,4},{1,5},{2,6},{3,7},{4,0},{5,1},{6,2},{7,3},{8,12},{9,13},{10,... | collective-permute-start | bytes 786440 | tf_op jit(solution)/shard_map/ppermute | solution.py:362
  132.5 6.9 %collective-permute-start.30 = (bf16[2,8,4096]{2,1,0:T(8,128)(2,1)S(1)}, bf16[2,8,4096]{2,1,0:T(8,128)(2,1)S(1)}, u32[]{:S(2)}, u32[]{:S(2)}) collective-permute-start(bf16[2,8,4096]{2,1,0:T(8,128)(2,1)S(1)} %get-tuple-element.26), channel_id=1, source_target_pairs={{0,4},{1,5},{2,6},{3,7},{4,0},{5,1},{6,2},{7,3},{8,12},{9,13},{10,... | collective-permute-start | bytes 393224 | tf_op jit(solution)/shard_map/ppermute | solution.py:362
  133.3 10.8 %collective-permute-start.34 = (bf16[2,8,4096]{2,1,0:T(8,128)(2,1)S(1)}, bf16[2,8,4096]{2,1,0:T(8,128)(2,1)S(1)}, u32[]{:S(2)}, u32[]{:S(2)}) collective-permute-start(bf16[2,8,4096]{2,1,0:T(8,128)(2,1)S(1)} %get-tuple-element.28), channel_id=1, source_target_pairs={{0,8},{1,9},{2,10},{3,11},{4,12},{5,13},{6,14},{7,15},{8,0},{9,1},... | collective-permute-start | bytes 393224 | tf_op jit(solution)/shard_map/ppermute | solution.py:362
  139.4 5.6 %collective-permute-start.31 = (bf16[1,8,4096]{2,1,0:T(8,128)(2,1)S(1)}, bf16[1,8,4096]{2,1,0:T(8,128)(2,1)S(1)}, u32[]{:S(2)}, u32[]{:S(2)}) collective-permute-start(bf16[1,8,4096]{2,1,0:T(8,128)(2,1)S(1)} %add_convert_fusion.10), channel_id=1, source_target_pairs={{0,8},{1,9},{2,10},{3,11},{4,12},{5,13},{6,14},{7,15},{8,0},{9,1},... | collective-permute-start | bytes 196616 | tf_op jit(solution)/shard_map/ppermute | solution.py:362
  144.1 4.3 %collective-permute-start.35 = (bf16[1,8,4096]{2,1,0:T(8,128)(2,1)S(1)}, bf16[1,8,4096]{2,1,0:T(8,128)(2,1)S(1)}, u32[]{:S(2)}, u32[]{:S(2)}) collective-permute-start(bf16[1,8,4096]{2,1,0:T(8,128)(2,1)S(1)} %add_convert_fusion.8), channel_id=1, source_target_pairs={{0,2},{1,3},{2,0},{3,1},{4,6},{5,7},{6,4},{7,5},{8,10},{9,11},{10,... | collective-permute-start | bytes 196616 | tf_op jit(solution)/shard_map/ppermute | solution.py:362

commit v3 on v2

--- a/solution.py
+++ b/solution.py
@@ -90,7 +90,7 @@
         cost_estimate=pl.CostEstimate(
             flops=rows * width * 4 * 256, bytes_accessed=rows << 18, transcendentals=0
         ),
-    )(lengths, queries, kv_cache)
+    )(lengths, queries, pltpu.with_memory_space_constraint(kv_cache, pltpu.HBM))
 
 
 def expand_kernel(stacked, table_ref, code_ref, *rest):
@@ -153,7 +153,7 @@
         cost_estimate=pl.CostEstimate(
             flops=rows * columns * 8000, bytes_accessed=10 * rows * columns, transcendentals=0
         ),
-    )(table, codes, *after)
+    )(table, pltpu.with_memory_space_constraint(codes, pltpu.HBM), *after)
     return out.reshape(4 * rows, columns) if stacked else out
 
 
@@ -220,7 +220,7 @@
             bytes_accessed=2 * depth * columns,
             transcendentals=0,
         ),
-    )(me, *pieces, out_weight, hidden_columns)
+    )(me, *pieces, pltpu.with_memory_space_constraint(out_weight, pltpu.HBM), hidden_columns)
 
 
 def experts_kernel(masks, counts, orders, me_ref, *refs):
@@ -233,79 +233,75 @@
         refs[8 + i * groups : 8 + (i + 1) * groups] for i in range(3)
     )
     token_scr, weight_scr, acc_ref = refs[-3:]
-    step = pl.program_id(0)
     _, shards, rows, columns = pieces[0].shape
     total, width = token_scr.shape
     part = shards * rows
+    hidden_units = gate_ref.shape[0]
     me = me_ref[0]
-
-    @pl.when(step == 0)
-    def _():
-        for m in range(groups):
-            mine = [
-                (ref, i, mask)
-                for ref, mask_list, n in zip(pieces, masks, counts)
-                if n == m
-                for i, mask in enumerate(mask_list)
-            ]
-            squares = jnp.zeros((part, columns), jnp.float32)
-            for ref, i, _ in mine:
-                value = ref[i].reshape(part, columns).astype(jnp.float32)
-                squares += value * value
-            mean = jnp.sum(squares, axis=-1, keepdims=True) / width
-            inverse = lax.rsqrt(mean + 1e-06)
-            for ref, i, mask in mine:
-                at = pl.ds(0, columns)
-                if len(mine) > 1:
-                    at = pl.ds(pl.multiple_of((me ^ mask) * columns, columns), columns)
-                value = ref[i].reshape(part, columns).astype(jnp.float32)
-                own_refs[m][:, at] = ref[i, me]
-                token_scr[m * part : (m + 1) * part, at] = (
-                    value * inverse * gain_ref[:, at]
-                ).astype(jnp.bfloat16)
-        logits = lax.dot_general(
-            token_scr[...],
-            router_ref[...],
-            (((1,), (1,)), ((), ())),
-            preferred_element_type=jnp.float32,
-        )
-        hot = hot_ref[...].astype(jnp.float32) > 0.5
-        logits = jnp.where(hot, logits, -1e30)
-        raised = jnp.where(hot, jnp.exp(logits - jnp.max(logits, axis=-1, keepdims=True)), 0.0)
-        raised = raised / jnp.sum(raised, axis=-1, keepdims=True)
-        mine = lax.broadcasted_iota(jnp.int32, raised.shape, 1) == me
-        weight = jnp.sum(jnp.where(mine, raised, 0.0), axis=-1, keepdims=True)
-        weight = weight.astype(jnp.bfloat16).astype(jnp.float32)
-        weight_scr[...] = jnp.broadcast_to(weight, (total, LANES)).reshape(weight_scr.shape)
-        acc_ref[...] = jnp.zeros_like(acc_ref)
-
     nt = (((1,), (1,)), ((), ()))
-    tokens = token_scr[...]
-    gate = lax.dot_general(tokens, gate_ref[...], nt, preferred_element_type=jnp.float32)
-    up = lax.dot_general(tokens, up_ref[...], nt, preferred_element_type=jnp.float32)
-    gate = gate * gu_scale_ref[0:1, :]
-    up = up * gu_scale_ref[1:2, :]
-    inner = (gate / (1.0 + jnp.exp(-gate)) * up).astype(jnp.bfloat16)
-    piece = 1024
-    for c in range(width // piece):
-        at = slice(c * piece, (c + 1) * piece)
-        product = jnp.dot(inner, down_ref[:, at], preferred_element_type=jnp.float32)
-        acc_ref[:, :, at] += product.reshape(groups * shards, rows, piece)
-
-    @pl.when(step == pl.num_programs(0) - 1)
-    def _():
-        half = shards // 2
-        for m, order in enumerate(orders):
-            for p, mask in enumerate(order):
-                source = m * shards + (me ^ mask)
-                value = (acc_ref[source] * down_scale_ref[...]).astype(jnp.bfloat16)
-                value = (value.astype(jnp.float32) * weight_scr[source][:, 0:1]).astype(
-                    jnp.bfloat16
-                )
-                if p < half:
-                    keep_refs[m][p] = value
-                else:
-                    send_refs[m][p - half] = value
+
+    for m in range(groups):
+        mine = [
+            (ref, i, mask)
+            for ref, mask_list, n in zip(pieces, masks, counts)
+            if n == m
+            for i, mask in enumerate(mask_list)
+        ]
+        squares = jnp.zeros((part, columns), jnp.float32)
+        for ref, i, _ in mine:
+            value = ref[i].reshape(part, columns).astype(jnp.float32)
+            squares += value * value
+        mean = jnp.sum(squares, axis=-1, keepdims=True) / width
+        inverse = lax.rsqrt(mean + 1e-06)
+        for ref, i, mask in mine:
+            at = pl.ds(0, columns)
+            if len(mine) > 1:
+                at = pl.ds(pl.multiple_of((me ^ mask) * columns, columns), columns)
+            value = ref[i].reshape(part, columns).astype(jnp.float32)
+            own_refs[m][:, at] = ref[i, me]
+            token_scr[m * part : (m + 1) * part, at] = (
+                value * inverse * gain_ref[:, at]
+            ).astype(jnp.bfloat16)
+    logits = lax.dot_general(
+        token_scr[...], router_ref[...], nt, preferred_element_type=jnp.float32
+    )
+    hot = hot_ref[...].astype(jnp.float32) > 0.5
+    logits = jnp.where(hot, logits, -1e30)
+    raised = jnp.where(hot, jnp.exp(logits - jnp.max(logits, axis=-1, keepdims=True)), 0.0)
+    raised = raised / jnp.sum(raised, axis=-1, keepdims=True)
+    column = lax.broadcasted_iota(jnp.int32, raised.shape, 1) == me
+    weight = jnp.sum(jnp.where(column, raised, 0.0), axis=-1, keepdims=True)
+    weight = weight.astype(jnp.bfloat16).astype(jnp.float32)
+    weight_scr[...] = jnp.broadcast_to(weight, (total, LANES)).reshape(weight_scr.shape)
+
+    block, piece = 256, 1024
+    for f in range(hidden_units // block):
+        units = slice(f * block, (f + 1) * block)
+        tokens = token_scr[...]
+        gate = lax.dot_general(tokens, gate_ref[units, :], nt, preferred_element_type=jnp.float32)
+        up = lax.dot_general(tokens, up_ref[units, :], nt, preferred_element_type=jnp.float32)
+        gate = gate * gu_scale_ref[0:1, units]
+        up = up * gu_scale_ref[1:2, units]
+        inner = (gate / (1.0 + jnp.exp(-gate)) * up).astype(jnp.bfloat16)
+        for c in range(width // piece):
+            at = slice(c * piece, (c + 1) * piece)
+            product = jnp.dot(inner, down_ref[units, at], preferred_element_type=jnp.float32)
+            product = product.reshape(groups * shards, rows, piece)
+            if f == 0:
+                acc_ref[:, :, at] = product
+            else:
+                acc_ref[:, :, at] += product
+
+    half = shards // 2
+    for m, order in enumerate(orders):
+        for p, mask in enumerate(order):
+            source = m * shards + (me ^ mask)
+            value = (acc_ref[source] * down_scale_ref[...]).astype(jnp.bfloat16)
+            value = (value.astype(jnp.float32) * weight_scr[source][:, 0:1]).astype(jnp.bfloat16)
+            if p < half:
+                keep_refs[m][p] = value
+            else:
+                send_refs[m][p - half] = value
 
 
 def run_experts(me, streams, gain, router, hot, gate, up, down, gu_scale, down_scale, orders):
@@ -316,45 +312,31 @@
     _, shards, rows, _ = pieces[0].shape
     hidden_units, width = gate.shape
     total = groups * shards * rows
-    block = 256
-    full = lambda f, n: (0, 0)
-    half_spec = pl.BlockSpec((shards // 2, rows, width), lambda f, n: (0, 0, 0))
     half_shape = jax.ShapeDtypeStruct((shards // 2, rows, width), jnp.bfloat16)
+    in_vmem = pl.BlockSpec(memory_space=pltpu.VMEM)
+    held = [gate, up, down]
+    if total <= 256:
+        held = [pltpu.with_memory_space_constraint(w, pltpu.VMEM) for w in held]
+        pieces = [pltpu.with_memory_space_constraint(w, pltpu.VMEM) for w in pieces]
     outs = pl.pallas_call(
         functools.partial(experts_kernel, masks, counts, orders),
-        grid_spec=pltpu.PrefetchScalarGridSpec(
-            num_scalar_prefetch=1,
-            grid=(hidden_units // block,),
-            in_specs=[pl.BlockSpec(piece.shape, lambda f, n: (0, 0, 0, 0)) for piece in pieces]
-            + [
-                pl.BlockSpec((1, width), full),
-                pl.BlockSpec(router.shape, full),
-                pl.BlockSpec(hot.shape, full),
-                pl.BlockSpec((block, width), lambda f, n: (f, 0)),
-                pl.BlockSpec((block, width), lambda f, n: (f, 0)),
-                pl.BlockSpec((block, width), lambda f, n: (f, 0)),
-                pl.BlockSpec((2, block), lambda f, n: (0, f)),
-                pl.BlockSpec((1, width), full),
-            ],
-            out_specs=[half_spec] * (2 * groups) + [pl.BlockSpec((rows, width), full)] * groups,
-            scratch_shapes=[
-                pltpu.VMEM((total, width), jnp.bfloat16),
-                pltpu.VMEM((groups * shards, rows, LANES), jnp.float32),
-                pltpu.VMEM((groups * shards, rows, width), jnp.float32),
-            ],
-        ),
+        in_specs=[pl.BlockSpec(memory_space=pltpu.SMEM)] + [in_vmem] * (len(pieces) + 8),
+        out_specs=[in_vmem] * (3 * groups),
         out_shape=[half_shape] * (2 * groups)
         + [jax.ShapeDtypeStruct((rows, width), jnp.bfloat16)] * groups,
+        scratch_shapes=[
+            pltpu.VMEM((total, width), jnp.bfloat16),
+            pltpu.VMEM((groups * shards, rows, LANES), jnp.float32),
+            pltpu.VMEM((groups * shards, rows, width), jnp.float32),
+        ],
         name="experts",
-        compiler_params=pltpu.CompilerParams(
-            vmem_limit_bytes=(36 if total <= 256 else 60) * MIB
-        ),
+        compiler_params=pltpu.CompilerParams(vmem_limit_bytes=(24 if total <= 256 else 62) * MIB),
         cost_estimate=pl.CostEstimate(
             flops=6 * total * width * hidden_units,
             bytes_accessed=6 * width * hidden_units,
             transcendentals=0,
         ),
-    )(me, *pieces, gain, router, hot, gate, up, down, gu_scale, down_scale)
+    )(me, *pieces, gain, router, hot, *held, gu_scale, down_scale)
     return [tuple(outs[i * groups + m] for i in range(3)) for m in range(groups)]
 
 
@@ -362,27 +344,38 @@
     return lax.ppermute(value, "expert", [(i, i ^ bit) for i in range(count)])
 
 
-def gather_all(value, count, near_first):
-    if count != 16:
-        held, masks = value[None], (0,)
-        for bit in [1 << b for b in reversed(range(count.bit_length() - 1))]:
-            held = jnp.concatenate([held, swap(held, bit, count)])
-            masks = masks + tuple(mask ^ bit for mask in masks)
-        return [(held, masks)], []
-    if near_first:
-        first = jnp.stack([value, swap(value, 2, count)])
-        far, near = swap(first, 8, count), swap(first, 4, count)
-        both = swap(far, 4, count)
-        chain = [(first, (0, 2)), (far, (8, 10)), (near, (4, 6)), (both, (12, 14))]
-        marks = [first, far]
-    else:
-        far, near = swap(value, 8, count), swap(value, 4, count)
-        both = swap(far, 4, count)
-        first = jnp.stack([value, far, near, both])
-        chain = [(first, (0, 8, 4, 12)), (swap(first, 2, count), (2, 10, 6, 14))]
-        marks = [far, first]
-    chain += [(swap(held, 1, count), tuple(m ^ 1 for m in masks)) for held, masks in chain]
-    return chain, marks
+def tie(value, *earlier):
+    return lax.optimization_barrier((value,) + earlier)[0]
+
+
+def gather_all(value, count):
+    held, masks = value[None], (0,)
+    for bit in [1 << b for b in reversed(range(count.bit_length() - 1))]:
+        held = jnp.concatenate([held, swap(held, bit, count)])
+        masks = masks + tuple(mask ^ bit for mask in masks)
+    return [(held, masks)]
+
+
+def gather_two(one, two, fillers):
+    count = 16
+    far_one, near_one = swap(one, 8, count), swap(one, 4, count)
+    pair_two = jnp.stack([two, swap(two, 2, count)])
+    far_two, near_two = swap(pair_two, 8, count), swap(pair_two, 4, count)
+    both_one = swap(far_one, 4, count)
+    four_one = jnp.stack([one, far_one, near_one, both_one])
+    side_one = swap(four_one, 2, count)
+    done = [fillers[0]((four_one, pair_two))]
+    both_two = swap(tie(far_two, done[0]), 4, count)
+    if len(fillers) > 1:
+        done.append(fillers[1]((far_two, done[0])))
+    chain_one = [(four_one, (0, 8, 4, 12)), (side_one, (2, 10, 6, 14))]
+    chain_two = [(pair_two, (0, 2)), (far_two, (8, 10)), (near_two, (4, 6)), (both_two, (12, 14))]
+    for chain in (chain_one, chain_two):
+        for i, (held, masks) in enumerate(list(chain)):
+            if i:
+                held = tie(held, done[-1])
+            chain.append((swap(held, 1, count), tuple(m ^ 1 for m in masks)))
+    return [chain_one, chain_two], done
 
 
 def reduce_order(count, flipped):
@@ -439,27 +432,27 @@
     hot_all = packed[..., columns:].transpose(1, 0, 2, 3).reshape(micro_count, count * rows, count)
 
     tables = codebooks[0].astype(jnp.float32).transpose(0, 2, 1).reshape(3, 8, LANES)
-    gathered, marks = [], []
-    for m in range(micro_count):
-        chain, seen = gather_all(attend(queries, kv_cache, lengths, m), count, m % 2 == 1)
-        gathered.append(chain)
-        marks.append(seen)
-    after = [tuple(seen[i] for seen in marks if seen) for i in range(2)]
-    gate = expand(tables[0], gate_codes[0].T, True)
-    up = expand(tables[1], up_codes[0].T, True, after[0] if marks[0] else ())
-    down = expand(tables[2], down_codes[0], False, after[1] if marks[0] else ())
-
-    columns_of = project(me_list, gathered, out_weight, hidden_columns)
-    streams = []
-    for m in range(micro_count):
-        chain, _ = gather_all(columns_of[m], count, m % 2 == 1)
-        if columns % LANES:
-            held, masks = chain[0]
-            place = [masks.index(i) for i in range(count)]
-            order = jnp.asarray(place, jnp.int32)[jnp.arange(count, dtype=jnp.int32) ^ me]
-            held = held[order].transpose(1, 2, 0, 3).reshape(1, count, rows, width)
-            chain = [(held, (0,))]
-        streams.append(chain)
+    attended = [attend(queries, kv_cache, lengths, m) for m in range(micro_count)]
+    make_gate = lambda after: expand(tables[0], gate_codes[0].T, True, after)
+    make_up = lambda after: expand(tables[1], up_codes[0].T, True, after + (packed,))
+    make_down = lambda after: expand(tables[2], down_codes[0], False, after)
+    if count == 16 and micro_count == 2:
+        gathered, (gate, up) = gather_two(*attended, [make_gate, make_up])
+        column_parts = project(me_list, gathered, out_weight, hidden_columns)
+        streams, (down,) = gather_two(*column_parts, [make_down])
+    else:
+        gate, up, down = make_gate(()), make_up(()), make_down(())
+        gathered = [gather_all(value, count) for value in attended]
+        column_parts = project(me_list, gathered, out_weight, hidden_columns)
+        streams = [gather_all(value, count) for value in column_parts]
+    if columns % LANES:
+        joined = []
+        for ((held, masks),) in streams:
+            place = jnp.asarray([masks.index(i) for i in range(count)], jnp.int32)
+            held = held[place[jnp.arange(count, dtype=jnp.int32) ^ me]]
+            held = held.transpose(1, 2, 0, 3).reshape(1, count, rows, width)
+            joined.append([(held, (0,))])
+        streams = joined
 
     plans = [reduce_order(count, m % 2 == 1) for m in range(micro_count)]
     batches = [list(range(micro_count))] if count * rows <= 128 else [[m] for m in range(micro_count)]

time: 150 us -> 130 us (0.87)
  waiting for transfers between devices: 53.9 us -> 32.9 us
  local copies, waits for them, and re-layouts: 14.6 us -> 9.87 us
  Pallas kernels: 43.6 us -> 48.2 us
    ppermute x36, waiting for transfers between devices: 53.9 us -> 32.9 us  [swap(): return lax.ppermute(value, 'expert', [(i, i ^ bit) for i in range(count)])]
    pallas_call x3, Pallas kernels: 23.5 us -> 26.6 us  [expand(): pl.pallas_call(functools.partial(expand_kernel, stacked), grid=grid, in_s...]
    unnamed x36, local copies, waits for them, and re-layouts: 12.8 us -> 9.79 us
    pallas_call x2, Pallas kernels: 5.74 us -> 8.19 us  [attend(): pl.pallas_call(functools.partial(attend_kernel, micro, span, KV_HEADS), g...]
    ppermute x36, starting transfers between devices: 29.9 us -> 32 us  [swap(): return lax.ppermute(value, 'expert', [(i, i ^ bit) for i in range(count)])]
    pallas_call x1, Pallas kernels: 10.6 us -> 8.88 us  [run_experts(): pl.pallas_call(functools.partial(experts_kernel, masks, counts, orders),...]
  transfers between devices with their start and end apart: 37 -> 37, of which waited for: 17 -> 16; matrix products, arithmetic and copies ran while one was open for 2% -> 1% of each run, Pallas kernels for 18% -> 24%
where the time goes in v3:
time: 130 us; the launch traced here: 129 us
  Pallas kernels  48.2 us (37%)
  starting transfers between devices  35.6 us (27%)
  waiting for transfers between devices  32.9 us (25%)
  local copies, waits for them, and re-layouts  9.87 us (8%)
  other arithmetic  2.15 us (2%)
    ppermute x36, waiting for transfers between devices, swap(): return lax.ppermute(value, 'expert', [(i, i ^ bit) for i in range(count)])  32.9 us
    ppermute x36, starting transfers between devices, swap(): return lax.ppermute(value, 'expert', [(i, i ^ bit) for i in range(count)])  32 us
    pallas_call x3, Pallas kernels, expand(): pl.pallas_call(functools.partial(expand_kernel, stacked), grid=grid, in_s...  26.6 us
    unnamed x36, local copies, waits for them, and re-layouts  9.79 us
    pallas_call x1, Pallas kernels, run_experts(): pl.pallas_call(functools.partial(experts_kernel, masks, counts, orders),...  8.88 us
    pallas_call x2, Pallas kernels, attend(): pl.pallas_call(functools.partial(attend_kernel, micro, span, KV_HEADS), g...  8.19 us
    pallas_call x1, Pallas kernels, project(): pl.pallas_call(functools.partial(project_kernel, masks, counts), grid_spe...  4.53 us
    all_to_all x1, starting transfers between devices, body(): lax.all_to_all(jnp.concatenate([lead, tail], axis=-1), 'expert', split_ax...  3.52 us
  transfers between devices with their start and end apart: 37, of which 16 were waited for; matrix products, arithmetic and copies ran while one was open for 1% of the time, Pallas kernels for 24%

profile of v3, /device:TPU:0, one launch (start us, length us, event | category | flops | bytes accessed | tf_op | source)
XLA Modules:
  0.0 129.1 jit_solution(2505691771052137500)
XLA Ops:
  0.0 0.9 copy-done.3
  1.0 0.7 copy-done.9
  1.7 4.1 %attend.2 = bf16[8,8192]{1,0:T(8,128)(2,1)S(1)} custom-call(s32[2,8]{1,0:T(2,128)S(1)} %copy-done.9, bf16[2,8,8192]{2,1,0:T(8,128)(2,1)S(1)} %copy-done.3, bf16[2,8,128,2,512]{4,3,2,1,0:T(2,128)(2,1)} %kv_ref.3), custom_call_target="tpu_custom_call" | custom-call | flops 67108864 | bytes 2097152 | tf_op jit(solution)/shard_map/attend/pallas_call | solution.py:75
  5.8 3.1 %collective-permute-start.1 = (bf16[8,8192]{1,0:T(8,128)(2,1)S(1)}, bf16[8,8192]{1,0:T(8,128)(2,1)S(1)}, u32[]{:S(2)}, u32[]{:S(2)}) collective-permute-start(bf16[8,8192]{1,0:T(8,128)(2,1)S(1)} %attend.2), channel_id=1, source_target_pairs={{0,4},{1,5},{2,6},{3,7},{4,0},{5,1},{6,2},{7,3},{8,12},{9,13},{10,... | collective-permute-start | bytes 393224 | tf_op jit(solution)/shard_map/ppermute | solution.py:344
  8.8 2.6 %collective-permute-start = (bf16[8,8192]{1,0:T(8,128)(2,1)S(1)}, bf16[8,8192]{1,0:T(8,128)(2,1)S(1)}, u32[]{:S(2)}, u32[]{:S(2)}) collective-permute-start(bf16[8,8192]{1,0:T(8,128)(2,1)S(1)} %attend.2), channel_id=1, source_target_pairs={{0,8},{1,9},{2,10},{3,11},{4,12},{5,13},{6,14},{7,15},{8,0},{9,1},... | collective-permute-start | bytes 393224 | tf_op jit(solution)/shard_map/ppermute | solution.py:344
  11.4 0.1 fusion.4
  11.6 0.7 pad_maximum_fusion.3
  12.3 3.5 %all-to-all-start = ((bf16[16,2,8,272]{3,2,1,0:T(8,128)(2,1)}), bf16[16,2,8,272]{3,2,1,0:T(8,128)(2,1)S(1)}, u32[]{:S(2)}, u32[]{:S(2)}) async-start(bf16[16,2,8,272]{3,2,1,0:T(8,128)(2,1)} %pad_maximum_fusion.3), calls=%async_computation | async-start | bytes 393216 | tf_op jit(solution)/shard_map/all_to_all | solution.py:428
  15.8 4.1 %attend.3 = bf16[8,8192]{1,0:T(8,128)(2,1)S(1)} custom-call(s32[2,8]{1,0:T(2,128)S(1)} %copy-done.10, bf16[2,8,8192]{2,1,0:T(8,128)(2,1)S(1)} %copy-done.4, bf16[2,8,128,2,512]{4,3,2,1,0:T(2,128)(2,1)} %kv_ref.3), custom_call_target="tpu_custom_call" | custom-call | flops 67108864 | bytes 2097152 | tf_op jit(solution)/shard_map/attend/pallas_call | solution.py:75
  19.9 1.9 %collective-permute-start.5 = (bf16[8,8192]{1,0:T(8,128)(2,1)S(1)}, bf16[8,8192]{1,0:T(8,128)(2,1)S(1)}, u32[]{:S(2)}, u32[]{:S(2)}) collective-permute-start(bf16[8,8192]{1,0:T(8,128)(2,1)S(1)} %attend.3), channel_id=1, source_target_pairs={{0,2},{1,3},{2,0},{3,1},{4,6},{5,7},{6,4},{7,5},{8,10},{9,11},{10,... | collective-permute-start | bytes 393224 | tf_op jit(solution)/shard_map/ppermute | solution.py:344
  21.9 1.6 %collective-permute-start.2 = (bf16[8,8192]{1,0:T(8,128)(2,1)S(1)}, bf16[8,8192]{1,0:T(8,128)(2,1)S(1)}, u32[]{:S(2)}, u32[]{:S(2)}) collective-permute-start(bf16[8,8192]{1,0:T(8,128)(2,1)S(1)} %collective-permute-done), channel_id=1, source_target_pairs={{0,4},{1,5},{2,6},{3,7},{4,0},{5,1},{6,2},{7,3},{8,12},{9,13},{10,... | collective-permute-start | bytes 393224 | tf_op jit(solution)/shard_map/ppermute | solution.py:344
  23.4 2.8 %collective-permute-done.5 = bf16[8,8192]{1,0:T(8,128)(2,1)S(1)} collective-permute-done((bf16[8,8192]{1,0:T(8,128)(2,1)S(1)}, bf16[8,8192]{1,0:T(8,128)(2,1)S(1)}, u32[]{:S(2)}, u32[]{:S(2)}) %collective-permute-start.5) | collective-permute-done | bytes 131104 | tf_op jit(solution)/shard_map/ppermute | solution.py:344
  26.3 0.1 collective-permute-start.10
  26.3 1.4 %collective-permute-start.8 = (bf16[2,8,8192]{2,1,0:T(8,128)(2,1)S(1)}, bf16[2,8,8192]{2,1,0:T(8,128)(2,1)S(1)}, u32[]{:S(2)}, u32[]{:S(2)}) collective-permute-start(bf16[2,8,8192]{2,1,0:T(8,128)(2,1)S(1)} %pad_maximum_fusion.1.rest_1_.refs_4_), channel_id=1, source_target_pairs={{0,4},{1,5},{2,6},{3,7},{4,0},{5,1},{6,2},{7,3},{8,12},{9,13},{10,... | collective-permute-start | bytes 786440 | tf_op jit(solution)/shard_map/ppermute | solution.py:344
  27.8 2.2 %collective-permute-start.6 = (bf16[2,8,8192]{2,1,0:T(8,128)(2,1)S(1)}, bf16[2,8,8192]{2,1,0:T(8,128)(2,1)S(1)}, u32[]{:S(2)}, u32[]{:S(2)}) collective-permute-start(bf16[2,8,8192]{2,1,0:T(8,128)(2,1)S(1)} %pad_maximum_fusion.1.rest_1_.refs_4_), channel_id=1, source_target_pairs={{0,8},{1,9},{2,10},{3,11},{4,12},{5,13},{6,14},{7,15},{8,0},{9,1},... | collective-permute-start | bytes 786440 | tf_op jit(solution)/shard_map/ppermute | solution.py:344
  30.1 1.5 %collective-permute-start.3 = (bf16[4,8,8192]{2,1,0:T(8,128)(2,1)S(1)}, bf16[4,8,8192]{2,1,0:T(8,128)(2,1)S(1)}, u32[]{:S(2)}, u32[]{:S(2)}) collective-permute-start(bf16[4,8,8192]{2,1,0:T(8,128)(2,1)S(1)} %pad_maximum_fusion.rest_0_.refs_0_), channel_id=1, source_target_pairs={{0,2},{1,3},{2,0},{3,1},{4,6},{5,7},{6,4},{7,5},{8,10},{9,11},{10,... | collective-permute-start | bytes 1572872 | tf_op jit(solution)/shard_map/ppermute | solution.py:344
  31.7 8.8 %expand.3 = bf16[4,192,4096]{2,1,0:T(8,128)(2,1)S(1)} custom-call(f32[8,128]{1,0:T(8,128)S(1)} %squeeze.34.table_ref, bf16[192,4096]{1,0:T(8,128)(2,1)} %bitcast.83, bf16[4,8,8192]{2,1,0:T(8,128)(2,1)S(1)} %pad_maximum_fusion.rest_0_.refs_0_, bf16[2,8,8192]{2,1,0:T(8,128)(2,1)S(1)} %pad_maximum_fusion.1.rest_1_.refs_4_), custom_call_target="tpu_custom_call" | custom-call | flops 6291456000 | bytes 7864320 | tf_op jit(solution)/shard_map/expand/pallas_call | solution.py:144
  40.5 2.6 %copy-done = bf16[4,192,4096]{2,1,0:T(8,128)(2,1)} copy-done((bf16[4,192,4096]{2,1,0:T(8,128)(2,1)}, bf16[4,192,4096]{2,1,0:T(8,128)(2,1)S(1)}, u32[]{:S(2)}) %copy-start) | copy-done | bytes 6291480
  43.2 0.5 collective-permute-start.9
  43.7 2.8 %copy-done.1 = bf16[4,192,4096]{2,1,0:T(8,128)(2,1)S(1)} copy-done((bf16[4,192,4096]{2,1,0:T(8,128)(2,1)S(1)}, bf16[4,192,4096]{2,1,0:T(8,128)(2,1)}, u32[]{:S(2)}) %copy-start.1) | copy-done | bytes 6291480
  46.5 8.8 %expand.4 = bf16[4,192,4096]{2,1,0:T(8,128)(2,1)S(1)} custom-call(f32[8,128]{1,0:T(8,128)S(1)} %squeeze.32.table_ref, bf16[192,4096]{1,0:T(8,128)(2,1)} %bitcast.84, bf16[2,8,8192]{2,1,0:T(8,128)(2,1)S(1)} %collective-permute-done.6.rest_0_.refs_5_, bf16[768,4096]{1,0:T(8,128)(2,1)S(1)} %bitcast.59, bf16[16,2,8,272]{3,2,1,0:T(8,128)(2,1)S(1)} %all-to-all-done.rest_2_), custom_call_target="tpu_custom_call" | custom-call | flops 6291456000 | bytes 7864320 | tf_op jit(solution)/shard_map/expand/pallas_call | solution.py:144
  55.4 2.7 %copy-done.2 = bf16[4,192,4096]{2,1,0:T(8,128)(2,1)} copy-done((bf16[4,192,4096]{2,1,0:T(8,128)(2,1)}, bf16[4,192,4096]{2,1,0:T(8,128)(2,1)S(1)}, u32[]{:S(2)}) %copy-start.2) | copy-done | bytes 6291480
  58.1 0.5 collective-permute-start.11
  58.6 0.4 collective-permute-start.13
  59.1 1.7 %collective-permute-done.11.refs_9_ = bf16[2,8,8192]{2,1,0:T(8,128)(2,1)} collective-permute-done((bf16[2,8,8192]{2,1,0:T(8,128)(2,1)S(1)}, bf16[2,8,8192]{2,1,0:T(8,128)(2,1)}, u32[]{:S(2)}, u32[]{:S(2)}) %collective-permute-start.11) | collective-permute-done | bytes 262176 | tf_op jit(solution)/shard_map/ppermute | solution.py:344
  60.8 0.4 collective-permute-done.12.refs_10_
  61.2 4.5 %project.1 = (bf16[16,8,256]{2,1,0:T(8,128)(2,1)S(1)}, bf16[16,8,256]{2,1,0:T(8,128)(2,1)S(1)}) custom-call(s32[1]{0:T(128)} %bitcast.me_ref, bf16[4,8,8192]{2,1,0:T(8,128)(2,1)S(1)} %pad_maximum_fusion.rest_0_.refs_0_, bf16[4,8,8192]{2,1,0:T(8,128)(2,1)S(1)} %collective-permute-done.3.refs_1_, bf16[4,8,8192]{2,1,0:T(8,128)(2,1)S(1)} %collective-permute-done.4.refs_2_, ...), custom_call_target="tpu_custom_call" | custom-call | flops 1073741824 | bytes 4194304 | tf_op jit(solution)/shard_map/project/pallas_call | solution.py:196
  65.8 1.8 %collective-permute-start.14 = (bf16[16,8,256]{2,1,0:T(8,128)(2,1)S(1)}, bf16[16,8,256]{2,1,0:T(8,128)(2,1)S(1)}, u32[]{:S(2)}, u32[]{:S(2)}) collective-permute-start(bf16[16,8,256]{2,1,0:T(8,128)(2,1)S(1)} %get-tuple-element.27), channel_id=1, source_target_pairs={{0,8},{1,9},{2,10},{3,11},{4,12},{5,13},{6,14},{7,15},{8,0},{9,1},... | collective-permute-start | bytes 196616 | tf_op jit(solution)/shard_map/ppermute | solution.py:344
  67.6 1.5 %collective-permute-start.19 = (bf16[16,8,256]{2,1,0:T(8,128)(2,1)S(1)}, bf16[16,8,256]{2,1,0:T(8,128)(2,1)S(1)}, u32[]{:S(2)}, u32[]{:S(2)}) collective-permute-start(bf16[16,8,256]{2,1,0:T(8,128)(2,1)S(1)} %get-tuple-element.28), channel_id=1, source_target_pairs={{0,2},{1,3},{2,0},{3,1},{4,6},{5,7},{6,4},{7,5},{8,10},{9,11},{10,... | collective-permute-start | bytes 196616 | tf_op jit(solution)/shard_map/ppermute | solution.py:344
  69.1 3.2 %collective-permute-done.14 = bf16[16,8,256]{2,1,0:T(8,128)(2,1)S(1)} collective-permute-done((bf16[16,8,256]{2,1,0:T(8,128)(2,1)S(1)}, bf16[16,8,256]{2,1,0:T(8,128)(2,1)S(1)}, u32[]{:S(2)}, u32[]{:S(2)}) %collective-permute-start.14) | collective-permute-done | bytes 65568 | tf_op jit(solution)/shard_map/ppermute | solution.py:344
  72.2 0.9 collective-permute-start.16
  73.1 0.1 collective-permute-start.24
  73.2 1.2 collective-permute-start.22
  74.4 0.9 collective-permute-start.21
  75.3 1.4 %collective-permute-done.16 = bf16[16,8,256]{2,1,0:T(8,128)(2,1)S(1)} collective-permute-done((bf16[16,8,256]{2,1,0:T(8,128)(2,1)S(1)}, bf16[16,8,256]{2,1,0:T(8,128)(2,1)S(1)}, u32[]{:S(2)}, u32[]{:S(2)}) %collective-permute-start.16) | collective-permute-done | bytes 65568 | tf_op jit(solution)/shard_map/ppermute | solution.py:344
  76.7 1.0 collective-permute-start.17
  77.7 8.9 %expand.5.refs_17_ = bf16[768,4096]{1,0:T(8,128)(2,1)S(1)} custom-call(f32[8,128]{1,0:T(8,128)S(1)} %squeeze.36.table_ref, bf16[768,1024]{1,0:T(8,128)(2,1)} %bitcast.85, bf16[4,16,8,256]{3,2,1,0:T(8,128)(2,1)S(1)} %pad_maximum_fusion.2.rest_0_.refs_0_, bf16[2,16,8,256]{3,2,1,0:T(8,128)(2,1)S(1)} %pad_maximum_fusion.4.rest_1_.refs_4_), custom_call_target="tpu_custom_call" | custom-call | flops 6291456000 | bytes 7864320 | tf_op jit(solution)/shard_map/expand/pallas_call | solution.py:144
  86.7 0.4 collective-permute-start.23
  87.1 0.1 collective-permute-start.18
  87.2 0.5 collective-permute-start.25
  87.7 4.0 %collective-permute-done.23.refs_7_ = bf16[2,16,8,256]{3,2,1,0:T(8,128)(2,1)S(1)} collective-permute-done((bf16[2,16,8,256]{3,2,1,0:T(8,128)(2,1)S(1)}, bf16[2,16,8,256]{3,2,1,0:T(8,128)(2,1)S(1)}, u32[]{:S(2)}, u32[]{:S(2)}) %collective-permute-start.23) | collective-permute-done | bytes 131104 | tf_op jit(solution)/shard_map/ppermute | solution.py:344
  91.7 0.5 collective-permute-start.27
  92.3 0.7 collective-permute-done.26.refs_10_
  93.1 0.2 collective-permute-done.27.refs_11_
  93.3 0.5 collective-permute-done.20.refs_3_
  93.9 8.9 %experts.1 = (bf16[8,8,4096]{2,1,0:T(8,128)(2,1)S(1)}, bf16[8,8,4096]{2,1,0:T(8,128)(2,1)S(1)}, bf16[8,8,4096]{2,1,0:T(8,128)(2,1)S(1)}, bf16[8,8,4096]{2,1,0:T(...) custom-call(s32[1]{0:T(128)} %bitcast.me_ref, ...), custom_call_target="tpu_custom_call" | custom-call | flops 4831838208 | bytes 18874368 | tf_op jit(solution)/shard_map/experts/pallas_call | solution.py:321
  102.7 0.3 collective-permute-start.28
  103.0 0.3 collective-permute-start.32
  103.3 1.4 %collective-permute-done.28 = bf16[8,8,4096]{2,1,0:T(8,128)(2,1)S(1)} collective-permute-done((bf16[8,8,4096]{2,1,0:T(8,128)(2,1)S(1)}, bf16[8,8,4096]{2,1,0:T(8,128)(2,1)S(1)}, u32[]{:S(2)}, u32[]{:S(2)}) %collective-permute-start.28) | collective-permute-done | bytes 524320 | tf_op jit(solution)/shard_map/ppermute | solution.py:344
  104.7 0.1 add_convert_fusion.3
  104.8 1.1 collective-permute-start.29
  105.9 0.1 add_convert_fusion.1
  106.1 0.7 collective-permute-start.33
  106.8 6.5 %collective-permute-done.29 = bf16[4,8,4096]{2,1,0:T(8,128)(2,1)S(1)} collective-permute-done((bf16[4,8,4096]{2,1,0:T(8,128)(2,1)S(1)}, bf16[4,8,4096]{2,1,0:T(8,128)(2,1)S(1)}, u32[]{:S(2)}, u32[]{:S(2)}) %collective-permute-start.29) | collective-permute-done | bytes 262176 | tf_op jit(solution)/shard_map/ppermute | solution.py:344
  113.4 0.4 collective-permute-start.30
  113.8 0.4 collective-permute-done.33
  114.3 1.9 %collective-permute-start.34 = (bf16[2,8,4096]{2,1,0:T(8,128)(2,1)S(1)}, bf16[2,8,4096]{2,1,0:T(8,128)(2,1)S(1)}, u32[]{:S(2)}, u32[]{:S(2)}) collective-permute-start(bf16[2,8,4096]{2,1,0:T(8,128)(2,1)S(1)} %get-tuple-element.46), channel_id=1, source_target_pairs={{0,8},{1,9},{2,10},{3,11},{4,12},{5,13},{6,14},{7,15},{8,0},{9,1},... | collective-permute-start | bytes 393224 | tf_op jit(solution)/shard_map/ppermute | solution.py:344
  116.3 4.3 %collective-permute-done.30 = bf16[2,8,4096]{2,1,0:T(8,128)(2,1)S(1)} collective-permute-done((bf16[2,8,4096]{2,1,0:T(8,128)(2,1)S(1)}, bf16[2,8,4096]{2,1,0:T(8,128)(2,1)S(1)}, u32[]{:S(2)}, u32[]{:S(2)}) %collective-permute-start.30) | collective-permute-done | bytes 131104 | tf_op jit(solution)/shard_map/ppermute | solution.py:344
  120.6 1.4 %collective-permute-start.31 = (bf16[1,8,4096]{2,1,0:T(8,128)(2,1)S(1)}, bf16[1,8,4096]{2,1,0:T(8,128)(2,1)S(1)}, u32[]{:S(2)}, u32[]{:S(2)}) collective-permute-start(bf16[1,8,4096]{2,1,0:T(8,128)(2,1)S(1)} %add_convert_fusion.10), channel_id=1, source_target_pairs={{0,8},{1,9},{2,10},{3,11},{4,12},{5,13},{6,14},{7,15},{8,0},{9,1},... | collective-permute-start | bytes 196616 | tf_op jit(solution)/shard_map/ppermute | solution.py:344
  122.0 2.0 %collective-permute-done.34 = bf16[2,8,4096]{2,1,0:T(8,128)(2,1)S(1)} collective-permute-done((bf16[2,8,4096]{2,1,0:T(8,128)(2,1)S(1)}, bf16[2,8,4096]{2,1,0:T(8,128)(2,1)S(1)}, u32[]{:S(2)}, u32[]{:S(2)}) %collective-permute-start.34) | collective-permute-done | bytes 131104 | tf_op jit(solution)/shard_map/ppermute | solution.py:344
  124.0 1.0 collective-permute-start.35
  125.1 0.8 collective-permute-done.31
  125.9 2.5 %collective-permute-done.35 = bf16[1,8,4096]{2,1,0:T(8,128)(2,1)S(1)} collective-permute-done((bf16[1,8,4096]{2,1,0:T(8,128)(2,1)S(1)}, bf16[1,8,4096]{2,1,0:T(8,128)(2,1)S(1)}, u32[]{:S(2)}, u32[]{:S(2)}) %collective-permute-start.35) | collective-permute-done | bytes 65568 | tf_op jit(solution)/shard_map/ppermute | solution.py:344
  128.4 0.7 pad_maximum_fusion.5
  (82 shorter events, 0.8 us)
Async XLA Ops:
  0.0 0.9 copy-start.3
  1.0 0.7 copy-start.9
  1.6 9.8 %copy-start.12 = (s32[2,8,8]{2,1,0:T(8,128)S(1)}, s32[2,8,8]{2,1,0:T(8,128)}, u32[]{:S(2)}) copy-start(s32[2,8,8]{2,1,0:T(8,128)} %param.18) | copy-start | bytes 1540
  1.6 9.9 %copy-start.11 = (bf16[2,8,4096]{2,1,0:T(8,128)(2,1)S(1)}, bf16[2,8,4096]{2,1,0:T(8,128)(2,1)}, u32[]{:S(2)}) copy-start(bf16[2,8,4096]{2,1,0:T(8,128)(2,1)} %param.14) | copy-start | bytes 393220
  1.6 14.2 %copy-start.4 = (bf16[2,8,8192]{2,1,0:T(8,128)(2,1)S(1)}, bf16[2,8,8192]{2,1,0:T(8,128)(2,1)}, u32[]{:S(2)}) copy-start(bf16[2,8,8192]{2,1,0:T(8,128)(2,1)} %q_ref.3) | copy-start | bytes 786436
  1.6 14.2 %copy-start.10 = (s32[2,8]{1,0:T(2,128)S(1)}, s32[2,8]{1,0:T(2,128)}, u32[]{:S(2)}) copy-start(s32[2,8]{1,0:T(2,128)} %len_ref.3) | copy-start | bytes 196
  1.6 20.2 %copy-start.13 = (bf16[1,3,256,4]{2,3,1,0:T(4,128)(2,1)S(1)}, bf16[1,3,256,4]{2,3,1,0:T(4,128)(2,1)}, u32[]{:S(2)}) copy-start(bf16[1,3,256,4]{2,3,1,0:T(4,128)(2,1)} %param.25) | copy-start | bytes 18436
  5.8 24.2 %collective-permute-start.1 = (bf16[8,8192]{1,0:T(8,128)(2,1)S(1)}, bf16[8,8192]{1,0:T(8,128)(2,1)S(1)}, u32[]{:S(2)}, u32[]{:S(2)}) collective-permute-start(bf16[8,8192]{1,0:T(8,128)(2,1)S(1)} %attend.2), channel_id=1, source_target_pairs={{0,4},{1,5},{2,6},{3,7},{4,0},{5,1},{6,2},{7,3},{8,12},{9,13},{10,... | collective-permute-start | bytes 393224 | tf_op jit(solution)/shard_map/ppermute | solution.py:344
  8.8 13.0 %collective-permute-start = (bf16[8,8192]{1,0:T(8,128)(2,1)S(1)}, bf16[8,8192]{1,0:T(8,128)(2,1)S(1)}, u32[]{:S(2)}, u32[]{:S(2)}) collective-permute-start(bf16[8,8192]{1,0:T(8,128)(2,1)S(1)} %attend.2), channel_id=1, source_target_pairs={{0,8},{1,9},{2,10},{3,11},{4,12},{5,13},{6,14},{7,15},{8,0},{9,1},... | collective-permute-start | bytes 393224 | tf_op jit(solution)/shard_map/ppermute | solution.py:344
  12.3 31.4 %all-to-all-start = ((bf16[16,2,8,272]{3,2,1,0:T(8,128)(2,1)}), bf16[16,2,8,272]{3,2,1,0:T(8,128)(2,1)S(1)}, u32[]{:S(2)}, u32[]{:S(2)}) async-start(bf16[16,2,8,272]{3,2,1,0:T(8,128)(2,1)} %pad_maximum_fusion.3), calls=%async_computation | async-start | bytes 393216 | tf_op jit(solution)/shard_map/all_to_all | solution.py:428
  19.9 6.3 %collective-permute-start.5 = (bf16[8,8192]{1,0:T(8,128)(2,1)S(1)}, bf16[8,8192]{1,0:T(8,128)(2,1)S(1)}, u32[]{:S(2)}, u32[]{:S(2)}) collective-permute-start(bf16[8,8192]{1,0:T(8,128)(2,1)S(1)} %attend.3), channel_id=1, source_target_pairs={{0,2},{1,3},{2,0},{3,1},{4,6},{5,7},{6,4},{7,5},{8,10},{9,11},{10,... | collective-permute-start | bytes 393224 | tf_op jit(solution)/shard_map/ppermute | solution.py:344
  21.9 8.1 %collective-permute-start.2 = (bf16[8,8192]{1,0:T(8,128)(2,1)S(1)}, bf16[8,8192]{1,0:T(8,128)(2,1)S(1)}, u32[]{:S(2)}, u32[]{:S(2)}) collective-permute-start(bf16[8,8192]{1,0:T(8,128)(2,1)S(1)} %collective-permute-done), channel_id=1, source_target_pairs={{0,4},{1,5},{2,6},{3,7},{4,0},{5,1},{6,2},{7,3},{8,12},{9,13},{10,... | collective-permute-start | bytes 393224 | tf_op jit(solution)/shard_map/ppermute | solution.py:344
  26.3 32.4 %collective-permute-start.10 = (bf16[2,8,8192]{2,1,0:T(8,128)(2,1)S(1)}, bf16[2,8,8192]{2,1,0:T(8,128)(2,1)S(1)}, u32[]{:S(2)}, u32[]{:S(2)}) collective-permute-start(bf16[2,8,8192]{2,1,0:T(8,128)(2,1)S(1)} %pad_maximum_fusion.1.rest_1_.refs_4_), channel_id=1, source_target_pairs={{0,1},{1,0},{2,3},{3,2},{4,5},{5,4},{6,7},{7,6},{8,9},{9,8},{10,11... | collective-permute-start | bytes 786440 | tf_op jit(solution)/shard_map/ppermute | solution.py:344
  26.3 31.7 %collective-permute-start.8 = (bf16[2,8,8192]{2,1,0:T(8,128)(2,1)S(1)}, bf16[2,8,8192]{2,1,0:T(8,128)(2,1)S(1)}, u32[]{:S(2)}, u32[]{:S(2)}) collective-permute-start(bf16[2,8,8192]{2,1,0:T(8,128)(2,1)S(1)} %pad_maximum_fusion.1.rest_1_.refs_4_), channel_id=1, source_target_pairs={{0,4},{1,5},{2,6},{3,7},{4,0},{5,1},{6,2},{7,3},{8,12},{9,13},{10,... | collective-permute-start | bytes 786440 | tf_op jit(solution)/shard_map/ppermute | solution.py:344
  27.8 15.4 %collective-permute-start.6 = (bf16[2,8,8192]{2,1,0:T(8,128)(2,1)S(1)}, bf16[2,8,8192]{2,1,0:T(8,128)(2,1)S(1)}, u32[]{:S(2)}, u32[]{:S(2)}) collective-permute-start(bf16[2,8,8192]{2,1,0:T(8,128)(2,1)S(1)} %pad_maximum_fusion.1.rest_1_.refs_4_), channel_id=1, source_target_pairs={{0,8},{1,9},{2,10},{3,11},{4,12},{5,13},{6,14},{7,15},{8,0},{9,1},... | collective-permute-start | bytes 786440 | tf_op jit(solution)/shard_map/ppermute | solution.py:344
  30.1 31.2 %collective-permute-start.4 = (bf16[4,8,8192]{2,1,0:T(8,128)(2,1)S(1)}, bf16[4,8,8192]{2,1,0:T(8,128)(2,1)S(1)}, u32[]{:S(2)}, u32[]{:S(2)}) collective-permute-start(bf16[4,8,8192]{2,1,0:T(8,128)(2,1)S(1)} %pad_maximum_fusion.rest_0_.refs_0_), channel_id=1, source_target_pairs={{0,1},{1,0},{2,3},{3,2},{4,5},{5,4},{6,7},{7,6},{8,9},{9,8},{10,11... | collective-permute-start | bytes 1572872 | tf_op jit(solution)/shard_map/ppermute | solution.py:344
  30.1 27.9 %collective-permute-start.3 = (bf16[4,8,8192]{2,1,0:T(8,128)(2,1)S(1)}, bf16[4,8,8192]{2,1,0:T(8,128)(2,1)S(1)}, u32[]{:S(2)}, u32[]{:S(2)}) collective-permute-start(bf16[4,8,8192]{2,1,0:T(8,128)(2,1)S(1)} %pad_maximum_fusion.rest_0_.refs_0_), channel_id=1, source_target_pairs={{0,2},{1,3},{2,0},{3,1},{4,6},{5,7},{6,4},{7,5},{8,10},{9,11},{10,... | collective-permute-start | bytes 1572872 | tf_op jit(solution)/shard_map/ppermute | solution.py:344
  40.5 2.6 %copy-start = (bf16[4,192,4096]{2,1,0:T(8,128)(2,1)}, bf16[4,192,4096]{2,1,0:T(8,128)(2,1)S(1)}, u32[]{:S(2)}) copy-start(bf16[4,192,4096]{2,1,0:T(8,128)(2,1)S(1)} %expand.3) | copy-start | bytes 18874372
  43.2 15.4 %collective-permute-start.9 = (bf16[2,8,8192]{2,1,0:T(8,128)(2,1)S(1)}, bf16[2,8,8192]{2,1,0:T(8,128)(2,1)}, u32[]{:S(2)}, u32[]{:S(2)}) collective-permute-start(bf16[2,8,8192]{2,1,0:T(8,128)(2,1)S(1)} %collective-permute-done.6.rest_0_.refs_5_), channel_id=1, source_target_pairs={{0,4},{1,5},{2,6},{3,7},{4,0},{5,1},{6,2},{7,3},{8,12},{9,13},{10,... | collective-permute-start | bytes 786440 | tf_op jit(solution)/shard_map/ppermute | solution.py:344
  43.7 2.8 %copy-start.1 = (bf16[4,192,4096]{2,1,0:T(8,128)(2,1)S(1)}, bf16[4,192,4096]{2,1,0:T(8,128)(2,1)}, u32[]{:S(2)}) copy-start(bf16[4,192,4096]{2,1,0:T(8,128)(2,1)} %copy-done) | copy-start | bytes 18874372
  55.4 2.7 %copy-start.2 = (bf16[4,192,4096]{2,1,0:T(8,128)(2,1)}, bf16[4,192,4096]{2,1,0:T(8,128)(2,1)S(1)}, u32[]{:S(2)}) copy-start(bf16[4,192,4096]{2,1,0:T(8,128)(2,1)S(1)} %expand.4) | copy-start | bytes 18874372
  58.0 3.2 %collective-permute-start.7 = (bf16[4,8,8192]{2,1,0:T(8,128)(2,1)S(1)}, bf16[4,8,8192]{2,1,0:T(8,128)(2,1)S(1)}, u32[]{:S(2)}, u32[]{:S(2)}) collective-permute-start(bf16[4,8,8192]{2,1,0:T(8,128)(2,1)S(1)} %collective-permute-done.3.refs_1_), channel_id=1, source_target_pairs={{0,1},{1,0},{2,3},{3,2},{4,5},{5,4},{6,7},{7,6},{8,9},{9,8},{10,11... | collective-permute-start | bytes 1572872 | tf_op jit(solution)/shard_map/ppermute | solution.py:344
  58.1 2.8 %collective-permute-start.11 = (bf16[2,8,8192]{2,1,0:T(8,128)(2,1)S(1)}, bf16[2,8,8192]{2,1,0:T(8,128)(2,1)}, u32[]{:S(2)}, u32[]{:S(2)}) collective-permute-start(bf16[2,8,8192]{2,1,0:T(8,128)(2,1)S(1)} %collective-permute-done.6.rest_0_.refs_5_), channel_id=1, source_target_pairs={{0,1},{1,0},{2,3},{3,2},{4,5},{5,4},{6,7},{7,6},{8,9},{9,8},{10,11... | collective-permute-start | bytes 786440 | tf_op jit(solution)/shard_map/ppermute | solution.py:344
  58.6 2.6 %collective-permute-start.12 = (bf16[2,8,8192]{2,1,0:T(8,128)(2,1)S(1)}, bf16[2,8,8192]{2,1,0:T(8,128)(2,1)}, u32[]{:S(2)}, u32[]{:S(2)}) collective-permute-start(bf16[2,8,8192]{2,1,0:T(8,128)(2,1)S(1)} %collective-permute-done.8.refs_6_), channel_id=1, source_target_pairs={{0,1},{1,0},{2,3},{3,2},{4,5},{5,4},{6,7},{7,6},{8,9},{9,8},{10,11... | collective-permute-start | bytes 786440 | tf_op jit(solution)/shard_map/ppermute | solution.py:344
  58.6 2.6 %collective-permute-start.13 = (bf16[2,8,8192]{2,1,0:T(8,128)(2,1)}, bf16[2,8,8192]{2,1,0:T(8,128)(2,1)}, u32[]{:S(2)}, u32[]{:S(2)}) collective-permute-start(bf16[2,8,8192]{2,1,0:T(8,128)(2,1)} %collective-permute-done.9.refs_7_), channel_id=1, source_target_pairs={{0,1},{1,0},{2,3},{3,2},{4,5},{5,4},{6,7},{7,6},{8,9},{9,8},{10,11... | collective-permute-start | bytes 786440 | tf_op jit(solution)/shard_map/ppermute | solution.py:344
  65.8 6.4 %collective-permute-start.14 = (bf16[16,8,256]{2,1,0:T(8,128)(2,1)S(1)}, bf16[16,8,256]{2,1,0:T(8,128)(2,1)S(1)}, u32[]{:S(2)}, u32[]{:S(2)}) collective-permute-start(bf16[16,8,256]{2,1,0:T(8,128)(2,1)S(1)} %get-tuple-element.27), channel_id=1, source_target_pairs={{0,8},{1,9},{2,10},{3,11},{4,12},{5,13},{6,14},{7,15},{8,0},{9,1},... | collective-permute-start | bytes 196616 | tf_op jit(solution)/shard_map/ppermute | solution.py:344
  67.6 5.5 %collective-permute-start.19 = (bf16[16,8,256]{2,1,0:T(8,128)(2,1)S(1)}, bf16[16,8,256]{2,1,0:T(8,128)(2,1)S(1)}, u32[]{:S(2)}, u32[]{:S(2)}) collective-permute-start(bf16[16,8,256]{2,1,0:T(8,128)(2,1)S(1)} %get-tuple-element.28), channel_id=1, source_target_pairs={{0,2},{1,3},{2,0},{3,1},{4,6},{5,7},{6,4},{7,5},{8,10},{9,11},{10,... | collective-permute-start | bytes 196616 | tf_op jit(solution)/shard_map/ppermute | solution.py:344
  69.0 6.2 %collective-permute-start.15 = (bf16[16,8,256]{2,1,0:T(8,128)(2,1)S(1)}, bf16[16,8,256]{2,1,0:T(8,128)(2,1)S(1)}, u32[]{:S(2)}, u32[]{:S(2)}) collective-permute-start(bf16[16,8,256]{2,1,0:T(8,128)(2,1)S(1)} %get-tuple-element.27), channel_id=1, source_target_pairs={{0,4},{1,5},{2,6},{3,7},{4,0},{5,1},{6,2},{7,3},{8,12},{9,13},{10,... | collective-permute-start | bytes 196616 | tf_op jit(solution)/shard_map/ppermute | solution.py:344
  72.2 4.5 %collective-permute-start.16 = (bf16[16,8,256]{2,1,0:T(8,128)(2,1)S(1)}, bf16[16,8,256]{2,1,0:T(8,128)(2,1)S(1)}, u32[]{:S(2)}, u32[]{:S(2)}) collective-permute-start(bf16[16,8,256]{2,1,0:T(8,128)(2,1)S(1)} %collective-permute-done.14), channel_id=1, source_target_pairs={{0,4},{1,5},{2,6},{3,7},{4,0},{5,1},{6,2},{7,3},{8,12},{9,13},{10,... | collective-permute-start | bytes 196616 | tf_op jit(solution)/shard_map/ppermute | solution.py:344
  73.1 20.7 %slice-start = ((s8[6291456]{0:T(1024)(128)(4,1)}), s8[4194304]{0:T(1024)(128)(4,1)S(1)}, s32[]{:S(2)}) async-start(s8[6291456]{0:T(1024)(128)(4,1)} %bitcast.60), calls=%async_computation.1 | async-start | bytes 8388608
  73.1 19.1 %collective-permute-start.24 = (bf16[2,16,8,256]{3,2,1,0:T(8,128)(2,1)S(1)}, bf16[2,16,8,256]{3,2,1,0:T(8,128)(2,1)S(1)}, u32[]{:S(2)}, u32[]{:S(2)}) collective-permute-start(bf16[2,16,8,256]{3,2,1,0:T(8,128)(2,1)S(1)} %pad_maximum_fusion.4.rest_1_.refs_4_), channel_id=1, source_target_pairs={{0,1},{1,0},{2,3},{3,2},{4,5},{5,4},{6,7},{7,6},{8,9},{9,8},{10,11... | collective-permute-start | bytes 393224 | tf_op jit(solution)/shard_map/ppermute | solution.py:344
  73.2 14.0 %collective-permute-start.22 = (bf16[2,16,8,256]{3,2,1,0:T(8,128)(2,1)S(1)}, bf16[2,16,8,256]{3,2,1,0:T(8,128)(2,1)S(1)}, u32[]{:S(2)}, u32[]{:S(2)}) collective-permute-start(bf16[2,16,8,256]{3,2,1,0:T(8,128)(2,1)S(1)} %pad_maximum_fusion.4.rest_1_.refs_4_), channel_id=1, source_target_pairs={{0,4},{1,5},{2,6},{3,7},{4,0},{5,1},{6,2},{7,3},{8,12},{9,13},{10,... | collective-permute-start | bytes 393224 | tf_op jit(solution)/shard_map/ppermute | solution.py:344
  74.4 12.3 %collective-permute-start.21 = (bf16[2,16,8,256]{3,2,1,0:T(8,128)(2,1)S(1)}, bf16[2,16,8,256]{3,2,1,0:T(8,128)(2,1)S(1)}, u32[]{:S(2)}, u32[]{:S(2)}) collective-permute-start(bf16[2,16,8,256]{3,2,1,0:T(8,128)(2,1)S(1)} %pad_maximum_fusion.4.rest_1_.refs_4_), channel_id=1, source_target_pairs={{0,8},{1,9},{2,10},{3,11},{4,12},{5,13},{6,14},{7,15},{8,0},{9,1},... | collective-permute-start | bytes 393224 | tf_op jit(solution)/shard_map/ppermute | solution.py:344
  76.7 17.1 %slice-start.2 = ((s8[6291456]{0:T(1024)(128)(4,1)}), s8[4194304]{0:T(1024)(128)(4,1)S(1)}, s32[]{:S(2)}) async-start(s8[6291456]{0:T(1024)(128)(4,1)} %bitcast.63), calls=%async_computation.3 | async-start | bytes 8388608
  76.7 15.0 %collective-permute-start.17 = (bf16[4,16,8,256]{3,2,1,0:T(8,128)(2,1)S(1)}, bf16[4,16,8,256]{3,2,1,0:T(8,128)(2,1)S(1)}, u32[]{:S(2)}, u32[]{:S(2)}) collective-permute-start(bf16[4,16,8,256]{3,2,1,0:T(8,128)(2,1)S(1)} %pad_maximum_fusion.2.rest_0_.refs_0_), channel_id=1, source_target_pairs={{0,2},{1,3},{2,0},{3,1},{4,6},{5,7},{6,4},{7,5},{8,10},{9,11},{10,... | collective-permute-start | bytes 786440 | tf_op jit(solution)/shard_map/ppermute | solution.py:344
  77.7 16.1 %slice-start.1 = ((s8[6291456]{0:T(1024)(128)(4,1)}), s8[2097152]{0:T(1024)(128)(4,1)S(1)}, s32[]{:S(2)}) async-start(s8[6291456]{0:T(1024)(128)(4,1)} %bitcast.60), calls=%async_computation.2 | async-start | bytes 4194304
  77.7 16.1 %slice-start.3 = ((s8[6291456]{0:T(1024)(128)(4,1)}), s8[2097152]{0:T(1024)(128)(4,1)S(1)}, s32[]{:S(2)}) async-start(s8[6291456]{0:T(1024)(128)(4,1)} %bitcast.63), calls=%async_computation.4 | async-start | bytes 4194304
  77.7 16.1 %copy-start.5 = (bf16[4096,16]{0,1:T(8,128)(2,1)S(1)}, bf16[4096,16]{0,1:T(8,128)(2,1)}, u32[]{:S(2)}) copy-start(bf16[4096,16]{0,1:T(8,128)(2,1)} %param.21) | copy-start | bytes 393220
  77.7 16.1 %copy-start.6 = (f32[4096]{0:T(1024)S(1)}, f32[4096]{0:T(1024)}, u32[]{:S(2)}) copy-start(f32[4096]{0:T(1024)} %param.20) | copy-start | bytes 49156
  77.7 16.1 %copy-start.7 = (f32[1,4096]{1,0:T(1,128)S(1)}, f32[1,4096]{1,0:T(1,128)}, u32[]{:S(2)}) copy-start(f32[1,4096]{1,0:T(1,128)} %refs_19_.1) | copy-start | bytes 49156
  77.7 16.1 %copy-start.8 = (f32[1,2,768]{2,1,0:T(2,128)S(1)}, f32[1,2,768]{2,1,0:T(2,128)}, u32[]{:S(2)}) copy-start(f32[1,2,768]{2,1,0:T(2,128)} %param.26) | copy-start | bytes 18436
  86.7 5.0 %collective-permute-start.23 = (bf16[2,16,8,256]{3,2,1,0:T(8,128)(2,1)S(1)}, bf16[2,16,8,256]{3,2,1,0:T(8,128)(2,1)S(1)}, u32[]{:S(2)}, u32[]{:S(2)}) collective-permute-start(bf16[2,16,8,256]{3,2,1,0:T(8,128)(2,1)S(1)} %collective-permute-done.21.refs_5_), channel_id=1, source_target_pairs={{0,4},{1,5},{2,6},{3,7},{4,0},{5,1},{6,2},{7,3},{8,12},{9,13},{10,... | collective-permute-start | bytes 393224 | tf_op jit(solution)/shard_map/ppermute | solution.py:344
  87.1 5.9 %collective-permute-start.18 = (bf16[4,16,8,256]{3,2,1,0:T(8,128)(2,1)S(1)}, bf16[4,16,8,256]{3,2,1,0:T(8,128)(2,1)S(1)}, u32[]{:S(2)}, u32[]{:S(2)}) collective-permute-start(bf16[4,16,8,256]{3,2,1,0:T(8,128)(2,1)S(1)} %pad_maximum_fusion.2.rest_0_.refs_0_), channel_id=1, source_target_pairs={{0,1},{1,0},{2,3},{3,2},{4,5},{5,4},{6,7},{7,6},{8,9},{9,8},{10,11... | collective-permute-start | bytes 786440 | tf_op jit(solution)/shard_map/ppermute | solution.py:344
  87.2 5.1 %collective-permute-start.25 = (bf16[2,16,8,256]{3,2,1,0:T(8,128)(2,1)S(1)}, bf16[2,16,8,256]{3,2,1,0:T(8,128)(2,1)S(1)}, u32[]{:S(2)}, u32[]{:S(2)}) collective-permute-start(bf16[2,16,8,256]{3,2,1,0:T(8,128)(2,1)S(1)} %collective-permute-done.21.refs_5_), channel_id=1, source_target_pairs={{0,1},{1,0},{2,3},{3,2},{4,5},{5,4},{6,7},{7,6},{8,9},{9,8},{10,11... | collective-permute-start | bytes 393224 | tf_op jit(solution)/shard_map/ppermute | solution.py:344
  91.7 1.3 %collective-permute-start.26 = (bf16[2,16,8,256]{3,2,1,0:T(8,128)(2,1)S(1)}, bf16[2,16,8,256]{3,2,1,0:T(8,128)(2,1)S(1)}, u32[]{:S(2)}, u32[]{:S(2)}) collective-permute-start(bf16[2,16,8,256]{3,2,1,0:T(8,128)(2,1)S(1)} %collective-permute-done.22.refs_6_), channel_id=1, source_target_pairs={{0,1},{1,0},{2,3},{3,2},{4,5},{5,4},{6,7},{7,6},{8,9},{9,8},{10,11... | collective-permute-start | bytes 393224 | tf_op jit(solution)/shard_map/ppermute | solution.py:344
  91.7 1.5 %collective-permute-start.27 = (bf16[2,16,8,256]{3,2,1,0:T(8,128)(2,1)S(1)}, bf16[2,16,8,256]{3,2,1,0:T(8,128)(2,1)S(1)}, u32[]{:S(2)}, u32[]{:S(2)}) collective-permute-start(bf16[2,16,8,256]{3,2,1,0:T(8,128)(2,1)S(1)} %collective-permute-done.23.refs_7_), channel_id=1, source_target_pairs={{0,1},{1,0},{2,3},{3,2},{4,5},{5,4},{6,7},{7,6},{8,9},{9,8},{10,11... | collective-permute-start | bytes 393224 | tf_op jit(solution)/shard_map/ppermute | solution.py:344
  92.2 1.5 %collective-permute-start.20 = (bf16[4,16,8,256]{3,2,1,0:T(8,128)(2,1)S(1)}, bf16[4,16,8,256]{3,2,1,0:T(8,128)(2,1)S(1)}, u32[]{:S(2)}, u32[]{:S(2)}) collective-permute-start(bf16[4,16,8,256]{3,2,1,0:T(8,128)(2,1)S(1)} %collective-permute-done.17.refs_1_), channel_id=1, source_target_pairs={{0,1},{1,0},{2,3},{3,2},{4,5},{5,4},{6,7},{7,6},{8,9},{9,8},{10,11... | collective-permute-start | bytes 786440 | tf_op jit(solution)/shard_map/ppermute | solution.py:344
  102.7 2.0 %collective-permute-start.28 = (bf16[8,8,4096]{2,1,0:T(8,128)(2,1)S(1)}, bf16[8,8,4096]{2,1,0:T(8,128)(2,1)S(1)}, u32[]{:S(2)}, u32[]{:S(2)}) collective-permute-start(bf16[8,8,4096]{2,1,0:T(8,128)(2,1)S(1)} %get-tuple-element.35), channel_id=1, source_target_pairs={{0,1},{1,0},{2,3},{3,2},{4,5},{5,4},{6,7},{7,6},{8,9},{9,8},{10,11... | collective-permute-start | bytes 1572872 | tf_op jit(solution)/shard_map/ppermute | solution.py:344
  103.0 2.9 %collective-permute-start.32 = (bf16[8,8,4096]{2,1,0:T(8,128)(2,1)S(1)}, bf16[8,8,4096]{2,1,0:T(8,128)(2,1)S(1)}, u32[]{:S(2)}, u32[]{:S(2)}) collective-permute-start(bf16[8,8,4096]{2,1,0:T(8,128)(2,1)S(1)} %get-tuple-element.38), channel_id=1, source_target_pairs={{0,1},{1,0},{2,3},{3,2},{4,5},{5,4},{6,7},{7,6},{8,9},{9,8},{10,11... | collective-permute-start | bytes 1572872 | tf_op jit(solution)/shard_map/ppermute | solution.py:344
  104.8 8.5 %collective-permute-start.29 = (bf16[4,8,4096]{2,1,0:T(8,128)(2,1)S(1)}, bf16[4,8,4096]{2,1,0:T(8,128)(2,1)S(1)}, u32[]{:S(2)}, u32[]{:S(2)}) collective-permute-start(bf16[4,8,4096]{2,1,0:T(8,128)(2,1)S(1)} %get-tuple-element.40), channel_id=1, source_target_pairs={{0,2},{1,3},{2,0},{3,1},{4,6},{5,7},{6,4},{7,5},{8,10},{9,11},{10,... | collective-permute-start | bytes 786440 | tf_op jit(solution)/shard_map/ppermute | solution.py:344
  106.1 8.2 %collective-permute-start.33 = (bf16[4,8,4096]{2,1,0:T(8,128)(2,1)S(1)}, bf16[4,8,4096]{2,1,0:T(8,128)(2,1)S(1)}, u32[]{:S(2)}, u32[]{:S(2)}) collective-permute-start(bf16[4,8,4096]{2,1,0:T(8,128)(2,1)S(1)} %get-tuple-element.42), channel_id=1, source_target_pairs={{0,4},{1,5},{2,6},{3,7},{4,0},{5,1},{6,2},{7,3},{8,12},{9,13},{10,... | collective-permute-start | bytes 786440 | tf_op jit(solution)/shard_map/ppermute | solution.py:344
  113.4 7.2 %collective-permute-start.30 = (bf16[2,8,4096]{2,1,0:T(8,128)(2,1)S(1)}, bf16[2,8,4096]{2,1,0:T(8,128)(2,1)S(1)}, u32[]{:S(2)}, u32[]{:S(2)}) collective-permute-start(bf16[2,8,4096]{2,1,0:T(8,128)(2,1)S(1)} %get-tuple-element.44), channel_id=1, source_target_pairs={{0,4},{1,5},{2,6},{3,7},{4,0},{5,1},{6,2},{7,3},{8,12},{9,13},{10,... | collective-permute-start | bytes 393224 | tf_op jit(solution)/shard_map/ppermute | solution.py:344
  114.3 9.7 %collective-permute-start.34 = (bf16[2,8,4096]{2,1,0:T(8,128)(2,1)S(1)}, bf16[2,8,4096]{2,1,0:T(8,128)(2,1)S(1)}, u32[]{:S(2)}, u32[]{:S(2)}) collective-permute-start(bf16[2,8,4096]{2,1,0:T(8,128)(2,1)S(1)} %get-tuple-element.46), channel_id=1, source_target_pairs={{0,8},{1,9},{2,10},{3,11},{4,12},{5,13},{6,14},{7,15},{8,0},{9,1},... | collective-permute-start | bytes 393224 | tf_op jit(solution)/shard_map/ppermute | solution.py:344
  120.6 5.2 %collective-permute-start.31 = (bf16[1,8,4096]{2,1,0:T(8,128)(2,1)S(1)}, bf16[1,8,4096]{2,1,0:T(8,128)(2,1)S(1)}, u32[]{:S(2)}, u32[]{:S(2)}) collective-permute-start(bf16[1,8,4096]{2,1,0:T(8,128)(2,1)S(1)} %add_convert_fusion.10), channel_id=1, source_target_pairs={{0,8},{1,9},{2,10},{3,11},{4,12},{5,13},{6,14},{7,15},{8,0},{9,1},... | collective-permute-start | bytes 196616 | tf_op jit(solution)/shard_map/ppermute | solution.py:344
  124.0 4.3 %collective-permute-start.35 = (bf16[1,8,4096]{2,1,0:T(8,128)(2,1)S(1)}, bf16[1,8,4096]{2,1,0:T(8,128)(2,1)S(1)}, u32[]{:S(2)}, u32[]{:S(2)}) collective-permute-start(bf16[1,8,4096]{2,1,0:T(8,128)(2,1)S(1)} %add_convert_fusion.8), channel_id=1, source_target_pairs={{0,2},{1,3},{2,0},{3,1},{4,6},{5,7},{6,4},{7,5},{8,10},{9,11},{10,... | collective-permute-start | bytes 196616 | tf_op jit(solution)/shard_map/ppermute | solution.py:344

commit v4 on v3

--- a/solution.py
+++ b/solution.py
@@ -93,8 +93,7 @@
     )(lengths, queries, pltpu.with_memory_space_constraint(kv_cache, pltpu.HBM))
 
 
-def expand_kernel(stacked, table_ref, code_ref, *rest):
-    out_ref = rest[-1]
+def expand_kernel(stacked, table_ref, code_ref, out_ref):
     rows, columns = code_ref.shape
     tile = 16
     tables = [jnp.broadcast_to(table_ref[i : i + 1], (tile, LANES)) for i in range(8)]
@@ -144,8 +143,7 @@
     out = pl.pallas_call(
         functools.partial(expand_kernel, stacked),
         grid=grid,
-        in_specs=[pl.BlockSpec((8, LANES), lambda b: (0, 0)), code_spec]
-        + [pl.BlockSpec(memory_space=pl.ANY) for _ in after],
+        in_specs=[pl.BlockSpec((8, LANES), lambda b: (0, 0)), code_spec],
         out_specs=out_spec,
         out_shape=jax.ShapeDtypeStruct(out_shape, jnp.bfloat16),
         name="expand",
@@ -153,7 +151,7 @@
         cost_estimate=pl.CostEstimate(
             flops=rows * columns * 8000, bytes_accessed=10 * rows * columns, transcendentals=0
         ),
-    )(table, pltpu.with_memory_space_constraint(codes, pltpu.HBM), *after)
+    )(tie(table, *after), pltpu.with_memory_space_constraint(codes, pltpu.HBM))
     return out.reshape(4 * rows, columns) if stacked else out
 
 

time: 130 us -> 127 us (0.977)
  waiting for transfers between devices: 32.9 us -> 31.4 us
    unnamed x36 -> x34, local copies, waits for them, and re-layouts: 9.79 us -> 7.01 us
    ppermute x36, waiting for transfers between devices: 32.9 us -> 31.4 us  [swap(): return lax.ppermute(value, 'expert', [(i, i ^ bit) for i in range(count)])]
  transfers between devices with their start and end apart: 37 -> 37, of which waited for: 16 -> 17; matrix products, arithmetic and copies ran while one was open for 1% -> 3% of each run, Pallas kernels for 24% -> 24%
where the time goes in v4:
time: 127 us
  Pallas kernels  48.1 us (38%)
  starting transfers between devices  35.9 us (28%)
  waiting for transfers between devices  31.4 us (25%)
  local copies, waits for them, and re-layouts  8.83 us (7%)
  other arithmetic  2.13 us (2%)
    ppermute x36, starting transfers between devices, swap(): return lax.ppermute(value, 'expert', [(i, i ^ bit) for i in range(count)])  31.7 us
    ppermute x36, waiting for transfers between devices, swap(): return lax.ppermute(value, 'expert', [(i, i ^ bit) for i in range(count)])  31.4 us
    pallas_call x3, Pallas kernels, expand(): pl.pallas_call(functools.partial(expand_kernel, stacked), grid=grid, in_s...  26.7 us
    pallas_call x1, Pallas kernels, run_experts(): pl.pallas_call(functools.partial(experts_kernel, masks, counts, orders),...  8.77 us
    pallas_call x2, Pallas kernels, attend(): pl.pallas_call(functools.partial(attend_kernel, micro, span, KV_HEADS), g...  8.19 us
    unnamed x34, local copies, waits for them, and re-layouts  7.01 us
    pallas_call x1, Pallas kernels, project(): pl.pallas_call(functools.partial(project_kernel, masks, counts), grid_spe...  4.48 us
    all_to_all x1, starting transfers between devices, body(): lax.all_to_all(jnp.concatenate([lead, tail], axis=-1), 'expert', split_ax...  4.17 us
  transfers between devices with their start and end apart: 37, of which 17 were waited for; matrix products, arithmetic and copies ran while one was open for 3% of the time, Pallas kernels for 24%

profile of v4, /device:TPU:0, one launch (start us, length us, event | category | flops | bytes accessed | tf_op | source)
XLA Modules:
  0.0 126.7 jit_solution(10657544925251739886)
XLA Ops:
  0.0 0.9 copy-done.2
  1.0 0.7 copy-done.8
  1.7 4.1 %attend.2 = bf16[8,8192]{1,0:T(8,128)(2,1)S(1)} custom-call(s32[2,8]{1,0:T(2,128)S(1)} %copy-done.8, bf16[2,8,8192]{2,1,0:T(8,128)(2,1)S(1)} %copy-done.2, bf16[2,8,128,2,512]{4,3,2,1,0:T(2,128)(2,1)} %kv_ref.3), custom_call_target="tpu_custom_call" | custom-call | flops 67108864 | bytes 2097152 | tf_op jit(solution)/shard_map/attend/pallas_call | solution.py:75
  5.8 3.1 %collective-permute-start.1 = (bf16[8,8192]{1,0:T(8,128)(2,1)S(1)}, bf16[8,8192]{1,0:T(8,128)(2,1)S(1)}, u32[]{:S(2)}, u32[]{:S(2)}) collective-permute-start(bf16[8,8192]{1,0:T(8,128)(2,1)S(1)} %attend.2), channel_id=1, source_target_pairs={{0,4},{1,5},{2,6},{3,7},{4,0},{5,1},{6,2},{7,3},{8,12},{9,13},{10,... | collective-permute-start | bytes 393224 | tf_op jit(solution)/shard_map/ppermute | solution.py:342
  8.8 2.6 %collective-permute-start = (bf16[8,8192]{1,0:T(8,128)(2,1)S(1)}, bf16[8,8192]{1,0:T(8,128)(2,1)S(1)}, u32[]{:S(2)}, u32[]{:S(2)}) collective-permute-start(bf16[8,8192]{1,0:T(8,128)(2,1)S(1)} %attend.2), channel_id=1, source_target_pairs={{0,8},{1,9},{2,10},{3,11},{4,12},{5,13},{6,14},{7,15},{8,0},{9,1},... | collective-permute-start | bytes 393224 | tf_op jit(solution)/shard_map/ppermute | solution.py:342
  11.4 0.1 fusion.4
  11.6 0.7 pad_maximum_fusion.3
  12.3 4.2 %all-to-all-start = ((bf16[16,2,8,272]{3,2,1,0:T(8,128)(2,1)}), bf16[16,2,8,272]{3,2,1,0:T(8,128)(2,1)}, u32[]{:S(2)}, u32[]{:S(2)}) async-start(bf16[16,2,8,272]{3,2,1,0:T(8,128)(2,1)} %pad_maximum_fusion.3), calls=%async_computation | async-start | bytes 393216 | tf_op jit(solution)/shard_map/all_to_all | solution.py:426
  16.5 4.1 %attend.3 = bf16[8,8192]{1,0:T(8,128)(2,1)S(1)} custom-call(s32[2,8]{1,0:T(2,128)S(1)} %copy-done.9, bf16[2,8,8192]{2,1,0:T(8,128)(2,1)S(1)} %copy-done.3, bf16[2,8,128,2,512]{4,3,2,1,0:T(2,128)(2,1)} %kv_ref.3), custom_call_target="tpu_custom_call" | custom-call | flops 67108864 | bytes 2097152 | tf_op jit(solution)/shard_map/attend/pallas_call | solution.py:75
  20.6 1.8 %collective-permute-start.5 = (bf16[8,8192]{1,0:T(8,128)(2,1)S(1)}, bf16[8,8192]{1,0:T(8,128)(2,1)S(1)}, u32[]{:S(2)}, u32[]{:S(2)}) collective-permute-start(bf16[8,8192]{1,0:T(8,128)(2,1)S(1)} %attend.3), channel_id=1, source_target_pairs={{0,2},{1,3},{2,0},{3,1},{4,6},{5,7},{6,4},{7,5},{8,10},{9,11},{10,... | collective-permute-start | bytes 393224 | tf_op jit(solution)/shard_map/ppermute | solution.py:342
  22.5 1.6 %collective-permute-start.2 = (bf16[8,8192]{1,0:T(8,128)(2,1)S(1)}, bf16[8,8192]{1,0:T(8,128)(2,1)S(1)}, u32[]{:S(2)}, u32[]{:S(2)}) collective-permute-start(bf16[8,8192]{1,0:T(8,128)(2,1)S(1)} %collective-permute-done), channel_id=1, source_target_pairs={{0,4},{1,5},{2,6},{3,7},{4,0},{5,1},{6,2},{7,3},{8,12},{9,13},{10,... | collective-permute-start | bytes 393224 | tf_op jit(solution)/shard_map/ppermute | solution.py:342
  24.0 2.8 %collective-permute-done.5 = bf16[8,8192]{1,0:T(8,128)(2,1)S(1)} collective-permute-done((bf16[8,8192]{1,0:T(8,128)(2,1)S(1)}, bf16[8,8192]{1,0:T(8,128)(2,1)S(1)}, u32[]{:S(2)}, u32[]{:S(2)}) %collective-permute-start.5) | collective-permute-done | bytes 131104 | tf_op jit(solution)/shard_map/ppermute | solution.py:342
  26.9 0.1 collective-permute-start.10
  26.9 1.4 %collective-permute-start.8 = (bf16[2,8,8192]{2,1,0:T(8,128)(2,1)S(1)}, bf16[2,8,8192]{2,1,0:T(8,128)(2,1)S(1)}, u32[]{:S(2)}, u32[]{:S(2)}) collective-permute-start(bf16[2,8,8192]{2,1,0:T(8,128)(2,1)S(1)} %pad_maximum_fusion.1.refs_4_), channel_id=1, source_target_pairs={{0,4},{1,5},{2,6},{3,7},{4,0},{5,1},{6,2},{7,3},{8,12},{9,13},{10,... | collective-permute-start | bytes 786440 | tf_op jit(solution)/shard_map/ppermute | solution.py:342
  28.4 2.2 %collective-permute-start.6 = (bf16[2,8,8192]{2,1,0:T(8,128)(2,1)S(1)}, bf16[2,8,8192]{2,1,0:T(8,128)(2,1)S(1)}, u32[]{:S(2)}, u32[]{:S(2)}) collective-permute-start(bf16[2,8,8192]{2,1,0:T(8,128)(2,1)S(1)} %pad_maximum_fusion.1.refs_4_), channel_id=1, source_target_pairs={{0,8},{1,9},{2,10},{3,11},{4,12},{5,13},{6,14},{7,15},{8,0},{9,1},... | collective-permute-start | bytes 786440 | tf_op jit(solution)/shard_map/ppermute | solution.py:342
  30.7 1.5 %collective-permute-start.3 = (bf16[4,8,8192]{2,1,0:T(8,128)(2,1)S(1)}, bf16[4,8,8192]{2,1,0:T(8,128)(2,1)S(1)}, u32[]{:S(2)}, u32[]{:S(2)}) collective-permute-start(bf16[4,8,8192]{2,1,0:T(8,128)(2,1)S(1)} %pad_maximum_fusion.refs_0_), channel_id=1, source_target_pairs={{0,2},{1,3},{2,0},{3,1},{4,6},{5,7},{6,4},{7,5},{8,10},{9,11},{10,... | collective-permute-start | bytes 1572872 | tf_op jit(solution)/shard_map/ppermute | solution.py:342
  32.3 8.9 %expand.3 = bf16[4,192,4096]{2,1,0:T(8,128)(2,1)S(1)} custom-call(f32[8,128]{1,0:T(8,128)S(1)} %squeeze.33.table_ref, bf16[192,4096]{1,0:T(8,128)(2,1)} %bitcast.82), custom_call_target="tpu_custom_call" | custom-call | flops 6291456000 | bytes 7864320 | tf_op jit(solution)/shard_map/expand/pallas_call | solution.py:143
  41.2 2.6 %copy-done = bf16[4,192,4096]{2,1,0:T(8,128)(2,1)} copy-done((bf16[4,192,4096]{2,1,0:T(8,128)(2,1)}, bf16[4,192,4096]{2,1,0:T(8,128)(2,1)S(1)}, u32[]{:S(2)}) %copy-start) | copy-done | bytes 6291480
  43.8 0.5 collective-permute-start.9
  44.3 8.8 %expand.4 = bf16[4,192,4096]{2,1,0:T(8,128)(2,1)S(1)} custom-call(f32[8,128]{1,0:T(8,128)S(1)} %squeeze.32.table_ref, bf16[192,4096]{1,0:T(8,128)(2,1)} %bitcast.83), custom_call_target="tpu_custom_call" | custom-call | flops 6291456000 | bytes 7864320 | tf_op jit(solution)/shard_map/expand/pallas_call | solution.py:143
  53.2 2.7 %copy-done.1 = bf16[4,192,4096]{2,1,0:T(8,128)(2,1)} copy-done((bf16[4,192,4096]{2,1,0:T(8,128)(2,1)}, bf16[4,192,4096]{2,1,0:T(8,128)(2,1)S(1)}, u32[]{:S(2)}) %copy-start.1) | copy-done | bytes 6291480
  55.9 0.5 collective-permute-start.11
  56.5 0.4 collective-permute-start.13
  56.9 0.9 slice.131.refs_13_
  57.8 0.5 collective-permute-done.11.refs_9_
  58.3 0.4 collective-permute-done.12.refs_10_
  58.7 0.4 collective-permute-done.13.refs_11_
  59.1 4.5 %project.1 = (bf16[16,8,256]{2,1,0:T(8,128)(2,1)S(1)}, bf16[16,8,256]{2,1,0:T(8,128)(2,1)S(1)}) custom-call(s32[1]{0:T(128)} %bitcast.me_ref, bf16[4,8,8192]{2,1,0:T(8,128)(2,1)S(1)} %pad_maximum_fusion.refs_0_, bf16[4,8,8192]{2,1,0:T(8,128)(2,1)S(1)} %collective-permute-done.3.refs_1_, bf16[4,8,8192]{2,1,0:T(8,128)(2,1)S(1)} %collective-permute-done.4.refs_2_, ...), custom_call_target="tpu_custom_call" | custom-call | flops 1073741824 | bytes 4194304 | tf_op jit(solution)/shard_map/project/pallas_call | solution.py:194
  63.6 1.8 %collective-permute-start.14 = (bf16[16,8,256]{2,1,0:T(8,128)(2,1)S(1)}, bf16[16,8,256]{2,1,0:T(8,128)(2,1)S(1)}, u32[]{:S(2)}, u32[]{:S(2)}) collective-permute-start(bf16[16,8,256]{2,1,0:T(8,128)(2,1)S(1)} %get-tuple-element.32), channel_id=1, source_target_pairs={{0,8},{1,9},{2,10},{3,11},{4,12},{5,13},{6,14},{7,15},{8,0},{9,1},... | collective-permute-start | bytes 196616 | tf_op jit(solution)/shard_map/ppermute | solution.py:342
  65.3 1.5 %collective-permute-start.19 = (bf16[16,8,256]{2,1,0:T(8,128)(2,1)S(1)}, bf16[16,8,256]{2,1,0:T(8,128)(2,1)S(1)}, u32[]{:S(2)}, u32[]{:S(2)}) collective-permute-start(bf16[16,8,256]{2,1,0:T(8,128)(2,1)S(1)} %get-tuple-element.33), channel_id=1, source_target_pairs={{0,2},{1,3},{2,0},{3,1},{4,6},{5,7},{6,4},{7,5},{8,10},{9,11},{10,... | collective-permute-start | bytes 196616 | tf_op jit(solution)/shard_map/ppermute | solution.py:342
  66.8 3.2 %collective-permute-done.14 = bf16[16,8,256]{2,1,0:T(8,128)(2,1)S(1)} collective-permute-done((bf16[16,8,256]{2,1,0:T(8,128)(2,1)S(1)}, bf16[16,8,256]{2,1,0:T(8,128)(2,1)S(1)}, u32[]{:S(2)}, u32[]{:S(2)}) %collective-permute-start.14) | collective-permute-done | bytes 65568 | tf_op jit(solution)/shard_map/ppermute | solution.py:342
  70.0 0.9 collective-permute-start.16
  70.9 1.2 collective-permute-start.22
  72.2 0.9 collective-permute-start.21
  73.1 1.4 %collective-permute-done.16 = bf16[16,8,256]{2,1,0:T(8,128)(2,1)S(1)} collective-permute-done((bf16[16,8,256]{2,1,0:T(8,128)(2,1)S(1)}, bf16[16,8,256]{2,1,0:T(8,128)(2,1)S(1)}, u32[]{:S(2)}, u32[]{:S(2)}) %collective-permute-start.16) | collective-permute-done | bytes 65568 | tf_op jit(solution)/shard_map/ppermute | solution.py:342
  74.6 0.9 collective-permute-start.17
  75.5 9.0 %expand.5.refs_17_ = bf16[768,4096]{1,0:T(8,128)(2,1)S(1)} custom-call(f32[8,128]{1,0:T(8,128)S(1)} %squeeze.36.table_ref, bf16[768,1024]{1,0:T(8,128)(2,1)} %bitcast.84), custom_call_target="tpu_custom_call" | custom-call | flops 6291456000 | bytes 7864320 | tf_op jit(solution)/shard_map/expand/pallas_call | solution.py:143
  84.5 0.5 collective-permute-start.23
  84.9 0.8 slice_bitcast_fusion
  85.8 0.5 collective-permute-start.25
  86.3 3.2 %collective-permute-done.23.refs_7_ = bf16[2,16,8,256]{3,2,1,0:T(8,128)(2,1)S(1)} collective-permute-done((bf16[2,16,8,256]{3,2,1,0:T(8,128)(2,1)S(1)}, bf16[2,16,8,256]{3,2,1,0:T(8,128)(2,1)S(1)}, u32[]{:S(2)}, u32[]{:S(2)}) %collective-permute-start.23) | collective-permute-done | bytes 131104 | tf_op jit(solution)/shard_map/ppermute | solution.py:342
  89.5 0.5 collective-permute-start.27
  90.2 0.7 collective-permute-done.26.refs_10_
  90.9 0.2 collective-permute-done.27.refs_11_
  91.1 0.5 collective-permute-done.20.refs_3_
  91.7 8.8 %experts.1 = (bf16[8,8,4096]{2,1,0:T(8,128)(2,1)S(1)}, bf16[8,8,4096]{2,1,0:T(8,128)(2,1)S(1)}, bf16[8,8,4096]{2,1,0:T(8,128)(2,1)S(1)}, bf16[8,8,4096]{2,1,0:T(...) custom-call(s32[1]{0:T(128)} %bitcast.me_ref, ...), custom_call_target="tpu_custom_call" | custom-call | flops 4831838208 | bytes 18874368 | tf_op jit(solution)/shard_map/experts/pallas_call | solution.py:319
  100.4 0.3 collective-permute-start.28
  100.7 0.3 collective-permute-start.32
  101.0 1.4 %collective-permute-done.28 = bf16[8,8,4096]{2,1,0:T(8,128)(2,1)S(1)} collective-permute-done((bf16[8,8,4096]{2,1,0:T(8,128)(2,1)S(1)}, bf16[8,8,4096]{2,1,0:T(8,128)(2,1)S(1)}, u32[]{:S(2)}, u32[]{:S(2)}) %collective-permute-start.28) | collective-permute-done | bytes 524320 | tf_op jit(solution)/shard_map/ppermute | solution.py:342
  102.4 0.1 add_convert_fusion.3
  102.5 1.1 collective-permute-start.29
  103.6 0.1 add_convert_fusion.1
  103.7 0.7 collective-permute-start.33
  104.4 6.6 %collective-permute-done.29 = bf16[4,8,4096]{2,1,0:T(8,128)(2,1)S(1)} collective-permute-done((bf16[4,8,4096]{2,1,0:T(8,128)(2,1)S(1)}, bf16[4,8,4096]{2,1,0:T(8,128)(2,1)S(1)}, u32[]{:S(2)}, u32[]{:S(2)}) %collective-permute-start.29) | collective-permute-done | bytes 262176 | tf_op jit(solution)/shard_map/ppermute | solution.py:342
  111.1 0.4 collective-permute-start.30
  111.5 0.4 collective-permute-done.33
  112.0 1.9 %collective-permute-start.34 = (bf16[2,8,4096]{2,1,0:T(8,128)(2,1)S(1)}, bf16[2,8,4096]{2,1,0:T(8,128)(2,1)S(1)}, u32[]{:S(2)}, u32[]{:S(2)}) collective-permute-start(bf16[2,8,4096]{2,1,0:T(8,128)(2,1)S(1)} %get-tuple-element.52), channel_id=1, source_target_pairs={{0,8},{1,9},{2,10},{3,11},{4,12},{5,13},{6,14},{7,15},{8,0},{9,1},... | collective-permute-start | bytes 393224 | tf_op jit(solution)/shard_map/ppermute | solution.py:342
  113.9 4.4 %collective-permute-done.30 = bf16[2,8,4096]{2,1,0:T(8,128)(2,1)S(1)} collective-permute-done((bf16[2,8,4096]{2,1,0:T(8,128)(2,1)S(1)}, bf16[2,8,4096]{2,1,0:T(8,128)(2,1)S(1)}, u32[]{:S(2)}, u32[]{:S(2)}) %collective-permute-start.30) | collective-permute-done | bytes 131104 | tf_op jit(solution)/shard_map/ppermute | solution.py:342
  118.3 1.3 %collective-permute-start.31 = (bf16[1,8,4096]{2,1,0:T(8,128)(2,1)S(1)}, bf16[1,8,4096]{2,1,0:T(8,128)(2,1)S(1)}, u32[]{:S(2)}, u32[]{:S(2)}) collective-permute-start(bf16[1,8,4096]{2,1,0:T(8,128)(2,1)S(1)} %add_convert_fusion.10), channel_id=1, source_target_pairs={{0,8},{1,9},{2,10},{3,11},{4,12},{5,13},{6,14},{7,15},{8,0},{9,1},... | collective-permute-start | bytes 196616 | tf_op jit(solution)/shard_map/ppermute | solution.py:342
  119.6 2.0 %collective-permute-done.34 = bf16[2,8,4096]{2,1,0:T(8,128)(2,1)S(1)} collective-permute-done((bf16[2,8,4096]{2,1,0:T(8,128)(2,1)S(1)}, bf16[2,8,4096]{2,1,0:T(8,128)(2,1)S(1)}, u32[]{:S(2)}, u32[]{:S(2)}) %collective-permute-start.34) | collective-permute-done | bytes 131104 | tf_op jit(solution)/shard_map/ppermute | solution.py:342
  121.7 1.0 collective-permute-start.35
  122.7 0.8 collective-permute-done.31
  123.6 2.4 %collective-permute-done.35 = bf16[1,8,4096]{2,1,0:T(8,128)(2,1)S(1)} collective-permute-done((bf16[1,8,4096]{2,1,0:T(8,128)(2,1)S(1)}, bf16[1,8,4096]{2,1,0:T(8,128)(2,1)S(1)}, u32[]{:S(2)}, u32[]{:S(2)}) %collective-permute-start.35) | collective-permute-done | bytes 65568 | tf_op jit(solution)/shard_map/ppermute | solution.py:342
  126.1 0.7 pad_maximum_fusion.5
  (80 shorter events, 0.9 us)
Async XLA Ops:
  0.0 0.9 copy-start.2
  1.0 0.7 copy-start.8
  1.6 9.8 %copy-start.11 = (s32[2,8,8]{2,1,0:T(8,128)S(1)}, s32[2,8,8]{2,1,0:T(8,128)}, u32[]{:S(2)}) copy-start(s32[2,8,8]{2,1,0:T(8,128)} %param.18) | copy-start | bytes 1540
  1.6 9.9 %copy-start.10 = (bf16[2,8,4096]{2,1,0:T(8,128)(2,1)S(1)}, bf16[2,8,4096]{2,1,0:T(8,128)(2,1)}, u32[]{:S(2)}) copy-start(bf16[2,8,4096]{2,1,0:T(8,128)(2,1)} %param.14) | copy-start | bytes 393220
  1.6 14.8 %copy-start.3 = (bf16[2,8,8192]{2,1,0:T(8,128)(2,1)S(1)}, bf16[2,8,8192]{2,1,0:T(8,128)(2,1)}, u32[]{:S(2)}) copy-start(bf16[2,8,8192]{2,1,0:T(8,128)(2,1)} %q_ref.3) | copy-start | bytes 786436
  1.6 14.9 %copy-start.9 = (s32[2,8]{1,0:T(2,128)S(1)}, s32[2,8]{1,0:T(2,128)}, u32[]{:S(2)}) copy-start(s32[2,8]{1,0:T(2,128)} %len_ref.3) | copy-start | bytes 196
  1.6 20.8 %copy-start.12 = (bf16[1,3,256,4]{2,3,1,0:T(4,128)(2,1)S(1)}, bf16[1,3,256,4]{2,3,1,0:T(4,128)(2,1)}, u32[]{:S(2)}) copy-start(bf16[1,3,256,4]{2,3,1,0:T(4,128)(2,1)} %param.25) | copy-start | bytes 18436
  5.8 24.8 %collective-permute-start.1 = (bf16[8,8192]{1,0:T(8,128)(2,1)S(1)}, bf16[8,8192]{1,0:T(8,128)(2,1)S(1)}, u32[]{:S(2)}, u32[]{:S(2)}) collective-permute-start(bf16[8,8192]{1,0:T(8,128)(2,1)S(1)} %attend.2), channel_id=1, source_target_pairs={{0,4},{1,5},{2,6},{3,7},{4,0},{5,1},{6,2},{7,3},{8,12},{9,13},{10,... | collective-permute-start | bytes 393224 | tf_op jit(solution)/shard_map/ppermute | solution.py:342
  8.8 13.6 %collective-permute-start = (bf16[8,8192]{1,0:T(8,128)(2,1)S(1)}, bf16[8,8192]{1,0:T(8,128)(2,1)S(1)}, u32[]{:S(2)}, u32[]{:S(2)}) collective-permute-start(bf16[8,8192]{1,0:T(8,128)(2,1)S(1)} %attend.2), channel_id=1, source_target_pairs={{0,8},{1,9},{2,10},{3,11},{4,12},{5,13},{6,14},{7,15},{8,0},{9,1},... | collective-permute-start | bytes 393224 | tf_op jit(solution)/shard_map/ppermute | solution.py:342
  12.3 31.5 %all-to-all-start = ((bf16[16,2,8,272]{3,2,1,0:T(8,128)(2,1)}), bf16[16,2,8,272]{3,2,1,0:T(8,128)(2,1)}, u32[]{:S(2)}, u32[]{:S(2)}) async-start(bf16[16,2,8,272]{3,2,1,0:T(8,128)(2,1)} %pad_maximum_fusion.3), calls=%async_computation | async-start | bytes 393216 | tf_op jit(solution)/shard_map/all_to_all | solution.py:426
  20.6 6.2 %collective-permute-start.5 = (bf16[8,8192]{1,0:T(8,128)(2,1)S(1)}, bf16[8,8192]{1,0:T(8,128)(2,1)S(1)}, u32[]{:S(2)}, u32[]{:S(2)}) collective-permute-start(bf16[8,8192]{1,0:T(8,128)(2,1)S(1)} %attend.3), channel_id=1, source_target_pairs={{0,2},{1,3},{2,0},{3,1},{4,6},{5,7},{6,4},{7,5},{8,10},{9,11},{10,... | collective-permute-start | bytes 393224 | tf_op jit(solution)/shard_map/ppermute | solution.py:342
  22.5 8.1 %collective-permute-start.2 = (bf16[8,8192]{1,0:T(8,128)(2,1)S(1)}, bf16[8,8192]{1,0:T(8,128)(2,1)S(1)}, u32[]{:S(2)}, u32[]{:S(2)}) collective-permute-start(bf16[8,8192]{1,0:T(8,128)(2,1)S(1)} %collective-permute-done), channel_id=1, source_target_pairs={{0,4},{1,5},{2,6},{3,7},{4,0},{5,1},{6,2},{7,3},{8,12},{9,13},{10,... | collective-permute-start | bytes 393224 | tf_op jit(solution)/shard_map/ppermute | solution.py:342
  26.9 29.6 %collective-permute-start.10 = (bf16[2,8,8192]{2,1,0:T(8,128)(2,1)S(1)}, bf16[2,8,8192]{2,1,0:T(8,128)(2,1)S(1)}, u32[]{:S(2)}, u32[]{:S(2)}) collective-permute-start(bf16[2,8,8192]{2,1,0:T(8,128)(2,1)S(1)} %pad_maximum_fusion.1.refs_4_), channel_id=1, source_target_pairs={{0,1},{1,0},{2,3},{3,2},{4,5},{5,4},{6,7},{7,6},{8,9},{9,8},{10,11... | collective-permute-start | bytes 786440 | tf_op jit(solution)/shard_map/ppermute | solution.py:342
  26.9 29.0 %collective-permute-start.8 = (bf16[2,8,8192]{2,1,0:T(8,128)(2,1)S(1)}, bf16[2,8,8192]{2,1,0:T(8,128)(2,1)S(1)}, u32[]{:S(2)}, u32[]{:S(2)}) collective-permute-start(bf16[2,8,8192]{2,1,0:T(8,128)(2,1)S(1)} %pad_maximum_fusion.1.refs_4_), channel_id=1, source_target_pairs={{0,4},{1,5},{2,6},{3,7},{4,0},{5,1},{6,2},{7,3},{8,12},{9,13},{10,... | collective-permute-start | bytes 786440 | tf_op jit(solution)/shard_map/ppermute | solution.py:342
  28.4 15.4 %collective-permute-start.6 = (bf16[2,8,8192]{2,1,0:T(8,128)(2,1)S(1)}, bf16[2,8,8192]{2,1,0:T(8,128)(2,1)S(1)}, u32[]{:S(2)}, u32[]{:S(2)}) collective-permute-start(bf16[2,8,8192]{2,1,0:T(8,128)(2,1)S(1)} %pad_maximum_fusion.1.refs_4_), channel_id=1, source_target_pairs={{0,8},{1,9},{2,10},{3,11},{4,12},{5,13},{6,14},{7,15},{8,0},{9,1},... | collective-permute-start | bytes 786440 | tf_op jit(solution)/shard_map/ppermute | solution.py:342
  30.7 28.0 %collective-permute-start.4 = (bf16[4,8,8192]{2,1,0:T(8,128)(2,1)S(1)}, bf16[4,8,8192]{2,1,0:T(8,128)(2,1)S(1)}, u32[]{:S(2)}, u32[]{:S(2)}) collective-permute-start(bf16[4,8,8192]{2,1,0:T(8,128)(2,1)S(1)} %pad_maximum_fusion.refs_0_), channel_id=1, source_target_pairs={{0,1},{1,0},{2,3},{3,2},{4,5},{5,4},{6,7},{7,6},{8,9},{9,8},{10,11... | collective-permute-start | bytes 1572872 | tf_op jit(solution)/shard_map/ppermute | solution.py:342
  30.7 25.2 %collective-permute-start.3 = (bf16[4,8,8192]{2,1,0:T(8,128)(2,1)S(1)}, bf16[4,8,8192]{2,1,0:T(8,128)(2,1)S(1)}, u32[]{:S(2)}, u32[]{:S(2)}) collective-permute-start(bf16[4,8,8192]{2,1,0:T(8,128)(2,1)S(1)} %pad_maximum_fusion.refs_0_), channel_id=1, source_target_pairs={{0,2},{1,3},{2,0},{3,1},{4,6},{5,7},{6,4},{7,5},{8,10},{9,11},{10,... | collective-permute-start | bytes 1572872 | tf_op jit(solution)/shard_map/ppermute | solution.py:342
  41.1 2.7 %copy-start = (bf16[4,192,4096]{2,1,0:T(8,128)(2,1)}, bf16[4,192,4096]{2,1,0:T(8,128)(2,1)S(1)}, u32[]{:S(2)}) copy-start(bf16[4,192,4096]{2,1,0:T(8,128)(2,1)S(1)} %expand.3) | copy-start | bytes 18874372
  43.8 12.6 %collective-permute-start.9 = (bf16[2,8,8192]{2,1,0:T(8,128)(2,1)S(1)}, bf16[2,8,8192]{2,1,0:T(8,128)(2,1)S(1)}, u32[]{:S(2)}, u32[]{:S(2)}) collective-permute-start(bf16[2,8,8192]{2,1,0:T(8,128)(2,1)S(1)} %collective-permute-done.6.refs_5_), channel_id=1, source_target_pairs={{0,4},{1,5},{2,6},{3,7},{4,0},{5,1},{6,2},{7,3},{8,12},{9,13},{10,... | collective-permute-start | bytes 786440 | tf_op jit(solution)/shard_map/ppermute | solution.py:342
  53.2 2.7 %copy-start.1 = (bf16[4,192,4096]{2,1,0:T(8,128)(2,1)}, bf16[4,192,4096]{2,1,0:T(8,128)(2,1)S(1)}, u32[]{:S(2)}) copy-start(bf16[4,192,4096]{2,1,0:T(8,128)(2,1)S(1)} %expand.4) | copy-start | bytes 18874372
  55.9 3.2 %collective-permute-start.7 = (bf16[4,8,8192]{2,1,0:T(8,128)(2,1)S(1)}, bf16[4,8,8192]{2,1,0:T(8,128)(2,1)S(1)}, u32[]{:S(2)}, u32[]{:S(2)}) collective-permute-start(bf16[4,8,8192]{2,1,0:T(8,128)(2,1)S(1)} %collective-permute-done.3.refs_1_), channel_id=1, source_target_pairs={{0,1},{1,0},{2,3},{3,2},{4,5},{5,4},{6,7},{7,6},{8,9},{9,8},{10,11... | collective-permute-start | bytes 1572872 | tf_op jit(solution)/shard_map/ppermute | solution.py:342
  55.9 2.4 %collective-permute-start.11 = (bf16[2,8,8192]{2,1,0:T(8,128)(2,1)S(1)}, bf16[2,8,8192]{2,1,0:T(8,128)(2,1)}, u32[]{:S(2)}, u32[]{:S(2)}) collective-permute-start(bf16[2,8,8192]{2,1,0:T(8,128)(2,1)S(1)} %collective-permute-done.6.refs_5_), channel_id=1, source_target_pairs={{0,1},{1,0},{2,3},{3,2},{4,5},{5,4},{6,7},{7,6},{8,9},{9,8},{10,11... | collective-permute-start | bytes 786440 | tf_op jit(solution)/shard_map/ppermute | solution.py:342
  56.4 2.3 %collective-permute-start.12 = (bf16[2,8,8192]{2,1,0:T(8,128)(2,1)S(1)}, bf16[2,8,8192]{2,1,0:T(8,128)(2,1)}, u32[]{:S(2)}, u32[]{:S(2)}) collective-permute-start(bf16[2,8,8192]{2,1,0:T(8,128)(2,1)S(1)} %collective-permute-done.8.refs_6_), channel_id=1, source_target_pairs={{0,1},{1,0},{2,3},{3,2},{4,5},{5,4},{6,7},{7,6},{8,9},{9,8},{10,11... | collective-permute-start | bytes 786440 | tf_op jit(solution)/shard_map/ppermute | solution.py:342
  56.5 2.6 %collective-permute-start.13 = (bf16[2,8,8192]{2,1,0:T(8,128)(2,1)S(1)}, bf16[2,8,8192]{2,1,0:T(8,128)(2,1)}, u32[]{:S(2)}, u32[]{:S(2)}) collective-permute-start(bf16[2,8,8192]{2,1,0:T(8,128)(2,1)S(1)} %collective-permute-done.9.refs_7_), channel_id=1, source_target_pairs={{0,1},{1,0},{2,3},{3,2},{4,5},{5,4},{6,7},{7,6},{8,9},{9,8},{10,11... | collective-permute-start | bytes 786440 | tf_op jit(solution)/shard_map/ppermute | solution.py:342
  63.6 6.4 %collective-permute-start.14 = (bf16[16,8,256]{2,1,0:T(8,128)(2,1)S(1)}, bf16[16,8,256]{2,1,0:T(8,128)(2,1)S(1)}, u32[]{:S(2)}, u32[]{:S(2)}) collective-permute-start(bf16[16,8,256]{2,1,0:T(8,128)(2,1)S(1)} %get-tuple-element.32), channel_id=1, source_target_pairs={{0,8},{1,9},{2,10},{3,11},{4,12},{5,13},{6,14},{7,15},{8,0},{9,1},... | collective-permute-start | bytes 196616 | tf_op jit(solution)/shard_map/ppermute | solution.py:342
  65.3 5.5 %collective-permute-start.19 = (bf16[16,8,256]{2,1,0:T(8,128)(2,1)S(1)}, bf16[16,8,256]{2,1,0:T(8,128)(2,1)S(1)}, u32[]{:S(2)}, u32[]{:S(2)}) collective-permute-start(bf16[16,8,256]{2,1,0:T(8,128)(2,1)S(1)} %get-tuple-element.33), channel_id=1, source_target_pairs={{0,2},{1,3},{2,0},{3,1},{4,6},{5,7},{6,4},{7,5},{8,10},{9,11},{10,... | collective-permute-start | bytes 196616 | tf_op jit(solution)/shard_map/ppermute | solution.py:342
  66.8 6.3 %collective-permute-start.15 = (bf16[16,8,256]{2,1,0:T(8,128)(2,1)S(1)}, bf16[16,8,256]{2,1,0:T(8,128)(2,1)S(1)}, u32[]{:S(2)}, u32[]{:S(2)}) collective-permute-start(bf16[16,8,256]{2,1,0:T(8,128)(2,1)S(1)} %get-tuple-element.32), channel_id=1, source_target_pairs={{0,4},{1,5},{2,6},{3,7},{4,0},{5,1},{6,2},{7,3},{8,12},{9,13},{10,... | collective-permute-start | bytes 196616 | tf_op jit(solution)/shard_map/ppermute | solution.py:342
  70.0 4.5 %collective-permute-start.16 = (bf16[16,8,256]{2,1,0:T(8,128)(2,1)S(1)}, bf16[16,8,256]{2,1,0:T(8,128)(2,1)S(1)}, u32[]{:S(2)}, u32[]{:S(2)}) collective-permute-start(bf16[16,8,256]{2,1,0:T(8,128)(2,1)S(1)} %collective-permute-done.14), channel_id=1, source_target_pairs={{0,4},{1,5},{2,6},{3,7},{4,0},{5,1},{6,2},{7,3},{8,12},{9,13},{10,... | collective-permute-start | bytes 196616 | tf_op jit(solution)/shard_map/ppermute | solution.py:342
  70.9 20.7 %slice-start = ((s8[6291456]{0:T(1024)(128)(4,1)}), s8[4194304]{0:T(1024)(128)(4,1)S(1)}, s32[]{:S(2)}) async-start(s8[6291456]{0:T(1024)(128)(4,1)} %bitcast.59), calls=%async_computation.1 | async-start | bytes 8388608
  70.9 19.2 %collective-permute-start.24 = (bf16[2,16,8,256]{3,2,1,0:T(8,128)(2,1)S(1)}, bf16[2,16,8,256]{3,2,1,0:T(8,128)(2,1)S(1)}, u32[]{:S(2)}, u32[]{:S(2)}) collective-permute-start(bf16[2,16,8,256]{3,2,1,0:T(8,128)(2,1)S(1)} %pad_maximum_fusion.4.refs_4_), channel_id=1, source_target_pairs={{0,1},{1,0},{2,3},{3,2},{4,5},{5,4},{6,7},{7,6},{8,9},{9,8},{10,11... | collective-permute-start | bytes 393224 | tf_op jit(solution)/shard_map/ppermute | solution.py:342
  70.9 14.8 %collective-permute-start.22 = (bf16[2,16,8,256]{3,2,1,0:T(8,128)(2,1)S(1)}, bf16[2,16,8,256]{3,2,1,0:T(8,128)(2,1)S(1)}, u32[]{:S(2)}, u32[]{:S(2)}) collective-permute-start(bf16[2,16,8,256]{3,2,1,0:T(8,128)(2,1)S(1)} %pad_maximum_fusion.4.refs_4_), channel_id=1, source_target_pairs={{0,4},{1,5},{2,6},{3,7},{4,0},{5,1},{6,2},{7,3},{8,12},{9,13},{10,... | collective-permute-start | bytes 393224 | tf_op jit(solution)/shard_map/ppermute | solution.py:342
  72.2 12.3 %collective-permute-start.21 = (bf16[2,16,8,256]{3,2,1,0:T(8,128)(2,1)S(1)}, bf16[2,16,8,256]{3,2,1,0:T(8,128)(2,1)S(1)}, u32[]{:S(2)}, u32[]{:S(2)}) collective-permute-start(bf16[2,16,8,256]{3,2,1,0:T(8,128)(2,1)S(1)} %pad_maximum_fusion.4.refs_4_), channel_id=1, source_target_pairs={{0,8},{1,9},{2,10},{3,11},{4,12},{5,13},{6,14},{7,15},{8,0},{9,1},... | collective-permute-start | bytes 393224 | tf_op jit(solution)/shard_map/ppermute | solution.py:342
  74.5 17.1 %slice-start.2 = ((s8[6291456]{0:T(1024)(128)(4,1)}), s8[4194304]{0:T(1024)(128)(4,1)S(1)}, s32[]{:S(2)}) async-start(s8[6291456]{0:T(1024)(128)(4,1)} %bitcast.62), calls=%async_computation.3 | async-start | bytes 8388608
  74.6 15.0 %collective-permute-start.17 = (bf16[4,16,8,256]{3,2,1,0:T(8,128)(2,1)S(1)}, bf16[4,16,8,256]{3,2,1,0:T(8,128)(2,1)S(1)}, u32[]{:S(2)}, u32[]{:S(2)}) collective-permute-start(bf16[4,16,8,256]{3,2,1,0:T(8,128)(2,1)S(1)} %pad_maximum_fusion.2.refs_0_), channel_id=1, source_target_pairs={{0,2},{1,3},{2,0},{3,1},{4,6},{5,7},{6,4},{7,5},{8,10},{9,11},{10,... | collective-permute-start | bytes 786440 | tf_op jit(solution)/shard_map/ppermute | solution.py:342
  75.5 16.1 %slice-start.1 = ((s8[6291456]{0:T(1024)(128)(4,1)}), s8[2097152]{0:T(1024)(128)(4,1)S(1)}, s32[]{:S(2)}) async-start(s8[6291456]{0:T(1024)(128)(4,1)} %bitcast.59), calls=%async_computation.2 | async-start | bytes 4194304
  75.5 16.1 %slice-start.3 = ((s8[6291456]{0:T(1024)(128)(4,1)}), s8[2097152]{0:T(1024)(128)(4,1)S(1)}, s32[]{:S(2)}) async-start(s8[6291456]{0:T(1024)(128)(4,1)} %bitcast.62), calls=%async_computation.4 | async-start | bytes 4194304
  75.5 16.1 %copy-start.4 = (bf16[4096,16]{0,1:T(8,128)(2,1)S(1)}, bf16[4096,16]{0,1:T(8,128)(2,1)}, u32[]{:S(2)}) copy-start(bf16[4096,16]{0,1:T(8,128)(2,1)} %param.21) | copy-start | bytes 393220
  75.5 16.1 %copy-start.5 = (f32[4096]{0:T(1024)S(1)}, f32[4096]{0:T(1024)}, u32[]{:S(2)}) copy-start(f32[4096]{0:T(1024)} %param.20) | copy-start | bytes 49156
  75.5 16.1 %copy-start.6 = (f32[1,4096]{1,0:T(1,128)S(1)}, f32[1,4096]{1,0:T(1,128)}, u32[]{:S(2)}) copy-start(f32[1,4096]{1,0:T(1,128)} %refs_19_.1) | copy-start | bytes 49156
  75.5 16.1 %copy-start.7 = (f32[1,2,768]{2,1,0:T(2,128)S(1)}, f32[1,2,768]{2,1,0:T(2,128)}, u32[]{:S(2)}) copy-start(f32[1,2,768]{2,1,0:T(2,128)} %param.26) | copy-start | bytes 18436
  84.5 5.0 %collective-permute-start.23 = (bf16[2,16,8,256]{3,2,1,0:T(8,128)(2,1)S(1)}, bf16[2,16,8,256]{3,2,1,0:T(8,128)(2,1)S(1)}, u32[]{:S(2)}, u32[]{:S(2)}) collective-permute-start(bf16[2,16,8,256]{3,2,1,0:T(8,128)(2,1)S(1)} %collective-permute-done.21.refs_5_), channel_id=1, source_target_pairs={{0,4},{1,5},{2,6},{3,7},{4,0},{5,1},{6,2},{7,3},{8,12},{9,13},{10,... | collective-permute-start | bytes 393224 | tf_op jit(solution)/shard_map/ppermute | solution.py:342
  85.8 5.1 %collective-permute-start.18 = (bf16[4,16,8,256]{3,2,1,0:T(8,128)(2,1)S(1)}, bf16[4,16,8,256]{3,2,1,0:T(8,128)(2,1)S(1)}, u32[]{:S(2)}, u32[]{:S(2)}) collective-permute-start(bf16[4,16,8,256]{3,2,1,0:T(8,128)(2,1)S(1)} %pad_maximum_fusion.2.refs_0_), channel_id=1, source_target_pairs={{0,1},{1,0},{2,3},{3,2},{4,5},{5,4},{6,7},{7,6},{8,9},{9,8},{10,11... | collective-permute-start | bytes 786440 | tf_op jit(solution)/shard_map/ppermute | solution.py:342
  85.8 4.3 %collective-permute-start.25 = (bf16[2,16,8,256]{3,2,1,0:T(8,128)(2,1)S(1)}, bf16[2,16,8,256]{3,2,1,0:T(8,128)(2,1)S(1)}, u32[]{:S(2)}, u32[]{:S(2)}) collective-permute-start(bf16[2,16,8,256]{3,2,1,0:T(8,128)(2,1)S(1)} %collective-permute-done.21.refs_5_), channel_id=1, source_target_pairs={{0,1},{1,0},{2,3},{3,2},{4,5},{5,4},{6,7},{7,6},{8,9},{9,8},{10,11... | collective-permute-start | bytes 393224 | tf_op jit(solution)/shard_map/ppermute | solution.py:342
  89.5 1.3 %collective-permute-start.26 = (bf16[2,16,8,256]{3,2,1,0:T(8,128)(2,1)S(1)}, bf16[2,16,8,256]{3,2,1,0:T(8,128)(2,1)S(1)}, u32[]{:S(2)}, u32[]{:S(2)}) collective-permute-start(bf16[2,16,8,256]{3,2,1,0:T(8,128)(2,1)S(1)} %collective-permute-done.22.refs_6_), channel_id=1, source_target_pairs={{0,1},{1,0},{2,3},{3,2},{4,5},{5,4},{6,7},{7,6},{8,9},{9,8},{10,11... | collective-permute-start | bytes 393224 | tf_op jit(solution)/shard_map/ppermute | solution.py:342
  89.5 1.5 %collective-permute-start.27 = (bf16[2,16,8,256]{3,2,1,0:T(8,128)(2,1)S(1)}, bf16[2,16,8,256]{3,2,1,0:T(8,128)(2,1)S(1)}, u32[]{:S(2)}, u32[]{:S(2)}) collective-permute-start(bf16[2,16,8,256]{3,2,1,0:T(8,128)(2,1)S(1)} %collective-permute-done.23.refs_7_), channel_id=1, source_target_pairs={{0,1},{1,0},{2,3},{3,2},{4,5},{5,4},{6,7},{7,6},{8,9},{9,8},{10,11... | collective-permute-start | bytes 393224 | tf_op jit(solution)/shard_map/ppermute | solution.py:342
  90.0 1.5 %collective-permute-start.20 = (bf16[4,16,8,256]{3,2,1,0:T(8,128)(2,1)S(1)}, bf16[4,16,8,256]{3,2,1,0:T(8,128)(2,1)S(1)}, u32[]{:S(2)}, u32[]{:S(2)}) collective-permute-start(bf16[4,16,8,256]{3,2,1,0:T(8,128)(2,1)S(1)} %collective-permute-done.17.refs_1_), channel_id=1, source_target_pairs={{0,1},{1,0},{2,3},{3,2},{4,5},{5,4},{6,7},{7,6},{8,9},{9,8},{10,11... | collective-permute-start | bytes 786440 | tf_op jit(solution)/shard_map/ppermute | solution.py:342
  100.4 2.0 %collective-permute-start.28 = (bf16[8,8,4096]{2,1,0:T(8,128)(2,1)S(1)}, bf16[8,8,4096]{2,1,0:T(8,128)(2,1)S(1)}, u32[]{:S(2)}, u32[]{:S(2)}) collective-permute-start(bf16[8,8,4096]{2,1,0:T(8,128)(2,1)S(1)} %get-tuple-element.41), channel_id=1, source_target_pairs={{0,1},{1,0},{2,3},{3,2},{4,5},{5,4},{6,7},{7,6},{8,9},{9,8},{10,11... | collective-permute-start | bytes 1572872 | tf_op jit(solution)/shard_map/ppermute | solution.py:342
  100.7 2.9 %collective-permute-start.32 = (bf16[8,8,4096]{2,1,0:T(8,128)(2,1)S(1)}, bf16[8,8,4096]{2,1,0:T(8,128)(2,1)S(1)}, u32[]{:S(2)}, u32[]{:S(2)}) collective-permute-start(bf16[8,8,4096]{2,1,0:T(8,128)(2,1)S(1)} %get-tuple-element.44), channel_id=1, source_target_pairs={{0,1},{1,0},{2,3},{3,2},{4,5},{5,4},{6,7},{7,6},{8,9},{9,8},{10,11... | collective-permute-start | bytes 1572872 | tf_op jit(solution)/shard_map/ppermute | solution.py:342
  102.5 8.5 %collective-permute-start.29 = (bf16[4,8,4096]{2,1,0:T(8,128)(2,1)S(1)}, bf16[4,8,4096]{2,1,0:T(8,128)(2,1)S(1)}, u32[]{:S(2)}, u32[]{:S(2)}) collective-permute-start(bf16[4,8,4096]{2,1,0:T(8,128)(2,1)S(1)} %get-tuple-element.46), channel_id=1, source_target_pairs={{0,2},{1,3},{2,0},{3,1},{4,6},{5,7},{6,4},{7,5},{8,10},{9,11},{10,... | collective-permute-start | bytes 786440 | tf_op jit(solution)/shard_map/ppermute | solution.py:342
  103.7 8.2 %collective-permute-start.33 = (bf16[4,8,4096]{2,1,0:T(8,128)(2,1)S(1)}, bf16[4,8,4096]{2,1,0:T(8,128)(2,1)S(1)}, u32[]{:S(2)}, u32[]{:S(2)}) collective-permute-start(bf16[4,8,4096]{2,1,0:T(8,128)(2,1)S(1)} %get-tuple-element.48), channel_id=1, source_target_pairs={{0,4},{1,5},{2,6},{3,7},{4,0},{5,1},{6,2},{7,3},{8,12},{9,13},{10,... | collective-permute-start | bytes 786440 | tf_op jit(solution)/shard_map/ppermute | solution.py:342
  111.1 7.2 %collective-permute-start.30 = (bf16[2,8,4096]{2,1,0:T(8,128)(2,1)S(1)}, bf16[2,8,4096]{2,1,0:T(8,128)(2,1)S(1)}, u32[]{:S(2)}, u32[]{:S(2)}) collective-permute-start(bf16[2,8,4096]{2,1,0:T(8,128)(2,1)S(1)} %get-tuple-element.50), channel_id=1, source_target_pairs={{0,4},{1,5},{2,6},{3,7},{4,0},{5,1},{6,2},{7,3},{8,12},{9,13},{10,... | collective-permute-start | bytes 393224 | tf_op jit(solution)/shard_map/ppermute | solution.py:342
  112.0 9.7 %collective-permute-start.34 = (bf16[2,8,4096]{2,1,0:T(8,128)(2,1)S(1)}, bf16[2,8,4096]{2,1,0:T(8,128)(2,1)S(1)}, u32[]{:S(2)}, u32[]{:S(2)}) collective-permute-start(bf16[2,8,4096]{2,1,0:T(8,128)(2,1)S(1)} %get-tuple-element.52), channel_id=1, source_target_pairs={{0,8},{1,9},{2,10},{3,11},{4,12},{5,13},{6,14},{7,15},{8,0},{9,1},... | collective-permute-start | bytes 393224 | tf_op jit(solution)/shard_map/ppermute | solution.py:342
  118.3 5.2 %collective-permute-start.31 = (bf16[1,8,4096]{2,1,0:T(8,128)(2,1)S(1)}, bf16[1,8,4096]{2,1,0:T(8,128)(2,1)S(1)}, u32[]{:S(2)}, u32[]{:S(2)}) collective-permute-start(bf16[1,8,4096]{2,1,0:T(8,128)(2,1)S(1)} %add_convert_fusion.10), channel_id=1, source_target_pairs={{0,8},{1,9},{2,10},{3,11},{4,12},{5,13},{6,14},{7,15},{8,0},{9,1},... | collective-permute-start | bytes 196616 | tf_op jit(solution)/shard_map/ppermute | solution.py:342
  121.7 4.3 %collective-permute-start.35 = (bf16[1,8,4096]{2,1,0:T(8,128)(2,1)S(1)}, bf16[1,8,4096]{2,1,0:T(8,128)(2,1)S(1)}, u32[]{:S(2)}, u32[]{:S(2)}) collective-permute-start(bf16[1,8,4096]{2,1,0:T(8,128)(2,1)S(1)} %add_convert_fusion.8), channel_id=1, source_target_pairs={{0,2},{1,3},{2,0},{3,1},{4,6},{5,7},{6,4},{7,5},{8,10},{9,11},{10,... | collective-permute-start | bytes 196616 | tf_op jit(solution)/shard_map/ppermute | solution.py:342

commit v5 on v4

--- a/solution.py
+++ b/solution.py
@@ -86,11 +86,11 @@
         ),
         out_shape=jax.ShapeDtypeStruct((rows, width), jnp.bfloat16),
         name="attend",
-        compiler_params=pltpu.CompilerParams(vmem_limit_bytes=16 * MIB),
+        compiler_params=pltpu.CompilerParams(vmem_limit_bytes=8 * MIB),
         cost_estimate=pl.CostEstimate(
             flops=rows * width * 4 * 256, bytes_accessed=rows << 18, transcendentals=0
         ),
-    )(lengths, queries, pltpu.with_memory_space_constraint(kv_cache, pltpu.HBM))
+    )(lengths, *(pltpu.with_memory_space_constraint(x, pltpu.HBM) for x in (queries, kv_cache)))
 
 
 def expand_kernel(stacked, table_ref, code_ref, out_ref):
@@ -143,11 +143,11 @@
     out = pl.pallas_call(
         functools.partial(expand_kernel, stacked),
         grid=grid,
-        in_specs=[pl.BlockSpec((8, LANES), lambda b: (0, 0)), code_spec],
+        in_specs=[pl.BlockSpec(table.shape, lambda b: (0, 0)), code_spec],
         out_specs=out_spec,
         out_shape=jax.ShapeDtypeStruct(out_shape, jnp.bfloat16),
         name="expand",
-        compiler_params=pltpu.CompilerParams(vmem_limit_bytes=10 * MIB),
+        compiler_params=pltpu.CompilerParams(vmem_limit_bytes=6 * MIB),
         cost_estimate=pl.CostEstimate(
             flops=rows * columns * 8000, bytes_accessed=10 * rows * columns, transcendentals=0
         ),
@@ -155,33 +155,27 @@
     return out.reshape(4 * rows, columns) if stacked else out
 
 
-def project_kernel(masks, counts, me_ref, *refs):
+def project_kernel(masks, counts, block, me_ref, *refs):
     pieces, refs = refs[: len(masks)], refs[len(masks) :]
     weight_ref, hidden_ref = refs[:2]
     out_refs, acc_ref = refs[2:-1], refs[-1]
-    step = pl.program_id(0)
     depth = weight_ref.shape[0]
-
-    @pl.when(step == 0)
-    def _():
-        acc_ref[...] = jnp.zeros_like(acc_ref)
-
-    rows_in = jnp.concatenate([ref[...].reshape(-1, depth) for ref in pieces], axis=0)
-    product = jnp.dot(rows_in, weight_ref[...], preferred_element_type=jnp.float32)
-    acc_ref[...] += product.reshape(acc_ref.shape)
-
-    @pl.when(step == pl.num_programs(0) - 1)
-    def _():
-        me = me_ref[0]
-        at = 0
-        for mask_list, m in zip(masks, counts):
-            for mask in mask_list:
-                source = me ^ mask
-                projected = acc_ref[at].astype(jnp.bfloat16).astype(jnp.float32)
-                out_refs[m][source] = (
-                    hidden_ref[source, m].astype(jnp.float32) + projected
-                ).astype(jnp.bfloat16)
-                at += 1
+    for first in range(0, depth, block):
+        at = slice(first, first + block)
+        rows_in = jnp.concatenate([ref[:, :, at].reshape(-1, block) for ref in pieces], axis=0)
+        product = jnp.dot(rows_in, weight_ref[at, :], preferred_element_type=jnp.float32)
+        product = product.reshape(acc_ref.shape)
+        acc_ref[...] = product if first == 0 else acc_ref[...] + product
+    me = me_ref[0]
+    entry = 0
+    for mask_list, m in zip(masks, counts):
+        for mask in mask_list:
+            source = me ^ mask
+            projected = acc_ref[entry].astype(jnp.bfloat16).astype(jnp.float32)
+            out_refs[m][source] = (hidden_ref[source, m].astype(jnp.float32) + projected).astype(
+                jnp.bfloat16
+            )
+            entry += 1
 
 
 def project(me, gathered, out_weight, hidden_columns):
@@ -190,35 +184,24 @@
     counts = tuple(m for m, chain in enumerate(gathered) for _ in chain)
     shards, micro_count, rows, columns = hidden_columns.shape
     depth = out_weight.shape[0]
-    block = 2048
+    in_vmem = pl.BlockSpec(memory_space=pltpu.VMEM)
+    held = [*pieces, out_weight, hidden_columns]
+    if shards <= 16:
+        held = [pltpu.with_memory_space_constraint(x, pltpu.VMEM) for x in held]
     return pl.pallas_call(
-        functools.partial(project_kernel, masks, counts),
-        grid_spec=pltpu.PrefetchScalarGridSpec(
-            num_scalar_prefetch=1,
-            grid=(depth // block,),
-            in_specs=[
-                pl.BlockSpec((piece.shape[0], rows, block), lambda k, n: (0, 0, k))
-                for piece in pieces
-            ]
-            + [
-                pl.BlockSpec((block, columns), lambda k, n: (k, 0)),
-                pl.BlockSpec(hidden_columns.shape, lambda k, n: (0, 0, 0, 0)),
-            ],
-            out_specs=[
-                pl.BlockSpec((shards, rows, columns), lambda k, n: (0, 0, 0))
-                for _ in range(micro_count)
-            ],
-            scratch_shapes=[pltpu.VMEM((shards * micro_count, rows, columns), jnp.float32)],
-        ),
+        functools.partial(project_kernel, masks, counts, 1024),
+        in_specs=[pl.BlockSpec(memory_space=pltpu.SMEM)] + [in_vmem] * len(held),
+        out_specs=[in_vmem] * micro_count,
         out_shape=[jax.ShapeDtypeStruct((shards, rows, columns), jnp.bfloat16)] * micro_count,
+        scratch_shapes=[pltpu.VMEM((shards * micro_count, rows, columns), jnp.float32)],
         name="project",
-        compiler_params=pltpu.CompilerParams(vmem_limit_bytes=24 * MIB),
+        compiler_params=pltpu.CompilerParams(vmem_limit_bytes=(8 if shards <= 16 else 60) * MIB),
         cost_estimate=pl.CostEstimate(
             flops=2 * shards * micro_count * rows * depth * columns,
             bytes_accessed=2 * depth * columns,
             transcendentals=0,
         ),
-    )(me, *pieces, pltpu.with_memory_space_constraint(out_weight, pltpu.HBM), hidden_columns)
+    )(me, *held)
 
 
 def experts_kernel(masks, counts, orders, me_ref, *refs):
@@ -328,7 +311,7 @@
             pltpu.VMEM((groups * shards, rows, width), jnp.float32),
         ],
         name="experts",
-        compiler_params=pltpu.CompilerParams(vmem_limit_bytes=(24 if total <= 256 else 62) * MIB),
+        compiler_params=pltpu.CompilerParams(vmem_limit_bytes=(14 if total <= 256 else 62) * MIB),
         cost_estimate=pl.CostEstimate(
             flops=6 * total * width * hidden_units,
             bytes_accessed=6 * width * hidden_units,
@@ -426,13 +409,16 @@
     packed = lax.all_to_all(
         jnp.concatenate([lead, tail], axis=-1), "expert", split_axis=0, concat_axis=0, tiled=True
     )
+    words = codebooks[0].astype(jnp.float32).transpose(0, 2, 1).reshape(3, 8, LANES)
+    *tables, me_list, packed = lax.optimization_barrier(
+        (words[0], words[1], words[2], me_list, packed)
+    )
     hidden_columns = packed[..., :columns]
     hot_all = packed[..., columns:].transpose(1, 0, 2, 3).reshape(micro_count, count * rows, count)
 
-    tables = codebooks[0].astype(jnp.float32).transpose(0, 2, 1).reshape(3, 8, LANES)
     attended = [attend(queries, kv_cache, lengths, m) for m in range(micro_count)]
     make_gate = lambda after: expand(tables[0], gate_codes[0].T, True, after)
-    make_up = lambda after: expand(tables[1], up_codes[0].T, True, after + (packed,))
+    make_up = lambda after: expand(tables[1], up_codes[0].T, True, after)
     make_down = lambda after: expand(tables[2], down_codes[0], False, after)
     if count == 16 and micro_count == 2:
         gathered, (gate, up) = gather_two(*attended, [make_gate, make_up])

time: 127 us -> 120 us (0.945)
  local copies, waits for them, and re-layouts: 8.83 us -> 0.79 us
  starting transfers between devices: 35.9 us -> 41.1 us
  Pallas kernels: 48.1 us -> 44.9 us
  waiting for transfers between devices: 31.4 us -> 30 us
    unnamed x34 -> x20, local copies, waits for them, and re-layouts: 7.01 us -> 0.71 us
    ppermute x36, starting transfers between devices: 31.7 us -> 37.6 us  [swap(): return lax.ppermute(value, 'expert', [(i, i ^ bit) for i in range(count)])]
    pallas_call x1, Pallas kernels: 4.48 us -> 1.27 us  [project(): pl.pallas_call(functools.partial(project_kernel, masks, counts, 1024), in...]
    ppermute x36, waiting for transfers between devices: 31.4 us -> 30 us  [swap(): return lax.ppermute(value, 'expert', [(i, i ^ bit) for i in range(count)])]
  transfers between devices with their start and end apart: 37 -> 37, of which waited for: 17 -> 18; matrix products, arithmetic and copies ran while one was open for 3% -> 1% of each run, Pallas kernels for 24% -> 26%
where the time goes in v5:
time: 120 us; the launch traced here: 119 us
  Pallas kernels  44.9 us (37%)
  starting transfers between devices  41.1 us (34%)
  waiting for transfers between devices  30 us (25%)
  other arithmetic  2.15 us (2%)
    ppermute x36, starting transfers between devices, swap(): return lax.ppermute(value, 'expert', [(i, i ^ bit) for i in range(count)])  37.6 us
    ppermute x36, waiting for transfers between devices, swap(): return lax.ppermute(value, 'expert', [(i, i ^ bit) for i in range(count)])  30 us
    pallas_call x3, Pallas kernels, expand(): pl.pallas_call(functools.partial(expand_kernel, stacked), grid=grid, in_s...  26.5 us
    pallas_call x1, Pallas kernels, run_experts(): pl.pallas_call(functools.partial(experts_kernel, masks, counts, orders),...  8.95 us
    pallas_call x2, Pallas kernels, attend(): pl.pallas_call(functools.partial(attend_kernel, micro, span, KV_HEADS), g...  8.2 us
    all_to_all x1, starting transfers between devices, body(): lax.all_to_all(jnp.concatenate([lead, tail], axis=-1), 'expert', split_ax...  3.52 us
  transfers between devices with their start and end apart: 37, of which 18 were waited for; matrix products, arithmetic and copies ran while one was open for 1% of the time, Pallas kernels for 26%

profile of v5, /device:TPU:0, one launch (start us, length us, event | category | flops | bytes accessed | tf_op | source)
XLA Modules:
  0.0 119.3 jit_solution(18246265047932197350)
XLA Ops:
  0.0 0.7 copy-done.5
  0.7 4.1 %attend.2 = bf16[8,8192]{1,0:T(8,128)(2,1)S(1)} custom-call(s32[2,8]{1,0:T(2,128)S(1)} %copy-done.5, bf16[2,8,8192]{2,1,0:T(8,128)(2,1)} %q_ref.3, bf16[2,8,128,2,512]{4,3,2,1,0:T(2,128)(2,1)} %kv_ref.3), custom_call_target="tpu_custom_call" | custom-call | flops 67108864 | bytes 2097152 | tf_op jit(solution)/shard_map/attend/pallas_call | solution.py:75
  4.8 3.1 %collective-permute-start.1 = (bf16[8,8192]{1,0:T(8,128)(2,1)S(1)}, bf16[8,8192]{1,0:T(8,128)(2,1)S(1)}, u32[]{:S(2)}, u32[]{:S(2)}) collective-permute-start(bf16[8,8192]{1,0:T(8,128)(2,1)S(1)} %attend.2), channel_id=1, source_target_pairs={{0,4},{1,5},{2,6},{3,7},{4,0},{5,1},{6,2},{7,3},{8,12},{9,13},{10,... | collective-permute-start | bytes 393224 | tf_op jit(solution)/shard_map/ppermute | solution.py:325
  7.9 2.6 %collective-permute-start = (bf16[8,8192]{1,0:T(8,128)(2,1)S(1)}, bf16[8,8192]{1,0:T(8,128)(2,1)S(1)}, u32[]{:S(2)}, u32[]{:S(2)}) collective-permute-start(bf16[8,8192]{1,0:T(8,128)(2,1)S(1)} %attend.2), channel_id=1, source_target_pairs={{0,8},{1,9},{2,10},{3,11},{4,12},{5,13},{6,14},{7,15},{8,0},{9,1},... | collective-permute-start | bytes 393224 | tf_op jit(solution)/shard_map/ppermute | solution.py:325
  10.5 0.1 fusion.4
  10.6 0.7 pad_maximum_fusion.3
  11.3 3.5 %all-to-all-start = ((bf16[16,2,8,272]{3,2,1,0:T(8,128)(2,1)}), bf16[16,2,8,272]{3,2,1,0:T(8,128)(2,1)S(1)}, u32[]{:S(2)}, u32[]{:S(2)}) async-start(bf16[16,2,8,272]{3,2,1,0:T(8,128)(2,1)} %pad_maximum_fusion.3), calls=%async_computation | async-start | bytes 393216 | tf_op jit(solution)/shard_map/all_to_all | solution.py:409
  14.9 4.1 %attend.3 = bf16[8,8192]{1,0:T(8,128)(2,1)S(1)} custom-call(s32[2,8]{1,0:T(2,128)S(1)} %copy-done.6, bf16[2,8,8192]{2,1,0:T(8,128)(2,1)} %q_ref.3, bf16[2,8,128,2,512]{4,3,2,1,0:T(2,128)(2,1)} %kv_ref.3), custom_call_target="tpu_custom_call" | custom-call | flops 67108864 | bytes 2097152 | tf_op jit(solution)/shard_map/attend/pallas_call | solution.py:75
  19.0 1.9 %collective-permute-start.5 = (bf16[8,8192]{1,0:T(8,128)(2,1)S(1)}, bf16[8,8192]{1,0:T(8,128)(2,1)S(1)}, u32[]{:S(2)}, u32[]{:S(2)}) collective-permute-start(bf16[8,8192]{1,0:T(8,128)(2,1)S(1)} %attend.3), channel_id=1, source_target_pairs={{0,2},{1,3},{2,0},{3,1},{4,6},{5,7},{6,4},{7,5},{8,10},{9,11},{10,... | collective-permute-start | bytes 393224 | tf_op jit(solution)/shard_map/ppermute | solution.py:325
  20.9 1.6 %collective-permute-start.2 = (bf16[8,8192]{1,0:T(8,128)(2,1)S(1)}, bf16[8,8192]{1,0:T(8,128)(2,1)S(1)}, u32[]{:S(2)}, u32[]{:S(2)}) collective-permute-start(bf16[8,8192]{1,0:T(8,128)(2,1)S(1)} %collective-permute-done), channel_id=1, source_target_pairs={{0,4},{1,5},{2,6},{3,7},{4,0},{5,1},{6,2},{7,3},{8,12},{9,13},{10,... | collective-permute-start | bytes 393224 | tf_op jit(solution)/shard_map/ppermute | solution.py:325
  22.5 2.8 %collective-permute-done.5 = bf16[8,8192]{1,0:T(8,128)(2,1)S(1)} collective-permute-done((bf16[8,8192]{1,0:T(8,128)(2,1)S(1)}, bf16[8,8192]{1,0:T(8,128)(2,1)S(1)}, u32[]{:S(2)}, u32[]{:S(2)}) %collective-permute-start.5) | collective-permute-done | bytes 131104 | tf_op jit(solution)/shard_map/ppermute | solution.py:325
  25.3 0.1 collective-permute-start.10
  25.4 1.4 %collective-permute-start.8 = (bf16[2,8,8192]{2,1,0:T(8,128)(2,1)S(1)}, bf16[2,8,8192]{2,1,0:T(8,128)(2,1)S(1)}, u32[]{:S(2)}, u32[]{:S(2)}) collective-permute-start(bf16[2,8,8192]{2,1,0:T(8,128)(2,1)S(1)} %pad_maximum_fusion.1.refs_4_), channel_id=1, source_target_pairs={{0,4},{1,5},{2,6},{3,7},{4,0},{5,1},{6,2},{7,3},{8,12},{9,13},{10,... | collective-permute-start | bytes 786440 | tf_op jit(solution)/shard_map/ppermute | solution.py:325
  26.8 2.2 %collective-permute-start.6 = (bf16[2,8,8192]{2,1,0:T(8,128)(2,1)S(1)}, bf16[2,8,8192]{2,1,0:T(8,128)(2,1)S(1)}, u32[]{:S(2)}, u32[]{:S(2)}) collective-permute-start(bf16[2,8,8192]{2,1,0:T(8,128)(2,1)S(1)} %pad_maximum_fusion.1.refs_4_), channel_id=1, source_target_pairs={{0,8},{1,9},{2,10},{3,11},{4,12},{5,13},{6,14},{7,15},{8,0},{9,1},... | collective-permute-start | bytes 786440 | tf_op jit(solution)/shard_map/ppermute | solution.py:325
  29.1 0.1 collective-permute-start.4
  29.2 1.5 %collective-permute-start.3 = (bf16[4,8,8192]{2,1,0:T(8,128)(2,1)S(1)}, bf16[4,8,8192]{2,1,0:T(8,128)(2,1)S(1)}, u32[]{:S(2)}, u32[]{:S(2)}) collective-permute-start(bf16[4,8,8192]{2,1,0:T(8,128)(2,1)S(1)} %pad_maximum_fusion.refs_0_), channel_id=1, source_target_pairs={{0,2},{1,3},{2,0},{3,1},{4,6},{5,7},{6,4},{7,5},{8,10},{9,11},{10,... | collective-permute-start | bytes 1572872 | tf_op jit(solution)/shard_map/ppermute | solution.py:325
  30.7 8.9 %expand.3 = bf16[4,192,4096]{2,1,0:T(8,128)(2,1)S(1)} custom-call(f32[8,128]{1,0:T(8,128)S(1)} %squeeze.32.table_ref, bf16[192,4096]{1,0:T(8,128)(2,1)} %bitcast.78), custom_call_target="tpu_custom_call" | custom-call | flops 6291456000 | bytes 7864320 | tf_op jit(solution)/shard_map/expand/pallas_call | solution.py:143
  39.6 2.2 %collective-permute-done.6.refs_5_ = bf16[2,8,8192]{2,1,0:T(8,128)(2,1)S(1)} collective-permute-done((bf16[2,8,8192]{2,1,0:T(8,128)(2,1)S(1)}, bf16[2,8,8192]{2,1,0:T(8,128)(2,1)S(1)}, u32[]{:S(2)}, u32[]{:S(2)}) %collective-permute-start.6) | collective-permute-done | bytes 262176 | tf_op jit(solution)/shard_map/ppermute | solution.py:325
  41.8 0.1 collective-permute-start.9
  41.9 9.0 %expand.4 = bf16[4,192,4096]{2,1,0:T(8,128)(2,1)S(1)} custom-call(f32[8,128]{1,0:T(8,128)S(1)} %squeeze.33.table_ref, bf16[192,4096]{1,0:T(8,128)(2,1)} %bitcast.79), custom_call_target="tpu_custom_call" | custom-call | flops 6291456000 | bytes 7864320 | tf_op jit(solution)/shard_map/expand/pallas_call | solution.py:143
  50.9 0.1 collective-permute-start.7
  51.0 0.5 collective-permute-start.11
  51.5 0.1 collective-permute-start.12
  51.6 0.4 collective-permute-start.13
  52.0 1.2 %collective-permute-done.11.refs_9_ = bf16[2,8,8192]{2,1,0:T(8,128)(2,1)S(1)} collective-permute-done((bf16[2,8,8192]{2,1,0:T(8,128)(2,1)S(1)}, bf16[2,8,8192]{2,1,0:T(8,128)(2,1)S(1)}, u32[]{:S(2)}, u32[]{:S(2)}) %collective-permute-start.11) | collective-permute-done | bytes 262176 | tf_op jit(solution)/shard_map/ppermute | solution.py:325
  53.3 0.4 collective-permute-done.12.refs_10_
  53.6 0.4 collective-permute-done.13.refs_11_
  54.0 1.3 %project.1 = (bf16[16,8,256]{2,1,0:T(8,128)(2,1)S(1)}, bf16[16,8,256]{2,1,0:T(8,128)(2,1)S(1)}) custom-call(s32[1]{0:T(128)} %bitcast.3.me_ref, bf16[4,8,8192]{2,1,0:T(8,128)(2,1)S(1)} %pad_maximum_fusion.refs_0_, bf16[4,8,8192]{2,1,0:T(8,128)(2,1)S(1)} %collective-permute-done.3.refs_1_, bf16[4,8,8192]{2,1,0:T(8,128)(2,1)S(1)} %collective-permute-done.4.refs_2_, ...), custom_call_target="tpu_custom_call" | custom-call | flops 1073741824 | bytes 4194304 | tf_op jit(solution)/shard_map/project/pallas_call | solution.py:191
  55.3 2.7 %collective-permute-start.14 = (bf16[16,8,256]{2,1,0:T(8,128)(2,1)S(1)}, bf16[16,8,256]{2,1,0:T(8,128)(2,1)S(1)}, u32[]{:S(2)}, u32[]{:S(2)}) collective-permute-start(bf16[16,8,256]{2,1,0:T(8,128)(2,1)S(1)} %get-tuple-element.41), channel_id=1, source_target_pairs={{0,8},{1,9},{2,10},{3,11},{4,12},{5,13},{6,14},{7,15},{8,0},{9,1},... | collective-permute-start | bytes 196616 | tf_op jit(solution)/shard_map/ppermute | solution.py:325
  58.0 1.5 %collective-permute-start.19 = (bf16[16,8,256]{2,1,0:T(8,128)(2,1)S(1)}, bf16[16,8,256]{2,1,0:T(8,128)(2,1)S(1)}, u32[]{:S(2)}, u32[]{:S(2)}) collective-permute-start(bf16[16,8,256]{2,1,0:T(8,128)(2,1)S(1)} %get-tuple-element.43), channel_id=1, source_target_pairs={{0,2},{1,3},{2,0},{3,1},{4,6},{5,7},{6,4},{7,5},{8,10},{9,11},{10,... | collective-permute-start | bytes 196616 | tf_op jit(solution)/shard_map/ppermute | solution.py:325
  59.4 2.1 %collective-permute-done.14 = bf16[16,8,256]{2,1,0:T(8,128)(2,1)S(1)} collective-permute-done((bf16[16,8,256]{2,1,0:T(8,128)(2,1)S(1)}, bf16[16,8,256]{2,1,0:T(8,128)(2,1)S(1)}, u32[]{:S(2)}, u32[]{:S(2)}) %collective-permute-start.14) | collective-permute-done | bytes 65568 | tf_op jit(solution)/shard_map/ppermute | solution.py:325
  61.5 1.3 %collective-permute-start.16 = (bf16[16,8,256]{2,1,0:T(8,128)(2,1)S(1)}, bf16[16,8,256]{2,1,0:T(8,128)(2,1)S(1)}, u32[]{:S(2)}, u32[]{:S(2)}) collective-permute-start(bf16[16,8,256]{2,1,0:T(8,128)(2,1)S(1)} %collective-permute-done.14), channel_id=1, source_target_pairs={{0,4},{1,5},{2,6},{3,7},{4,0},{5,1},{6,2},{7,3},{8,12},{9,13},{10,... | collective-permute-start | bytes 196616 | tf_op jit(solution)/shard_map/ppermute | solution.py:325
  62.9 0.1 collective-permute-start.24
  63.0 0.8 collective-permute-start.22
  63.7 2.0 %collective-permute-start.21 = (bf16[2,16,8,256]{3,2,1,0:T(8,128)(2,1)S(1)}, bf16[2,16,8,256]{3,2,1,0:T(8,128)(2,1)S(1)}, u32[]{:S(2)}, u32[]{:S(2)}) collective-permute-start(bf16[2,16,8,256]{3,2,1,0:T(8,128)(2,1)S(1)} %pad_maximum_fusion.4.refs_4_), channel_id=1, source_target_pairs={{0,8},{1,9},{2,10},{3,11},{4,12},{5,13},{6,14},{7,15},{8,0},{9,1},... | collective-permute-start | bytes 393224 | tf_op jit(solution)/shard_map/ppermute | solution.py:325
  65.9 1.6 %collective-permute-start.17 = (bf16[4,16,8,256]{3,2,1,0:T(8,128)(2,1)S(1)}, bf16[4,16,8,256]{3,2,1,0:T(8,128)(2,1)S(1)}, u32[]{:S(2)}, u32[]{:S(2)}) collective-permute-start(bf16[4,16,8,256]{3,2,1,0:T(8,128)(2,1)S(1)} %pad_maximum_fusion.2.refs_0_), channel_id=1, source_target_pairs={{0,2},{1,3},{2,0},{3,1},{4,6},{5,7},{6,4},{7,5},{8,10},{9,11},{10,... | collective-permute-start | bytes 786440 | tf_op jit(solution)/shard_map/ppermute | solution.py:325
  67.5 8.7 %expand.5.refs_17_ = bf16[768,4096]{1,0:T(8,128)(2,1)S(1)} custom-call(f32[8,128]{1,0:T(8,128)S(1)} %squeeze.34.table_ref, bf16[768,1024]{1,0:T(8,128)(2,1)} %bitcast.80), custom_call_target="tpu_custom_call" | custom-call | flops 6291456000 | bytes 7864320 | tf_op jit(solution)/shard_map/expand/pallas_call | solution.py:143
  76.2 1.5 %collective-permute-start.23 = (bf16[2,16,8,256]{3,2,1,0:T(8,128)(2,1)S(1)}, bf16[2,16,8,256]{3,2,1,0:T(8,128)(2,1)S(1)}, u32[]{:S(2)}, u32[]{:S(2)}) collective-permute-start(bf16[2,16,8,256]{3,2,1,0:T(8,128)(2,1)S(1)} %collective-permute-done.21.refs_5_), channel_id=1, source_target_pairs={{0,4},{1,5},{2,6},{3,7},{4,0},{5,1},{6,2},{7,3},{8,12},{9,13},{10,... | collective-permute-start | bytes 393224 | tf_op jit(solution)/shard_map/ppermute | solution.py:325
  77.7 0.1 collective-permute-start.18
  77.8 0.5 collective-permute-start.25
  78.3 3.0 %collective-permute-done.23.refs_7_ = bf16[2,16,8,256]{3,2,1,0:T(8,128)(2,1)S(1)} collective-permute-done((bf16[2,16,8,256]{3,2,1,0:T(8,128)(2,1)S(1)}, bf16[2,16,8,256]{3,2,1,0:T(8,128)(2,1)S(1)}, u32[]{:S(2)}, u32[]{:S(2)}) %collective-permute-start.23) | collective-permute-done | bytes 131104 | tf_op jit(solution)/shard_map/ppermute | solution.py:325
  81.3 0.5 collective-permute-start.27
  81.9 0.7 collective-permute-done.26.refs_10_
  82.6 0.2 collective-permute-done.27.refs_11_
  82.8 0.5 collective-permute-done.20.refs_3_
  83.3 8.9 %experts.1 = (bf16[8,8,4096]{2,1,0:T(8,128)(2,1)S(1)}, bf16[8,8,4096]{2,1,0:T(8,128)(2,1)S(1)}, bf16[8,8,4096]{2,1,0:T(8,128)(2,1)S(1)}, bf16[8,8,4096]{2,1,0:T(...) custom-call(s32[1]{0:T(128)} %bitcast.3.me_ref, ...), custom_call_target="tpu_custom_call" | custom-call | flops 4831838208 | bytes 18874368 | tf_op jit(solution)/shard_map/experts/pallas_call | solution.py:302
  92.3 0.3 collective-permute-start.28
  92.6 0.3 collective-permute-start.32
  92.9 1.4 %collective-permute-done.28 = bf16[8,8,4096]{2,1,0:T(8,128)(2,1)S(1)} collective-permute-done((bf16[8,8,4096]{2,1,0:T(8,128)(2,1)S(1)}, bf16[8,8,4096]{2,1,0:T(8,128)(2,1)S(1)}, u32[]{:S(2)}, u32[]{:S(2)}) %collective-permute-start.28) | collective-permute-done | bytes 524320 | tf_op jit(solution)/shard_map/ppermute | solution.py:325
  94.3 0.1 add_convert_fusion.3
  94.4 0.5 collective-permute-start.29
  94.9 0.1 collective-permute-done.32
  95.0 0.1 add_convert_fusion.1
  95.2 1.7 %collective-permute-start.33 = (bf16[4,8,4096]{2,1,0:T(8,128)(2,1)S(1)}, bf16[4,8,4096]{2,1,0:T(8,128)(2,1)S(1)}, u32[]{:S(2)}, u32[]{:S(2)}) collective-permute-start(bf16[4,8,4096]{2,1,0:T(8,128)(2,1)S(1)} %get-tuple-element.58), channel_id=1, source_target_pairs={{0,4},{1,5},{2,6},{3,7},{4,0},{5,1},{6,2},{7,3},{8,12},{9,13},{10,... | collective-permute-start | bytes 786440 | tf_op jit(solution)/shard_map/ppermute | solution.py:325
  96.8 6.1 %collective-permute-done.29 = bf16[4,8,4096]{2,1,0:T(8,128)(2,1)S(1)} collective-permute-done((bf16[4,8,4096]{2,1,0:T(8,128)(2,1)S(1)}, bf16[4,8,4096]{2,1,0:T(8,128)(2,1)S(1)}, u32[]{:S(2)}, u32[]{:S(2)}) %collective-permute-start.29) | collective-permute-done | bytes 262176 | tf_op jit(solution)/shard_map/ppermute | solution.py:325
  103.0 1.5 %collective-permute-start.30 = (bf16[2,8,4096]{2,1,0:T(8,128)(2,1)S(1)}, bf16[2,8,4096]{2,1,0:T(8,128)(2,1)S(1)}, u32[]{:S(2)}, u32[]{:S(2)}) collective-permute-start(bf16[2,8,4096]{2,1,0:T(8,128)(2,1)S(1)} %get-tuple-element.60), channel_id=1, source_target_pairs={{0,4},{1,5},{2,6},{3,7},{4,0},{5,1},{6,2},{7,3},{8,12},{9,13},{10,... | collective-permute-start | bytes 393224 | tf_op jit(solution)/shard_map/ppermute | solution.py:325
  104.5 2.0 %collective-permute-start.34 = (bf16[2,8,4096]{2,1,0:T(8,128)(2,1)S(1)}, bf16[2,8,4096]{2,1,0:T(8,128)(2,1)S(1)}, u32[]{:S(2)}, u32[]{:S(2)}) collective-permute-start(bf16[2,8,4096]{2,1,0:T(8,128)(2,1)S(1)} %get-tuple-element.62), channel_id=1, source_target_pairs={{0,8},{1,9},{2,10},{3,11},{4,12},{5,13},{6,14},{7,15},{8,0},{9,1},... | collective-permute-start | bytes 393224 | tf_op jit(solution)/shard_map/ppermute | solution.py:325
  106.5 3.3 %collective-permute-done.30 = bf16[2,8,4096]{2,1,0:T(8,128)(2,1)S(1)} collective-permute-done((bf16[2,8,4096]{2,1,0:T(8,128)(2,1)S(1)}, bf16[2,8,4096]{2,1,0:T(8,128)(2,1)S(1)}, u32[]{:S(2)}, u32[]{:S(2)}) %collective-permute-start.30) | collective-permute-done | bytes 131104 | tf_op jit(solution)/shard_map/ppermute | solution.py:325
  109.8 2.5 %collective-permute-start.31 = (bf16[1,8,4096]{2,1,0:T(8,128)(2,1)S(1)}, bf16[1,8,4096]{2,1,0:T(8,128)(2,1)S(1)}, u32[]{:S(2)}, u32[]{:S(2)}) collective-permute-start(bf16[1,8,4096]{2,1,0:T(8,128)(2,1)S(1)} %add_convert_fusion.10), channel_id=1, source_target_pairs={{0,8},{1,9},{2,10},{3,11},{4,12},{5,13},{6,14},{7,15},{8,0},{9,1},... | collective-permute-start | bytes 196616 | tf_op jit(solution)/shard_map/ppermute | solution.py:325
  112.3 2.0 %collective-permute-done.34 = bf16[2,8,4096]{2,1,0:T(8,128)(2,1)S(1)} collective-permute-done((bf16[2,8,4096]{2,1,0:T(8,128)(2,1)S(1)}, bf16[2,8,4096]{2,1,0:T(8,128)(2,1)S(1)}, u32[]{:S(2)}, u32[]{:S(2)}) %collective-permute-start.34) | collective-permute-done | bytes 131104 | tf_op jit(solution)/shard_map/ppermute | solution.py:325
  114.3 0.7 collective-permute-start.35
  115.0 0.7 collective-permute-done.31
  115.8 2.9 %collective-permute-done.35 = bf16[1,8,4096]{2,1,0:T(8,128)(2,1)S(1)} collective-permute-done((bf16[1,8,4096]{2,1,0:T(8,128)(2,1)S(1)}, bf16[1,8,4096]{2,1,0:T(8,128)(2,1)S(1)}, u32[]{:S(2)}, u32[]{:S(2)}) %collective-permute-start.35) | collective-permute-done | bytes 65568 | tf_op jit(solution)/shard_map/ppermute | solution.py:325
  118.7 0.7 pad_maximum_fusion.5
  (64 shorter events, 0.7 us)
Async XLA Ops:
  0.0 0.7 copy-start.5
  0.7 9.8 %copy-start.8 = (s32[2,8,8]{2,1,0:T(8,128)S(1)}, s32[2,8,8]{2,1,0:T(8,128)}, u32[]{:S(2)}) copy-start(s32[2,8,8]{2,1,0:T(8,128)} %param.18) | copy-start | bytes 1540
  0.7 9.9 %copy-start.7 = (bf16[2,8,4096]{2,1,0:T(8,128)(2,1)S(1)}, bf16[2,8,4096]{2,1,0:T(8,128)(2,1)}, u32[]{:S(2)}) copy-start(bf16[2,8,4096]{2,1,0:T(8,128)(2,1)} %param.14) | copy-start | bytes 393220
  0.7 14.2 %copy-start.6 = (s32[2,8]{1,0:T(2,128)S(1)}, s32[2,8]{1,0:T(2,128)}, u32[]{:S(2)}) copy-start(s32[2,8]{1,0:T(2,128)} %len_ref.3) | copy-start | bytes 196
  0.7 20.2 %copy-start.9 = (bf16[1,3,256,4]{2,3,1,0:T(4,128)(2,1)S(1)}, bf16[1,3,256,4]{2,3,1,0:T(4,128)(2,1)}, u32[]{:S(2)}) copy-start(bf16[1,3,256,4]{2,3,1,0:T(4,128)(2,1)} %param.25) | copy-start | bytes 18436
  4.8 24.2 %collective-permute-start.1 = (bf16[8,8192]{1,0:T(8,128)(2,1)S(1)}, bf16[8,8192]{1,0:T(8,128)(2,1)S(1)}, u32[]{:S(2)}, u32[]{:S(2)}) collective-permute-start(bf16[8,8192]{1,0:T(8,128)(2,1)S(1)} %attend.2), channel_id=1, source_target_pairs={{0,4},{1,5},{2,6},{3,7},{4,0},{5,1},{6,2},{7,3},{8,12},{9,13},{10,... | collective-permute-start | bytes 393224 | tf_op jit(solution)/shard_map/ppermute | solution.py:325
  7.9 13.0 %collective-permute-start = (bf16[8,8192]{1,0:T(8,128)(2,1)S(1)}, bf16[8,8192]{1,0:T(8,128)(2,1)S(1)}, u32[]{:S(2)}, u32[]{:S(2)}) collective-permute-start(bf16[8,8192]{1,0:T(8,128)(2,1)S(1)} %attend.2), channel_id=1, source_target_pairs={{0,8},{1,9},{2,10},{3,11},{4,12},{5,13},{6,14},{7,15},{8,0},{9,1},... | collective-permute-start | bytes 393224 | tf_op jit(solution)/shard_map/ppermute | solution.py:325
  11.3 17.7 %all-to-all-start = ((bf16[16,2,8,272]{3,2,1,0:T(8,128)(2,1)}), bf16[16,2,8,272]{3,2,1,0:T(8,128)(2,1)S(1)}, u32[]{:S(2)}, u32[]{:S(2)}) async-start(bf16[16,2,8,272]{3,2,1,0:T(8,128)(2,1)} %pad_maximum_fusion.3), calls=%async_computation | async-start | bytes 393216 | tf_op jit(solution)/shard_map/all_to_all | solution.py:409
  19.0 6.3 %collective-permute-start.5 = (bf16[8,8192]{1,0:T(8,128)(2,1)S(1)}, bf16[8,8192]{1,0:T(8,128)(2,1)S(1)}, u32[]{:S(2)}, u32[]{:S(2)}) collective-permute-start(bf16[8,8192]{1,0:T(8,128)(2,1)S(1)} %attend.3), channel_id=1, source_target_pairs={{0,2},{1,3},{2,0},{3,1},{4,6},{5,7},{6,4},{7,5},{8,10},{9,11},{10,... | collective-permute-start | bytes 393224 | tf_op jit(solution)/shard_map/ppermute | solution.py:325
  20.9 8.1 %collective-permute-start.2 = (bf16[8,8192]{1,0:T(8,128)(2,1)S(1)}, bf16[8,8192]{1,0:T(8,128)(2,1)S(1)}, u32[]{:S(2)}, u32[]{:S(2)}) collective-permute-start(bf16[8,8192]{1,0:T(8,128)(2,1)S(1)} %collective-permute-done), channel_id=1, source_target_pairs={{0,4},{1,5},{2,6},{3,7},{4,0},{5,1},{6,2},{7,3},{8,12},{9,13},{10,... | collective-permute-start | bytes 393224 | tf_op jit(solution)/shard_map/ppermute | solution.py:325
  25.3 26.3 %collective-permute-start.10 = (bf16[2,8,8192]{2,1,0:T(8,128)(2,1)S(1)}, bf16[2,8,8192]{2,1,0:T(8,128)(2,1)S(1)}, u32[]{:S(2)}, u32[]{:S(2)}) collective-permute-start(bf16[2,8,8192]{2,1,0:T(8,128)(2,1)S(1)} %pad_maximum_fusion.1.refs_4_), channel_id=1, source_target_pairs={{0,1},{1,0},{2,3},{3,2},{4,5},{5,4},{6,7},{7,6},{8,9},{9,8},{10,11... | collective-permute-start | bytes 786440 | tf_op jit(solution)/shard_map/ppermute | solution.py:325
  25.4 25.6 %collective-permute-start.8 = (bf16[2,8,8192]{2,1,0:T(8,128)(2,1)S(1)}, bf16[2,8,8192]{2,1,0:T(8,128)(2,1)S(1)}, u32[]{:S(2)}, u32[]{:S(2)}) collective-permute-start(bf16[2,8,8192]{2,1,0:T(8,128)(2,1)S(1)} %pad_maximum_fusion.1.refs_4_), channel_id=1, source_target_pairs={{0,4},{1,5},{2,6},{3,7},{4,0},{5,1},{6,2},{7,3},{8,12},{9,13},{10,... | collective-permute-start | bytes 786440 | tf_op jit(solution)/shard_map/ppermute | solution.py:325
  26.8 14.9 %collective-permute-start.6 = (bf16[2,8,8192]{2,1,0:T(8,128)(2,1)S(1)}, bf16[2,8,8192]{2,1,0:T(8,128)(2,1)S(1)}, u32[]{:S(2)}, u32[]{:S(2)}) collective-permute-start(bf16[2,8,8192]{2,1,0:T(8,128)(2,1)S(1)} %pad_maximum_fusion.1.refs_4_), channel_id=1, source_target_pairs={{0,8},{1,9},{2,10},{3,11},{4,12},{5,13},{6,14},{7,15},{8,0},{9,1},... | collective-permute-start | bytes 786440 | tf_op jit(solution)/shard_map/ppermute | solution.py:325
  29.1 24.5 %collective-permute-start.4 = (bf16[4,8,8192]{2,1,0:T(8,128)(2,1)S(1)}, bf16[4,8,8192]{2,1,0:T(8,128)(2,1)S(1)}, u32[]{:S(2)}, u32[]{:S(2)}) collective-permute-start(bf16[4,8,8192]{2,1,0:T(8,128)(2,1)S(1)} %pad_maximum_fusion.refs_0_), channel_id=1, source_target_pairs={{0,1},{1,0},{2,3},{3,2},{4,5},{5,4},{6,7},{7,6},{8,9},{9,8},{10,11... | collective-permute-start | bytes 1572872 | tf_op jit(solution)/shard_map/ppermute | solution.py:325
  29.2 21.7 %collective-permute-start.3 = (bf16[4,8,8192]{2,1,0:T(8,128)(2,1)S(1)}, bf16[4,8,8192]{2,1,0:T(8,128)(2,1)S(1)}, u32[]{:S(2)}, u32[]{:S(2)}) collective-permute-start(bf16[4,8,8192]{2,1,0:T(8,128)(2,1)S(1)} %pad_maximum_fusion.refs_0_), channel_id=1, source_target_pairs={{0,2},{1,3},{2,0},{3,1},{4,6},{5,7},{6,4},{7,5},{8,10},{9,11},{10,... | collective-permute-start | bytes 1572872 | tf_op jit(solution)/shard_map/ppermute | solution.py:325
  41.8 9.7 %collective-permute-start.9 = (bf16[2,8,8192]{2,1,0:T(8,128)(2,1)S(1)}, bf16[2,8,8192]{2,1,0:T(8,128)(2,1)S(1)}, u32[]{:S(2)}, u32[]{:S(2)}) collective-permute-start(bf16[2,8,8192]{2,1,0:T(8,128)(2,1)S(1)} %collective-permute-done.6.refs_5_), channel_id=1, source_target_pairs={{0,4},{1,5},{2,6},{3,7},{4,0},{5,1},{6,2},{7,3},{8,12},{9,13},{10,... | collective-permute-start | bytes 786440 | tf_op jit(solution)/shard_map/ppermute | solution.py:325
  41.9 12.1 %copy-start = (bf16[8192,256]{1,0:T(8,128)(2,1)S(1)}, bf16[8192,256]{1,0:T(8,128)(2,1)}, u32[]{:S(2)}) copy-start(bf16[8192,256]{1,0:T(8,128)(2,1)} %refs_12_.1) | copy-start | bytes 12582916
  50.9 3.1 %collective-permute-start.7 = (bf16[4,8,8192]{2,1,0:T(8,128)(2,1)S(1)}, bf16[4,8,8192]{2,1,0:T(8,128)(2,1)S(1)}, u32[]{:S(2)}, u32[]{:S(2)}) collective-permute-start(bf16[4,8,8192]{2,1,0:T(8,128)(2,1)S(1)} %collective-permute-done.3.refs_1_), channel_id=1, source_target_pairs={{0,1},{1,0},{2,3},{3,2},{4,5},{5,4},{6,7},{7,6},{8,9},{9,8},{10,11... | collective-permute-start | bytes 1572872 | tf_op jit(solution)/shard_map/ppermute | solution.py:325
  51.0 2.3 %collective-permute-start.11 = (bf16[2,8,8192]{2,1,0:T(8,128)(2,1)S(1)}, bf16[2,8,8192]{2,1,0:T(8,128)(2,1)S(1)}, u32[]{:S(2)}, u32[]{:S(2)}) collective-permute-start(bf16[2,8,8192]{2,1,0:T(8,128)(2,1)S(1)} %collective-permute-done.6.refs_5_), channel_id=1, source_target_pairs={{0,1},{1,0},{2,3},{3,2},{4,5},{5,4},{6,7},{7,6},{8,9},{9,8},{10,11... | collective-permute-start | bytes 786440 | tf_op jit(solution)/shard_map/ppermute | solution.py:325
  51.5 2.1 %collective-permute-start.12 = (bf16[2,8,8192]{2,1,0:T(8,128)(2,1)S(1)}, bf16[2,8,8192]{2,1,0:T(8,128)(2,1)S(1)}, u32[]{:S(2)}, u32[]{:S(2)}) collective-permute-start(bf16[2,8,8192]{2,1,0:T(8,128)(2,1)S(1)} %collective-permute-done.8.refs_6_), channel_id=1, source_target_pairs={{0,1},{1,0},{2,3},{3,2},{4,5},{5,4},{6,7},{7,6},{8,9},{9,8},{10,11... | collective-permute-start | bytes 786440 | tf_op jit(solution)/shard_map/ppermute | solution.py:325
  51.6 2.4 %collective-permute-start.13 = (bf16[2,8,8192]{2,1,0:T(8,128)(2,1)S(1)}, bf16[2,8,8192]{2,1,0:T(8,128)(2,1)S(1)}, u32[]{:S(2)}, u32[]{:S(2)}) collective-permute-start(bf16[2,8,8192]{2,1,0:T(8,128)(2,1)S(1)} %collective-permute-done.9.refs_7_), channel_id=1, source_target_pairs={{0,1},{1,0},{2,3},{3,2},{4,5},{5,4},{6,7},{7,6},{8,9},{9,8},{10,11... | collective-permute-start | bytes 786440 | tf_op jit(solution)/shard_map/ppermute | solution.py:325
  55.3 6.2 %collective-permute-start.14 = (bf16[16,8,256]{2,1,0:T(8,128)(2,1)S(1)}, bf16[16,8,256]{2,1,0:T(8,128)(2,1)S(1)}, u32[]{:S(2)}, u32[]{:S(2)}) collective-permute-start(bf16[16,8,256]{2,1,0:T(8,128)(2,1)S(1)} %get-tuple-element.41), channel_id=1, source_target_pairs={{0,8},{1,9},{2,10},{3,11},{4,12},{5,13},{6,14},{7,15},{8,0},{9,1},... | collective-permute-start | bytes 196616 | tf_op jit(solution)/shard_map/ppermute | solution.py:325
  58.0 4.9 %collective-permute-start.19 = (bf16[16,8,256]{2,1,0:T(8,128)(2,1)S(1)}, bf16[16,8,256]{2,1,0:T(8,128)(2,1)S(1)}, u32[]{:S(2)}, u32[]{:S(2)}) collective-permute-start(bf16[16,8,256]{2,1,0:T(8,128)(2,1)S(1)} %get-tuple-element.43), channel_id=1, source_target_pairs={{0,2},{1,3},{2,0},{3,1},{4,6},{5,7},{6,4},{7,5},{8,10},{9,11},{10,... | collective-permute-start | bytes 196616 | tf_op jit(solution)/shard_map/ppermute | solution.py:325
  59.4 6.3 %collective-permute-start.15 = (bf16[16,8,256]{2,1,0:T(8,128)(2,1)S(1)}, bf16[16,8,256]{2,1,0:T(8,128)(2,1)S(1)}, u32[]{:S(2)}, u32[]{:S(2)}) collective-permute-start(bf16[16,8,256]{2,1,0:T(8,128)(2,1)S(1)} %get-tuple-element.41), channel_id=1, source_target_pairs={{0,4},{1,5},{2,6},{3,7},{4,0},{5,1},{6,2},{7,3},{8,12},{9,13},{10,... | collective-permute-start | bytes 196616 | tf_op jit(solution)/shard_map/ppermute | solution.py:325
  61.5 4.3 %collective-permute-start.16 = (bf16[16,8,256]{2,1,0:T(8,128)(2,1)S(1)}, bf16[16,8,256]{2,1,0:T(8,128)(2,1)S(1)}, u32[]{:S(2)}, u32[]{:S(2)}) collective-permute-start(bf16[16,8,256]{2,1,0:T(8,128)(2,1)S(1)} %collective-permute-done.14), channel_id=1, source_target_pairs={{0,4},{1,5},{2,6},{3,7},{4,0},{5,1},{6,2},{7,3},{8,12},{9,13},{10,... | collective-permute-start | bytes 196616 | tf_op jit(solution)/shard_map/ppermute | solution.py:325
  62.9 18.9 %collective-permute-start.24 = (bf16[2,16,8,256]{3,2,1,0:T(8,128)(2,1)S(1)}, bf16[2,16,8,256]{3,2,1,0:T(8,128)(2,1)S(1)}, u32[]{:S(2)}, u32[]{:S(2)}) collective-permute-start(bf16[2,16,8,256]{3,2,1,0:T(8,128)(2,1)S(1)} %pad_maximum_fusion.4.refs_4_), channel_id=1, source_target_pairs={{0,1},{1,0},{2,3},{3,2},{4,5},{5,4},{6,7},{7,6},{8,9},{9,8},{10,11... | collective-permute-start | bytes 393224 | tf_op jit(solution)/shard_map/ppermute | solution.py:325
  63.0 14.8 %collective-permute-start.22 = (bf16[2,16,8,256]{3,2,1,0:T(8,128)(2,1)S(1)}, bf16[2,16,8,256]{3,2,1,0:T(8,128)(2,1)S(1)}, u32[]{:S(2)}, u32[]{:S(2)}) collective-permute-start(bf16[2,16,8,256]{3,2,1,0:T(8,128)(2,1)S(1)} %pad_maximum_fusion.4.refs_4_), channel_id=1, source_target_pairs={{0,4},{1,5},{2,6},{3,7},{4,0},{5,1},{6,2},{7,3},{8,12},{9,13},{10,... | collective-permute-start | bytes 393224 | tf_op jit(solution)/shard_map/ppermute | solution.py:325
  63.7 12.4 %collective-permute-start.21 = (bf16[2,16,8,256]{3,2,1,0:T(8,128)(2,1)S(1)}, bf16[2,16,8,256]{3,2,1,0:T(8,128)(2,1)S(1)}, u32[]{:S(2)}, u32[]{:S(2)}) collective-permute-start(bf16[2,16,8,256]{3,2,1,0:T(8,128)(2,1)S(1)} %pad_maximum_fusion.4.refs_4_), channel_id=1, source_target_pairs={{0,8},{1,9},{2,10},{3,11},{4,12},{5,13},{6,14},{7,15},{8,0},{9,1},... | collective-permute-start | bytes 393224 | tf_op jit(solution)/shard_map/ppermute | solution.py:325
  65.9 15.4 %collective-permute-start.17 = (bf16[4,16,8,256]{3,2,1,0:T(8,128)(2,1)S(1)}, bf16[4,16,8,256]{3,2,1,0:T(8,128)(2,1)S(1)}, u32[]{:S(2)}, u32[]{:S(2)}) collective-permute-start(bf16[4,16,8,256]{3,2,1,0:T(8,128)(2,1)S(1)} %pad_maximum_fusion.2.refs_0_), channel_id=1, source_target_pairs={{0,2},{1,3},{2,0},{3,1},{4,6},{5,7},{6,4},{7,5},{8,10},{9,11},{10,... | collective-permute-start | bytes 786440 | tf_op jit(solution)/shard_map/ppermute | solution.py:325
  67.5 15.8 %copy-start.1 = (bf16[4096,16]{0,1:T(8,128)(2,1)S(1)}, bf16[4096,16]{0,1:T(8,128)(2,1)}, u32[]{:S(2)}) copy-start(bf16[4096,16]{0,1:T(8,128)(2,1)} %param.21) | copy-start | bytes 393220
  67.5 15.8 %copy-start.2 = (f32[4096]{0:T(1024)S(1)}, f32[4096]{0:T(1024)}, u32[]{:S(2)}) copy-start(f32[4096]{0:T(1024)} %param.20) | copy-start | bytes 49156
  67.5 15.8 %copy-start.3 = (f32[1,4096]{1,0:T(1,128)S(1)}, f32[1,4096]{1,0:T(1,128)}, u32[]{:S(2)}) copy-start(f32[1,4096]{1,0:T(1,128)} %refs_19_.1) | copy-start | bytes 49156
  67.5 15.8 %copy-start.4 = (f32[1,2,768]{2,1,0:T(2,128)S(1)}, f32[1,2,768]{2,1,0:T(2,128)}, u32[]{:S(2)}) copy-start(f32[1,2,768]{2,1,0:T(2,128)} %param.26) | copy-start | bytes 18436
  76.2 5.1 %collective-permute-start.23 = (bf16[2,16,8,256]{3,2,1,0:T(8,128)(2,1)S(1)}, bf16[2,16,8,256]{3,2,1,0:T(8,128)(2,1)S(1)}, u32[]{:S(2)}, u32[]{:S(2)}) collective-permute-start(bf16[2,16,8,256]{3,2,1,0:T(8,128)(2,1)S(1)} %collective-permute-done.21.refs_5_), channel_id=1, source_target_pairs={{0,4},{1,5},{2,6},{3,7},{4,0},{5,1},{6,2},{7,3},{8,12},{9,13},{10,... | collective-permute-start | bytes 393224 | tf_op jit(solution)/shard_map/ppermute | solution.py:325
  77.7 4.9 %collective-permute-start.18 = (bf16[4,16,8,256]{3,2,1,0:T(8,128)(2,1)S(1)}, bf16[4,16,8,256]{3,2,1,0:T(8,128)(2,1)S(1)}, u32[]{:S(2)}, u32[]{:S(2)}) collective-permute-start(bf16[4,16,8,256]{3,2,1,0:T(8,128)(2,1)S(1)} %pad_maximum_fusion.2.refs_0_), channel_id=1, source_target_pairs={{0,1},{1,0},{2,3},{3,2},{4,5},{5,4},{6,7},{7,6},{8,9},{9,8},{10,11... | collective-permute-start | bytes 786440 | tf_op jit(solution)/shard_map/ppermute | solution.py:325
  77.8 4.1 %collective-permute-start.25 = (bf16[2,16,8,256]{3,2,1,0:T(8,128)(2,1)S(1)}, bf16[2,16,8,256]{3,2,1,0:T(8,128)(2,1)S(1)}, u32[]{:S(2)}, u32[]{:S(2)}) collective-permute-start(bf16[2,16,8,256]{3,2,1,0:T(8,128)(2,1)S(1)} %collective-permute-done.21.refs_5_), channel_id=1, source_target_pairs={{0,1},{1,0},{2,3},{3,2},{4,5},{5,4},{6,7},{7,6},{8,9},{9,8},{10,11... | collective-permute-start | bytes 393224 | tf_op jit(solution)/shard_map/ppermute | solution.py:325
  81.3 1.3 %collective-permute-start.26 = (bf16[2,16,8,256]{3,2,1,0:T(8,128)(2,1)S(1)}, bf16[2,16,8,256]{3,2,1,0:T(8,128)(2,1)S(1)}, u32[]{:S(2)}, u32[]{:S(2)}) collective-permute-start(bf16[2,16,8,256]{3,2,1,0:T(8,128)(2,1)S(1)} %collective-permute-done.22.refs_6_), channel_id=1, source_target_pairs={{0,1},{1,0},{2,3},{3,2},{4,5},{5,4},{6,7},{7,6},{8,9},{9,8},{10,11... | collective-permute-start | bytes 393224 | tf_op jit(solution)/shard_map/ppermute | solution.py:325
  81.3 1.5 %collective-permute-start.27 = (bf16[2,16,8,256]{3,2,1,0:T(8,128)(2,1)S(1)}, bf16[2,16,8,256]{3,2,1,0:T(8,128)(2,1)S(1)}, u32[]{:S(2)}, u32[]{:S(2)}) collective-permute-start(bf16[2,16,8,256]{3,2,1,0:T(8,128)(2,1)S(1)} %collective-permute-done.23.refs_7_), channel_id=1, source_target_pairs={{0,1},{1,0},{2,3},{3,2},{4,5},{5,4},{6,7},{7,6},{8,9},{9,8},{10,11... | collective-permute-start | bytes 393224 | tf_op jit(solution)/shard_map/ppermute | solution.py:325
  81.8 1.5 %collective-permute-start.20 = (bf16[4,16,8,256]{3,2,1,0:T(8,128)(2,1)S(1)}, bf16[4,16,8,256]{3,2,1,0:T(8,128)(2,1)S(1)}, u32[]{:S(2)}, u32[]{:S(2)}) collective-permute-start(bf16[4,16,8,256]{3,2,1,0:T(8,128)(2,1)S(1)} %collective-permute-done.17.refs_1_), channel_id=1, source_target_pairs={{0,1},{1,0},{2,3},{3,2},{4,5},{5,4},{6,7},{7,6},{8,9},{9,8},{10,11... | collective-permute-start | bytes 786440 | tf_op jit(solution)/shard_map/ppermute | solution.py:325
  92.3 2.0 %collective-permute-start.28 = (bf16[8,8,4096]{2,1,0:T(8,128)(2,1)S(1)}, bf16[8,8,4096]{2,1,0:T(8,128)(2,1)S(1)}, u32[]{:S(2)}, u32[]{:S(2)}) collective-permute-start(bf16[8,8,4096]{2,1,0:T(8,128)(2,1)S(1)} %get-tuple-element.51), channel_id=1, source_target_pairs={{0,1},{1,0},{2,3},{3,2},{4,5},{5,4},{6,7},{7,6},{8,9},{9,8},{10,11... | collective-permute-start | bytes 1572872 | tf_op jit(solution)/shard_map/ppermute | solution.py:325
  92.6 2.5 %collective-permute-start.32 = (bf16[8,8,4096]{2,1,0:T(8,128)(2,1)S(1)}, bf16[8,8,4096]{2,1,0:T(8,128)(2,1)S(1)}, u32[]{:S(2)}, u32[]{:S(2)}) collective-permute-start(bf16[8,8,4096]{2,1,0:T(8,128)(2,1)S(1)} %get-tuple-element.54), channel_id=1, source_target_pairs={{0,1},{1,0},{2,3},{3,2},{4,5},{5,4},{6,7},{7,6},{8,9},{9,8},{10,11... | collective-permute-start | bytes 1572872 | tf_op jit(solution)/shard_map/ppermute | solution.py:325
  94.4 8.5 %collective-permute-start.29 = (bf16[4,8,4096]{2,1,0:T(8,128)(2,1)S(1)}, bf16[4,8,4096]{2,1,0:T(8,128)(2,1)S(1)}, u32[]{:S(2)}, u32[]{:S(2)}) collective-permute-start(bf16[4,8,4096]{2,1,0:T(8,128)(2,1)S(1)} %get-tuple-element.56), channel_id=1, source_target_pairs={{0,2},{1,3},{2,0},{3,1},{4,6},{5,7},{6,4},{7,5},{8,10},{9,11},{10,... | collective-permute-start | bytes 786440 | tf_op jit(solution)/shard_map/ppermute | solution.py:325
  95.2 9.3 %collective-permute-start.33 = (bf16[4,8,4096]{2,1,0:T(8,128)(2,1)S(1)}, bf16[4,8,4096]{2,1,0:T(8,128)(2,1)S(1)}, u32[]{:S(2)}, u32[]{:S(2)}) collective-permute-start(bf16[4,8,4096]{2,1,0:T(8,128)(2,1)S(1)} %get-tuple-element.58), channel_id=1, source_target_pairs={{0,4},{1,5},{2,6},{3,7},{4,0},{5,1},{6,2},{7,3},{8,12},{9,13},{10,... | collective-permute-start | bytes 786440 | tf_op jit(solution)/shard_map/ppermute | solution.py:325
  103.0 6.8 %collective-permute-start.30 = (bf16[2,8,4096]{2,1,0:T(8,128)(2,1)S(1)}, bf16[2,8,4096]{2,1,0:T(8,128)(2,1)S(1)}, u32[]{:S(2)}, u32[]{:S(2)}) collective-permute-start(bf16[2,8,4096]{2,1,0:T(8,128)(2,1)S(1)} %get-tuple-element.60), channel_id=1, source_target_pairs={{0,4},{1,5},{2,6},{3,7},{4,0},{5,1},{6,2},{7,3},{8,12},{9,13},{10,... | collective-permute-start | bytes 393224 | tf_op jit(solution)/shard_map/ppermute | solution.py:325
  104.5 9.8 %collective-permute-start.34 = (bf16[2,8,4096]{2,1,0:T(8,128)(2,1)S(1)}, bf16[2,8,4096]{2,1,0:T(8,128)(2,1)S(1)}, u32[]{:S(2)}, u32[]{:S(2)}) collective-permute-start(bf16[2,8,4096]{2,1,0:T(8,128)(2,1)S(1)} %get-tuple-element.62), channel_id=1, source_target_pairs={{0,8},{1,9},{2,10},{3,11},{4,12},{5,13},{6,14},{7,15},{8,0},{9,1},... | collective-permute-start | bytes 393224 | tf_op jit(solution)/shard_map/ppermute | solution.py:325
  109.8 5.9 %collective-permute-start.31 = (bf16[1,8,4096]{2,1,0:T(8,128)(2,1)S(1)}, bf16[1,8,4096]{2,1,0:T(8,128)(2,1)S(1)}, u32[]{:S(2)}, u32[]{:S(2)}) collective-permute-start(bf16[1,8,4096]{2,1,0:T(8,128)(2,1)S(1)} %add_convert_fusion.10), channel_id=1, source_target_pairs={{0,8},{1,9},{2,10},{3,11},{4,12},{5,13},{6,14},{7,15},{8,0},{9,1},... | collective-permute-start | bytes 196616 | tf_op jit(solution)/shard_map/ppermute | solution.py:325
  114.3 4.3 %collective-permute-start.35 = (bf16[1,8,4096]{2,1,0:T(8,128)(2,1)S(1)}, bf16[1,8,4096]{2,1,0:T(8,128)(2,1)S(1)}, u32[]{:S(2)}, u32[]{:S(2)}) collective-permute-start(bf16[1,8,4096]{2,1,0:T(8,128)(2,1)S(1)} %add_convert_fusion.8), channel_id=1, source_target_pairs={{0,2},{1,3},{2,0},{3,1},{4,6},{5,7},{6,4},{7,5},{8,10},{9,11},{10,... | collective-permute-start | bytes 196616 | tf_op jit(solution)/shard_map/ppermute | solution.py:325

commit v6 on v5

--- a/solution.py
+++ b/solution.py
@@ -126,8 +126,9 @@
         lax.fori_loop(0, rows // tile, body, 0, unroll=rows // tile if rows // tile <= 12 else 8)
 
 
-def expand(table, codes, stacked, after=()):
+def expand(table, codes, stacked, after=(), part=None):
     rows, columns = codes.shape
+    skip = 0
     if stacked:
         block = 512
         grid = (columns // block,)
@@ -136,8 +137,10 @@
         out_shape = (4, rows, columns)
     else:
         block = 128
+        if part is not None:
+            skip, rows = part[0] // block, part[1]
         grid = (rows // block,)
-        code_spec = pl.BlockSpec((block, columns), lambda b: (b, 0))
+        code_spec = pl.BlockSpec((block, columns), lambda b: (b + skip, 0))
         out_spec = pl.BlockSpec((block, 4 * columns), lambda b: (b, 0))
         out_shape = (rows, 4 * columns)
     out = pl.pallas_call(
@@ -204,85 +207,90 @@
     )(me, *held)
 
 
-def experts_kernel(masks, counts, orders, me_ref, *refs):
+def experts_kernel(masks, counts, orders, downs, me_ref, *refs):
     pieces, refs = refs[: len(masks)], refs[len(masks) :]
-    gain_ref, router_ref, hot_ref, gate_ref, up_ref, down_ref, gu_scale_ref, down_scale_ref = refs[
-        :8
-    ]
+    gain_ref, router_ref, hot_ref, gate_ref, up_ref, gu_scale_ref, down_scale_ref = refs[:7]
+    down_refs, refs = refs[7 : 7 + downs], refs[7 + downs :]
     groups = len(orders)
     send_refs, keep_refs, own_refs = (
-        refs[8 + i * groups : 8 + (i + 1) * groups] for i in range(3)
-    )
-    token_scr, weight_scr, acc_ref = refs[-3:]
+        refs[i * groups : (i + 1) * groups] for i in range(3)
+    )
+    token_scr = refs[-1]
     _, shards, rows, columns = pieces[0].shape
     total, width = token_scr.shape
     part = shards * rows
-    hidden_units = gate_ref.shape[0]
     me = me_ref[0]
     nt = (((1,), (1,)), ((), ()))
 
-    for m in range(groups):
+    hots = []
+    for m, order in enumerate(orders):
+        places = [me ^ mask for mask in order]
+        hots += [hot_ref[m, place].astype(jnp.float32) for place in places]
         mine = [
             (ref, i, mask)
             for ref, mask_list, n in zip(pieces, masks, counts)
             if n == m
             for i, mask in enumerate(mask_list)
         ]
+        chunk = slice(m * part, (m + 1) * part)
         squares = jnp.zeros((part, columns), jnp.float32)
-        for ref, i, _ in mine:
-            value = ref[i].reshape(part, columns).astype(jnp.float32)
-            squares += value * value
-        mean = jnp.sum(squares, axis=-1, keepdims=True) / width
-        inverse = lax.rsqrt(mean + 1e-06)
         for ref, i, mask in mine:
             at = pl.ds(0, columns)
             if len(mine) > 1:
                 at = pl.ds(pl.multiple_of((me ^ mask) * columns, columns), columns)
-            value = ref[i].reshape(part, columns).astype(jnp.float32)
+            value = jnp.concatenate([ref[i, place].astype(jnp.float32) for place in places])
             own_refs[m][:, at] = ref[i, me]
-            token_scr[m * part : (m + 1) * part, at] = (
-                value * inverse * gain_ref[:, at]
-            ).astype(jnp.bfloat16)
+            token_scr[chunk, at] = value.astype(jnp.bfloat16)
+            squares += value * value
+        mean = jnp.sum(squares, axis=-1, keepdims=True) / width
+        inverse = lax.rsqrt(mean + 1e-06)
+        for first in range(0, width, 256):
+            at = slice(first, first + 256)
+            value = token_scr[chunk, at].astype(jnp.float32)
+            token_scr[chunk, at] = (value * inverse * gain_ref[:, at]).astype(jnp.bfloat16)
     logits = lax.dot_general(
         token_scr[...], router_ref[...], nt, preferred_element_type=jnp.float32
     )
-    hot = hot_ref[...].astype(jnp.float32) > 0.5
+    hot = jnp.concatenate(hots)[:, : logits.shape[1]] > 0.5
     logits = jnp.where(hot, logits, -1e30)
     raised = jnp.where(hot, jnp.exp(logits - jnp.max(logits, axis=-1, keepdims=True)), 0.0)
     raised = raised / jnp.sum(raised, axis=-1, keepdims=True)
     column = lax.broadcasted_iota(jnp.int32, raised.shape, 1) == me
     weight = jnp.sum(jnp.where(column, raised, 0.0), axis=-1, keepdims=True)
     weight = weight.astype(jnp.bfloat16).astype(jnp.float32)
-    weight_scr[...] = jnp.broadcast_to(weight, (total, LANES)).reshape(weight_scr.shape)
-
-    block, piece = 256, 1024
-    for f in range(hidden_units // block):
-        units = slice(f * block, (f + 1) * block)
+
+    block, piece = 256, 512
+    inner = []
+    for first in range(0, gate_ref.shape[0], block):
+        units = slice(first, first + block)
         tokens = token_scr[...]
         gate = lax.dot_general(tokens, gate_ref[units, :], nt, preferred_element_type=jnp.float32)
         up = lax.dot_general(tokens, up_ref[units, :], nt, preferred_element_type=jnp.float32)
         gate = gate * gu_scale_ref[0:1, units]
         up = up * gu_scale_ref[1:2, units]
-        inner = (gate / (1.0 + jnp.exp(-gate)) * up).astype(jnp.bfloat16)
-        for c in range(width // piece):
-            at = slice(c * piece, (c + 1) * piece)
-            product = jnp.dot(inner, down_ref[units, at], preferred_element_type=jnp.float32)
-            product = product.reshape(groups * shards, rows, piece)
-            if f == 0:
-                acc_ref[:, :, at] = product
-            else:
-                acc_ref[:, :, at] += product
+        inner.append((gate / (1.0 + jnp.exp(-gate)) * up).astype(jnp.bfloat16))
+    inner = jnp.concatenate(inner, axis=1)
 
     half = shards // 2
-    for m, order in enumerate(orders):
-        for p, mask in enumerate(order):
-            source = m * shards + (me ^ mask)
-            value = (acc_ref[source] * down_scale_ref[...]).astype(jnp.bfloat16)
-            value = (value.astype(jnp.float32) * weight_scr[source][:, 0:1]).astype(jnp.bfloat16)
-            if p < half:
-                keep_refs[m][p] = value
-            else:
-                send_refs[m][p - half] = value
+    for first in range(0, width, piece):
+        at = slice(first, first + piece)
+        product, begin = None, 0
+        for down_ref in down_refs:
+            end = begin + down_ref.shape[0]
+            term = jnp.dot(
+                inner[:, begin:end], down_ref[:, at], preferred_element_type=jnp.float32
+            )
+            product, begin = term if product is None else product + term, end
+        product = (product * down_scale_ref[:, at]).astype(jnp.bfloat16).astype(jnp.float32)
+        product = product * weight
+        for m in range(groups):
+            for p in range(shards):
+                row = m * part + p * rows
+                value = product[row : row + rows].astype(jnp.bfloat16)
+                if p < half:
+                    keep_refs[m][p, :, at] = value
+                else:
+                    send_refs[m][p - half, :, at] = value
 
 
 def run_experts(me, streams, gain, router, hot, gate, up, down, gu_scale, down_scale, orders):
@@ -295,21 +303,17 @@
     total = groups * shards * rows
     half_shape = jax.ShapeDtypeStruct((shards // 2, rows, width), jnp.bfloat16)
     in_vmem = pl.BlockSpec(memory_space=pltpu.VMEM)
-    held = [gate, up, down]
+    held = [gate, up, *down]
     if total <= 256:
         held = [pltpu.with_memory_space_constraint(w, pltpu.VMEM) for w in held]
         pieces = [pltpu.with_memory_space_constraint(w, pltpu.VMEM) for w in pieces]
     outs = pl.pallas_call(
-        functools.partial(experts_kernel, masks, counts, orders),
-        in_specs=[pl.BlockSpec(memory_space=pltpu.SMEM)] + [in_vmem] * (len(pieces) + 8),
+        functools.partial(experts_kernel, masks, counts, orders, len(down)),
+        in_specs=[pl.BlockSpec(memory_space=pltpu.SMEM)] + [in_vmem] * (len(pieces) + 7 + len(down)),
         out_specs=[in_vmem] * (3 * groups),
         out_shape=[half_shape] * (2 * groups)
         + [jax.ShapeDtypeStruct((rows, width), jnp.bfloat16)] * groups,
-        scratch_shapes=[
-            pltpu.VMEM((total, width), jnp.bfloat16),
-            pltpu.VMEM((groups * shards, rows, LANES), jnp.float32),
-            pltpu.VMEM((groups * shards, rows, width), jnp.float32),
-        ],
+        scratch_shapes=[pltpu.VMEM((total, width), jnp.bfloat16)],
         name="experts",
         compiler_params=pltpu.CompilerParams(vmem_limit_bytes=(14 if total <= 256 else 62) * MIB),
         cost_estimate=pl.CostEstimate(
@@ -317,7 +321,7 @@
             bytes_accessed=6 * width * hidden_units,
             transcendentals=0,
         ),
-    )(me, *pieces, gain, router, hot, *held, gu_scale, down_scale)
+    )(me, *pieces, gain, router, hot, *held[:2], gu_scale, down_scale, *held[2:])
     return [tuple(outs[i * groups + m] for i in range(3)) for m in range(groups)]
 
 
@@ -414,18 +418,22 @@
         (words[0], words[1], words[2], me_list, packed)
     )
     hidden_columns = packed[..., :columns]
-    hot_all = packed[..., columns:].transpose(1, 0, 2, 3).reshape(micro_count, count * rows, count)
+    hot_all = packed[..., columns:].transpose(1, 0, 2, 3)
 
     attended = [attend(queries, kv_cache, lengths, m) for m in range(micro_count)]
     make_gate = lambda after: expand(tables[0], gate_codes[0].T, True, after)
     make_up = lambda after: expand(tables[1], up_codes[0].T, True, after)
-    make_down = lambda after: expand(tables[2], down_codes[0], False, after)
+    units = down_codes.shape[1]
+    make_down = [
+        lambda after, part=part: expand(tables[2], down_codes[0], False, after, part)
+        for part in ((0, 2 * units // 3), (2 * units // 3, units // 3))
+    ]
     if count == 16 and micro_count == 2:
         gathered, (gate, up) = gather_two(*attended, [make_gate, make_up])
         column_parts = project(me_list, gathered, out_weight, hidden_columns)
-        streams, (down,) = gather_two(*column_parts, [make_down])
+        streams, down = gather_two(*column_parts, make_down)
     else:
-        gate, up, down = make_gate(()), make_up(()), make_down(())
+        gate, up, down = make_gate(()), make_up(()), [make(()) for make in make_down]
         gathered = [gather_all(value, count) for value in attended]
         column_parts = project(me_list, gathered, out_weight, hidden_columns)
         streams = [gather_all(value, count) for value in column_parts]
@@ -447,7 +455,7 @@
             [streams[m] for m in batch],
             norm_gain.reshape(1, width),
             router_weight.T,
-            jnp.concatenate([hot_all[m] for m in batch]),
+            hot_all[batch[0] : batch[-1] + 1],
             gate,
             up,
             down,

time: 120 us -> 117 us (0.975)
  waiting for transfers between devices: 30 us -> 27.8 us
    ppermute x36, waiting for transfers between devices: 30 us -> 27.8 us  [swap(): return lax.ppermute(value, 'expert', [(i, i ^ bit) for i in range(count)])]
    pallas_call x1, Pallas kernels: 8.95 us -> 7.54 us  [run_experts(): pl.pallas_call(functools.partial(experts_kernel, masks, counts, orders, l...]
    pallas_call x3 -> x4, Pallas kernels: 26.5 us -> 27.4 us  [expand(): pl.pallas_call(functools.partial(expand_kernel, stacked), grid=grid, in_s...]
  transfers between devices with their start and end apart: 37 -> 37, of which waited for: 18 -> 15; matrix products, arithmetic and copies ran while one was open for 1% -> 1% of each run, Pallas kernels for 26% -> 27%
where the time goes in v6:
time: 117 us; the launch traced here: 116 us
  Pallas kernels  44.5 us (38%)
  starting transfers between devices  40.9 us (35%)
  waiting for transfers between devices  27.8 us (24%)
  local copies, waits for them, and re-layouts  1.52 us (1%)
  other arithmetic  1.46 us (1%)
    ppermute x36, starting transfers between devices, swap(): return lax.ppermute(value, 'expert', [(i, i ^ bit) for i in range(count)])  37.4 us
    ppermute x36, waiting for transfers between devices, swap(): return lax.ppermute(value, 'expert', [(i, i ^ bit) for i in range(count)])  27.8 us
    pallas_call x4, Pallas kernels, expand(): pl.pallas_call(functools.partial(expand_kernel, stacked), grid=grid, in_s...  27.4 us
    pallas_call x2, Pallas kernels, attend(): pl.pallas_call(functools.partial(attend_kernel, micro, span, KV_HEADS), g...  8.2 us
    pallas_call x1, Pallas kernels, run_experts(): pl.pallas_call(functools.partial(experts_kernel, masks, counts, orders, l...  7.54 us
    all_to_all x1, starting transfers between devices, body(): lax.all_to_all(jnp.concatenate([lead, tail], axis=-1), 'expert', split_ax...  3.52 us
  transfers between devices with their start and end apart: 37, of which 15 were waited for; matrix products, arithmetic and copies ran while one was open for 1% of the time, Pallas kernels for 27%

profile of v6, /device:TPU:0, one launch (start us, length us, event | category | flops | bytes accessed | tf_op | source)
XLA Modules:
  0.0 116.5 jit_solution(2292444184793918010)
XLA Ops:
  0.0 0.7 copy-done.5
  0.7 4.1 %attend.2 = bf16[8,8192]{1,0:T(8,128)(2,1)S(1)} custom-call(s32[2,8]{1,0:T(2,128)S(1)} %copy-done.5, bf16[2,8,8192]{2,1,0:T(8,128)(2,1)} %q_ref.3, bf16[2,8,128,2,512]{4,3,2,1,0:T(2,128)(2,1)} %kv_ref.3), custom_call_target="tpu_custom_call" | custom-call | flops 67108864 | bytes 2097152 | tf_op jit(solution)/shard_map/attend/pallas_call | solution.py:75
  4.8 3.1 %collective-permute-start.1 = (bf16[8,8192]{1,0:T(8,128)(2,1)S(1)}, bf16[8,8192]{1,0:T(8,128)(2,1)S(1)}, u32[]{:S(2)}, u32[]{:S(2)}) collective-permute-start(bf16[8,8192]{1,0:T(8,128)(2,1)S(1)} %attend.2), channel_id=1, source_target_pairs={{0,4},{1,5},{2,6},{3,7},{4,0},{5,1},{6,2},{7,3},{8,12},{9,13},{10,... | collective-permute-start | bytes 393224 | tf_op jit(solution)/shard_map/ppermute | solution.py:329
  7.9 2.6 %collective-permute-start = (bf16[8,8192]{1,0:T(8,128)(2,1)S(1)}, bf16[8,8192]{1,0:T(8,128)(2,1)S(1)}, u32[]{:S(2)}, u32[]{:S(2)}) collective-permute-start(bf16[8,8192]{1,0:T(8,128)(2,1)S(1)} %attend.2), channel_id=1, source_target_pairs={{0,8},{1,9},{2,10},{3,11},{4,12},{5,13},{6,14},{7,15},{8,0},{9,1},... | collective-permute-start | bytes 393224 | tf_op jit(solution)/shard_map/ppermute | solution.py:329
  10.5 0.1 fusion.4
  10.7 0.7 copy.19
  11.4 3.5 %all-to-all-start = ((bf16[16,2,8,272]{3,2,1,0:T(8,128)(2,1)}), bf16[16,2,8,272]{3,2,1,0:T(8,128)(2,1)S(1)}, u32[]{:S(2)}, u32[]{:S(2)}) async-start(bf16[16,2,8,272]{3,2,1,0:T(8,128)(2,1)} %copy.19), calls=%async_computation | async-start | bytes 393216 | tf_op jit(solution)/shard_map/all_to_all | solution.py:413
  14.9 4.1 %attend.3 = bf16[8,8192]{1,0:T(8,128)(2,1)S(1)} custom-call(s32[2,8]{1,0:T(2,128)S(1)} %copy-done.6, bf16[2,8,8192]{2,1,0:T(8,128)(2,1)} %q_ref.3, bf16[2,8,128,2,512]{4,3,2,1,0:T(2,128)(2,1)} %kv_ref.3), custom_call_target="tpu_custom_call" | custom-call | flops 67108864 | bytes 2097152 | tf_op jit(solution)/shard_map/attend/pallas_call | solution.py:75
  19.1 1.9 %collective-permute-start.5 = (bf16[8,8192]{1,0:T(8,128)(2,1)S(1)}, bf16[8,8192]{1,0:T(8,128)(2,1)S(1)}, u32[]{:S(2)}, u32[]{:S(2)}) collective-permute-start(bf16[8,8192]{1,0:T(8,128)(2,1)S(1)} %attend.3), channel_id=1, source_target_pairs={{0,2},{1,3},{2,0},{3,1},{4,6},{5,7},{6,4},{7,5},{8,10},{9,11},{10,... | collective-permute-start | bytes 393224 | tf_op jit(solution)/shard_map/ppermute | solution.py:329
  21.0 1.6 %collective-permute-start.2 = (bf16[8,8192]{1,0:T(8,128)(2,1)S(1)}, bf16[8,8192]{1,0:T(8,128)(2,1)S(1)}, u32[]{:S(2)}, u32[]{:S(2)}) collective-permute-start(bf16[8,8192]{1,0:T(8,128)(2,1)S(1)} %collective-permute-done), channel_id=1, source_target_pairs={{0,4},{1,5},{2,6},{3,7},{4,0},{5,1},{6,2},{7,3},{8,12},{9,13},{10,... | collective-permute-start | bytes 393224 | tf_op jit(solution)/shard_map/ppermute | solution.py:329
  22.5 2.8 %collective-permute-done.5 = bf16[8,8192]{1,0:T(8,128)(2,1)S(1)} collective-permute-done((bf16[8,8192]{1,0:T(8,128)(2,1)S(1)}, bf16[8,8192]{1,0:T(8,128)(2,1)S(1)}, u32[]{:S(2)}, u32[]{:S(2)}) %collective-permute-start.5) | collective-permute-done | bytes 131104 | tf_op jit(solution)/shard_map/ppermute | solution.py:329
  25.4 0.1 collective-permute-start.10
  25.4 1.4 %collective-permute-start.8 = (bf16[2,8,8192]{2,1,0:T(8,128)(2,1)S(1)}, bf16[2,8,8192]{2,1,0:T(8,128)(2,1)S(1)}, u32[]{:S(2)}, u32[]{:S(2)}) collective-permute-start(bf16[2,8,8192]{2,1,0:T(8,128)(2,1)S(1)} %pad_maximum_fusion.1.refs_4_), channel_id=1, source_target_pairs={{0,4},{1,5},{2,6},{3,7},{4,0},{5,1},{6,2},{7,3},{8,12},{9,13},{10,... | collective-permute-start | bytes 786440 | tf_op jit(solution)/shard_map/ppermute | solution.py:329
  26.9 2.2 %collective-permute-start.6 = (bf16[2,8,8192]{2,1,0:T(8,128)(2,1)S(1)}, bf16[2,8,8192]{2,1,0:T(8,128)(2,1)S(1)}, u32[]{:S(2)}, u32[]{:S(2)}) collective-permute-start(bf16[2,8,8192]{2,1,0:T(8,128)(2,1)S(1)} %pad_maximum_fusion.1.refs_4_), channel_id=1, source_target_pairs={{0,8},{1,9},{2,10},{3,11},{4,12},{5,13},{6,14},{7,15},{8,0},{9,1},... | collective-permute-start | bytes 786440 | tf_op jit(solution)/shard_map/ppermute | solution.py:329
  29.2 0.1 collective-permute-start.4
  29.3 1.5 %collective-permute-start.3 = (bf16[4,8,8192]{2,1,0:T(8,128)(2,1)S(1)}, bf16[4,8,8192]{2,1,0:T(8,128)(2,1)S(1)}, u32[]{:S(2)}, u32[]{:S(2)}) collective-permute-start(bf16[4,8,8192]{2,1,0:T(8,128)(2,1)S(1)} %pad_maximum_fusion.refs_0_), channel_id=1, source_target_pairs={{0,2},{1,3},{2,0},{3,1},{4,6},{5,7},{6,4},{7,5},{8,10},{9,11},{10,... | collective-permute-start | bytes 1572872 | tf_op jit(solution)/shard_map/ppermute | solution.py:329
  30.8 8.9 %expand.4 = bf16[4,192,4096]{2,1,0:T(8,128)(2,1)S(1)} custom-call(f32[8,128]{1,0:T(8,128)S(1)} %squeeze.27.table_ref, bf16[192,4096]{1,0:T(8,128)(2,1)} %bitcast.76), custom_call_target="tpu_custom_call" | custom-call | flops 6291456000 | bytes 7864320 | tf_op jit(solution)/shard_map/expand/pallas_call | solution.py:146
  39.7 2.2 %collective-permute-done.6.refs_5_ = bf16[2,8,8192]{2,1,0:T(8,128)(2,1)S(1)} collective-permute-done((bf16[2,8,8192]{2,1,0:T(8,128)(2,1)S(1)}, bf16[2,8,8192]{2,1,0:T(8,128)(2,1)S(1)}, u32[]{:S(2)}, u32[]{:S(2)}) %collective-permute-start.6) | collective-permute-done | bytes 262176 | tf_op jit(solution)/shard_map/ppermute | solution.py:329
  41.8 0.1 collective-permute-start.9
  42.0 9.0 %expand.5 = bf16[4,192,4096]{2,1,0:T(8,128)(2,1)S(1)} custom-call(f32[8,128]{1,0:T(8,128)S(1)} %squeeze.28.table_ref, bf16[192,4096]{1,0:T(8,128)(2,1)} %bitcast.77), custom_call_target="tpu_custom_call" | custom-call | flops 6291456000 | bytes 7864320 | tf_op jit(solution)/shard_map/expand/pallas_call | solution.py:146
  51.0 0.1 collective-permute-start.7
  51.1 0.5 collective-permute-start.11
  51.6 0.1 collective-permute-start.12
  51.7 0.4 collective-permute-start.13
  52.1 1.2 %collective-permute-done.11.refs_9_ = bf16[2,8,8192]{2,1,0:T(8,128)(2,1)S(1)} collective-permute-done((bf16[2,8,8192]{2,1,0:T(8,128)(2,1)S(1)}, bf16[2,8,8192]{2,1,0:T(8,128)(2,1)S(1)}, u32[]{:S(2)}, u32[]{:S(2)}) %collective-permute-start.11) | collective-permute-done | bytes 262176 | tf_op jit(solution)/shard_map/ppermute | solution.py:329
  53.3 0.4 collective-permute-done.12.refs_10_
  53.7 0.4 collective-permute-done.13.refs_11_
  54.1 1.3 %project.1 = (bf16[16,8,256]{2,1,0:T(8,128)(2,1)S(1)}, bf16[16,8,256]{2,1,0:T(8,128)(2,1)S(1)}) custom-call(s32[1]{0:T(128)} %bitcast.3.me_ref, bf16[4,8,8192]{2,1,0:T(8,128)(2,1)S(1)} %pad_maximum_fusion.refs_0_, bf16[4,8,8192]{2,1,0:T(8,128)(2,1)S(1)} %collective-permute-done.3.refs_1_, bf16[4,8,8192]{2,1,0:T(8,128)(2,1)S(1)} %collective-permute-done.4.refs_2_, ...), custom_call_target="tpu_custom_call" | custom-call | flops 1073741824 | bytes 4194304 | tf_op jit(solution)/shard_map/project/pallas_call | solution.py:194
  55.4 2.7 %collective-permute-start.14 = (bf16[16,8,256]{2,1,0:T(8,128)(2,1)S(1)}, bf16[16,8,256]{2,1,0:T(8,128)(2,1)S(1)}, u32[]{:S(2)}, u32[]{:S(2)}) collective-permute-start(bf16[16,8,256]{2,1,0:T(8,128)(2,1)S(1)} %get-tuple-element.43), channel_id=1, source_target_pairs={{0,8},{1,9},{2,10},{3,11},{4,12},{5,13},{6,14},{7,15},{8,0},{9,1},... | collective-permute-start | bytes 196616 | tf_op jit(solution)/shard_map/ppermute | solution.py:329
  58.0 1.5 %collective-permute-start.19 = (bf16[16,8,256]{2,1,0:T(8,128)(2,1)S(1)}, bf16[16,8,256]{2,1,0:T(8,128)(2,1)S(1)}, u32[]{:S(2)}, u32[]{:S(2)}) collective-permute-start(bf16[16,8,256]{2,1,0:T(8,128)(2,1)S(1)} %get-tuple-element.45), channel_id=1, source_target_pairs={{0,2},{1,3},{2,0},{3,1},{4,6},{5,7},{6,4},{7,5},{8,10},{9,11},{10,... | collective-permute-start | bytes 196616 | tf_op jit(solution)/shard_map/ppermute | solution.py:329
  59.5 2.1 %collective-permute-done.14 = bf16[16,8,256]{2,1,0:T(8,128)(2,1)S(1)} collective-permute-done((bf16[16,8,256]{2,1,0:T(8,128)(2,1)S(1)}, bf16[16,8,256]{2,1,0:T(8,128)(2,1)S(1)}, u32[]{:S(2)}, u32[]{:S(2)}) %collective-permute-start.14) | collective-permute-done | bytes 65568 | tf_op jit(solution)/shard_map/ppermute | solution.py:329
  61.6 1.3 %collective-permute-start.16 = (bf16[16,8,256]{2,1,0:T(8,128)(2,1)S(1)}, bf16[16,8,256]{2,1,0:T(8,128)(2,1)S(1)}, u32[]{:S(2)}, u32[]{:S(2)}) collective-permute-start(bf16[16,8,256]{2,1,0:T(8,128)(2,1)S(1)} %collective-permute-done.14), channel_id=1, source_target_pairs={{0,4},{1,5},{2,6},{3,7},{4,0},{5,1},{6,2},{7,3},{8,12},{9,13},{10,... | collective-permute-start | bytes 196616 | tf_op jit(solution)/shard_map/ppermute | solution.py:329
  63.0 0.1 collective-permute-start.24
  63.1 0.8 collective-permute-start.22
  63.8 2.0 %collective-permute-start.20 = (bf16[2,16,8,256]{3,2,1,0:T(8,128)(2,1)S(1)}, bf16[2,16,8,256]{3,2,1,0:T(8,128)(2,1)S(1)}, u32[]{:S(2)}, u32[]{:S(2)}) collective-permute-start(bf16[2,16,8,256]{3,2,1,0:T(8,128)(2,1)S(1)} %pad_maximum_fusion.4.refs_4_), channel_id=1, source_target_pairs={{0,8},{1,9},{2,10},{3,11},{4,12},{5,13},{6,14},{7,15},{8,0},{9,1},... | collective-permute-start | bytes 393224 | tf_op jit(solution)/shard_map/ppermute | solution.py:329
  65.8 0.1 collective-permute-done.16
  65.9 0.1 collective-permute-start.18
  66.0 1.6 %collective-permute-start.17 = (bf16[4,16,8,256]{3,2,1,0:T(8,128)(2,1)S(1)}, bf16[4,16,8,256]{3,2,1,0:T(8,128)(2,1)S(1)}, u32[]{:S(2)}, u32[]{:S(2)}) collective-permute-start(bf16[4,16,8,256]{3,2,1,0:T(8,128)(2,1)S(1)} %pad_maximum_fusion.2.refs_0_), channel_id=1, source_target_pairs={{0,2},{1,3},{2,0},{3,1},{4,6},{5,7},{6,4},{7,5},{8,10},{9,11},{10,... | collective-permute-start | bytes 786440 | tf_op jit(solution)/shard_map/ppermute | solution.py:329
  67.6 6.0 %expand.6.refs_19_ = bf16[512,4096]{1,0:T(8,128)(2,1)S(1)} custom-call(f32[8,128]{1,0:T(8,128)S(1)} %squeeze.29.table_ref, bf16[768,1024]{1,0:T(8,128)(2,1)} %bitcast.78), custom_call_target="tpu_custom_call" | custom-call | flops 4194304000 | bytes 5242880 | tf_op jit(solution)/shard_map/expand/pallas_call | solution.py:146
  73.6 1.5 %collective-permute-start.23 = (bf16[2,16,8,256]{3,2,1,0:T(8,128)(2,1)S(1)}, bf16[2,16,8,256]{3,2,1,0:T(8,128)(2,1)S(1)}, u32[]{:S(2)}, u32[]{:S(2)}) collective-permute-start(bf16[2,16,8,256]{3,2,1,0:T(8,128)(2,1)S(1)} %collective-permute-done.20.refs_5_), channel_id=1, source_target_pairs={{0,4},{1,5},{2,6},{3,7},{4,0},{5,1},{6,2},{7,3},{8,12},{9,13},{10,... | collective-permute-start | bytes 393224 | tf_op jit(solution)/shard_map/ppermute | solution.py:329
  75.2 3.6 %expand.7.refs_20_ = bf16[256,4096]{1,0:T(8,128)(2,1)S(1)} custom-call(f32[8,128]{1,0:T(8,128)S(1)} %squeeze.29.table_ref, bf16[768,1024]{1,0:T(8,128)(2,1)} %bitcast.79), custom_call_target="tpu_custom_call" | custom-call | flops 2097152000 | bytes 2621440 | tf_op jit(solution)/shard_map/expand/pallas_call | solution.py:146
  78.9 0.5 collective-permute-start.25
  79.4 0.1 collective-permute-start.26
  79.5 0.4 collective-permute-start.27
  79.9 0.7 collective-permute-done.25.refs_9_
  80.6 0.2 collective-permute-done.26.refs_10_
  80.8 0.2 collective-permute-done.27.refs_11_
  81.0 7.5 %experts.1 = (bf16[8,8,4096]{2,1,0:T(8,128)(2,1)S(1)}, bf16[8,8,4096]{2,1,0:T(8,128)(2,1)S(1)}, bf16[8,8,4096]{2,1,0:T(8,128)(2,1)S(1)}, bf16[8,8,4096]{2,1,0:T(...) custom-call(s32[1]{0:T(128)} %bitcast.3.me_ref, ...), custom_call_target="tpu_custom_call" | custom-call | flops 4831838208 | bytes 18874368 | tf_op jit(solution)/shard_map/experts/pallas_call | solution.py:310
  88.6 0.4 collective-permute-start.28
  88.9 0.2 collective-permute-start.32
  89.1 1.4 %collective-permute-done.28 = bf16[8,8,4096]{2,1,0:T(8,128)(2,1)S(1)} collective-permute-done((bf16[8,8,4096]{2,1,0:T(8,128)(2,1)S(1)}, bf16[8,8,4096]{2,1,0:T(8,128)(2,1)S(1)}, u32[]{:S(2)}, u32[]{:S(2)}) %collective-permute-start.28) | collective-permute-done | bytes 524320 | tf_op jit(solution)/shard_map/ppermute | solution.py:329
  90.5 0.1 add_convert_fusion.3
  90.7 0.8 collective-permute-start.29
  91.5 0.1 add_convert_fusion.1
  91.6 1.3 %collective-permute-start.33 = (bf16[4,8,4096]{2,1,0:T(8,128)(2,1)S(1)}, bf16[4,8,4096]{2,1,0:T(8,128)(2,1)S(1)}, u32[]{:S(2)}, u32[]{:S(2)}) collective-permute-start(bf16[4,8,4096]{2,1,0:T(8,128)(2,1)S(1)} %get-tuple-element.62), channel_id=1, source_target_pairs={{0,4},{1,5},{2,6},{3,7},{4,0},{5,1},{6,2},{7,3},{8,12},{9,13},{10,... | collective-permute-start | bytes 786440 | tf_op jit(solution)/shard_map/ppermute | solution.py:329
  92.9 6.3 %collective-permute-done.29 = bf16[4,8,4096]{2,1,0:T(8,128)(2,1)S(1)} collective-permute-done((bf16[4,8,4096]{2,1,0:T(8,128)(2,1)S(1)}, bf16[4,8,4096]{2,1,0:T(8,128)(2,1)S(1)}, u32[]{:S(2)}, u32[]{:S(2)}) %collective-permute-start.29) | collective-permute-done | bytes 262176 | tf_op jit(solution)/shard_map/ppermute | solution.py:329
  99.3 1.4 %collective-permute-start.30 = (bf16[2,8,4096]{2,1,0:T(8,128)(2,1)S(1)}, bf16[2,8,4096]{2,1,0:T(8,128)(2,1)S(1)}, u32[]{:S(2)}, u32[]{:S(2)}) collective-permute-start(bf16[2,8,4096]{2,1,0:T(8,128)(2,1)S(1)} %get-tuple-element.64), channel_id=1, source_target_pairs={{0,4},{1,5},{2,6},{3,7},{4,0},{5,1},{6,2},{7,3},{8,12},{9,13},{10,... | collective-permute-start | bytes 393224 | tf_op jit(solution)/shard_map/ppermute | solution.py:329
  100.8 2.1 %collective-permute-start.34 = (bf16[2,8,4096]{2,1,0:T(8,128)(2,1)S(1)}, bf16[2,8,4096]{2,1,0:T(8,128)(2,1)S(1)}, u32[]{:S(2)}, u32[]{:S(2)}) collective-permute-start(bf16[2,8,4096]{2,1,0:T(8,128)(2,1)S(1)} %get-tuple-element.66), channel_id=1, source_target_pairs={{0,8},{1,9},{2,10},{3,11},{4,12},{5,13},{6,14},{7,15},{8,0},{9,1},... | collective-permute-start | bytes 393224 | tf_op jit(solution)/shard_map/ppermute | solution.py:329
  102.8 3.4 %collective-permute-done.30 = bf16[2,8,4096]{2,1,0:T(8,128)(2,1)S(1)} collective-permute-done((bf16[2,8,4096]{2,1,0:T(8,128)(2,1)S(1)}, bf16[2,8,4096]{2,1,0:T(8,128)(2,1)S(1)}, u32[]{:S(2)}, u32[]{:S(2)}) %collective-permute-start.30) | collective-permute-done | bytes 131104 | tf_op jit(solution)/shard_map/ppermute | solution.py:329
  106.2 2.3 %collective-permute-start.31 = (bf16[1,8,4096]{2,1,0:T(8,128)(2,1)S(1)}, bf16[1,8,4096]{2,1,0:T(8,128)(2,1)S(1)}, u32[]{:S(2)}, u32[]{:S(2)}) collective-permute-start(bf16[1,8,4096]{2,1,0:T(8,128)(2,1)S(1)} %add_convert_fusion.10), channel_id=1, source_target_pairs={{0,8},{1,9},{2,10},{3,11},{4,12},{5,13},{6,14},{7,15},{8,0},{9,1},... | collective-permute-start | bytes 196616 | tf_op jit(solution)/shard_map/ppermute | solution.py:329
  108.5 2.9 %collective-permute-done.34 = bf16[2,8,4096]{2,1,0:T(8,128)(2,1)S(1)} collective-permute-done((bf16[2,8,4096]{2,1,0:T(8,128)(2,1)S(1)}, bf16[2,8,4096]{2,1,0:T(8,128)(2,1)S(1)}, u32[]{:S(2)}, u32[]{:S(2)}) %collective-permute-start.34) | collective-permute-done | bytes 131104 | tf_op jit(solution)/shard_map/ppermute | solution.py:329
  111.4 0.7 collective-permute-start.35
  112.2 3.6 %collective-permute-done.35 = bf16[1,8,4096]{2,1,0:T(8,128)(2,1)S(1)} collective-permute-done((bf16[1,8,4096]{2,1,0:T(8,128)(2,1)S(1)}, bf16[1,8,4096]{2,1,0:T(8,128)(2,1)S(1)}, u32[]{:S(2)}, u32[]{:S(2)}) %collective-permute-start.35) | collective-permute-done | bytes 65568 | tf_op jit(solution)/shard_map/ppermute | solution.py:329
  115.8 0.7 pad_maximum_fusion.5
  (64 shorter events, 0.7 us)
Async XLA Ops:
  0.0 0.7 copy-start.5
  0.7 9.8 %copy-start.8 = (s32[2,8,8]{2,1,0:T(8,128)S(1)}, s32[2,8,8]{2,1,0:T(8,128)}, u32[]{:S(2)}) copy-start(s32[2,8,8]{2,1,0:T(8,128)} %param.18) | copy-start | bytes 1540
  0.7 9.9 %copy-start.7 = (bf16[2,8,4096]{2,1,0:T(8,128)(2,1)S(1)}, bf16[2,8,4096]{2,1,0:T(8,128)(2,1)}, u32[]{:S(2)}) copy-start(bf16[2,8,4096]{2,1,0:T(8,128)(2,1)} %param.14) | copy-start | bytes 393220
  0.7 14.3 %copy-start.6 = (s32[2,8]{1,0:T(2,128)S(1)}, s32[2,8]{1,0:T(2,128)}, u32[]{:S(2)}) copy-start(s32[2,8]{1,0:T(2,128)} %len_ref.3) | copy-start | bytes 196
  4.8 16.1 %copy-start.9 = (bf16[1,3,256,4]{2,3,1,0:T(4,128)(2,1)S(1)}, bf16[1,3,256,4]{2,3,1,0:T(4,128)(2,1)}, u32[]{:S(2)}) copy-start(bf16[1,3,256,4]{2,3,1,0:T(4,128)(2,1)} %param.25) | copy-start | bytes 18436
  4.8 24.3 %collective-permute-start.1 = (bf16[8,8192]{1,0:T(8,128)(2,1)S(1)}, bf16[8,8192]{1,0:T(8,128)(2,1)S(1)}, u32[]{:S(2)}, u32[]{:S(2)}) collective-permute-start(bf16[8,8192]{1,0:T(8,128)(2,1)S(1)} %attend.2), channel_id=1, source_target_pairs={{0,4},{1,5},{2,6},{3,7},{4,0},{5,1},{6,2},{7,3},{8,12},{9,13},{10,... | collective-permute-start | bytes 393224 | tf_op jit(solution)/shard_map/ppermute | solution.py:329
  7.9 13.1 %collective-permute-start = (bf16[8,8192]{1,0:T(8,128)(2,1)S(1)}, bf16[8,8192]{1,0:T(8,128)(2,1)S(1)}, u32[]{:S(2)}, u32[]{:S(2)}) collective-permute-start(bf16[8,8192]{1,0:T(8,128)(2,1)S(1)} %attend.2), channel_id=1, source_target_pairs={{0,8},{1,9},{2,10},{3,11},{4,12},{5,13},{6,14},{7,15},{8,0},{9,1},... | collective-permute-start | bytes 393224 | tf_op jit(solution)/shard_map/ppermute | solution.py:329
  11.4 17.7 %all-to-all-start = ((bf16[16,2,8,272]{3,2,1,0:T(8,128)(2,1)}), bf16[16,2,8,272]{3,2,1,0:T(8,128)(2,1)S(1)}, u32[]{:S(2)}, u32[]{:S(2)}) async-start(bf16[16,2,8,272]{3,2,1,0:T(8,128)(2,1)} %copy.19), calls=%async_computation | async-start | bytes 393216 | tf_op jit(solution)/shard_map/all_to_all | solution.py:413
  19.1 6.3 %collective-permute-start.5 = (bf16[8,8192]{1,0:T(8,128)(2,1)S(1)}, bf16[8,8192]{1,0:T(8,128)(2,1)S(1)}, u32[]{:S(2)}, u32[]{:S(2)}) collective-permute-start(bf16[8,8192]{1,0:T(8,128)(2,1)S(1)} %attend.3), channel_id=1, source_target_pairs={{0,2},{1,3},{2,0},{3,1},{4,6},{5,7},{6,4},{7,5},{8,10},{9,11},{10,... | collective-permute-start | bytes 393224 | tf_op jit(solution)/shard_map/ppermute | solution.py:329
  21.0 8.1 %collective-permute-start.2 = (bf16[8,8192]{1,0:T(8,128)(2,1)S(1)}, bf16[8,8192]{1,0:T(8,128)(2,1)S(1)}, u32[]{:S(2)}, u32[]{:S(2)}) collective-permute-start(bf16[8,8192]{1,0:T(8,128)(2,1)S(1)} %collective-permute-done), channel_id=1, source_target_pairs={{0,4},{1,5},{2,6},{3,7},{4,0},{5,1},{6,2},{7,3},{8,12},{9,13},{10,... | collective-permute-start | bytes 393224 | tf_op jit(solution)/shard_map/ppermute | solution.py:329
  25.4 26.3 %collective-permute-start.10 = (bf16[2,8,8192]{2,1,0:T(8,128)(2,1)S(1)}, bf16[2,8,8192]{2,1,0:T(8,128)(2,1)S(1)}, u32[]{:S(2)}, u32[]{:S(2)}) collective-permute-start(bf16[2,8,8192]{2,1,0:T(8,128)(2,1)S(1)} %pad_maximum_fusion.1.refs_4_), channel_id=1, source_target_pairs={{0,1},{1,0},{2,3},{3,2},{4,5},{5,4},{6,7},{7,6},{8,9},{9,8},{10,11... | collective-permute-start | bytes 786440 | tf_op jit(solution)/shard_map/ppermute | solution.py:329
  25.4 25.6 %collective-permute-start.8 = (bf16[2,8,8192]{2,1,0:T(8,128)(2,1)S(1)}, bf16[2,8,8192]{2,1,0:T(8,128)(2,1)S(1)}, u32[]{:S(2)}, u32[]{:S(2)}) collective-permute-start(bf16[2,8,8192]{2,1,0:T(8,128)(2,1)S(1)} %pad_maximum_fusion.1.refs_4_), channel_id=1, source_target_pairs={{0,4},{1,5},{2,6},{3,7},{4,0},{5,1},{6,2},{7,3},{8,12},{9,13},{10,... | collective-permute-start | bytes 786440 | tf_op jit(solution)/shard_map/ppermute | solution.py:329
  26.9 14.9 %collective-permute-start.6 = (bf16[2,8,8192]{2,1,0:T(8,128)(2,1)S(1)}, bf16[2,8,8192]{2,1,0:T(8,128)(2,1)S(1)}, u32[]{:S(2)}, u32[]{:S(2)}) collective-permute-start(bf16[2,8,8192]{2,1,0:T(8,128)(2,1)S(1)} %pad_maximum_fusion.1.refs_4_), channel_id=1, source_target_pairs={{0,8},{1,9},{2,10},{3,11},{4,12},{5,13},{6,14},{7,15},{8,0},{9,1},... | collective-permute-start | bytes 786440 | tf_op jit(solution)/shard_map/ppermute | solution.py:329
  29.2 24.5 %collective-permute-start.4 = (bf16[4,8,8192]{2,1,0:T(8,128)(2,1)S(1)}, bf16[4,8,8192]{2,1,0:T(8,128)(2,1)S(1)}, u32[]{:S(2)}, u32[]{:S(2)}) collective-permute-start(bf16[4,8,8192]{2,1,0:T(8,128)(2,1)S(1)} %pad_maximum_fusion.refs_0_), channel_id=1, source_target_pairs={{0,1},{1,0},{2,3},{3,2},{4,5},{5,4},{6,7},{7,6},{8,9},{9,8},{10,11... | collective-permute-start | bytes 1572872 | tf_op jit(solution)/shard_map/ppermute | solution.py:329
  29.3 21.7 %collective-permute-start.3 = (bf16[4,8,8192]{2,1,0:T(8,128)(2,1)S(1)}, bf16[4,8,8192]{2,1,0:T(8,128)(2,1)S(1)}, u32[]{:S(2)}, u32[]{:S(2)}) collective-permute-start(bf16[4,8,8192]{2,1,0:T(8,128)(2,1)S(1)} %pad_maximum_fusion.refs_0_), channel_id=1, source_target_pairs={{0,2},{1,3},{2,0},{3,1},{4,6},{5,7},{6,4},{7,5},{8,10},{9,11},{10,... | collective-permute-start | bytes 1572872 | tf_op jit(solution)/shard_map/ppermute | solution.py:329
  41.8 9.7 %collective-permute-start.9 = (bf16[2,8,8192]{2,1,0:T(8,128)(2,1)S(1)}, bf16[2,8,8192]{2,1,0:T(8,128)(2,1)S(1)}, u32[]{:S(2)}, u32[]{:S(2)}) collective-permute-start(bf16[2,8,8192]{2,1,0:T(8,128)(2,1)S(1)} %collective-permute-done.6.refs_5_), channel_id=1, source_target_pairs={{0,4},{1,5},{2,6},{3,7},{4,0},{5,1},{6,2},{7,3},{8,12},{9,13},{10,... | collective-permute-start | bytes 786440 | tf_op jit(solution)/shard_map/ppermute | solution.py:329
  42.0 12.1 %copy-start = (bf16[8192,256]{1,0:T(8,128)(2,1)S(1)}, bf16[8192,256]{1,0:T(8,128)(2,1)}, u32[]{:S(2)}) copy-start(bf16[8192,256]{1,0:T(8,128)(2,1)} %refs_12_.1) | copy-start | bytes 12582916
  51.0 3.1 %collective-permute-start.7 = (bf16[4,8,8192]{2,1,0:T(8,128)(2,1)S(1)}, bf16[4,8,8192]{2,1,0:T(8,128)(2,1)S(1)}, u32[]{:S(2)}, u32[]{:S(2)}) collective-permute-start(bf16[4,8,8192]{2,1,0:T(8,128)(2,1)S(1)} %collective-permute-done.3.refs_1_), channel_id=1, source_target_pairs={{0,1},{1,0},{2,3},{3,2},{4,5},{5,4},{6,7},{7,6},{8,9},{9,8},{10,11... | collective-permute-start | bytes 1572872 | tf_op jit(solution)/shard_map/ppermute | solution.py:329
  51.1 2.3 %collective-permute-start.11 = (bf16[2,8,8192]{2,1,0:T(8,128)(2,1)S(1)}, bf16[2,8,8192]{2,1,0:T(8,128)(2,1)S(1)}, u32[]{:S(2)}, u32[]{:S(2)}) collective-permute-start(bf16[2,8,8192]{2,1,0:T(8,128)(2,1)S(1)} %collective-permute-done.6.refs_5_), channel_id=1, source_target_pairs={{0,1},{1,0},{2,3},{3,2},{4,5},{5,4},{6,7},{7,6},{8,9},{9,8},{10,11... | collective-permute-start | bytes 786440 | tf_op jit(solution)/shard_map/ppermute | solution.py:329
  51.6 2.1 %collective-permute-start.12 = (bf16[2,8,8192]{2,1,0:T(8,128)(2,1)S(1)}, bf16[2,8,8192]{2,1,0:T(8,128)(2,1)S(1)}, u32[]{:S(2)}, u32[]{:S(2)}) collective-permute-start(bf16[2,8,8192]{2,1,0:T(8,128)(2,1)S(1)} %collective-permute-done.8.refs_6_), channel_id=1, source_target_pairs={{0,1},{1,0},{2,3},{3,2},{4,5},{5,4},{6,7},{7,6},{8,9},{9,8},{10,11... | collective-permute-start | bytes 786440 | tf_op jit(solution)/shard_map/ppermute | solution.py:329
  51.7 2.4 %collective-permute-start.13 = (bf16[2,8,8192]{2,1,0:T(8,128)(2,1)S(1)}, bf16[2,8,8192]{2,1,0:T(8,128)(2,1)S(1)}, u32[]{:S(2)}, u32[]{:S(2)}) collective-permute-start(bf16[2,8,8192]{2,1,0:T(8,128)(2,1)S(1)} %collective-permute-done.9.refs_7_), channel_id=1, source_target_pairs={{0,1},{1,0},{2,3},{3,2},{4,5},{5,4},{6,7},{7,6},{8,9},{9,8},{10,11... | collective-permute-start | bytes 786440 | tf_op jit(solution)/shard_map/ppermute | solution.py:329
  55.4 6.2 %collective-permute-start.14 = (bf16[16,8,256]{2,1,0:T(8,128)(2,1)S(1)}, bf16[16,8,256]{2,1,0:T(8,128)(2,1)S(1)}, u32[]{:S(2)}, u32[]{:S(2)}) collective-permute-start(bf16[16,8,256]{2,1,0:T(8,128)(2,1)S(1)} %get-tuple-element.43), channel_id=1, source_target_pairs={{0,8},{1,9},{2,10},{3,11},{4,12},{5,13},{6,14},{7,15},{8,0},{9,1},... | collective-permute-start | bytes 196616 | tf_op jit(solution)/shard_map/ppermute | solution.py:329
  58.0 4.9 %collective-permute-start.19 = (bf16[16,8,256]{2,1,0:T(8,128)(2,1)S(1)}, bf16[16,8,256]{2,1,0:T(8,128)(2,1)S(1)}, u32[]{:S(2)}, u32[]{:S(2)}) collective-permute-start(bf16[16,8,256]{2,1,0:T(8,128)(2,1)S(1)} %get-tuple-element.45), channel_id=1, source_target_pairs={{0,2},{1,3},{2,0},{3,1},{4,6},{5,7},{6,4},{7,5},{8,10},{9,11},{10,... | collective-permute-start | bytes 196616 | tf_op jit(solution)/shard_map/ppermute | solution.py:329
  59.5 6.3 %collective-permute-start.15 = (bf16[16,8,256]{2,1,0:T(8,128)(2,1)S(1)}, bf16[16,8,256]{2,1,0:T(8,128)(2,1)S(1)}, u32[]{:S(2)}, u32[]{:S(2)}) collective-permute-start(bf16[16,8,256]{2,1,0:T(8,128)(2,1)S(1)} %get-tuple-element.43), channel_id=1, source_target_pairs={{0,4},{1,5},{2,6},{3,7},{4,0},{5,1},{6,2},{7,3},{8,12},{9,13},{10,... | collective-permute-start | bytes 196616 | tf_op jit(solution)/shard_map/ppermute | solution.py:329
  61.6 4.3 %collective-permute-start.16 = (bf16[16,8,256]{2,1,0:T(8,128)(2,1)S(1)}, bf16[16,8,256]{2,1,0:T(8,128)(2,1)S(1)}, u32[]{:S(2)}, u32[]{:S(2)}) collective-permute-start(bf16[16,8,256]{2,1,0:T(8,128)(2,1)S(1)} %collective-permute-done.14), channel_id=1, source_target_pairs={{0,4},{1,5},{2,6},{3,7},{4,0},{5,1},{6,2},{7,3},{8,12},{9,13},{10,... | collective-permute-start | bytes 196616 | tf_op jit(solution)/shard_map/ppermute | solution.py:329
  63.0 16.5 %collective-permute-start.24 = (bf16[2,16,8,256]{3,2,1,0:T(8,128)(2,1)S(1)}, bf16[2,16,8,256]{3,2,1,0:T(8,128)(2,1)S(1)}, u32[]{:S(2)}, u32[]{:S(2)}) collective-permute-start(bf16[2,16,8,256]{3,2,1,0:T(8,128)(2,1)S(1)} %pad_maximum_fusion.4.refs_4_), channel_id=1, source_target_pairs={{0,1},{1,0},{2,3},{3,2},{4,5},{5,4},{6,7},{7,6},{8,9},{9,8},{10,11... | collective-permute-start | bytes 393224 | tf_op jit(solution)/shard_map/ppermute | solution.py:329
  63.1 15.8 %collective-permute-start.22 = (bf16[2,16,8,256]{3,2,1,0:T(8,128)(2,1)S(1)}, bf16[2,16,8,256]{3,2,1,0:T(8,128)(2,1)S(1)}, u32[]{:S(2)}, u32[]{:S(2)}) collective-permute-start(bf16[2,16,8,256]{3,2,1,0:T(8,128)(2,1)S(1)} %pad_maximum_fusion.4.refs_4_), channel_id=1, source_target_pairs={{0,4},{1,5},{2,6},{3,7},{4,0},{5,1},{6,2},{7,3},{8,12},{9,13},{10,... | collective-permute-start | bytes 393224 | tf_op jit(solution)/shard_map/ppermute | solution.py:329
  63.8 9.8 %collective-permute-start.20 = (bf16[2,16,8,256]{3,2,1,0:T(8,128)(2,1)S(1)}, bf16[2,16,8,256]{3,2,1,0:T(8,128)(2,1)S(1)}, u32[]{:S(2)}, u32[]{:S(2)}) collective-permute-start(bf16[2,16,8,256]{3,2,1,0:T(8,128)(2,1)S(1)} %pad_maximum_fusion.4.refs_4_), channel_id=1, source_target_pairs={{0,8},{1,9},{2,10},{3,11},{4,12},{5,13},{6,14},{7,15},{8,0},{9,1},... | collective-permute-start | bytes 393224 | tf_op jit(solution)/shard_map/ppermute | solution.py:329
  65.9 14.9 %collective-permute-start.18 = (bf16[4,16,8,256]{3,2,1,0:T(8,128)(2,1)S(1)}, bf16[4,16,8,256]{3,2,1,0:T(8,128)(2,1)S(1)}, u32[]{:S(2)}, u32[]{:S(2)}) collective-permute-start(bf16[4,16,8,256]{3,2,1,0:T(8,128)(2,1)S(1)} %pad_maximum_fusion.2.refs_0_), channel_id=1, source_target_pairs={{0,1},{1,0},{2,3},{3,2},{4,5},{5,4},{6,7},{7,6},{8,9},{9,8},{10,11... | collective-permute-start | bytes 786440 | tf_op jit(solution)/shard_map/ppermute | solution.py:329
  66.0 12.8 %collective-permute-start.17 = (bf16[4,16,8,256]{3,2,1,0:T(8,128)(2,1)S(1)}, bf16[4,16,8,256]{3,2,1,0:T(8,128)(2,1)S(1)}, u32[]{:S(2)}, u32[]{:S(2)}) collective-permute-start(bf16[4,16,8,256]{3,2,1,0:T(8,128)(2,1)S(1)} %pad_maximum_fusion.2.refs_0_), channel_id=1, source_target_pairs={{0,2},{1,3},{2,0},{3,1},{4,6},{5,7},{6,4},{7,5},{8,10},{9,11},{10,... | collective-permute-start | bytes 786440 | tf_op jit(solution)/shard_map/ppermute | solution.py:329
  73.6 7.4 %copy-start.1 = (bf16[4096,16]{0,1:T(8,128)(2,1)S(1)}, bf16[4096,16]{0,1:T(8,128)(2,1)}, u32[]{:S(2)}) copy-start(bf16[4096,16]{0,1:T(8,128)(2,1)} %param.21) | copy-start | bytes 393220
  73.6 7.4 %copy-start.2 = (f32[4096]{0:T(1024)S(1)}, f32[4096]{0:T(1024)}, u32[]{:S(2)}) copy-start(f32[4096]{0:T(1024)} %param.20) | copy-start | bytes 49156
  73.6 7.4 %copy-start.3 = (f32[1,4096]{1,0:T(1,128)S(1)}, f32[1,4096]{1,0:T(1,128)}, u32[]{:S(2)}) copy-start(f32[1,4096]{1,0:T(1,128)} %refs_18_.1) | copy-start | bytes 49156
  73.6 7.4 %copy-start.4 = (f32[1,2,768]{2,1,0:T(2,128)S(1)}, f32[1,2,768]{2,1,0:T(2,128)}, u32[]{:S(2)}) copy-start(f32[1,2,768]{2,1,0:T(2,128)} %param.26) | copy-start | bytes 18436
  73.6 5.8 %collective-permute-start.23 = (bf16[2,16,8,256]{3,2,1,0:T(8,128)(2,1)S(1)}, bf16[2,16,8,256]{3,2,1,0:T(8,128)(2,1)S(1)}, u32[]{:S(2)}, u32[]{:S(2)}) collective-permute-start(bf16[2,16,8,256]{3,2,1,0:T(8,128)(2,1)S(1)} %collective-permute-done.20.refs_5_), channel_id=1, source_target_pairs={{0,4},{1,5},{2,6},{3,7},{4,0},{5,1},{6,2},{7,3},{8,12},{9,13},{10,... | collective-permute-start | bytes 393224 | tf_op jit(solution)/shard_map/ppermute | solution.py:329
  78.8 2.2 %collective-permute-start.21 = (bf16[4,16,8,256]{3,2,1,0:T(8,128)(2,1)S(1)}, bf16[4,16,8,256]{3,2,1,0:T(8,128)(2,1)S(1)}, u32[]{:S(2)}, u32[]{:S(2)}) collective-permute-start(bf16[4,16,8,256]{3,2,1,0:T(8,128)(2,1)S(1)} %collective-permute-done.17.refs_1_), channel_id=1, source_target_pairs={{0,1},{1,0},{2,3},{3,2},{4,5},{5,4},{6,7},{7,6},{8,9},{9,8},{10,11... | collective-permute-start | bytes 786440 | tf_op jit(solution)/shard_map/ppermute | solution.py:329
  78.9 1.7 %collective-permute-start.25 = (bf16[2,16,8,256]{3,2,1,0:T(8,128)(2,1)S(1)}, bf16[2,16,8,256]{3,2,1,0:T(8,128)(2,1)S(1)}, u32[]{:S(2)}, u32[]{:S(2)}) collective-permute-start(bf16[2,16,8,256]{3,2,1,0:T(8,128)(2,1)S(1)} %collective-permute-done.20.refs_5_), channel_id=1, source_target_pairs={{0,1},{1,0},{2,3},{3,2},{4,5},{5,4},{6,7},{7,6},{8,9},{9,8},{10,11... | collective-permute-start | bytes 393224 | tf_op jit(solution)/shard_map/ppermute | solution.py:329
  79.4 1.4 %collective-permute-start.26 = (bf16[2,16,8,256]{3,2,1,0:T(8,128)(2,1)S(1)}, bf16[2,16,8,256]{3,2,1,0:T(8,128)(2,1)S(1)}, u32[]{:S(2)}, u32[]{:S(2)}) collective-permute-start(bf16[2,16,8,256]{3,2,1,0:T(8,128)(2,1)S(1)} %collective-permute-done.22.refs_6_), channel_id=1, source_target_pairs={{0,1},{1,0},{2,3},{3,2},{4,5},{5,4},{6,7},{7,6},{8,9},{9,8},{10,11... | collective-permute-start | bytes 393224 | tf_op jit(solution)/shard_map/ppermute | solution.py:329
  79.5 1.5 %collective-permute-start.27 = (bf16[2,16,8,256]{3,2,1,0:T(8,128)(2,1)S(1)}, bf16[2,16,8,256]{3,2,1,0:T(8,128)(2,1)S(1)}, u32[]{:S(2)}, u32[]{:S(2)}) collective-permute-start(bf16[2,16,8,256]{3,2,1,0:T(8,128)(2,1)S(1)} %collective-permute-done.23.refs_7_), channel_id=1, source_target_pairs={{0,1},{1,0},{2,3},{3,2},{4,5},{5,4},{6,7},{7,6},{8,9},{9,8},{10,11... | collective-permute-start | bytes 393224 | tf_op jit(solution)/shard_map/ppermute | solution.py:329
  88.6 2.0 %collective-permute-start.28 = (bf16[8,8,4096]{2,1,0:T(8,128)(2,1)S(1)}, bf16[8,8,4096]{2,1,0:T(8,128)(2,1)S(1)}, u32[]{:S(2)}, u32[]{:S(2)}) collective-permute-start(bf16[8,8,4096]{2,1,0:T(8,128)(2,1)S(1)} %get-tuple-element.55), channel_id=1, source_target_pairs={{0,1},{1,0},{2,3},{3,2},{4,5},{5,4},{6,7},{7,6},{8,9},{9,8},{10,11... | collective-permute-start | bytes 1572872 | tf_op jit(solution)/shard_map/ppermute | solution.py:329
  88.9 2.5 %collective-permute-start.32 = (bf16[8,8,4096]{2,1,0:T(8,128)(2,1)S(1)}, bf16[8,8,4096]{2,1,0:T(8,128)(2,1)S(1)}, u32[]{:S(2)}, u32[]{:S(2)}) collective-permute-start(bf16[8,8,4096]{2,1,0:T(8,128)(2,1)S(1)} %get-tuple-element.58), channel_id=1, source_target_pairs={{0,1},{1,0},{2,3},{3,2},{4,5},{5,4},{6,7},{7,6},{8,9},{9,8},{10,11... | collective-permute-start | bytes 1572872 | tf_op jit(solution)/shard_map/ppermute | solution.py:329
  90.7 8.6 %collective-permute-start.29 = (bf16[4,8,4096]{2,1,0:T(8,128)(2,1)S(1)}, bf16[4,8,4096]{2,1,0:T(8,128)(2,1)S(1)}, u32[]{:S(2)}, u32[]{:S(2)}) collective-permute-start(bf16[4,8,4096]{2,1,0:T(8,128)(2,1)S(1)} %get-tuple-element.60), channel_id=1, source_target_pairs={{0,2},{1,3},{2,0},{3,1},{4,6},{5,7},{6,4},{7,5},{8,10},{9,11},{10,... | collective-permute-start | bytes 786440 | tf_op jit(solution)/shard_map/ppermute | solution.py:329
  91.6 9.1 %collective-permute-start.33 = (bf16[4,8,4096]{2,1,0:T(8,128)(2,1)S(1)}, bf16[4,8,4096]{2,1,0:T(8,128)(2,1)S(1)}, u32[]{:S(2)}, u32[]{:S(2)}) collective-permute-start(bf16[4,8,4096]{2,1,0:T(8,128)(2,1)S(1)} %get-tuple-element.62), channel_id=1, source_target_pairs={{0,4},{1,5},{2,6},{3,7},{4,0},{5,1},{6,2},{7,3},{8,12},{9,13},{10,... | collective-permute-start | bytes 786440 | tf_op jit(solution)/shard_map/ppermute | solution.py:329
  99.3 6.9 %collective-permute-start.30 = (bf16[2,8,4096]{2,1,0:T(8,128)(2,1)S(1)}, bf16[2,8,4096]{2,1,0:T(8,128)(2,1)S(1)}, u32[]{:S(2)}, u32[]{:S(2)}) collective-permute-start(bf16[2,8,4096]{2,1,0:T(8,128)(2,1)S(1)} %get-tuple-element.64), channel_id=1, source_target_pairs={{0,4},{1,5},{2,6},{3,7},{4,0},{5,1},{6,2},{7,3},{8,12},{9,13},{10,... | collective-permute-start | bytes 393224 | tf_op jit(solution)/shard_map/ppermute | solution.py:329
  100.8 10.6 %collective-permute-start.34 = (bf16[2,8,4096]{2,1,0:T(8,128)(2,1)S(1)}, bf16[2,8,4096]{2,1,0:T(8,128)(2,1)S(1)}, u32[]{:S(2)}, u32[]{:S(2)}) collective-permute-start(bf16[2,8,4096]{2,1,0:T(8,128)(2,1)S(1)} %get-tuple-element.66), channel_id=1, source_target_pairs={{0,8},{1,9},{2,10},{3,11},{4,12},{5,13},{6,14},{7,15},{8,0},{9,1},... | collective-permute-start | bytes 393224 | tf_op jit(solution)/shard_map/ppermute | solution.py:329
  106.2 5.9 %collective-permute-start.31 = (bf16[1,8,4096]{2,1,0:T(8,128)(2,1)S(1)}, bf16[1,8,4096]{2,1,0:T(8,128)(2,1)S(1)}, u32[]{:S(2)}, u32[]{:S(2)}) collective-permute-start(bf16[1,8,4096]{2,1,0:T(8,128)(2,1)S(1)} %add_convert_fusion.10), channel_id=1, source_target_pairs={{0,8},{1,9},{2,10},{3,11},{4,12},{5,13},{6,14},{7,15},{8,0},{9,1},... | collective-permute-start | bytes 196616 | tf_op jit(solution)/shard_map/ppermute | solution.py:329
  111.4 4.3 %collective-permute-start.35 = (bf16[1,8,4096]{2,1,0:T(8,128)(2,1)S(1)}, bf16[1,8,4096]{2,1,0:T(8,128)(2,1)S(1)}, u32[]{:S(2)}, u32[]{:S(2)}) collective-permute-start(bf16[1,8,4096]{2,1,0:T(8,128)(2,1)S(1)} %add_convert_fusion.8), channel_id=1, source_target_pairs={{0,2},{1,3},{2,0},{3,1},{4,6},{5,7},{6,4},{7,5},{8,10},{9,11},{10,... | collective-permute-start | bytes 196616 | tf_op jit(solution)/shard_map/ppermute | solution.py:329

commit v7 on v6

--- a/solution.py
+++ b/solution.py
@@ -93,17 +93,17 @@
     )(lengths, *(pltpu.with_memory_space_constraint(x, pltpu.HBM) for x in (queries, kv_cache)))
 
 
-def expand_kernel(stacked, table_ref, code_ref, out_ref):
+def expand_kernel(stacked, skip, table_ref, code_ref, out_ref):
     rows, columns = code_ref.shape
     tile = 16
     tables = [jnp.broadcast_to(table_ref[i : i + 1], (tile, LANES)) for i in range(8)]
 
-    def one(i, lane):
-        at = pl.ds(pl.multiple_of(i * tile, tile), tile)
-        codes = code_ref[at, lane * LANES : (lane + 1) * LANES]
+    def one(row, lane):
+        codes = code_ref[pl.ds(skip + row, tile), pl.ds(lane, LANES)]
         codes = codes.astype(jnp.float32).astype(jnp.int32)
         upper = codes >= LANES
         low = jnp.bitwise_and(codes, LANES - 1)
+        at = pl.ds(row, tile)
 
         def take(table):
             return jnp.take_along_axis(table, low, axis=1, mode="promise_in_bounds")
@@ -112,49 +112,45 @@
             value = jnp.where(upper, take(tables[2 * q + 1]), take(tables[2 * q]))
             value = value.astype(jnp.bfloat16)
             if stacked:
-                out_ref[q, at, lane * LANES : (lane + 1) * LANES] = value
+                out_ref[q, at, pl.ds(lane, LANES)] = value
             else:
-                first = q * columns + lane * LANES
-                out_ref[at, first : first + LANES] = value
-
-    for lane in range(columns // LANES):
-
-        def body(i, _, lane=lane):
-            one(i, lane)
+                out_ref[at, pl.ds(q * columns + lane, LANES)] = value
+
+    if stacked:
+        steps = columns // LANES
+
+        def body(k, _):
+            for row in range(0, rows, tile):
+                one(row, pl.multiple_of(k * LANES, LANES))
             return 0
 
-        lax.fori_loop(0, rows // tile, body, 0, unroll=rows // tile if rows // tile <= 12 else 8)
+    else:
+        steps = out_ref.shape[0] // tile
+
+        def body(k, _):
+            for lane in range(0, columns, LANES):
+                one(pl.multiple_of(k * tile, tile), lane)
+            return 0
+
+    lax.fori_loop(0, steps, body, 0, unroll=16)
 
 
 def expand(table, codes, stacked, after=(), part=None):
     rows, columns = codes.shape
-    skip = 0
-    if stacked:
-        block = 512
-        grid = (columns // block,)
-        code_spec = pl.BlockSpec((rows, block), lambda b: (0, b))
-        out_spec = pl.BlockSpec((4, rows, block), lambda b: (0, 0, b))
-        out_shape = (4, rows, columns)
-    else:
-        block = 128
-        if part is not None:
-            skip, rows = part[0] // block, part[1]
-        grid = (rows // block,)
-        code_spec = pl.BlockSpec((block, columns), lambda b: (b + skip, 0))
-        out_spec = pl.BlockSpec((block, 4 * columns), lambda b: (b, 0))
-        out_shape = (rows, 4 * columns)
+    skip, count = part or (0, rows)
+    out_shape = (4, rows, columns) if stacked else (count, 4 * columns)
+    in_vmem = pl.BlockSpec(memory_space=pltpu.VMEM)
     out = pl.pallas_call(
-        functools.partial(expand_kernel, stacked),
-        grid=grid,
-        in_specs=[pl.BlockSpec(table.shape, lambda b: (0, 0)), code_spec],
-        out_specs=out_spec,
+        functools.partial(expand_kernel, stacked, skip),
+        in_specs=[in_vmem, in_vmem],
+        out_specs=in_vmem,
         out_shape=jax.ShapeDtypeStruct(out_shape, jnp.bfloat16),
         name="expand",
-        compiler_params=pltpu.CompilerParams(vmem_limit_bytes=6 * MIB),
+        compiler_params=pltpu.CompilerParams(vmem_limit_bytes=12 * MIB),
         cost_estimate=pl.CostEstimate(
-            flops=rows * columns * 8000, bytes_accessed=10 * rows * columns, transcendentals=0
+            flops=count * columns * 8000, bytes_accessed=10 * count * columns, transcendentals=0
         ),
-    )(tie(table, *after), pltpu.with_memory_space_constraint(codes, pltpu.HBM))
+    )(tie(table, *after), pltpu.with_memory_space_constraint(codes, pltpu.VMEM))
     return out.reshape(4 * rows, columns) if stacked else out
 
 

time: 117 us -> 114 us (0.974)
  Pallas kernels: 44.5 us -> 38.5 us
  waiting for transfers between devices: 27.8 us -> 30.8 us
    pallas_call x4, Pallas kernels: 27.4 us -> 21.5 us  [expand(): pl.pallas_call(functools.partial(expand_kernel, stacked, skip), in_specs=...]
    ppermute x36, waiting for transfers between devices: 27.8 us -> 30.8 us  [swap(): return lax.ppermute(value, 'expert', [(i, i ^ bit) for i in range(count)])]
  transfers between devices with their start and end apart: 37 -> 37, of which waited for: 15 -> 16; matrix products, arithmetic and copies ran while one was open for 1% -> 1% of each run, Pallas kernels for 27% -> 23%
where the time goes in v7:
time: 114 us; the launch traced here: 113 us
  starting transfers between devices  40.8 us (36%)
  Pallas kernels  38.5 us (34%)
  waiting for transfers between devices  30.8 us (27%)
  local copies, waits for them, and re-layouts  1.54 us (1%)
  other arithmetic  1.46 us (1%)
    ppermute x36, starting transfers between devices, swap(): return lax.ppermute(value, 'expert', [(i, i ^ bit) for i in range(count)])  37.3 us
    ppermute x36, waiting for transfers between devices, swap(): return lax.ppermute(value, 'expert', [(i, i ^ bit) for i in range(count)])  30.8 us
    pallas_call x4, Pallas kernels, expand(): pl.pallas_call(functools.partial(expand_kernel, stacked, skip), in_specs=...  21.5 us
    pallas_call x2, Pallas kernels, attend(): pl.pallas_call(functools.partial(attend_kernel, micro, span, KV_HEADS), g...  8.2 us
    pallas_call x1, Pallas kernels, run_experts(): pl.pallas_call(functools.partial(experts_kernel, masks, counts, orders, l...  7.55 us
    all_to_all x1, starting transfers between devices, body(): lax.all_to_all(jnp.concatenate([lead, tail], axis=-1), 'expert', split_ax...  3.52 us
  transfers between devices with their start and end apart: 37, of which 16 were waited for; matrix products, arithmetic and copies ran while one was open for 1% of the time, Pallas kernels for 23%

profile of v7, /device:TPU:0, one launch (start us, length us, event | category | flops | bytes accessed | tf_op | source)
XLA Modules:
  0.0 113.5 jit_solution(16582059772076503909)
XLA Ops:
  0.0 0.7 copy-done.5
  0.7 4.1 %attend.2 = bf16[8,8192]{1,0:T(8,128)(2,1)S(1)} custom-call(s32[2,8]{1,0:T(2,128)S(1)} %copy-done.5, bf16[2,8,8192]{2,1,0:T(8,128)(2,1)} %q_ref.3, bf16[2,8,128,2,512]{4,3,2,1,0:T(2,128)(2,1)} %kv_ref.3), custom_call_target="tpu_custom_call" | custom-call | flops 67108864 | bytes 2097152 | tf_op jit(solution)/shard_map/attend/pallas_call | solution.py:75
  4.8 3.1 %collective-permute-start.1 = (bf16[8,8192]{1,0:T(8,128)(2,1)S(1)}, bf16[8,8192]{1,0:T(8,128)(2,1)S(1)}, u32[]{:S(2)}, u32[]{:S(2)}) collective-permute-start(bf16[8,8192]{1,0:T(8,128)(2,1)S(1)} %attend.2), channel_id=1, source_target_pairs={{0,4},{1,5},{2,6},{3,7},{4,0},{5,1},{6,2},{7,3},{8,12},{9,13},{10,... | collective-permute-start | bytes 393224 | tf_op jit(solution)/shard_map/ppermute | solution.py:325
  7.9 2.6 %collective-permute-start = (bf16[8,8192]{1,0:T(8,128)(2,1)S(1)}, bf16[8,8192]{1,0:T(8,128)(2,1)S(1)}, u32[]{:S(2)}, u32[]{:S(2)}) collective-permute-start(bf16[8,8192]{1,0:T(8,128)(2,1)S(1)} %attend.2), channel_id=1, source_target_pairs={{0,8},{1,9},{2,10},{3,11},{4,12},{5,13},{6,14},{7,15},{8,0},{9,1},... | collective-permute-start | bytes 393224 | tf_op jit(solution)/shard_map/ppermute | solution.py:325
  10.5 0.1 fusion.4
  10.7 0.7 copy.19
  11.4 3.5 %all-to-all-start = ((bf16[16,2,8,272]{3,2,1,0:T(8,128)(2,1)}), bf16[16,2,8,272]{3,2,1,0:T(8,128)(2,1)S(1)}, u32[]{:S(2)}, u32[]{:S(2)}) async-start(bf16[16,2,8,272]{3,2,1,0:T(8,128)(2,1)} %copy.19), calls=%async_computation | async-start | bytes 393216 | tf_op jit(solution)/shard_map/all_to_all | solution.py:409
  15.0 4.1 %attend.3 = bf16[8,8192]{1,0:T(8,128)(2,1)S(1)} custom-call(s32[2,8]{1,0:T(2,128)S(1)} %copy-done.6, bf16[2,8,8192]{2,1,0:T(8,128)(2,1)} %q_ref.3, bf16[2,8,128,2,512]{4,3,2,1,0:T(2,128)(2,1)} %kv_ref.3), custom_call_target="tpu_custom_call" | custom-call | flops 67108864 | bytes 2097152 | tf_op jit(solution)/shard_map/attend/pallas_call | solution.py:75
  19.1 1.9 %collective-permute-start.5 = (bf16[8,8192]{1,0:T(8,128)(2,1)S(1)}, bf16[8,8192]{1,0:T(8,128)(2,1)S(1)}, u32[]{:S(2)}, u32[]{:S(2)}) collective-permute-start(bf16[8,8192]{1,0:T(8,128)(2,1)S(1)} %attend.3), channel_id=1, source_target_pairs={{0,2},{1,3},{2,0},{3,1},{4,6},{5,7},{6,4},{7,5},{8,10},{9,11},{10,... | collective-permute-start | bytes 393224 | tf_op jit(solution)/shard_map/ppermute | solution.py:325
  21.0 1.6 %collective-permute-start.2 = (bf16[8,8192]{1,0:T(8,128)(2,1)S(1)}, bf16[8,8192]{1,0:T(8,128)(2,1)S(1)}, u32[]{:S(2)}, u32[]{:S(2)}) collective-permute-start(bf16[8,8192]{1,0:T(8,128)(2,1)S(1)} %collective-permute-done), channel_id=1, source_target_pairs={{0,4},{1,5},{2,6},{3,7},{4,0},{5,1},{6,2},{7,3},{8,12},{9,13},{10,... | collective-permute-start | bytes 393224 | tf_op jit(solution)/shard_map/ppermute | solution.py:325
  22.6 2.8 %collective-permute-done.5 = bf16[8,8192]{1,0:T(8,128)(2,1)S(1)} collective-permute-done((bf16[8,8192]{1,0:T(8,128)(2,1)S(1)}, bf16[8,8192]{1,0:T(8,128)(2,1)S(1)}, u32[]{:S(2)}, u32[]{:S(2)}) %collective-permute-start.5) | collective-permute-done | bytes 131104 | tf_op jit(solution)/shard_map/ppermute | solution.py:325
  25.4 0.1 collective-permute-start.10
  25.5 1.4 %collective-permute-start.8 = (bf16[2,8,8192]{2,1,0:T(8,128)(2,1)S(1)}, bf16[2,8,8192]{2,1,0:T(8,128)(2,1)S(1)}, u32[]{:S(2)}, u32[]{:S(2)}) collective-permute-start(bf16[2,8,8192]{2,1,0:T(8,128)(2,1)S(1)} %pad_maximum_fusion.1.refs_4_), channel_id=1, source_target_pairs={{0,4},{1,5},{2,6},{3,7},{4,0},{5,1},{6,2},{7,3},{8,12},{9,13},{10,... | collective-permute-start | bytes 786440 | tf_op jit(solution)/shard_map/ppermute | solution.py:325
  26.9 2.2 %collective-permute-start.6 = (bf16[2,8,8192]{2,1,0:T(8,128)(2,1)S(1)}, bf16[2,8,8192]{2,1,0:T(8,128)(2,1)S(1)}, u32[]{:S(2)}, u32[]{:S(2)}) collective-permute-start(bf16[2,8,8192]{2,1,0:T(8,128)(2,1)S(1)} %pad_maximum_fusion.1.refs_4_), channel_id=1, source_target_pairs={{0,8},{1,9},{2,10},{3,11},{4,12},{5,13},{6,14},{7,15},{8,0},{9,1},... | collective-permute-start | bytes 786440 | tf_op jit(solution)/shard_map/ppermute | solution.py:325
  29.2 0.1 collective-permute-start.4
  29.3 1.5 %collective-permute-start.3 = (bf16[4,8,8192]{2,1,0:T(8,128)(2,1)S(1)}, bf16[4,8,8192]{2,1,0:T(8,128)(2,1)S(1)}, u32[]{:S(2)}, u32[]{:S(2)}) collective-permute-start(bf16[4,8,8192]{2,1,0:T(8,128)(2,1)S(1)} %pad_maximum_fusion.refs_0_), channel_id=1, source_target_pairs={{0,2},{1,3},{2,0},{3,1},{4,6},{5,7},{6,4},{7,5},{8,10},{9,11},{10,... | collective-permute-start | bytes 1572872 | tf_op jit(solution)/shard_map/ppermute | solution.py:325
  30.8 7.2 %expand.4 = bf16[4,192,4096]{2,1,0:T(8,128)(2,1)S(1)} custom-call(f32[8,128]{1,0:T(8,128)S(1)} %squeeze.27.table_ref, bf16[192,4096]{1,0:T(8,128)(2,1)S(1)} %bitcast.66), custom_call_target="tpu_custom_call" | custom-call | flops 6291456000 | bytes 7864320 | tf_op jit(solution)/shard_map/expand/pallas_call | solution.py:143
  38.0 3.9 %collective-permute-done.6.refs_5_ = bf16[2,8,8192]{2,1,0:T(8,128)(2,1)S(1)} collective-permute-done((bf16[2,8,8192]{2,1,0:T(8,128)(2,1)S(1)}, bf16[2,8,8192]{2,1,0:T(8,128)(2,1)S(1)}, u32[]{:S(2)}, u32[]{:S(2)}) %collective-permute-start.6) | collective-permute-done | bytes 262176 | tf_op jit(solution)/shard_map/ppermute | solution.py:325
  41.8 0.1 collective-permute-start.9
  42.0 7.2 %expand.5 = bf16[4,192,4096]{2,1,0:T(8,128)(2,1)S(1)} custom-call(f32[8,128]{1,0:T(8,128)S(1)} %squeeze.28.table_ref, bf16[192,4096]{1,0:T(8,128)(2,1)S(1)} %bitcast.67), custom_call_target="tpu_custom_call" | custom-call | flops 6291456000 | bytes 7864320 | tf_op jit(solution)/shard_map/expand/pallas_call | solution.py:143
  49.2 0.1 collective-permute-start.7
  49.2 0.5 collective-permute-start.11
  49.7 0.1 collective-permute-start.12
  49.8 0.4 collective-permute-start.13
  50.3 1.2 %collective-permute-done.11.refs_9_ = bf16[2,8,8192]{2,1,0:T(8,128)(2,1)S(1)} collective-permute-done((bf16[2,8,8192]{2,1,0:T(8,128)(2,1)S(1)}, bf16[2,8,8192]{2,1,0:T(8,128)(2,1)S(1)}, u32[]{:S(2)}, u32[]{:S(2)}) %collective-permute-start.11) | collective-permute-done | bytes 262176 | tf_op jit(solution)/shard_map/ppermute | solution.py:325
  51.5 0.4 collective-permute-done.12.refs_10_
  51.9 0.4 collective-permute-done.13.refs_11_
  52.3 1.3 %project.1 = (bf16[16,8,256]{2,1,0:T(8,128)(2,1)S(1)}, bf16[16,8,256]{2,1,0:T(8,128)(2,1)S(1)}) custom-call(s32[1]{0:T(128)} %bitcast.3.me_ref, bf16[4,8,8192]{2,1,0:T(8,128)(2,1)S(1)} %pad_maximum_fusion.refs_0_, bf16[4,8,8192]{2,1,0:T(8,128)(2,1)S(1)} %collective-permute-done.3.refs_1_, bf16[4,8,8192]{2,1,0:T(8,128)(2,1)S(1)} %collective-permute-done.4.refs_2_, ...), custom_call_target="tpu_custom_call" | custom-call | flops 1073741824 | bytes 4194304 | tf_op jit(solution)/shard_map/project/pallas_call | solution.py:190
  53.5 2.7 %collective-permute-start.14 = (bf16[16,8,256]{2,1,0:T(8,128)(2,1)S(1)}, bf16[16,8,256]{2,1,0:T(8,128)(2,1)S(1)}, u32[]{:S(2)}, u32[]{:S(2)}) collective-permute-start(bf16[16,8,256]{2,1,0:T(8,128)(2,1)S(1)} %get-tuple-element.43), channel_id=1, source_target_pairs={{0,8},{1,9},{2,10},{3,11},{4,12},{5,13},{6,14},{7,15},{8,0},{9,1},... | collective-permute-start | bytes 196616 | tf_op jit(solution)/shard_map/ppermute | solution.py:325
  56.2 1.5 %collective-permute-start.19 = (bf16[16,8,256]{2,1,0:T(8,128)(2,1)S(1)}, bf16[16,8,256]{2,1,0:T(8,128)(2,1)S(1)}, u32[]{:S(2)}, u32[]{:S(2)}) collective-permute-start(bf16[16,8,256]{2,1,0:T(8,128)(2,1)S(1)} %get-tuple-element.45), channel_id=1, source_target_pairs={{0,2},{1,3},{2,0},{3,1},{4,6},{5,7},{6,4},{7,5},{8,10},{9,11},{10,... | collective-permute-start | bytes 196616 | tf_op jit(solution)/shard_map/ppermute | solution.py:325
  57.7 2.1 %collective-permute-done.14 = bf16[16,8,256]{2,1,0:T(8,128)(2,1)S(1)} collective-permute-done((bf16[16,8,256]{2,1,0:T(8,128)(2,1)S(1)}, bf16[16,8,256]{2,1,0:T(8,128)(2,1)S(1)}, u32[]{:S(2)}, u32[]{:S(2)}) %collective-permute-start.14) | collective-permute-done | bytes 65568 | tf_op jit(solution)/shard_map/ppermute | solution.py:325
  59.8 1.3 %collective-permute-start.16 = (bf16[16,8,256]{2,1,0:T(8,128)(2,1)S(1)}, bf16[16,8,256]{2,1,0:T(8,128)(2,1)S(1)}, u32[]{:S(2)}, u32[]{:S(2)}) collective-permute-start(bf16[16,8,256]{2,1,0:T(8,128)(2,1)S(1)} %collective-permute-done.14), channel_id=1, source_target_pairs={{0,4},{1,5},{2,6},{3,7},{4,0},{5,1},{6,2},{7,3},{8,12},{9,13},{10,... | collective-permute-start | bytes 196616 | tf_op jit(solution)/shard_map/ppermute | solution.py:325
  61.1 0.1 collective-permute-start.24
  61.2 0.8 collective-permute-start.22
  62.0 2.0 %collective-permute-start.20 = (bf16[2,16,8,256]{3,2,1,0:T(8,128)(2,1)S(1)}, bf16[2,16,8,256]{3,2,1,0:T(8,128)(2,1)S(1)}, u32[]{:S(2)}, u32[]{:S(2)}) collective-permute-start(bf16[2,16,8,256]{3,2,1,0:T(8,128)(2,1)S(1)} %pad_maximum_fusion.4.refs_4_), channel_id=1, source_target_pairs={{0,8},{1,9},{2,10},{3,11},{4,12},{5,13},{6,14},{7,15},{8,0},{9,1},... | collective-permute-start | bytes 393224 | tf_op jit(solution)/shard_map/ppermute | solution.py:325
  64.0 0.1 collective-permute-done.16
  64.1 0.1 collective-permute-start.18
  64.2 1.6 %collective-permute-start.17 = (bf16[4,16,8,256]{3,2,1,0:T(8,128)(2,1)S(1)}, bf16[4,16,8,256]{3,2,1,0:T(8,128)(2,1)S(1)}, u32[]{:S(2)}, u32[]{:S(2)}) collective-permute-start(bf16[4,16,8,256]{3,2,1,0:T(8,128)(2,1)S(1)} %pad_maximum_fusion.2.refs_0_), channel_id=1, source_target_pairs={{0,2},{1,3},{2,0},{3,1},{4,6},{5,7},{6,4},{7,5},{8,10},{9,11},{10,... | collective-permute-start | bytes 786440 | tf_op jit(solution)/shard_map/ppermute | solution.py:325
  65.8 4.8 %expand.6.refs_19_ = bf16[512,4096]{1,0:T(8,128)(2,1)S(1)} custom-call(f32[8,128]{1,0:T(8,128)S(1)} %squeeze.29.table_ref, bf16[768,1024]{1,0:T(8,128)(2,1)S(1)} %bitcast.68), custom_call_target="tpu_custom_call" | custom-call | flops 4194304000 | bytes 5242880 | tf_op jit(solution)/shard_map/expand/pallas_call | solution.py:143
  70.7 0.6 collective-permute-done.20.refs_5_
  71.3 0.9 collective-permute-start.23
  72.2 2.4 %expand.7.refs_20_ = bf16[256,4096]{1,0:T(8,128)(2,1)S(1)} custom-call(f32[8,128]{1,0:T(8,128)S(1)} %squeeze.29.table_ref, bf16[768,1024]{1,0:T(8,128)(2,1)S(1)} %bitcast.69), custom_call_target="tpu_custom_call" | custom-call | flops 2097152000 | bytes 2621440 | tf_op jit(solution)/shard_map/expand/pallas_call | solution.py:143
  74.7 0.5 collective-permute-start.25
  75.2 1.1 collective-permute-done.23.refs_7_
  76.3 0.5 collective-permute-start.27
  76.8 0.8 collective-permute-done.26.refs_10_
  77.6 0.2 collective-permute-done.27.refs_11_
  77.9 7.6 %experts.1 = (bf16[8,8,4096]{2,1,0:T(8,128)(2,1)S(1)}, bf16[8,8,4096]{2,1,0:T(8,128)(2,1)S(1)}, bf16[8,8,4096]{2,1,0:T(8,128)(2,1)S(1)}, bf16[8,8,4096]{2,1,0:T(...) custom-call(s32[1]{0:T(128)} %bitcast.3.me_ref, ...), custom_call_target="tpu_custom_call" | custom-call | flops 4831838208 | bytes 18874368 | tf_op jit(solution)/shard_map/experts/pallas_call | solution.py:306
  85.4 0.4 collective-permute-start.28
  85.8 0.2 collective-permute-start.32
  86.0 1.4 %collective-permute-done.28 = bf16[8,8,4096]{2,1,0:T(8,128)(2,1)S(1)} collective-permute-done((bf16[8,8,4096]{2,1,0:T(8,128)(2,1)S(1)}, bf16[8,8,4096]{2,1,0:T(8,128)(2,1)S(1)}, u32[]{:S(2)}, u32[]{:S(2)}) %collective-permute-start.28) | collective-permute-done | bytes 524320 | tf_op jit(solution)/shard_map/ppermute | solution.py:325
  87.4 0.1 add_convert_fusion.3
  87.5 1.5 %collective-permute-start.29 = (bf16[4,8,4096]{2,1,0:T(8,128)(2,1)S(1)}, bf16[4,8,4096]{2,1,0:T(8,128)(2,1)S(1)}, u32[]{:S(2)}, u32[]{:S(2)}) collective-permute-start(bf16[4,8,4096]{2,1,0:T(8,128)(2,1)S(1)} %get-tuple-element.60), channel_id=1, source_target_pairs={{0,2},{1,3},{2,0},{3,1},{4,6},{5,7},{6,4},{7,5},{8,10},{9,11},{10,... | collective-permute-start | bytes 786440 | tf_op jit(solution)/shard_map/ppermute | solution.py:325
  89.1 0.1 add_convert_fusion.1
  89.2 0.8 collective-permute-start.33
  90.0 6.2 %collective-permute-done.29 = bf16[4,8,4096]{2,1,0:T(8,128)(2,1)S(1)} collective-permute-done((bf16[4,8,4096]{2,1,0:T(8,128)(2,1)S(1)}, bf16[4,8,4096]{2,1,0:T(8,128)(2,1)S(1)}, u32[]{:S(2)}, u32[]{:S(2)}) %collective-permute-start.29) | collective-permute-done | bytes 262176 | tf_op jit(solution)/shard_map/ppermute | solution.py:325
  96.2 1.5 %collective-permute-start.30 = (bf16[2,8,4096]{2,1,0:T(8,128)(2,1)S(1)}, bf16[2,8,4096]{2,1,0:T(8,128)(2,1)S(1)}, u32[]{:S(2)}, u32[]{:S(2)}) collective-permute-start(bf16[2,8,4096]{2,1,0:T(8,128)(2,1)S(1)} %get-tuple-element.64), channel_id=1, source_target_pairs={{0,4},{1,5},{2,6},{3,7},{4,0},{5,1},{6,2},{7,3},{8,12},{9,13},{10,... | collective-permute-start | bytes 393224 | tf_op jit(solution)/shard_map/ppermute | solution.py:325
  97.8 2.0 %collective-permute-start.34 = (bf16[2,8,4096]{2,1,0:T(8,128)(2,1)S(1)}, bf16[2,8,4096]{2,1,0:T(8,128)(2,1)S(1)}, u32[]{:S(2)}, u32[]{:S(2)}) collective-permute-start(bf16[2,8,4096]{2,1,0:T(8,128)(2,1)S(1)} %get-tuple-element.66), channel_id=1, source_target_pairs={{0,8},{1,9},{2,10},{3,11},{4,12},{5,13},{6,14},{7,15},{8,0},{9,1},... | collective-permute-start | bytes 393224 | tf_op jit(solution)/shard_map/ppermute | solution.py:325
  99.8 3.2 %collective-permute-done.30 = bf16[2,8,4096]{2,1,0:T(8,128)(2,1)S(1)} collective-permute-done((bf16[2,8,4096]{2,1,0:T(8,128)(2,1)S(1)}, bf16[2,8,4096]{2,1,0:T(8,128)(2,1)S(1)}, u32[]{:S(2)}, u32[]{:S(2)}) %collective-permute-start.30) | collective-permute-done | bytes 131104 | tf_op jit(solution)/shard_map/ppermute | solution.py:325
  103.0 2.5 %collective-permute-start.31 = (bf16[1,8,4096]{2,1,0:T(8,128)(2,1)S(1)}, bf16[1,8,4096]{2,1,0:T(8,128)(2,1)S(1)}, u32[]{:S(2)}, u32[]{:S(2)}) collective-permute-start(bf16[1,8,4096]{2,1,0:T(8,128)(2,1)S(1)} %add_convert_fusion.10), channel_id=1, source_target_pairs={{0,8},{1,9},{2,10},{3,11},{4,12},{5,13},{6,14},{7,15},{8,0},{9,1},... | collective-permute-start | bytes 196616 | tf_op jit(solution)/shard_map/ppermute | solution.py:325
  105.5 2.9 %collective-permute-done.34 = bf16[2,8,4096]{2,1,0:T(8,128)(2,1)S(1)} collective-permute-done((bf16[2,8,4096]{2,1,0:T(8,128)(2,1)S(1)}, bf16[2,8,4096]{2,1,0:T(8,128)(2,1)S(1)}, u32[]{:S(2)}, u32[]{:S(2)}) %collective-permute-start.34) | collective-permute-done | bytes 131104 | tf_op jit(solution)/shard_map/ppermute | solution.py:325
  108.4 0.8 collective-permute-start.35
  109.3 3.5 %collective-permute-done.35 = bf16[1,8,4096]{2,1,0:T(8,128)(2,1)S(1)} collective-permute-done((bf16[1,8,4096]{2,1,0:T(8,128)(2,1)S(1)}, bf16[1,8,4096]{2,1,0:T(8,128)(2,1)S(1)}, u32[]{:S(2)}, u32[]{:S(2)}) %collective-permute-start.35) | collective-permute-done | bytes 65568 | tf_op jit(solution)/shard_map/ppermute | solution.py:325
  112.8 0.7 pad_maximum_fusion.5
  (70 shorter events, 0.7 us)
Async XLA Ops:
  0.0 0.7 copy-start.5
  0.7 9.8 %copy-start.11 = (s32[2,8,8]{2,1,0:T(8,128)S(1)}, s32[2,8,8]{2,1,0:T(8,128)}, u32[]{:S(2)}) copy-start(s32[2,8,8]{2,1,0:T(8,128)} %param.18) | copy-start | bytes 1540
  0.7 9.9 %copy-start.10 = (bf16[2,8,4096]{2,1,0:T(8,128)(2,1)S(1)}, bf16[2,8,4096]{2,1,0:T(8,128)(2,1)}, u32[]{:S(2)}) copy-start(bf16[2,8,4096]{2,1,0:T(8,128)(2,1)} %param.14) | copy-start | bytes 393220
  0.7 14.3 %copy-start.6 = (s32[2,8]{1,0:T(2,128)S(1)}, s32[2,8]{1,0:T(2,128)}, u32[]{:S(2)}) copy-start(s32[2,8]{1,0:T(2,128)} %len_ref.3) | copy-start | bytes 196
  4.8 16.2 %copy-start.12 = (bf16[1,3,256,4]{2,3,1,0:T(4,128)(2,1)S(1)}, bf16[1,3,256,4]{2,3,1,0:T(4,128)(2,1)}, u32[]{:S(2)}) copy-start(bf16[1,3,256,4]{2,3,1,0:T(4,128)(2,1)} %param.25) | copy-start | bytes 18436
  4.8 26.0 %copy-start.7 = (bf16[1,4096,192]{1,2,0:T(8,128)(2,1)S(1)}, bf16[1,4096,192]{1,2,0:T(8,128)(2,1)}, u32[]{:S(2)}) copy-start(bf16[1,4096,192]{1,2,0:T(8,128)(2,1)} %param.22) | copy-start | bytes 4718596
  4.8 24.3 %collective-permute-start.1 = (bf16[8,8192]{1,0:T(8,128)(2,1)S(1)}, bf16[8,8192]{1,0:T(8,128)(2,1)S(1)}, u32[]{:S(2)}, u32[]{:S(2)}) collective-permute-start(bf16[8,8192]{1,0:T(8,128)(2,1)S(1)} %attend.2), channel_id=1, source_target_pairs={{0,4},{1,5},{2,6},{3,7},{4,0},{5,1},{6,2},{7,3},{8,12},{9,13},{10,... | collective-permute-start | bytes 393224 | tf_op jit(solution)/shard_map/ppermute | solution.py:325
  7.9 13.1 %collective-permute-start = (bf16[8,8192]{1,0:T(8,128)(2,1)S(1)}, bf16[8,8192]{1,0:T(8,128)(2,1)S(1)}, u32[]{:S(2)}, u32[]{:S(2)}) collective-permute-start(bf16[8,8192]{1,0:T(8,128)(2,1)S(1)} %attend.2), channel_id=1, source_target_pairs={{0,8},{1,9},{2,10},{3,11},{4,12},{5,13},{6,14},{7,15},{8,0},{9,1},... | collective-permute-start | bytes 393224 | tf_op jit(solution)/shard_map/ppermute | solution.py:325
  11.4 17.7 %all-to-all-start = ((bf16[16,2,8,272]{3,2,1,0:T(8,128)(2,1)}), bf16[16,2,8,272]{3,2,1,0:T(8,128)(2,1)S(1)}, u32[]{:S(2)}, u32[]{:S(2)}) async-start(bf16[16,2,8,272]{3,2,1,0:T(8,128)(2,1)} %copy.19), calls=%async_computation | async-start | bytes 393216 | tf_op jit(solution)/shard_map/all_to_all | solution.py:409
  19.1 6.3 %collective-permute-start.5 = (bf16[8,8192]{1,0:T(8,128)(2,1)S(1)}, bf16[8,8192]{1,0:T(8,128)(2,1)S(1)}, u32[]{:S(2)}, u32[]{:S(2)}) collective-permute-start(bf16[8,8192]{1,0:T(8,128)(2,1)S(1)} %attend.3), channel_id=1, source_target_pairs={{0,2},{1,3},{2,0},{3,1},{4,6},{5,7},{6,4},{7,5},{8,10},{9,11},{10,... | collective-permute-start | bytes 393224 | tf_op jit(solution)/shard_map/ppermute | solution.py:325
  21.0 8.1 %collective-permute-start.2 = (bf16[8,8192]{1,0:T(8,128)(2,1)S(1)}, bf16[8,8192]{1,0:T(8,128)(2,1)S(1)}, u32[]{:S(2)}, u32[]{:S(2)}) collective-permute-start(bf16[8,8192]{1,0:T(8,128)(2,1)S(1)} %collective-permute-done), channel_id=1, source_target_pairs={{0,4},{1,5},{2,6},{3,7},{4,0},{5,1},{6,2},{7,3},{8,12},{9,13},{10,... | collective-permute-start | bytes 393224 | tf_op jit(solution)/shard_map/ppermute | solution.py:325
  25.4 24.5 %collective-permute-start.10 = (bf16[2,8,8192]{2,1,0:T(8,128)(2,1)S(1)}, bf16[2,8,8192]{2,1,0:T(8,128)(2,1)S(1)}, u32[]{:S(2)}, u32[]{:S(2)}) collective-permute-start(bf16[2,8,8192]{2,1,0:T(8,128)(2,1)S(1)} %pad_maximum_fusion.1.refs_4_), channel_id=1, source_target_pairs={{0,1},{1,0},{2,3},{3,2},{4,5},{5,4},{6,7},{7,6},{8,9},{9,8},{10,11... | collective-permute-start | bytes 786440 | tf_op jit(solution)/shard_map/ppermute | solution.py:325
  25.5 23.8 %collective-permute-start.8 = (bf16[2,8,8192]{2,1,0:T(8,128)(2,1)S(1)}, bf16[2,8,8192]{2,1,0:T(8,128)(2,1)S(1)}, u32[]{:S(2)}, u32[]{:S(2)}) collective-permute-start(bf16[2,8,8192]{2,1,0:T(8,128)(2,1)S(1)} %pad_maximum_fusion.1.refs_4_), channel_id=1, source_target_pairs={{0,4},{1,5},{2,6},{3,7},{4,0},{5,1},{6,2},{7,3},{8,12},{9,13},{10,... | collective-permute-start | bytes 786440 | tf_op jit(solution)/shard_map/ppermute | solution.py:325
  26.9 14.9 %collective-permute-start.6 = (bf16[2,8,8192]{2,1,0:T(8,128)(2,1)S(1)}, bf16[2,8,8192]{2,1,0:T(8,128)(2,1)S(1)}, u32[]{:S(2)}, u32[]{:S(2)}) collective-permute-start(bf16[2,8,8192]{2,1,0:T(8,128)(2,1)S(1)} %pad_maximum_fusion.1.refs_4_), channel_id=1, source_target_pairs={{0,8},{1,9},{2,10},{3,11},{4,12},{5,13},{6,14},{7,15},{8,0},{9,1},... | collective-permute-start | bytes 786440 | tf_op jit(solution)/shard_map/ppermute | solution.py:325
  29.2 22.7 %collective-permute-start.4 = (bf16[4,8,8192]{2,1,0:T(8,128)(2,1)S(1)}, bf16[4,8,8192]{2,1,0:T(8,128)(2,1)S(1)}, u32[]{:S(2)}, u32[]{:S(2)}) collective-permute-start(bf16[4,8,8192]{2,1,0:T(8,128)(2,1)S(1)} %pad_maximum_fusion.refs_0_), channel_id=1, source_target_pairs={{0,1},{1,0},{2,3},{3,2},{4,5},{5,4},{6,7},{7,6},{8,9},{9,8},{10,11... | collective-permute-start | bytes 1572872 | tf_op jit(solution)/shard_map/ppermute | solution.py:325
  29.3 19.9 %collective-permute-start.3 = (bf16[4,8,8192]{2,1,0:T(8,128)(2,1)S(1)}, bf16[4,8,8192]{2,1,0:T(8,128)(2,1)S(1)}, u32[]{:S(2)}, u32[]{:S(2)}) collective-permute-start(bf16[4,8,8192]{2,1,0:T(8,128)(2,1)S(1)} %pad_maximum_fusion.refs_0_), channel_id=1, source_target_pairs={{0,2},{1,3},{2,0},{3,1},{4,6},{5,7},{6,4},{7,5},{8,10},{9,11},{10,... | collective-permute-start | bytes 1572872 | tf_op jit(solution)/shard_map/ppermute | solution.py:325
  30.8 11.2 %copy-start.8 = (bf16[1,4096,192]{1,2,0:T(8,128)(2,1)S(1)}, bf16[1,4096,192]{1,2,0:T(8,128)(2,1)}, u32[]{:S(2)}) copy-start(bf16[1,4096,192]{1,2,0:T(8,128)(2,1)} %param.23) | copy-start | bytes 4718596
  41.8 7.9 %collective-permute-start.9 = (bf16[2,8,8192]{2,1,0:T(8,128)(2,1)S(1)}, bf16[2,8,8192]{2,1,0:T(8,128)(2,1)S(1)}, u32[]{:S(2)}, u32[]{:S(2)}) collective-permute-start(bf16[2,8,8192]{2,1,0:T(8,128)(2,1)S(1)} %collective-permute-done.6.refs_5_), channel_id=1, source_target_pairs={{0,4},{1,5},{2,6},{3,7},{4,0},{5,1},{6,2},{7,3},{8,12},{9,13},{10,... | collective-permute-start | bytes 786440 | tf_op jit(solution)/shard_map/ppermute | solution.py:325
  42.0 10.3 %copy-start = (bf16[8192,256]{1,0:T(8,128)(2,1)S(1)}, bf16[8192,256]{1,0:T(8,128)(2,1)}, u32[]{:S(2)}) copy-start(bf16[8192,256]{1,0:T(8,128)(2,1)} %refs_12_.1) | copy-start | bytes 12582916
  49.2 3.1 %collective-permute-start.7 = (bf16[4,8,8192]{2,1,0:T(8,128)(2,1)S(1)}, bf16[4,8,8192]{2,1,0:T(8,128)(2,1)S(1)}, u32[]{:S(2)}, u32[]{:S(2)}) collective-permute-start(bf16[4,8,8192]{2,1,0:T(8,128)(2,1)S(1)} %collective-permute-done.3.refs_1_), channel_id=1, source_target_pairs={{0,1},{1,0},{2,3},{3,2},{4,5},{5,4},{6,7},{7,6},{8,9},{9,8},{10,11... | collective-permute-start | bytes 1572872 | tf_op jit(solution)/shard_map/ppermute | solution.py:325
  49.2 2.3 %collective-permute-start.11 = (bf16[2,8,8192]{2,1,0:T(8,128)(2,1)S(1)}, bf16[2,8,8192]{2,1,0:T(8,128)(2,1)S(1)}, u32[]{:S(2)}, u32[]{:S(2)}) collective-permute-start(bf16[2,8,8192]{2,1,0:T(8,128)(2,1)S(1)} %collective-permute-done.6.refs_5_), channel_id=1, source_target_pairs={{0,1},{1,0},{2,3},{3,2},{4,5},{5,4},{6,7},{7,6},{8,9},{9,8},{10,11... | collective-permute-start | bytes 786440 | tf_op jit(solution)/shard_map/ppermute | solution.py:325
  49.7 2.1 %collective-permute-start.12 = (bf16[2,8,8192]{2,1,0:T(8,128)(2,1)S(1)}, bf16[2,8,8192]{2,1,0:T(8,128)(2,1)S(1)}, u32[]{:S(2)}, u32[]{:S(2)}) collective-permute-start(bf16[2,8,8192]{2,1,0:T(8,128)(2,1)S(1)} %collective-permute-done.8.refs_6_), channel_id=1, source_target_pairs={{0,1},{1,0},{2,3},{3,2},{4,5},{5,4},{6,7},{7,6},{8,9},{9,8},{10,11... | collective-permute-start | bytes 786440 | tf_op jit(solution)/shard_map/ppermute | solution.py:325
  49.8 2.4 %collective-permute-start.13 = (bf16[2,8,8192]{2,1,0:T(8,128)(2,1)S(1)}, bf16[2,8,8192]{2,1,0:T(8,128)(2,1)S(1)}, u32[]{:S(2)}, u32[]{:S(2)}) collective-permute-start(bf16[2,8,8192]{2,1,0:T(8,128)(2,1)S(1)} %collective-permute-done.9.refs_7_), channel_id=1, source_target_pairs={{0,1},{1,0},{2,3},{3,2},{4,5},{5,4},{6,7},{7,6},{8,9},{9,8},{10,11... | collective-permute-start | bytes 786440 | tf_op jit(solution)/shard_map/ppermute | solution.py:325
  50.3 15.5 %copy-start.9 = (bf16[1,768,1024]{2,1,0:T(8,128)(2,1)S(1)}, bf16[1,768,1024]{2,1,0:T(8,128)(2,1)}, u32[]{:S(2)}) copy-start(bf16[1,768,1024]{2,1,0:T(8,128)(2,1)} %param.24) | copy-start | bytes 4718596
  53.5 6.2 %collective-permute-start.14 = (bf16[16,8,256]{2,1,0:T(8,128)(2,1)S(1)}, bf16[16,8,256]{2,1,0:T(8,128)(2,1)S(1)}, u32[]{:S(2)}, u32[]{:S(2)}) collective-permute-start(bf16[16,8,256]{2,1,0:T(8,128)(2,1)S(1)} %get-tuple-element.43), channel_id=1, source_target_pairs={{0,8},{1,9},{2,10},{3,11},{4,12},{5,13},{6,14},{7,15},{8,0},{9,1},... | collective-permute-start | bytes 196616 | tf_op jit(solution)/shard_map/ppermute | solution.py:325
  56.2 4.9 %collective-permute-start.19 = (bf16[16,8,256]{2,1,0:T(8,128)(2,1)S(1)}, bf16[16,8,256]{2,1,0:T(8,128)(2,1)S(1)}, u32[]{:S(2)}, u32[]{:S(2)}) collective-permute-start(bf16[16,8,256]{2,1,0:T(8,128)(2,1)S(1)} %get-tuple-element.45), channel_id=1, source_target_pairs={{0,2},{1,3},{2,0},{3,1},{4,6},{5,7},{6,4},{7,5},{8,10},{9,11},{10,... | collective-permute-start | bytes 196616 | tf_op jit(solution)/shard_map/ppermute | solution.py:325
  57.7 6.3 %collective-permute-start.15 = (bf16[16,8,256]{2,1,0:T(8,128)(2,1)S(1)}, bf16[16,8,256]{2,1,0:T(8,128)(2,1)S(1)}, u32[]{:S(2)}, u32[]{:S(2)}) collective-permute-start(bf16[16,8,256]{2,1,0:T(8,128)(2,1)S(1)} %get-tuple-element.43), channel_id=1, source_target_pairs={{0,4},{1,5},{2,6},{3,7},{4,0},{5,1},{6,2},{7,3},{8,12},{9,13},{10,... | collective-permute-start | bytes 196616 | tf_op jit(solution)/shard_map/ppermute | solution.py:325
  59.8 4.3 %collective-permute-start.16 = (bf16[16,8,256]{2,1,0:T(8,128)(2,1)S(1)}, bf16[16,8,256]{2,1,0:T(8,128)(2,1)S(1)}, u32[]{:S(2)}, u32[]{:S(2)}) collective-permute-start(bf16[16,8,256]{2,1,0:T(8,128)(2,1)S(1)} %collective-permute-done.14), channel_id=1, source_target_pairs={{0,4},{1,5},{2,6},{3,7},{4,0},{5,1},{6,2},{7,3},{8,12},{9,13},{10,... | collective-permute-start | bytes 196616 | tf_op jit(solution)/shard_map/ppermute | solution.py:325
  61.1 15.2 %collective-permute-start.24 = (bf16[2,16,8,256]{3,2,1,0:T(8,128)(2,1)S(1)}, bf16[2,16,8,256]{3,2,1,0:T(8,128)(2,1)S(1)}, u32[]{:S(2)}, u32[]{:S(2)}) collective-permute-start(bf16[2,16,8,256]{3,2,1,0:T(8,128)(2,1)S(1)} %pad_maximum_fusion.4.refs_4_), channel_id=1, source_target_pairs={{0,1},{1,0},{2,3},{3,2},{4,5},{5,4},{6,7},{7,6},{8,9},{9,8},{10,11... | collective-permute-start | bytes 393224 | tf_op jit(solution)/shard_map/ppermute | solution.py:325
  61.2 13.5 %collective-permute-start.22 = (bf16[2,16,8,256]{3,2,1,0:T(8,128)(2,1)S(1)}, bf16[2,16,8,256]{3,2,1,0:T(8,128)(2,1)S(1)}, u32[]{:S(2)}, u32[]{:S(2)}) collective-permute-start(bf16[2,16,8,256]{3,2,1,0:T(8,128)(2,1)S(1)} %pad_maximum_fusion.4.refs_4_), channel_id=1, source_target_pairs={{0,4},{1,5},{2,6},{3,7},{4,0},{5,1},{6,2},{7,3},{8,12},{9,13},{10,... | collective-permute-start | bytes 393224 | tf_op jit(solution)/shard_map/ppermute | solution.py:325
  62.0 9.3 %collective-permute-start.20 = (bf16[2,16,8,256]{3,2,1,0:T(8,128)(2,1)S(1)}, bf16[2,16,8,256]{3,2,1,0:T(8,128)(2,1)S(1)}, u32[]{:S(2)}, u32[]{:S(2)}) collective-permute-start(bf16[2,16,8,256]{3,2,1,0:T(8,128)(2,1)S(1)} %pad_maximum_fusion.4.refs_4_), channel_id=1, source_target_pairs={{0,8},{1,9},{2,10},{3,11},{4,12},{5,13},{6,14},{7,15},{8,0},{9,1},... | collective-permute-start | bytes 393224 | tf_op jit(solution)/shard_map/ppermute | solution.py:325
  64.1 13.6 %collective-permute-start.18 = (bf16[4,16,8,256]{3,2,1,0:T(8,128)(2,1)S(1)}, bf16[4,16,8,256]{3,2,1,0:T(8,128)(2,1)S(1)}, u32[]{:S(2)}, u32[]{:S(2)}) collective-permute-start(bf16[4,16,8,256]{3,2,1,0:T(8,128)(2,1)S(1)} %pad_maximum_fusion.2.refs_0_), channel_id=1, source_target_pairs={{0,1},{1,0},{2,3},{3,2},{4,5},{5,4},{6,7},{7,6},{8,9},{9,8},{10,11... | collective-permute-start | bytes 786440 | tf_op jit(solution)/shard_map/ppermute | solution.py:325
  64.2 10.4 %collective-permute-start.17 = (bf16[4,16,8,256]{3,2,1,0:T(8,128)(2,1)S(1)}, bf16[4,16,8,256]{3,2,1,0:T(8,128)(2,1)S(1)}, u32[]{:S(2)}, u32[]{:S(2)}) collective-permute-start(bf16[4,16,8,256]{3,2,1,0:T(8,128)(2,1)S(1)} %pad_maximum_fusion.2.refs_0_), channel_id=1, source_target_pairs={{0,2},{1,3},{2,0},{3,1},{4,6},{5,7},{6,4},{7,5},{8,10},{9,11},{10,... | collective-permute-start | bytes 786440 | tf_op jit(solution)/shard_map/ppermute | solution.py:325
  70.6 7.2 %copy-start.1 = (bf16[4096,16]{0,1:T(8,128)(2,1)S(1)}, bf16[4096,16]{0,1:T(8,128)(2,1)}, u32[]{:S(2)}) copy-start(bf16[4096,16]{0,1:T(8,128)(2,1)} %param.21) | copy-start | bytes 393220
  70.6 7.2 %copy-start.2 = (f32[4096]{0:T(1024)S(1)}, f32[4096]{0:T(1024)}, u32[]{:S(2)}) copy-start(f32[4096]{0:T(1024)} %param.20) | copy-start | bytes 49156
  70.6 7.2 %copy-start.3 = (f32[1,4096]{1,0:T(1,128)S(1)}, f32[1,4096]{1,0:T(1,128)}, u32[]{:S(2)}) copy-start(f32[1,4096]{1,0:T(1,128)} %refs_18_.1) | copy-start | bytes 49156
  70.6 7.2 %copy-start.4 = (f32[1,2,768]{2,1,0:T(2,128)S(1)}, f32[1,2,768]{2,1,0:T(2,128)}, u32[]{:S(2)}) copy-start(f32[1,2,768]{2,1,0:T(2,128)} %param.26) | copy-start | bytes 18436
  71.3 5.0 %collective-permute-start.23 = (bf16[2,16,8,256]{3,2,1,0:T(8,128)(2,1)S(1)}, bf16[2,16,8,256]{3,2,1,0:T(8,128)(2,1)S(1)}, u32[]{:S(2)}, u32[]{:S(2)}) collective-permute-start(bf16[2,16,8,256]{3,2,1,0:T(8,128)(2,1)S(1)} %collective-permute-done.20.refs_5_), channel_id=1, source_target_pairs={{0,4},{1,5},{2,6},{3,7},{4,0},{5,1},{6,2},{7,3},{8,12},{9,13},{10,... | collective-permute-start | bytes 393224 | tf_op jit(solution)/shard_map/ppermute | solution.py:325
  74.6 3.2 %collective-permute-start.21 = (bf16[4,16,8,256]{3,2,1,0:T(8,128)(2,1)S(1)}, bf16[4,16,8,256]{3,2,1,0:T(8,128)(2,1)S(1)}, u32[]{:S(2)}, u32[]{:S(2)}) collective-permute-start(bf16[4,16,8,256]{3,2,1,0:T(8,128)(2,1)S(1)} %collective-permute-done.17.refs_1_), channel_id=1, source_target_pairs={{0,1},{1,0},{2,3},{3,2},{4,5},{5,4},{6,7},{7,6},{8,9},{9,8},{10,11... | collective-permute-start | bytes 786440 | tf_op jit(solution)/shard_map/ppermute | solution.py:325
  74.7 2.1 %collective-permute-start.25 = (bf16[2,16,8,256]{3,2,1,0:T(8,128)(2,1)S(1)}, bf16[2,16,8,256]{3,2,1,0:T(8,128)(2,1)S(1)}, u32[]{:S(2)}, u32[]{:S(2)}) collective-permute-start(bf16[2,16,8,256]{3,2,1,0:T(8,128)(2,1)S(1)} %collective-permute-done.20.refs_5_), channel_id=1, source_target_pairs={{0,1},{1,0},{2,3},{3,2},{4,5},{5,4},{6,7},{7,6},{8,9},{9,8},{10,11... | collective-permute-start | bytes 393224 | tf_op jit(solution)/shard_map/ppermute | solution.py:325
  76.3 1.3 %collective-permute-start.26 = (bf16[2,16,8,256]{3,2,1,0:T(8,128)(2,1)S(1)}, bf16[2,16,8,256]{3,2,1,0:T(8,128)(2,1)S(1)}, u32[]{:S(2)}, u32[]{:S(2)}) collective-permute-start(bf16[2,16,8,256]{3,2,1,0:T(8,128)(2,1)S(1)} %collective-permute-done.22.refs_6_), channel_id=1, source_target_pairs={{0,1},{1,0},{2,3},{3,2},{4,5},{5,4},{6,7},{7,6},{8,9},{9,8},{10,11... | collective-permute-start | bytes 393224 | tf_op jit(solution)/shard_map/ppermute | solution.py:325
  76.3 1.5 %collective-permute-start.27 = (bf16[2,16,8,256]{3,2,1,0:T(8,128)(2,1)S(1)}, bf16[2,16,8,256]{3,2,1,0:T(8,128)(2,1)S(1)}, u32[]{:S(2)}, u32[]{:S(2)}) collective-permute-start(bf16[2,16,8,256]{3,2,1,0:T(8,128)(2,1)S(1)} %collective-permute-done.23.refs_7_), channel_id=1, source_target_pairs={{0,1},{1,0},{2,3},{3,2},{4,5},{5,4},{6,7},{7,6},{8,9},{9,8},{10,11... | collective-permute-start | bytes 393224 | tf_op jit(solution)/shard_map/ppermute | solution.py:325
  85.4 2.0 %collective-permute-start.28 = (bf16[8,8,4096]{2,1,0:T(8,128)(2,1)S(1)}, bf16[8,8,4096]{2,1,0:T(8,128)(2,1)S(1)}, u32[]{:S(2)}, u32[]{:S(2)}) collective-permute-start(bf16[8,8,4096]{2,1,0:T(8,128)(2,1)S(1)} %get-tuple-element.55), channel_id=1, source_target_pairs={{0,1},{1,0},{2,3},{3,2},{4,5},{5,4},{6,7},{7,6},{8,9},{9,8},{10,11... | collective-permute-start | bytes 1572872 | tf_op jit(solution)/shard_map/ppermute | solution.py:325
  85.8 3.2 %collective-permute-start.32 = (bf16[8,8,4096]{2,1,0:T(8,128)(2,1)S(1)}, bf16[8,8,4096]{2,1,0:T(8,128)(2,1)S(1)}, u32[]{:S(2)}, u32[]{:S(2)}) collective-permute-start(bf16[8,8,4096]{2,1,0:T(8,128)(2,1)S(1)} %get-tuple-element.58), channel_id=1, source_target_pairs={{0,1},{1,0},{2,3},{3,2},{4,5},{5,4},{6,7},{7,6},{8,9},{9,8},{10,11... | collective-permute-start | bytes 1572872 | tf_op jit(solution)/shard_map/ppermute | solution.py:325
  87.5 8.6 %collective-permute-start.29 = (bf16[4,8,4096]{2,1,0:T(8,128)(2,1)S(1)}, bf16[4,8,4096]{2,1,0:T(8,128)(2,1)S(1)}, u32[]{:S(2)}, u32[]{:S(2)}) collective-permute-start(bf16[4,8,4096]{2,1,0:T(8,128)(2,1)S(1)} %get-tuple-element.60), channel_id=1, source_target_pairs={{0,2},{1,3},{2,0},{3,1},{4,6},{5,7},{6,4},{7,5},{8,10},{9,11},{10,... | collective-permute-start | bytes 786440 | tf_op jit(solution)/shard_map/ppermute | solution.py:325
  89.2 8.5 %collective-permute-start.33 = (bf16[4,8,4096]{2,1,0:T(8,128)(2,1)S(1)}, bf16[4,8,4096]{2,1,0:T(8,128)(2,1)S(1)}, u32[]{:S(2)}, u32[]{:S(2)}) collective-permute-start(bf16[4,8,4096]{2,1,0:T(8,128)(2,1)S(1)} %get-tuple-element.62), channel_id=1, source_target_pairs={{0,4},{1,5},{2,6},{3,7},{4,0},{5,1},{6,2},{7,3},{8,12},{9,13},{10,... | collective-permute-start | bytes 786440 | tf_op jit(solution)/shard_map/ppermute | solution.py:325
  96.2 6.8 %collective-permute-start.30 = (bf16[2,8,4096]{2,1,0:T(8,128)(2,1)S(1)}, bf16[2,8,4096]{2,1,0:T(8,128)(2,1)S(1)}, u32[]{:S(2)}, u32[]{:S(2)}) collective-permute-start(bf16[2,8,4096]{2,1,0:T(8,128)(2,1)S(1)} %get-tuple-element.64), channel_id=1, source_target_pairs={{0,4},{1,5},{2,6},{3,7},{4,0},{5,1},{6,2},{7,3},{8,12},{9,13},{10,... | collective-permute-start | bytes 393224 | tf_op jit(solution)/shard_map/ppermute | solution.py:325
  97.8 10.6 %collective-permute-start.34 = (bf16[2,8,4096]{2,1,0:T(8,128)(2,1)S(1)}, bf16[2,8,4096]{2,1,0:T(8,128)(2,1)S(1)}, u32[]{:S(2)}, u32[]{:S(2)}) collective-permute-start(bf16[2,8,4096]{2,1,0:T(8,128)(2,1)S(1)} %get-tuple-element.66), channel_id=1, source_target_pairs={{0,8},{1,9},{2,10},{3,11},{4,12},{5,13},{6,14},{7,15},{8,0},{9,1},... | collective-permute-start | bytes 393224 | tf_op jit(solution)/shard_map/ppermute | solution.py:325
  103.0 6.2 %collective-permute-start.31 = (bf16[1,8,4096]{2,1,0:T(8,128)(2,1)S(1)}, bf16[1,8,4096]{2,1,0:T(8,128)(2,1)S(1)}, u32[]{:S(2)}, u32[]{:S(2)}) collective-permute-start(bf16[1,8,4096]{2,1,0:T(8,128)(2,1)S(1)} %add_convert_fusion.10), channel_id=1, source_target_pairs={{0,8},{1,9},{2,10},{3,11},{4,12},{5,13},{6,14},{7,15},{8,0},{9,1},... | collective-permute-start | bytes 196616 | tf_op jit(solution)/shard_map/ppermute | solution.py:325
  108.4 4.3 %collective-permute-start.35 = (bf16[1,8,4096]{2,1,0:T(8,128)(2,1)S(1)}, bf16[1,8,4096]{2,1,0:T(8,128)(2,1)S(1)}, u32[]{:S(2)}, u32[]{:S(2)}) collective-permute-start(bf16[1,8,4096]{2,1,0:T(8,128)(2,1)S(1)} %add_convert_fusion.8), channel_id=1, source_target_pairs={{0,2},{1,3},{2,0},{3,1},{4,6},{5,7},{6,4},{7,5},{8,10},{9,11},{10,... | collective-permute-start | bytes 196616 | tf_op jit(solution)/shard_map/ppermute | solution.py:325

commit v8 on v7

--- a/solution.py
+++ b/solution.py
@@ -70,7 +70,7 @@
 def attend(queries, kv_cache, lengths, micro):
     _, rows, width = queries.shape
     heads = width // HEAD_DIM
-    span = 4 if rows % 4 == 0 else 1
+    span = rows
     kv_shape = kv_cache.shape[2:]
     return pl.pallas_call(
         functools.partial(attend_kernel, micro, span, KV_HEADS),
@@ -86,7 +86,7 @@
         ),
         out_shape=jax.ShapeDtypeStruct((rows, width), jnp.bfloat16),
         name="attend",
-        compiler_params=pltpu.CompilerParams(vmem_limit_bytes=8 * MIB),
+        compiler_params=pltpu.CompilerParams(vmem_limit_bytes=12 * MIB),
         cost_estimate=pl.CostEstimate(
             flops=rows * width * 4 * 256, bytes_accessed=rows << 18, transcendentals=0
         ),

time: 114 us -> 114 us (level)
  transfers between devices with their start and end apart: 37 -> 37, of which waited for: 16 -> 15; matrix products, arithmetic and copies ran while one was open for 1% -> 1% of each run, Pallas kernels for 23% -> 23%
where the time goes in v8:
time: 114 us; the launch traced here: 113 us
  starting transfers between devices  41.2 us (36%)
  Pallas kernels  38.4 us (34%)
  waiting for transfers between devices  30.4 us (27%)
  local copies, waits for them, and re-layouts  1.54 us (1%)
  other arithmetic  1.46 us (1%)
    ppermute x36, starting transfers between devices, swap(): return lax.ppermute(value, 'expert', [(i, i ^ bit) for i in range(count)])  37.5 us
    ppermute x36, waiting for transfers between devices, swap(): return lax.ppermute(value, 'expert', [(i, i ^ bit) for i in range(count)])  30.4 us
    pallas_call x4, Pallas kernels, expand(): pl.pallas_call(functools.partial(expand_kernel, stacked, skip), in_specs=...  21.5 us
    pallas_call x2, Pallas kernels, attend(): pl.pallas_call(functools.partial(attend_kernel, micro, span, KV_HEADS), g...  8.11 us
    pallas_call x1, Pallas kernels, run_experts(): pl.pallas_call(functools.partial(experts_kernel, masks, counts, orders, l...  7.53 us
    all_to_all x1, starting transfers between devices, body(): lax.all_to_all(jnp.concatenate([lead, tail], axis=-1), 'expert', split_ax...  3.7 us
  transfers between devices with their start and end apart: 37, of which 15 were waited for; matrix products, arithmetic and copies ran while one was open for 1% of the time, Pallas kernels for 23%

profile of v8, /device:TPU:0, one launch (start us, length us, event | category | flops | bytes accessed | tf_op | source)
XLA Modules:
  0.0 113.4 jit_solution(4596176703983510977)
XLA Ops:
  0.0 0.7 copy-done.5
  0.7 4.1 %attend.2 = bf16[8,8192]{1,0:T(8,128)(2,1)S(1)} custom-call(s32[2,8]{1,0:T(2,128)S(1)} %copy-done.5, bf16[2,8,8192]{2,1,0:T(8,128)(2,1)} %q_ref.3, bf16[2,8,128,2,512]{4,3,2,1,0:T(2,128)(2,1)} %kv_ref.3), custom_call_target="tpu_custom_call" | custom-call | flops 67108864 | bytes 2097152 | tf_op jit(solution)/shard_map/attend/pallas_call | solution.py:75
  4.8 3.1 %collective-permute-start.1 = (bf16[8,8192]{1,0:T(8,128)(2,1)S(1)}, bf16[8,8192]{1,0:T(8,128)(2,1)S(1)}, u32[]{:S(2)}, u32[]{:S(2)}) collective-permute-start(bf16[8,8192]{1,0:T(8,128)(2,1)S(1)} %attend.2), channel_id=1, source_target_pairs={{0,4},{1,5},{2,6},{3,7},{4,0},{5,1},{6,2},{7,3},{8,12},{9,13},{10,... | collective-permute-start | bytes 393224 | tf_op jit(solution)/shard_map/ppermute | solution.py:325
  7.9 2.6 %collective-permute-start = (bf16[8,8192]{1,0:T(8,128)(2,1)S(1)}, bf16[8,8192]{1,0:T(8,128)(2,1)S(1)}, u32[]{:S(2)}, u32[]{:S(2)}) collective-permute-start(bf16[8,8192]{1,0:T(8,128)(2,1)S(1)} %attend.2), channel_id=1, source_target_pairs={{0,8},{1,9},{2,10},{3,11},{4,12},{5,13},{6,14},{7,15},{8,0},{9,1},... | collective-permute-start | bytes 393224 | tf_op jit(solution)/shard_map/ppermute | solution.py:325
  10.5 0.1 fusion.4
  10.7 0.7 copy.19
  11.4 3.7 %all-to-all-start = ((bf16[16,2,8,272]{3,2,1,0:T(8,128)(2,1)}), bf16[16,2,8,272]{3,2,1,0:T(8,128)(2,1)S(1)}, u32[]{:S(2)}, u32[]{:S(2)}) async-start(bf16[16,2,8,272]{3,2,1,0:T(8,128)(2,1)} %copy.19), calls=%async_computation | async-start | bytes 393216 | tf_op jit(solution)/shard_map/all_to_all | solution.py:409
  15.1 4.1 %attend.3 = bf16[8,8192]{1,0:T(8,128)(2,1)S(1)} custom-call(s32[2,8]{1,0:T(2,128)S(1)} %copy-done.6, bf16[2,8,8192]{2,1,0:T(8,128)(2,1)} %q_ref.3, bf16[2,8,128,2,512]{4,3,2,1,0:T(2,128)(2,1)} %kv_ref.3), custom_call_target="tpu_custom_call" | custom-call | flops 67108864 | bytes 2097152 | tf_op jit(solution)/shard_map/attend/pallas_call | solution.py:75
  19.2 1.7 %collective-permute-start.5 = (bf16[8,8192]{1,0:T(8,128)(2,1)S(1)}, bf16[8,8192]{1,0:T(8,128)(2,1)S(1)}, u32[]{:S(2)}, u32[]{:S(2)}) collective-permute-start(bf16[8,8192]{1,0:T(8,128)(2,1)S(1)} %attend.3), channel_id=1, source_target_pairs={{0,2},{1,3},{2,0},{3,1},{4,6},{5,7},{6,4},{7,5},{8,10},{9,11},{10,... | collective-permute-start | bytes 393224 | tf_op jit(solution)/shard_map/ppermute | solution.py:325
  20.9 1.6 %collective-permute-start.2 = (bf16[8,8192]{1,0:T(8,128)(2,1)S(1)}, bf16[8,8192]{1,0:T(8,128)(2,1)S(1)}, u32[]{:S(2)}, u32[]{:S(2)}) collective-permute-start(bf16[8,8192]{1,0:T(8,128)(2,1)S(1)} %collective-permute-done), channel_id=1, source_target_pairs={{0,4},{1,5},{2,6},{3,7},{4,0},{5,1},{6,2},{7,3},{8,12},{9,13},{10,... | collective-permute-start | bytes 393224 | tf_op jit(solution)/shard_map/ppermute | solution.py:325
  22.5 2.8 %collective-permute-done.5 = bf16[8,8192]{1,0:T(8,128)(2,1)S(1)} collective-permute-done((bf16[8,8192]{1,0:T(8,128)(2,1)S(1)}, bf16[8,8192]{1,0:T(8,128)(2,1)S(1)}, u32[]{:S(2)}, u32[]{:S(2)}) %collective-permute-start.5) | collective-permute-done | bytes 131104 | tf_op jit(solution)/shard_map/ppermute | solution.py:325
  25.3 0.1 collective-permute-start.10
  25.4 1.5 %collective-permute-start.8 = (bf16[2,8,8192]{2,1,0:T(8,128)(2,1)S(1)}, bf16[2,8,8192]{2,1,0:T(8,128)(2,1)S(1)}, u32[]{:S(2)}, u32[]{:S(2)}) collective-permute-start(bf16[2,8,8192]{2,1,0:T(8,128)(2,1)S(1)} %pad_maximum_fusion.1.refs_4_), channel_id=1, source_target_pairs={{0,4},{1,5},{2,6},{3,7},{4,0},{5,1},{6,2},{7,3},{8,12},{9,13},{10,... | collective-permute-start | bytes 786440 | tf_op jit(solution)/shard_map/ppermute | solution.py:325
  26.8 2.2 %collective-permute-start.6 = (bf16[2,8,8192]{2,1,0:T(8,128)(2,1)S(1)}, bf16[2,8,8192]{2,1,0:T(8,128)(2,1)S(1)}, u32[]{:S(2)}, u32[]{:S(2)}) collective-permute-start(bf16[2,8,8192]{2,1,0:T(8,128)(2,1)S(1)} %pad_maximum_fusion.1.refs_4_), channel_id=1, source_target_pairs={{0,8},{1,9},{2,10},{3,11},{4,12},{5,13},{6,14},{7,15},{8,0},{9,1},... | collective-permute-start | bytes 786440 | tf_op jit(solution)/shard_map/ppermute | solution.py:325
  29.1 0.1 collective-permute-start.4
  29.2 1.5 %collective-permute-start.3 = (bf16[4,8,8192]{2,1,0:T(8,128)(2,1)S(1)}, bf16[4,8,8192]{2,1,0:T(8,128)(2,1)S(1)}, u32[]{:S(2)}, u32[]{:S(2)}) collective-permute-start(bf16[4,8,8192]{2,1,0:T(8,128)(2,1)S(1)} %pad_maximum_fusion.refs_0_), channel_id=1, source_target_pairs={{0,2},{1,3},{2,0},{3,1},{4,6},{5,7},{6,4},{7,5},{8,10},{9,11},{10,... | collective-permute-start | bytes 1572872 | tf_op jit(solution)/shard_map/ppermute | solution.py:325
  30.7 7.2 %expand.4 = bf16[4,192,4096]{2,1,0:T(8,128)(2,1)S(1)} custom-call(f32[8,128]{1,0:T(8,128)S(1)} %squeeze.27.table_ref, bf16[192,4096]{1,0:T(8,128)(2,1)S(1)} %bitcast.66), custom_call_target="tpu_custom_call" | custom-call | flops 6291456000 | bytes 7864320 | tf_op jit(solution)/shard_map/expand/pallas_call | solution.py:143
  37.9 3.9 %collective-permute-done.6.refs_5_ = bf16[2,8,8192]{2,1,0:T(8,128)(2,1)S(1)} collective-permute-done((bf16[2,8,8192]{2,1,0:T(8,128)(2,1)S(1)}, bf16[2,8,8192]{2,1,0:T(8,128)(2,1)S(1)}, u32[]{:S(2)}, u32[]{:S(2)}) %collective-permute-start.6) | collective-permute-done | bytes 262176 | tf_op jit(solution)/shard_map/ppermute | solution.py:325
  41.8 0.1 collective-permute-start.9
  41.9 7.2 %expand.5 = bf16[4,192,4096]{2,1,0:T(8,128)(2,1)S(1)} custom-call(f32[8,128]{1,0:T(8,128)S(1)} %squeeze.28.table_ref, bf16[192,4096]{1,0:T(8,128)(2,1)S(1)} %bitcast.67), custom_call_target="tpu_custom_call" | custom-call | flops 6291456000 | bytes 7864320 | tf_op jit(solution)/shard_map/expand/pallas_call | solution.py:143
  49.1 0.1 collective-permute-start.7
  49.2 0.5 collective-permute-start.11
  49.6 0.1 collective-permute-start.12
  49.7 0.4 collective-permute-start.13
  50.2 1.2 %collective-permute-done.11.refs_9_ = bf16[2,8,8192]{2,1,0:T(8,128)(2,1)S(1)} collective-permute-done((bf16[2,8,8192]{2,1,0:T(8,128)(2,1)S(1)}, bf16[2,8,8192]{2,1,0:T(8,128)(2,1)S(1)}, u32[]{:S(2)}, u32[]{:S(2)}) %collective-permute-start.11) | collective-permute-done | bytes 262176 | tf_op jit(solution)/shard_map/ppermute | solution.py:325
  51.4 0.4 collective-permute-done.12.refs_10_
  51.8 0.4 collective-permute-done.13.refs_11_
  52.2 1.3 %project.1 = (bf16[16,8,256]{2,1,0:T(8,128)(2,1)S(1)}, bf16[16,8,256]{2,1,0:T(8,128)(2,1)S(1)}) custom-call(s32[1]{0:T(128)} %bitcast.3.me_ref, bf16[4,8,8192]{2,1,0:T(8,128)(2,1)S(1)} %pad_maximum_fusion.refs_0_, bf16[4,8,8192]{2,1,0:T(8,128)(2,1)S(1)} %collective-permute-done.3.refs_1_, bf16[4,8,8192]{2,1,0:T(8,128)(2,1)S(1)} %collective-permute-done.4.refs_2_, ...), custom_call_target="tpu_custom_call" | custom-call | flops 1073741824 | bytes 4194304 | tf_op jit(solution)/shard_map/project/pallas_call | solution.py:190
  53.4 2.7 %collective-permute-start.14 = (bf16[16,8,256]{2,1,0:T(8,128)(2,1)S(1)}, bf16[16,8,256]{2,1,0:T(8,128)(2,1)S(1)}, u32[]{:S(2)}, u32[]{:S(2)}) collective-permute-start(bf16[16,8,256]{2,1,0:T(8,128)(2,1)S(1)} %get-tuple-element.43), channel_id=1, source_target_pairs={{0,8},{1,9},{2,10},{3,11},{4,12},{5,13},{6,14},{7,15},{8,0},{9,1},... | collective-permute-start | bytes 196616 | tf_op jit(solution)/shard_map/ppermute | solution.py:325
  56.1 1.5 %collective-permute-start.19 = (bf16[16,8,256]{2,1,0:T(8,128)(2,1)S(1)}, bf16[16,8,256]{2,1,0:T(8,128)(2,1)S(1)}, u32[]{:S(2)}, u32[]{:S(2)}) collective-permute-start(bf16[16,8,256]{2,1,0:T(8,128)(2,1)S(1)} %get-tuple-element.45), channel_id=1, source_target_pairs={{0,2},{1,3},{2,0},{3,1},{4,6},{5,7},{6,4},{7,5},{8,10},{9,11},{10,... | collective-permute-start | bytes 196616 | tf_op jit(solution)/shard_map/ppermute | solution.py:325
  57.6 2.1 %collective-permute-done.14 = bf16[16,8,256]{2,1,0:T(8,128)(2,1)S(1)} collective-permute-done((bf16[16,8,256]{2,1,0:T(8,128)(2,1)S(1)}, bf16[16,8,256]{2,1,0:T(8,128)(2,1)S(1)}, u32[]{:S(2)}, u32[]{:S(2)}) %collective-permute-start.14) | collective-permute-done | bytes 65568 | tf_op jit(solution)/shard_map/ppermute | solution.py:325
  59.7 1.4 %collective-permute-start.16 = (bf16[16,8,256]{2,1,0:T(8,128)(2,1)S(1)}, bf16[16,8,256]{2,1,0:T(8,128)(2,1)S(1)}, u32[]{:S(2)}, u32[]{:S(2)}) collective-permute-start(bf16[16,8,256]{2,1,0:T(8,128)(2,1)S(1)} %collective-permute-done.14), channel_id=1, source_target_pairs={{0,4},{1,5},{2,6},{3,7},{4,0},{5,1},{6,2},{7,3},{8,12},{9,13},{10,... | collective-permute-start | bytes 196616 | tf_op jit(solution)/shard_map/ppermute | solution.py:325
  61.1 0.1 collective-permute-start.24
  61.2 0.7 collective-permute-start.22
  61.8 2.0 %collective-permute-start.20 = (bf16[2,16,8,256]{3,2,1,0:T(8,128)(2,1)S(1)}, bf16[2,16,8,256]{3,2,1,0:T(8,128)(2,1)S(1)}, u32[]{:S(2)}, u32[]{:S(2)}) collective-permute-start(bf16[2,16,8,256]{3,2,1,0:T(8,128)(2,1)S(1)} %pad_maximum_fusion.4.refs_4_), channel_id=1, source_target_pairs={{0,8},{1,9},{2,10},{3,11},{4,12},{5,13},{6,14},{7,15},{8,0},{9,1},... | collective-permute-start | bytes 393224 | tf_op jit(solution)/shard_map/ppermute | solution.py:325
  64.0 0.1 collective-permute-start.18
  64.0 1.7 %collective-permute-start.17 = (bf16[4,16,8,256]{3,2,1,0:T(8,128)(2,1)S(1)}, bf16[4,16,8,256]{3,2,1,0:T(8,128)(2,1)S(1)}, u32[]{:S(2)}, u32[]{:S(2)}) collective-permute-start(bf16[4,16,8,256]{3,2,1,0:T(8,128)(2,1)S(1)} %pad_maximum_fusion.2.refs_0_), channel_id=1, source_target_pairs={{0,2},{1,3},{2,0},{3,1},{4,6},{5,7},{6,4},{7,5},{8,10},{9,11},{10,... | collective-permute-start | bytes 786440 | tf_op jit(solution)/shard_map/ppermute | solution.py:325
  65.7 4.8 %expand.6.refs_19_ = bf16[512,4096]{1,0:T(8,128)(2,1)S(1)} custom-call(f32[8,128]{1,0:T(8,128)S(1)} %squeeze.29.table_ref, bf16[768,1024]{1,0:T(8,128)(2,1)S(1)} %bitcast.68), custom_call_target="tpu_custom_call" | custom-call | flops 4194304000 | bytes 5242880 | tf_op jit(solution)/shard_map/expand/pallas_call | solution.py:143
  70.6 0.6 collective-permute-done.20.refs_5_
  71.2 1.0 collective-permute-start.23
  72.1 2.4 %expand.7.refs_20_ = bf16[256,4096]{1,0:T(8,128)(2,1)S(1)} custom-call(f32[8,128]{1,0:T(8,128)S(1)} %squeeze.29.table_ref, bf16[768,1024]{1,0:T(8,128)(2,1)S(1)} %bitcast.69), custom_call_target="tpu_custom_call" | custom-call | flops 2097152000 | bytes 2621440 | tf_op jit(solution)/shard_map/expand/pallas_call | solution.py:143
  74.6 0.1 collective-permute-start.21
  74.6 0.5 collective-permute-start.25
  75.1 1.1 collective-permute-done.23.refs_7_
  76.2 0.5 collective-permute-start.27
  76.7 0.8 collective-permute-done.26.refs_10_
  77.6 0.2 collective-permute-done.27.refs_11_
  77.8 7.5 %experts.1 = (bf16[8,8,4096]{2,1,0:T(8,128)(2,1)S(1)}, bf16[8,8,4096]{2,1,0:T(8,128)(2,1)S(1)}, bf16[8,8,4096]{2,1,0:T(8,128)(2,1)S(1)}, bf16[8,8,4096]{2,1,0:T(...) custom-call(s32[1]{0:T(128)} %bitcast.3.me_ref, ...), custom_call_target="tpu_custom_call" | custom-call | flops 4831838208 | bytes 18874368 | tf_op jit(solution)/shard_map/experts/pallas_call | solution.py:306
  85.3 0.4 collective-permute-start.28
  85.7 0.2 collective-permute-start.32
  85.9 1.4 %collective-permute-done.28 = bf16[8,8,4096]{2,1,0:T(8,128)(2,1)S(1)} collective-permute-done((bf16[8,8,4096]{2,1,0:T(8,128)(2,1)S(1)}, bf16[8,8,4096]{2,1,0:T(8,128)(2,1)S(1)}, u32[]{:S(2)}, u32[]{:S(2)}) %collective-permute-start.28) | collective-permute-done | bytes 524320 | tf_op jit(solution)/shard_map/ppermute | solution.py:325
  87.3 0.1 add_convert_fusion.3
  87.4 1.5 %collective-permute-start.29 = (bf16[4,8,4096]{2,1,0:T(8,128)(2,1)S(1)}, bf16[4,8,4096]{2,1,0:T(8,128)(2,1)S(1)}, u32[]{:S(2)}, u32[]{:S(2)}) collective-permute-start(bf16[4,8,4096]{2,1,0:T(8,128)(2,1)S(1)} %get-tuple-element.60), channel_id=1, source_target_pairs={{0,2},{1,3},{2,0},{3,1},{4,6},{5,7},{6,4},{7,5},{8,10},{9,11},{10,... | collective-permute-start | bytes 786440 | tf_op jit(solution)/shard_map/ppermute | solution.py:325
  88.9 0.1 add_convert_fusion.1
  89.1 0.9 collective-permute-start.33
  90.0 6.0 %collective-permute-done.29 = bf16[4,8,4096]{2,1,0:T(8,128)(2,1)S(1)} collective-permute-done((bf16[4,8,4096]{2,1,0:T(8,128)(2,1)S(1)}, bf16[4,8,4096]{2,1,0:T(8,128)(2,1)S(1)}, u32[]{:S(2)}, u32[]{:S(2)}) %collective-permute-start.29) | collective-permute-done | bytes 262176 | tf_op jit(solution)/shard_map/ppermute | solution.py:325
  96.1 1.6 %collective-permute-start.30 = (bf16[2,8,4096]{2,1,0:T(8,128)(2,1)S(1)}, bf16[2,8,4096]{2,1,0:T(8,128)(2,1)S(1)}, u32[]{:S(2)}, u32[]{:S(2)}) collective-permute-start(bf16[2,8,4096]{2,1,0:T(8,128)(2,1)S(1)} %get-tuple-element.64), channel_id=1, source_target_pairs={{0,4},{1,5},{2,6},{3,7},{4,0},{5,1},{6,2},{7,3},{8,12},{9,13},{10,... | collective-permute-start | bytes 393224 | tf_op jit(solution)/shard_map/ppermute | solution.py:325
  97.7 2.0 %collective-permute-start.34 = (bf16[2,8,4096]{2,1,0:T(8,128)(2,1)S(1)}, bf16[2,8,4096]{2,1,0:T(8,128)(2,1)S(1)}, u32[]{:S(2)}, u32[]{:S(2)}) collective-permute-start(bf16[2,8,4096]{2,1,0:T(8,128)(2,1)S(1)} %get-tuple-element.66), channel_id=1, source_target_pairs={{0,8},{1,9},{2,10},{3,11},{4,12},{5,13},{6,14},{7,15},{8,0},{9,1},... | collective-permute-start | bytes 393224 | tf_op jit(solution)/shard_map/ppermute | solution.py:325
  99.7 3.1 %collective-permute-done.30 = bf16[2,8,4096]{2,1,0:T(8,128)(2,1)S(1)} collective-permute-done((bf16[2,8,4096]{2,1,0:T(8,128)(2,1)S(1)}, bf16[2,8,4096]{2,1,0:T(8,128)(2,1)S(1)}, u32[]{:S(2)}, u32[]{:S(2)}) %collective-permute-start.30) | collective-permute-done | bytes 131104 | tf_op jit(solution)/shard_map/ppermute | solution.py:325
  102.8 2.6 %collective-permute-start.31 = (bf16[1,8,4096]{2,1,0:T(8,128)(2,1)S(1)}, bf16[1,8,4096]{2,1,0:T(8,128)(2,1)S(1)}, u32[]{:S(2)}, u32[]{:S(2)}) collective-permute-start(bf16[1,8,4096]{2,1,0:T(8,128)(2,1)S(1)} %add_convert_fusion.10), channel_id=1, source_target_pairs={{0,8},{1,9},{2,10},{3,11},{4,12},{5,13},{6,14},{7,15},{8,0},{9,1},... | collective-permute-start | bytes 196616 | tf_op jit(solution)/shard_map/ppermute | solution.py:325
  105.5 2.9 %collective-permute-done.34 = bf16[2,8,4096]{2,1,0:T(8,128)(2,1)S(1)} collective-permute-done((bf16[2,8,4096]{2,1,0:T(8,128)(2,1)S(1)}, bf16[2,8,4096]{2,1,0:T(8,128)(2,1)S(1)}, u32[]{:S(2)}, u32[]{:S(2)}) %collective-permute-start.34) | collective-permute-done | bytes 131104 | tf_op jit(solution)/shard_map/ppermute | solution.py:325
  108.4 0.8 collective-permute-start.35
  109.2 3.5 %collective-permute-done.35 = bf16[1,8,4096]{2,1,0:T(8,128)(2,1)S(1)} collective-permute-done((bf16[1,8,4096]{2,1,0:T(8,128)(2,1)S(1)}, bf16[1,8,4096]{2,1,0:T(8,128)(2,1)S(1)}, u32[]{:S(2)}, u32[]{:S(2)}) %collective-permute-start.35) | collective-permute-done | bytes 65568 | tf_op jit(solution)/shard_map/ppermute | solution.py:325
  112.7 0.7 pad_maximum_fusion.5
  (70 shorter events, 0.7 us)
Async XLA Ops:
  0.0 0.7 copy-start.5
  0.7 9.8 %copy-start.11 = (s32[2,8,8]{2,1,0:T(8,128)S(1)}, s32[2,8,8]{2,1,0:T(8,128)}, u32[]{:S(2)}) copy-start(s32[2,8,8]{2,1,0:T(8,128)} %param.18) | copy-start | bytes 1540
  0.7 9.9 %copy-start.10 = (bf16[2,8,4096]{2,1,0:T(8,128)(2,1)S(1)}, bf16[2,8,4096]{2,1,0:T(8,128)(2,1)}, u32[]{:S(2)}) copy-start(bf16[2,8,4096]{2,1,0:T(8,128)(2,1)} %param.14) | copy-start | bytes 393220
  0.7 14.4 %copy-start.6 = (s32[2,8]{1,0:T(2,128)S(1)}, s32[2,8]{1,0:T(2,128)}, u32[]{:S(2)}) copy-start(s32[2,8]{1,0:T(2,128)} %len_ref.3) | copy-start | bytes 196
  4.7 16.1 %copy-start.12 = (bf16[1,3,256,4]{2,3,1,0:T(4,128)(2,1)S(1)}, bf16[1,3,256,4]{2,3,1,0:T(4,128)(2,1)}, u32[]{:S(2)}) copy-start(bf16[1,3,256,4]{2,3,1,0:T(4,128)(2,1)} %param.25) | copy-start | bytes 18436
  4.8 26.0 %copy-start.7 = (bf16[1,4096,192]{1,2,0:T(8,128)(2,1)S(1)}, bf16[1,4096,192]{1,2,0:T(8,128)(2,1)}, u32[]{:S(2)}) copy-start(bf16[1,4096,192]{1,2,0:T(8,128)(2,1)} %param.22) | copy-start | bytes 4718596
  4.8 24.2 %collective-permute-start.1 = (bf16[8,8192]{1,0:T(8,128)(2,1)S(1)}, bf16[8,8192]{1,0:T(8,128)(2,1)S(1)}, u32[]{:S(2)}, u32[]{:S(2)}) collective-permute-start(bf16[8,8192]{1,0:T(8,128)(2,1)S(1)} %attend.2), channel_id=1, source_target_pairs={{0,4},{1,5},{2,6},{3,7},{4,0},{5,1},{6,2},{7,3},{8,12},{9,13},{10,... | collective-permute-start | bytes 393224 | tf_op jit(solution)/shard_map/ppermute | solution.py:325
  7.9 13.0 %collective-permute-start = (bf16[8,8192]{1,0:T(8,128)(2,1)S(1)}, bf16[8,8192]{1,0:T(8,128)(2,1)S(1)}, u32[]{:S(2)}, u32[]{:S(2)}) collective-permute-start(bf16[8,8192]{1,0:T(8,128)(2,1)S(1)} %attend.2), channel_id=1, source_target_pairs={{0,8},{1,9},{2,10},{3,11},{4,12},{5,13},{6,14},{7,15},{8,0},{9,1},... | collective-permute-start | bytes 393224 | tf_op jit(solution)/shard_map/ppermute | solution.py:325
  11.4 17.6 %all-to-all-start = ((bf16[16,2,8,272]{3,2,1,0:T(8,128)(2,1)}), bf16[16,2,8,272]{3,2,1,0:T(8,128)(2,1)S(1)}, u32[]{:S(2)}, u32[]{:S(2)}) async-start(bf16[16,2,8,272]{3,2,1,0:T(8,128)(2,1)} %copy.19), calls=%async_computation | async-start | bytes 393216 | tf_op jit(solution)/shard_map/all_to_all | solution.py:409
  19.2 6.1 %collective-permute-start.5 = (bf16[8,8192]{1,0:T(8,128)(2,1)S(1)}, bf16[8,8192]{1,0:T(8,128)(2,1)S(1)}, u32[]{:S(2)}, u32[]{:S(2)}) collective-permute-start(bf16[8,8192]{1,0:T(8,128)(2,1)S(1)} %attend.3), channel_id=1, source_target_pairs={{0,2},{1,3},{2,0},{3,1},{4,6},{5,7},{6,4},{7,5},{8,10},{9,11},{10,... | collective-permute-start | bytes 393224 | tf_op jit(solution)/shard_map/ppermute | solution.py:325
  20.9 8.1 %collective-permute-start.2 = (bf16[8,8192]{1,0:T(8,128)(2,1)S(1)}, bf16[8,8192]{1,0:T(8,128)(2,1)S(1)}, u32[]{:S(2)}, u32[]{:S(2)}) collective-permute-start(bf16[8,8192]{1,0:T(8,128)(2,1)S(1)} %collective-permute-done), channel_id=1, source_target_pairs={{0,4},{1,5},{2,6},{3,7},{4,0},{5,1},{6,2},{7,3},{8,12},{9,13},{10,... | collective-permute-start | bytes 393224 | tf_op jit(solution)/shard_map/ppermute | solution.py:325
  25.3 24.5 %collective-permute-start.10 = (bf16[2,8,8192]{2,1,0:T(8,128)(2,1)S(1)}, bf16[2,8,8192]{2,1,0:T(8,128)(2,1)S(1)}, u32[]{:S(2)}, u32[]{:S(2)}) collective-permute-start(bf16[2,8,8192]{2,1,0:T(8,128)(2,1)S(1)} %pad_maximum_fusion.1.refs_4_), channel_id=1, source_target_pairs={{0,1},{1,0},{2,3},{3,2},{4,5},{5,4},{6,7},{7,6},{8,9},{9,8},{10,11... | collective-permute-start | bytes 786440 | tf_op jit(solution)/shard_map/ppermute | solution.py:325
  25.4 23.8 %collective-permute-start.8 = (bf16[2,8,8192]{2,1,0:T(8,128)(2,1)S(1)}, bf16[2,8,8192]{2,1,0:T(8,128)(2,1)S(1)}, u32[]{:S(2)}, u32[]{:S(2)}) collective-permute-start(bf16[2,8,8192]{2,1,0:T(8,128)(2,1)S(1)} %pad_maximum_fusion.1.refs_4_), channel_id=1, source_target_pairs={{0,4},{1,5},{2,6},{3,7},{4,0},{5,1},{6,2},{7,3},{8,12},{9,13},{10,... | collective-permute-start | bytes 786440 | tf_op jit(solution)/shard_map/ppermute | solution.py:325
  26.8 14.9 %collective-permute-start.6 = (bf16[2,8,8192]{2,1,0:T(8,128)(2,1)S(1)}, bf16[2,8,8192]{2,1,0:T(8,128)(2,1)S(1)}, u32[]{:S(2)}, u32[]{:S(2)}) collective-permute-start(bf16[2,8,8192]{2,1,0:T(8,128)(2,1)S(1)} %pad_maximum_fusion.1.refs_4_), channel_id=1, source_target_pairs={{0,8},{1,9},{2,10},{3,11},{4,12},{5,13},{6,14},{7,15},{8,0},{9,1},... | collective-permute-start | bytes 786440 | tf_op jit(solution)/shard_map/ppermute | solution.py:325
  29.1 22.7 %collective-permute-start.4 = (bf16[4,8,8192]{2,1,0:T(8,128)(2,1)S(1)}, bf16[4,8,8192]{2,1,0:T(8,128)(2,1)S(1)}, u32[]{:S(2)}, u32[]{:S(2)}) collective-permute-start(bf16[4,8,8192]{2,1,0:T(8,128)(2,1)S(1)} %pad_maximum_fusion.refs_0_), channel_id=1, source_target_pairs={{0,1},{1,0},{2,3},{3,2},{4,5},{5,4},{6,7},{7,6},{8,9},{9,8},{10,11... | collective-permute-start | bytes 1572872 | tf_op jit(solution)/shard_map/ppermute | solution.py:325
  29.2 19.9 %collective-permute-start.3 = (bf16[4,8,8192]{2,1,0:T(8,128)(2,1)S(1)}, bf16[4,8,8192]{2,1,0:T(8,128)(2,1)S(1)}, u32[]{:S(2)}, u32[]{:S(2)}) collective-permute-start(bf16[4,8,8192]{2,1,0:T(8,128)(2,1)S(1)} %pad_maximum_fusion.refs_0_), channel_id=1, source_target_pairs={{0,2},{1,3},{2,0},{3,1},{4,6},{5,7},{6,4},{7,5},{8,10},{9,11},{10,... | collective-permute-start | bytes 1572872 | tf_op jit(solution)/shard_map/ppermute | solution.py:325
  30.7 11.2 %copy-start.8 = (bf16[1,4096,192]{1,2,0:T(8,128)(2,1)S(1)}, bf16[1,4096,192]{1,2,0:T(8,128)(2,1)}, u32[]{:S(2)}) copy-start(bf16[1,4096,192]{1,2,0:T(8,128)(2,1)} %param.23) | copy-start | bytes 4718596
  41.8 7.9 %collective-permute-start.9 = (bf16[2,8,8192]{2,1,0:T(8,128)(2,1)S(1)}, bf16[2,8,8192]{2,1,0:T(8,128)(2,1)S(1)}, u32[]{:S(2)}, u32[]{:S(2)}) collective-permute-start(bf16[2,8,8192]{2,1,0:T(8,128)(2,1)S(1)} %collective-permute-done.6.refs_5_), channel_id=1, source_target_pairs={{0,4},{1,5},{2,6},{3,7},{4,0},{5,1},{6,2},{7,3},{8,12},{9,13},{10,... | collective-permute-start | bytes 786440 | tf_op jit(solution)/shard_map/ppermute | solution.py:325
  41.9 10.3 %copy-start = (bf16[8192,256]{1,0:T(8,128)(2,1)S(1)}, bf16[8192,256]{1,0:T(8,128)(2,1)}, u32[]{:S(2)}) copy-start(bf16[8192,256]{1,0:T(8,128)(2,1)} %refs_12_.1) | copy-start | bytes 12582916
  49.1 3.1 %collective-permute-start.7 = (bf16[4,8,8192]{2,1,0:T(8,128)(2,1)S(1)}, bf16[4,8,8192]{2,1,0:T(8,128)(2,1)S(1)}, u32[]{:S(2)}, u32[]{:S(2)}) collective-permute-start(bf16[4,8,8192]{2,1,0:T(8,128)(2,1)S(1)} %collective-permute-done.3.refs_1_), channel_id=1, source_target_pairs={{0,1},{1,0},{2,3},{3,2},{4,5},{5,4},{6,7},{7,6},{8,9},{9,8},{10,11... | collective-permute-start | bytes 1572872 | tf_op jit(solution)/shard_map/ppermute | solution.py:325
  49.2 2.3 %collective-permute-start.11 = (bf16[2,8,8192]{2,1,0:T(8,128)(2,1)S(1)}, bf16[2,8,8192]{2,1,0:T(8,128)(2,1)S(1)}, u32[]{:S(2)}, u32[]{:S(2)}) collective-permute-start(bf16[2,8,8192]{2,1,0:T(8,128)(2,1)S(1)} %collective-permute-done.6.refs_5_), channel_id=1, source_target_pairs={{0,1},{1,0},{2,3},{3,2},{4,5},{5,4},{6,7},{7,6},{8,9},{9,8},{10,11... | collective-permute-start | bytes 786440 | tf_op jit(solution)/shard_map/ppermute | solution.py:325
  49.6 2.1 %collective-permute-start.12 = (bf16[2,8,8192]{2,1,0:T(8,128)(2,1)S(1)}, bf16[2,8,8192]{2,1,0:T(8,128)(2,1)S(1)}, u32[]{:S(2)}, u32[]{:S(2)}) collective-permute-start(bf16[2,8,8192]{2,1,0:T(8,128)(2,1)S(1)} %collective-permute-done.8.refs_6_), channel_id=1, source_target_pairs={{0,1},{1,0},{2,3},{3,2},{4,5},{5,4},{6,7},{7,6},{8,9},{9,8},{10,11... | collective-permute-start | bytes 786440 | tf_op jit(solution)/shard_map/ppermute | solution.py:325
  49.7 2.4 %collective-permute-start.13 = (bf16[2,8,8192]{2,1,0:T(8,128)(2,1)S(1)}, bf16[2,8,8192]{2,1,0:T(8,128)(2,1)S(1)}, u32[]{:S(2)}, u32[]{:S(2)}) collective-permute-start(bf16[2,8,8192]{2,1,0:T(8,128)(2,1)S(1)} %collective-permute-done.9.refs_7_), channel_id=1, source_target_pairs={{0,1},{1,0},{2,3},{3,2},{4,5},{5,4},{6,7},{7,6},{8,9},{9,8},{10,11... | collective-permute-start | bytes 786440 | tf_op jit(solution)/shard_map/ppermute | solution.py:325
  50.2 15.5 %copy-start.9 = (bf16[1,768,1024]{2,1,0:T(8,128)(2,1)S(1)}, bf16[1,768,1024]{2,1,0:T(8,128)(2,1)}, u32[]{:S(2)}) copy-start(bf16[1,768,1024]{2,1,0:T(8,128)(2,1)} %param.24) | copy-start | bytes 4718596
  53.4 6.2 %collective-permute-start.14 = (bf16[16,8,256]{2,1,0:T(8,128)(2,1)S(1)}, bf16[16,8,256]{2,1,0:T(8,128)(2,1)S(1)}, u32[]{:S(2)}, u32[]{:S(2)}) collective-permute-start(bf16[16,8,256]{2,1,0:T(8,128)(2,1)S(1)} %get-tuple-element.43), channel_id=1, source_target_pairs={{0,8},{1,9},{2,10},{3,11},{4,12},{5,13},{6,14},{7,15},{8,0},{9,1},... | collective-permute-start | bytes 196616 | tf_op jit(solution)/shard_map/ppermute | solution.py:325
  56.1 5.0 %collective-permute-start.19 = (bf16[16,8,256]{2,1,0:T(8,128)(2,1)S(1)}, bf16[16,8,256]{2,1,0:T(8,128)(2,1)S(1)}, u32[]{:S(2)}, u32[]{:S(2)}) collective-permute-start(bf16[16,8,256]{2,1,0:T(8,128)(2,1)S(1)} %get-tuple-element.45), channel_id=1, source_target_pairs={{0,2},{1,3},{2,0},{3,1},{4,6},{5,7},{6,4},{7,5},{8,10},{9,11},{10,... | collective-permute-start | bytes 196616 | tf_op jit(solution)/shard_map/ppermute | solution.py:325
  57.6 6.3 %collective-permute-start.15 = (bf16[16,8,256]{2,1,0:T(8,128)(2,1)S(1)}, bf16[16,8,256]{2,1,0:T(8,128)(2,1)S(1)}, u32[]{:S(2)}, u32[]{:S(2)}) collective-permute-start(bf16[16,8,256]{2,1,0:T(8,128)(2,1)S(1)} %get-tuple-element.43), channel_id=1, source_target_pairs={{0,4},{1,5},{2,6},{3,7},{4,0},{5,1},{6,2},{7,3},{8,12},{9,13},{10,... | collective-permute-start | bytes 196616 | tf_op jit(solution)/shard_map/ppermute | solution.py:325
  59.7 4.3 %collective-permute-start.16 = (bf16[16,8,256]{2,1,0:T(8,128)(2,1)S(1)}, bf16[16,8,256]{2,1,0:T(8,128)(2,1)S(1)}, u32[]{:S(2)}, u32[]{:S(2)}) collective-permute-start(bf16[16,8,256]{2,1,0:T(8,128)(2,1)S(1)} %collective-permute-done.14), channel_id=1, source_target_pairs={{0,4},{1,5},{2,6},{3,7},{4,0},{5,1},{6,2},{7,3},{8,12},{9,13},{10,... | collective-permute-start | bytes 196616 | tf_op jit(solution)/shard_map/ppermute | solution.py:325
  61.1 15.1 %collective-permute-start.24 = (bf16[2,16,8,256]{3,2,1,0:T(8,128)(2,1)S(1)}, bf16[2,16,8,256]{3,2,1,0:T(8,128)(2,1)S(1)}, u32[]{:S(2)}, u32[]{:S(2)}) collective-permute-start(bf16[2,16,8,256]{3,2,1,0:T(8,128)(2,1)S(1)} %pad_maximum_fusion.4.refs_4_), channel_id=1, source_target_pairs={{0,1},{1,0},{2,3},{3,2},{4,5},{5,4},{6,7},{7,6},{8,9},{9,8},{10,11... | collective-permute-start | bytes 393224 | tf_op jit(solution)/shard_map/ppermute | solution.py:325
  61.2 13.5 %collective-permute-start.22 = (bf16[2,16,8,256]{3,2,1,0:T(8,128)(2,1)S(1)}, bf16[2,16,8,256]{3,2,1,0:T(8,128)(2,1)S(1)}, u32[]{:S(2)}, u32[]{:S(2)}) collective-permute-start(bf16[2,16,8,256]{3,2,1,0:T(8,128)(2,1)S(1)} %pad_maximum_fusion.4.refs_4_), channel_id=1, source_target_pairs={{0,4},{1,5},{2,6},{3,7},{4,0},{5,1},{6,2},{7,3},{8,12},{9,13},{10,... | collective-permute-start | bytes 393224 | tf_op jit(solution)/shard_map/ppermute | solution.py:325
  61.8 9.3 %collective-permute-start.20 = (bf16[2,16,8,256]{3,2,1,0:T(8,128)(2,1)S(1)}, bf16[2,16,8,256]{3,2,1,0:T(8,128)(2,1)S(1)}, u32[]{:S(2)}, u32[]{:S(2)}) collective-permute-start(bf16[2,16,8,256]{3,2,1,0:T(8,128)(2,1)S(1)} %pad_maximum_fusion.4.refs_4_), channel_id=1, source_target_pairs={{0,8},{1,9},{2,10},{3,11},{4,12},{5,13},{6,14},{7,15},{8,0},{9,1},... | collective-permute-start | bytes 393224 | tf_op jit(solution)/shard_map/ppermute | solution.py:325
  64.0 13.6 %collective-permute-start.18 = (bf16[4,16,8,256]{3,2,1,0:T(8,128)(2,1)S(1)}, bf16[4,16,8,256]{3,2,1,0:T(8,128)(2,1)S(1)}, u32[]{:S(2)}, u32[]{:S(2)}) collective-permute-start(bf16[4,16,8,256]{3,2,1,0:T(8,128)(2,1)S(1)} %pad_maximum_fusion.2.refs_0_), channel_id=1, source_target_pairs={{0,1},{1,0},{2,3},{3,2},{4,5},{5,4},{6,7},{7,6},{8,9},{9,8},{10,11... | collective-permute-start | bytes 786440 | tf_op jit(solution)/shard_map/ppermute | solution.py:325
  64.0 10.5 %collective-permute-start.17 = (bf16[4,16,8,256]{3,2,1,0:T(8,128)(2,1)S(1)}, bf16[4,16,8,256]{3,2,1,0:T(8,128)(2,1)S(1)}, u32[]{:S(2)}, u32[]{:S(2)}) collective-permute-start(bf16[4,16,8,256]{3,2,1,0:T(8,128)(2,1)S(1)} %pad_maximum_fusion.2.refs_0_), channel_id=1, source_target_pairs={{0,2},{1,3},{2,0},{3,1},{4,6},{5,7},{6,4},{7,5},{8,10},{9,11},{10,... | collective-permute-start | bytes 786440 | tf_op jit(solution)/shard_map/ppermute | solution.py:325
  70.5 7.2 %copy-start.1 = (bf16[4096,16]{0,1:T(8,128)(2,1)S(1)}, bf16[4096,16]{0,1:T(8,128)(2,1)}, u32[]{:S(2)}) copy-start(bf16[4096,16]{0,1:T(8,128)(2,1)} %param.21) | copy-start | bytes 393220
  70.5 7.2 %copy-start.2 = (f32[4096]{0:T(1024)S(1)}, f32[4096]{0:T(1024)}, u32[]{:S(2)}) copy-start(f32[4096]{0:T(1024)} %param.20) | copy-start | bytes 49156
  70.5 7.2 %copy-start.3 = (f32[1,4096]{1,0:T(1,128)S(1)}, f32[1,4096]{1,0:T(1,128)}, u32[]{:S(2)}) copy-start(f32[1,4096]{1,0:T(1,128)} %refs_18_.1) | copy-start | bytes 49156
  70.5 7.2 %copy-start.4 = (f32[1,2,768]{2,1,0:T(2,128)S(1)}, f32[1,2,768]{2,1,0:T(2,128)}, u32[]{:S(2)}) copy-start(f32[1,2,768]{2,1,0:T(2,128)} %param.26) | copy-start | bytes 18436
  71.2 5.0 %collective-permute-start.23 = (bf16[2,16,8,256]{3,2,1,0:T(8,128)(2,1)S(1)}, bf16[2,16,8,256]{3,2,1,0:T(8,128)(2,1)S(1)}, u32[]{:S(2)}, u32[]{:S(2)}) collective-permute-start(bf16[2,16,8,256]{3,2,1,0:T(8,128)(2,1)S(1)} %collective-permute-done.20.refs_5_), channel_id=1, source_target_pairs={{0,4},{1,5},{2,6},{3,7},{4,0},{5,1},{6,2},{7,3},{8,12},{9,13},{10,... | collective-permute-start | bytes 393224 | tf_op jit(solution)/shard_map/ppermute | solution.py:325
  74.6 3.2 %collective-permute-start.21 = (bf16[4,16,8,256]{3,2,1,0:T(8,128)(2,1)S(1)}, bf16[4,16,8,256]{3,2,1,0:T(8,128)(2,1)S(1)}, u32[]{:S(2)}, u32[]{:S(2)}) collective-permute-start(bf16[4,16,8,256]{3,2,1,0:T(8,128)(2,1)S(1)} %collective-permute-done.17.refs_1_), channel_id=1, source_target_pairs={{0,1},{1,0},{2,3},{3,2},{4,5},{5,4},{6,7},{7,6},{8,9},{9,8},{10,11... | collective-permute-start | bytes 786440 | tf_op jit(solution)/shard_map/ppermute | solution.py:325
  74.6 2.1 %collective-permute-start.25 = (bf16[2,16,8,256]{3,2,1,0:T(8,128)(2,1)S(1)}, bf16[2,16,8,256]{3,2,1,0:T(8,128)(2,1)S(1)}, u32[]{:S(2)}, u32[]{:S(2)}) collective-permute-start(bf16[2,16,8,256]{3,2,1,0:T(8,128)(2,1)S(1)} %collective-permute-done.20.refs_5_), channel_id=1, source_target_pairs={{0,1},{1,0},{2,3},{3,2},{4,5},{5,4},{6,7},{7,6},{8,9},{9,8},{10,11... | collective-permute-start | bytes 393224 | tf_op jit(solution)/shard_map/ppermute | solution.py:325
  76.2 1.3 %collective-permute-start.26 = (bf16[2,16,8,256]{3,2,1,0:T(8,128)(2,1)S(1)}, bf16[2,16,8,256]{3,2,1,0:T(8,128)(2,1)S(1)}, u32[]{:S(2)}, u32[]{:S(2)}) collective-permute-start(bf16[2,16,8,256]{3,2,1,0:T(8,128)(2,1)S(1)} %collective-permute-done.22.refs_6_), channel_id=1, source_target_pairs={{0,1},{1,0},{2,3},{3,2},{4,5},{5,4},{6,7},{7,6},{8,9},{9,8},{10,11... | collective-permute-start | bytes 393224 | tf_op jit(solution)/shard_map/ppermute | solution.py:325
  76.2 1.5 %collective-permute-start.27 = (bf16[2,16,8,256]{3,2,1,0:T(8,128)(2,1)S(1)}, bf16[2,16,8,256]{3,2,1,0:T(8,128)(2,1)S(1)}, u32[]{:S(2)}, u32[]{:S(2)}) collective-permute-start(bf16[2,16,8,256]{3,2,1,0:T(8,128)(2,1)S(1)} %collective-permute-done.23.refs_7_), channel_id=1, source_target_pairs={{0,1},{1,0},{2,3},{3,2},{4,5},{5,4},{6,7},{7,6},{8,9},{9,8},{10,11... | collective-permute-start | bytes 393224 | tf_op jit(solution)/shard_map/ppermute | solution.py:325
  85.3 2.0 %collective-permute-start.28 = (bf16[8,8,4096]{2,1,0:T(8,128)(2,1)S(1)}, bf16[8,8,4096]{2,1,0:T(8,128)(2,1)S(1)}, u32[]{:S(2)}, u32[]{:S(2)}) collective-permute-start(bf16[8,8,4096]{2,1,0:T(8,128)(2,1)S(1)} %get-tuple-element.55), channel_id=1, source_target_pairs={{0,1},{1,0},{2,3},{3,2},{4,5},{5,4},{6,7},{7,6},{8,9},{9,8},{10,11... | collective-permute-start | bytes 1572872 | tf_op jit(solution)/shard_map/ppermute | solution.py:325
  85.7 3.2 %collective-permute-start.32 = (bf16[8,8,4096]{2,1,0:T(8,128)(2,1)S(1)}, bf16[8,8,4096]{2,1,0:T(8,128)(2,1)S(1)}, u32[]{:S(2)}, u32[]{:S(2)}) collective-permute-start(bf16[8,8,4096]{2,1,0:T(8,128)(2,1)S(1)} %get-tuple-element.58), channel_id=1, source_target_pairs={{0,1},{1,0},{2,3},{3,2},{4,5},{5,4},{6,7},{7,6},{8,9},{9,8},{10,11... | collective-permute-start | bytes 1572872 | tf_op jit(solution)/shard_map/ppermute | solution.py:325
  87.4 8.6 %collective-permute-start.29 = (bf16[4,8,4096]{2,1,0:T(8,128)(2,1)S(1)}, bf16[4,8,4096]{2,1,0:T(8,128)(2,1)S(1)}, u32[]{:S(2)}, u32[]{:S(2)}) collective-permute-start(bf16[4,8,4096]{2,1,0:T(8,128)(2,1)S(1)} %get-tuple-element.60), channel_id=1, source_target_pairs={{0,2},{1,3},{2,0},{3,1},{4,6},{5,7},{6,4},{7,5},{8,10},{9,11},{10,... | collective-permute-start | bytes 786440 | tf_op jit(solution)/shard_map/ppermute | solution.py:325
  89.1 8.6 %collective-permute-start.33 = (bf16[4,8,4096]{2,1,0:T(8,128)(2,1)S(1)}, bf16[4,8,4096]{2,1,0:T(8,128)(2,1)S(1)}, u32[]{:S(2)}, u32[]{:S(2)}) collective-permute-start(bf16[4,8,4096]{2,1,0:T(8,128)(2,1)S(1)} %get-tuple-element.62), channel_id=1, source_target_pairs={{0,4},{1,5},{2,6},{3,7},{4,0},{5,1},{6,2},{7,3},{8,12},{9,13},{10,... | collective-permute-start | bytes 786440 | tf_op jit(solution)/shard_map/ppermute | solution.py:325
  96.1 6.7 %collective-permute-start.30 = (bf16[2,8,4096]{2,1,0:T(8,128)(2,1)S(1)}, bf16[2,8,4096]{2,1,0:T(8,128)(2,1)S(1)}, u32[]{:S(2)}, u32[]{:S(2)}) collective-permute-start(bf16[2,8,4096]{2,1,0:T(8,128)(2,1)S(1)} %get-tuple-element.64), channel_id=1, source_target_pairs={{0,4},{1,5},{2,6},{3,7},{4,0},{5,1},{6,2},{7,3},{8,12},{9,13},{10,... | collective-permute-start | bytes 393224 | tf_op jit(solution)/shard_map/ppermute | solution.py:325
  97.7 10.6 %collective-permute-start.34 = (bf16[2,8,4096]{2,1,0:T(8,128)(2,1)S(1)}, bf16[2,8,4096]{2,1,0:T(8,128)(2,1)S(1)}, u32[]{:S(2)}, u32[]{:S(2)}) collective-permute-start(bf16[2,8,4096]{2,1,0:T(8,128)(2,1)S(1)} %get-tuple-element.66), channel_id=1, source_target_pairs={{0,8},{1,9},{2,10},{3,11},{4,12},{5,13},{6,14},{7,15},{8,0},{9,1},... | collective-permute-start | bytes 393224 | tf_op jit(solution)/shard_map/ppermute | solution.py:325
  102.8 6.3 %collective-permute-start.31 = (bf16[1,8,4096]{2,1,0:T(8,128)(2,1)S(1)}, bf16[1,8,4096]{2,1,0:T(8,128)(2,1)S(1)}, u32[]{:S(2)}, u32[]{:S(2)}) collective-permute-start(bf16[1,8,4096]{2,1,0:T(8,128)(2,1)S(1)} %add_convert_fusion.10), channel_id=1, source_target_pairs={{0,8},{1,9},{2,10},{3,11},{4,12},{5,13},{6,14},{7,15},{8,0},{9,1},... | collective-permute-start | bytes 196616 | tf_op jit(solution)/shard_map/ppermute | solution.py:325
  108.4 4.3 %collective-permute-start.35 = (bf16[1,8,4096]{2,1,0:T(8,128)(2,1)S(1)}, bf16[1,8,4096]{2,1,0:T(8,128)(2,1)S(1)}, u32[]{:S(2)}, u32[]{:S(2)}) collective-permute-start(bf16[1,8,4096]{2,1,0:T(8,128)(2,1)S(1)} %add_convert_fusion.8), channel_id=1, source_target_pairs={{0,2},{1,3},{2,0},{3,1},{4,6},{5,7},{6,4},{7,5},{8,10},{9,11},{10,... | collective-permute-start | bytes 196616 | tf_op jit(solution)/shard_map/ppermute | solution.py:325
